TPU v7x, 256 devices: a whole 4x4x8 slice. The times are simulated.
256 devices in a mesh: bra: 8 (over z), ket: 8 (over y, core), pair: 4 (over x).
Axes of the slice: x: 4, y: 4, z: 8, core: 2. Of those that a mesh axis runs over, the one named last changes fastest.
Arguments:
- amplitudes: bfloat16 [1536, 64, 1536], P('pair', ('bra', 'ket')), may hold values from -6 to 6
- integrals: bfloat16 [64, 32, 128, 1536], P(('bra', 'ket'), 'pair'), may hold values from -0.09375 to 0.09375
- screen_list: int32 [64, 32], P(('bra', 'ket')), may hold values from 0 to 11
- block_owner: int32 [64, 32], P(('bra', 'ket')), may hold values from 0 to 63, all different within a row
- mirror_map: int32 [64, 1536], replicated, may hold values from 0 to 1535, as said below
- pair_virt: int32 [64, 2, 1536], P(('bra', 'ket')), may hold values from 0 to 2047, as said below
- vir_energy: float32 [2048], replicated, may hold values from 0.1 to 1.5
- pair_energy: float32 [1536], P('pair'), may hold values from -1.5 to -0.4
Outputs:
- new_amplitudes: bfloat16 [1536, 64, 1536], P('pair', ('bra', 'ket'))
Inputs may be any that keep to these rules, and one draw needn't show every extreme that they name: `block_owner`: the 32 entries of a row are distinct. `mirror_map`: every row is a permutation of 0 to 1535, and row t + 32 is the inverse permutation of row t. `pair_virt`: if position p of tile t < 32 holds the orbitals (a, b), position mirror_map[t, p] of tile t + 32 holds (b, a).
All inputs are finite; a program needn't handle non-finite values.
Results may differ from a plain program's by a relative error of at most 0.0045.
Values may be sent and summed in bfloat16 or wider, within the bound.
No kernel may reach another device: no remote copies, remote signals or barrier semaphores. Data moves between devices by JAX's collectives and lax.ppermute only.
A program may use at most 64 MiB of HBM per device.

v0:
```python
import jax
import jax.numpy as jnp
from jax import lax
from jax.sharding import PartitionSpec as P


def partner(block, axis, apart):
    count = lax.axis_size(axis)
    route = []
    for low in range(count):
        high = low | 1 << apart
        if high != low and high < count:
            route += [(low, high), (high, low)]
    return lax.ppermute(block, axis, route)


def permute_columns(tile_data, indices):
    return jnp.take(tile_data, indices, axis=1)


def local(
    amplitudes, integrals, screen_list, block_owner, mirror_map, pair_virt, vir_energy, pair_energy
):
    owners = lax.axis_size(("bra", "ket"))
    half_tiles = owners // 2
    mirror_bit = owners.bit_length() - 2
    self_index = lax.axis_index(("bra", "ket"))
    is_upper = self_index >= half_tiles
    folded_index = self_index % half_tiles
    map_lower = lax.dynamic_index_in_dim(mirror_map, folded_index, 0, keepdims=False)
    map_upper = lax.dynamic_index_in_dim(mirror_map, folded_index + half_tiles, 0, keepdims=False)
    own_tile = amplitudes[:, 0, :]
    rows_dev, block_len = own_tile.shape
    seg_width = integrals.shape[2]
    seg_count = block_len // seg_width
    partner_tile = partner(own_tile, ("bra", "ket"), mirror_bit)
    lower_raw = jnp.where(is_upper, partner_tile, own_tile)
    upper_raw = jnp.where(is_upper, own_tile, partner_tile)
    sym_fold = (
        (lower_raw.astype(jnp.float32) + permute_columns(upper_raw, map_lower).astype(jnp.float32))
        * 0.5
    ).astype(jnp.bfloat16)
    anti_fold = (
        (upper_raw.astype(jnp.float32) - permute_columns(lower_raw, map_upper).astype(jnp.float32))
        * 0.5
    ).astype(jnp.bfloat16)
    wanted_owner = block_owner[0]
    wanted_segment = screen_list[0]
    sender_ids = jnp.arange(owners, dtype=jnp.int32)
    matches = wanted_owner[None, :] == sender_ids[:, None]
    request = jnp.sum(jnp.where(matches, wanted_segment[None, :] + 1, 0), axis=1) - 1
    requested = lax.all_to_all(
        request[:, None], ("bra", "ket"), split_axis=0, concat_axis=0, tiled=True
    )[:, 0]
    receiver_upper = (sender_ids >= half_tiles).astype(jnp.int32)
    slot_index = receiver_upper * seg_count + jnp.maximum(requested, 0)
    folded_both = jnp.concatenate(
        [
            sym_fold.reshape(rows_dev, seg_count, seg_width),
            anti_fold.reshape(rows_dev, seg_count, seg_width),
        ],
        axis=1,
    )
    outgoing = jnp.take(folded_both, slot_index, axis=1)
    incoming = lax.all_to_all(outgoing, ("bra", "ket"), split_axis=1, concat_axis=1, tiled=True)
    operand = jnp.take(incoming, wanted_owner, axis=1).reshape(rows_dev, -1)
    local_count = integrals.shape[1]
    pair_count = lax.axis_size("pair")
    grouped = operand.reshape(rows_dev, pair_count, local_count * seg_width)
    received = lax.all_to_all(grouped, "pair", split_axis=1, concat_axis=0, tiled=True)
    all_rows = received.reshape(rows_dev * pair_count, local_count * seg_width)
    flat_blocks = integrals[0].reshape(local_count * seg_width, block_len)
    ladder = lax.psum_scatter(
        jnp.dot(all_rows, flat_blocks, preferred_element_type=jnp.float32),
        "pair",
        scatter_dimension=0,
        tiled=True,
    )
    partner_ladder = partner(ladder.astype(jnp.bfloat16), ("bra", "ket"), mirror_bit).astype(
        ladder.dtype
    )
    own_map = jnp.where(is_upper, map_upper, map_lower)
    direction = jnp.where(is_upper, 1.0, -1.0).astype(jnp.float32)
    residual = ladder + direction * permute_columns(partner_ladder, own_map)
    energy_first = jnp.take(vir_energy, pair_virt[0, 0])
    energy_second = jnp.take(vir_energy, pair_virt[0, 1])
    denominator = pair_energy[:, None] - energy_first[None, :] - energy_second[None, :]
    updated = own_tile.astype(jnp.float32) + residual / denominator
    return updated.astype(jnp.bfloat16)[:, None, :]


def solution(mesh):
    placed = (
        P("pair", ("bra", "ket"), None),
        P(("bra", "ket"), "pair", None, None),
        P(("bra", "ket"), None),
        P(("bra", "ket"), None),
        P(),
        P(("bra", "ket"), None, None),
        P(),
        P("pair"),
    )
    return jax.shard_map(
        local,
        mesh=mesh,
        in_specs=placed,
        out_specs=P("pair", ("bra", "ket"), None),
        check_vma=False,
    )
```

profile of v0, /device:TPU:47, one launch (start us, length us, event | category | flops | bytes accessed | tf_op | source)
XLA Modules:
  0.0 507.5 jit_solution(11525132559040597424)
XLA Ops:
  6.5 6.0 %collective-permute-start = (bf16[384,1536]{1,0:T(8,128)(2,1)}, bf16[384,1536]{1,0:T(8,128)(2,1)}, u32[]{:S(2)}, u32[]{:S(2)}) collective-permute-start(bf16[384,1536]{1,0:T(8,128)(2,1)} %bitcast.64), channel_id=1, source_target_pairs={{0,128},{128,0},{4,132},{132,4},{8,136},{136,8},{12,140},{140,12},... | collective-permute-start | bytes 3538952 | tf_op jit(solution)/shard_map/ppermute | solution.py:14
  12.5 0.7 add_bitcast_fusion.1
  13.2 0.7 select_reduce_fusion
  14.0 0.7 copy.63
  14.7 7.9 %all-to-all-start = ((s32[64,1,1]{2,1,0:T(1,128)}), s32[64,1,1]{2,1,0:T(1,128)S(1)}, u32[]{:S(2)}, u32[]{:S(2)}) async-start(s32[64,1,1]{2,1,0:T(1,128)} %copy.63), calls=%async_computation | async-start | bytes 65536 | tf_op jit(solution)/shard_map/all_to_all | solution.py:52
  22.6 0.9 dynamic-slice_reduce_fusion.1
  23.5 43.4 %all-to-all-done = s32[64,1,1]{2,1,0:T(1,128)S(1)} async-done(((s32[64,1,1]{2,1,0:T(1,128)}), s32[64,1,1]{2,1,0:T(1,128)S(1)}, u32[]{:S(2)}, u32[]{:S(2)}) %all-to-all-start) | async-done | bytes 288 | tf_op jit(solution)/shard_map/all_to_all | solution.py:52
  66.9 1.2 maximum_reduce_fusion
  68.2 2.8 broadcast_select_fusion
  71.0 2.4 copy.64
  73.3 6.4 %gather_fusion.3 = bf16[1536,384]{1,0:T(8,128)(2,1)} fusion(bf16[384,1536]{0,1:T(8,128)(2,1)} %copy.64, s32[2048]{0:T(1024)S(1)} %pad_clamp_fusion.4), kind=kCustom, calls=%fused_computation.clone | custom fusion | bytes 2365440 | tf_op jit(solution)/shard_map/jit(_take)/gather | solution.py:18
  79.8 2.4 copy.65
  82.2 3.6 multiply_convert_fusion.1
  85.8 2.4 copy.67
  88.2 6.4 %gather_fusion.4 = bf16[1536,384]{1,0:T(8,128)(2,1)} fusion(bf16[384,1536]{0,1:T(8,128)(2,1)} %copy.67, s32[2048]{0:T(1024)S(1)} %pad_clamp_fusion.3), kind=kCustom, calls=%fused_computation.2.clone | custom fusion | bytes 2365440 | tf_op jit(solution)/shard_map/jit(_take)/gather | solution.py:18
  94.6 2.4 copy.68
  97.0 3.1 multiply_convert_fusion
  100.1 2.4 copy.69
  102.5 2.4 copy.71
  104.9 2.4 copy.66
  107.2 2.4 copy.70
  109.6 3.2 pad_maximum_fusion
  112.9 5.7 %gather_fusion = bf16[64,384,128]{2,1,0:T(8,128)(2,1)} fusion(bf16[384,24,128]{2,0,1:T(8,128)(2,1)} %pad_maximum_fusion, s32[1024]{0:T(1024)S(1)} %pad_clamp_fusion.6), kind=kCustom, calls=%fused_computation.4 | custom fusion | bytes 12583168 | tf_op jit(solution)/shard_map/jit(_take)/gather | solution.py:64
  118.5 6.1 %select_bitcast_fusion = bf16[384,64,128]{2,0,1:T(8,128)(2,1)} fusion(bf16[64,384,128]{2,1,0:T(8,128)(2,1)} %gather_fusion, pred[64]{0:T(512)(128)(4,1)S(1)} %compare_and_fusion.3), kind=kLoop, calls=%fused_computation.7 | loop fusion | flops 3145728 | bytes 12582976 | tf_op jit(solution)/shard_map/jit(_take)/select_n | solution.py:64
  124.6 10.0 %all-to-all-start.1 = ((bf16[384,64,128]{2,0,1:T(8,128)(2,1)}), bf16[384,64,128]{2,0,1:T(8,128)(2,1)}, u32[]{:S(2)}, u32[]{:S(2)}) async-start(bf16[384,64,128]{2,0,1:T(8,128)(2,1)} %select_bitcast_fusion), calls=%async_computation.1 | async-start | bytes 12582912 | tf_op jit(solution)/shard_map/all_to_all | solution.py:65
  134.6 0.0 reduce-scatter.2.cloned.1.call-start
  134.7 0.5 broadcast.245
  135.2 0.7 reduce.16
  135.9 0.1 squeeze.25
  136.0 0.1 broadcast_bitcast_fusion
  136.1 139.0 %all-to-all-done.1 = bf16[384,64,128]{2,0,1:T(8,128)(2,1)} async-done(((bf16[384,64,128]{2,0,1:T(8,128)(2,1)}), bf16[384,64,128]{2,0,1:T(8,128)(2,1)}, u32[]{:S(2)}, u32[]{:S(2)}) %all-to-all-start.1) | async-done | bytes 6291488 | tf_op jit(solution)/shard_map/all_to_all | solution.py:65
  275.1 5.4 %gather_fusion.1 = bf16[32,384,128]{2,1,0:T(8,128)(2,1)} fusion(bf16[384,64,128]{2,0,1:T(8,128)(2,1)} %all-to-all-done.1, s32[1024]{0:T(1024)S(1)} %pad_clamp_fusion.5), kind=kCustom, calls=%fused_computation.5 | custom fusion | bytes 6291584 | tf_op jit(solution)/shard_map/jit(_take)/gather | solution.py:66
  280.5 4.6 copy.72
  285.2 2.3 bitcast_select_fusion
  287.4 39.0 %all_to_all.26 = bf16[384,4,1024]{0,2,1:T(8,128)(2,1)} all-to-all(bf16[384,4,1024]{0,2,1:T(8,128)(2,1)S(1)} %bitcast_select_fusion), channel_id=1, replica_groups=mesh['bra'=8,'ket'=8,'pair'=4] {'pair'}, dimensions={1} | all-to-all | bytes 6291456 | tf_op jit(solution)/shard_map/all_to_all | solution.py:70
  326.4 4.6 copy.73
  331.1 9.5 %fusion.10 = f32[1536,1536]{1,0:T(8,128)} fusion(bf16[1536,1024]{1,0:T(8,128)(2,1)} %bitcast.67, bf16[1024,1536]{1,0:T(8,128)(2,1)S(1)} %bitcast.60), kind=kOutput, calls=%fused_computation.63 | convolution fusion | flops 4831838208 | bytes 15728640 | tf_op jit(solution)/shard_map/dot_general | solution.py:74
  340.6 87.8 %reduce-scatter.2.cloned.1.call-done = f32[384,1536]{1,0:T(8,128)} async-done(((f32[1536,1536]{1,0:T(8,128)}), f32[384,1536]{1,0:T(8,128)}) %reduce-scatter.2.cloned.1.call-update) | async-done | bytes 2359312 | tf_op jit(solution)/shard_map/reduce_scatter | solution.py:73
  428.4 1.8 convert_element_type.38
  430.2 4.6 collective-permute-start.1
  434.9 8.4 %gather_fusion.5 = f32[1536]{0:T(1024)S(1)} fusion(f32[2048]{0:T(1024)S(1)} %copy-done.2, s32[2048]{0:T(1024)S(1)} %pad_clamp_fusion.1), kind=kCustom, calls=%fused_computation.1.clone | custom fusion | bytes 18432 | tf_op jit(solution)/shard_map/jit(_take)/gather | solution.py:85
  443.3 8.4 %gather_fusion.6 = f32[1536]{0:T(1024)S(1)} fusion(f32[2048]{0:T(1024)S(1)} %copy-done.2, s32[2048]{0:T(1024)S(1)} %pad_clamp_fusion), kind=kCustom, calls=%fused_computation.3.clone | custom fusion | bytes 18432 | tf_op jit(solution)/shard_map/jit(_take)/gather | solution.py:86
  451.7 0.9 fusion.4
  452.6 33.8 %collective-permute-done.1 = bf16[384,1536]{1,0:T(8,128)(2,1)} collective-permute-done((bf16[384,1536]{1,0:T(8,128)(2,1)S(1)}, bf16[384,1536]{1,0:T(8,128)(2,1)}, u32[]{:S(2)}, u32[]{:S(2)}) %collective-permute-start.1) | collective-permute-done | bytes 1179680 | tf_op jit(solution)/shard_map/ppermute | solution.py:14
  486.4 1.6 copy.74
  488.0 4.8 gather_fusion.2
  492.8 3.1 copy.75
  495.9 4.7 fusion.3
  (33 shorter events, 0.2 us)
Async XLA Ops:
  6.5 324.5 %copy-start = (bf16[1,8,128,1536]{3,2,1,0:T(8,128)(2,1)S(1)}, bf16[1,8,128,1536]{3,2,1,0:T(8,128)(2,1)}, u32[]{:S(2)}) copy-start(bf16[1,8,128,1536]{3,2,1,0:T(8,128)(2,1)} %param.13) | copy-start | bytes 9437188
  6.5 61.7 %collective-permute-start = (bf16[384,1536]{1,0:T(8,128)(2,1)}, bf16[384,1536]{1,0:T(8,128)(2,1)}, u32[]{:S(2)}, u32[]{:S(2)}) collective-permute-start(bf16[384,1536]{1,0:T(8,128)(2,1)} %bitcast.64), channel_id=1, source_target_pairs={{0,128},{128,0},{4,132},{132,4},{8,136},{136,8},{12,140},{140,12},... | collective-permute-start | bytes 3538952 | tf_op jit(solution)/shard_map/ppermute | solution.py:14
  14.7 52.3 %all-to-all-start = ((s32[64,1,1]{2,1,0:T(1,128)}), s32[64,1,1]{2,1,0:T(1,128)S(1)}, u32[]{:S(2)}, u32[]{:S(2)}) async-start(s32[64,1,1]{2,1,0:T(1,128)} %copy.63), calls=%async_computation | async-start | bytes 65536 | tf_op jit(solution)/shard_map/all_to_all | solution.py:52
  124.6 10.6 %copy-start.5 = (s32[1,32]{1,0:T(1,128)S(1)}, s32[1,32]{1,0:T(1,128)}, u32[]{:S(2)}) copy-start(s32[1,32]{1,0:T(1,128)} %param.15) | copy-start | bytes 388
  124.6 150.5 %all-to-all-start.1 = ((bf16[384,64,128]{2,0,1:T(8,128)(2,1)}), bf16[384,64,128]{2,0,1:T(8,128)(2,1)}, u32[]{:S(2)}, u32[]{:S(2)}) async-start(bf16[384,64,128]{2,0,1:T(8,128)(2,1)} %select_bitcast_fusion), calls=%async_computation.1 | async-start | bytes 12582912 | tf_op jit(solution)/shard_map/all_to_all | solution.py:65
  134.6 293.7 %reduce-scatter.2.cloned.1.call-start = ((), (), s32[]{:S(2)}) async-start(), calls=%async_computation.4 | async-start | bytes 11796480 | tf_op jit(solution)/shard_map/reduce_scatter | solution.py:73
  340.5 94.3 %copy-start.3 = (s32[1,2,1536]{2,1,0:T(2,128)S(1)}, s32[1,2,1536]{2,1,0:T(2,128)}, u32[]{:S(2)}) copy-start(s32[1,2,1536]{2,1,0:T(2,128)} %param.17) | copy-start | bytes 36868
  340.6 94.3 %copy-start.2 = (f32[2048]{0:T(1024)S(1)}, f32[2048]{0:T(1024)}, u32[]{:S(2)}) copy-start(f32[2048]{0:T(1024)} %param.18) | copy-start | bytes 24580
  430.2 56.3 %collective-permute-start.1 = (bf16[384,1536]{1,0:T(8,128)(2,1)S(1)}, bf16[384,1536]{1,0:T(8,128)(2,1)}, u32[]{:S(2)}, u32[]{:S(2)}) collective-permute-start(bf16[384,1536]{1,0:T(8,128)(2,1)S(1)} %convert_element_type.38), channel_id=1, source_target_pairs={{0,128},{128,0},{4,132},{132,4},{8,136},{136,8},{12,140},{140,12},... | collective-permute-start | bytes 3538952 | tf_op jit(solution)/shard_map/ppermute | solution.py:14
  492.8 3.2 copy-start.4
  495.9 4.7 copy-start.1
Sparse Core Ops, SparseCore 0:
  340.7 87.6 reduce-scatter.1
where the time goes:
time: 511 us; the launch traced here: 507 us
  waiting for transfers between devices  304 us (59%)
  local copies, waits for them, and re-layouts  80.9 us (16%)
  blocking collectives  39 us (8%)
  other arithmetic  31.8 us (6%)
  starting transfers between devices  28.6 us (6%)
  between operations  13.7 us (3%)
  matrix products  9.45 us (2%)
    all_to_all x1, waiting for transfers between devices, local(): lax.all_to_all(outgoing, ('bra', 'ket'), split_axis=1, concat_axis=1, til...  139 us
    reduce_scatter x1, waiting for transfers between devices, local(): lax.psum_scatter(jnp.dot(all_rows, flat_blocks, preferred_element_type=jn...  87.8 us
    all_to_all x1, waiting for transfers between devices, local(): lax.all_to_all(request[:, None], ('bra', 'ket'), split_axis=0, concat_axi...  43.4 us
    all_to_all x1, blocking collectives, local(): lax.all_to_all(grouped, 'pair', split_axis=1, concat_axis=0, tiled=True)  39 us
    ppermute x2, waiting for transfers between devices, partner(): return lax.ppermute(block, axis, route)  33.8 us
    gather x6, local copies, waits for them, and re-layouts, permute_columns(): return jnp.take(tile_data, indices, axis=1)  25.6 us
    ppermute x2, starting transfers between devices, partner(): return lax.ppermute(block, axis, route)  10.7 us
  transfers between devices with their start and end apart: 5, of which 4 were waited for; matrix products, arithmetic and copies ran while one was open for 5% of the time, Pallas kernels for 0%

commit v1 on v0

v1 whole, which is shorter than its diff:
```python
import functools

import jax
import jax.numpy as jnp
from jax import lax
from jax.experimental import pallas as pl
from jax.experimental.pallas import tpu as pltpu
from jax.sharding import PartitionSpec as P

COLS = 256
VMEM = 48 * 1024 * 1024


def one_hot(row, length, width):
    number = lax.broadcasted_iota(jnp.int32, (length, width), 0)
    return jnp.where(number == row, 1.0, 0.0).astype(jnp.bfloat16)


def fold_body(shifts, facts, maps, *refs):
    count = len(shifts)
    tiles, out = refs[: 2 * count], refs[2 * count]
    base, other, folded, base_sem, other_sem, out_sem = refs[2 * count + 1 :]
    z = facts[0]
    sign = jnp.where(z < 4, 1.0, -1.0).astype(jnp.float32)
    rows, length = folded.shape[1:]

    def fetch(i, turned):
        first, second = tiles[2 * i], tiles[2 * i + 1]
        if turned:
            first, second = second, first
        return (
            pltpu.make_async_copy(first, base.at[i], base_sem.at[i]),
            pltpu.make_async_copy(second, other.at[i], other_sem.at[i]),
        )

    def straight(shift):
        moved = z + shift
        return ((moved + 8) & 7) >> 2 == z >> 2

    for i, shift in enumerate(shifts):
        for turned in (False, True):

            @pl.when(straight(shift) != turned)
            def _():
                for copy in fetch(i, turned):
                    copy.start()

    for i, shift in enumerate(shifts):
        low = (z + shift + 8) & 3
        for copy in fetch(i, False):
            copy.wait()

        def column(c, carry):
            start = pl.multiple_of(c * COLS, COLS)
            picks = one_hot(maps[low, :, pl.ds(start, COLS)], length, COLS)
            turned = jnp.dot(other[i], picks, preferred_element_type=jnp.float32)
            mine = base[i, :, pl.ds(start, COLS)].astype(jnp.float32)
            folded[i, :, pl.ds(start, COLS)] = ((mine + sign * turned) * 0.5).astype(jnp.bfloat16)
            return carry

        lax.fori_loop(0, length // COLS, column, 0)

        for receiver in range(8):
            for half in range(2):
                segment = facts[1 + receiver * 8 + low + 4 * half]

                @pl.when(segment >= 0)
                def _():
                    start = pl.multiple_of(segment * 128, 128)
                    pltpu.make_async_copy(
                        folded.at[i, :, pl.ds(start, 128)],
                        out.at[receiver, 2 * i + half],
                        out_sem.at[i, receiver, half],
                    ).start()

    for i, shift in enumerate(shifts):
        low = (z + shift + 8) & 3
        for receiver in range(8):
            for half in range(2):

                @pl.when(facts[1 + receiver * 8 + low + 4 * half] >= 0)
                def _():
                    pltpu.make_async_copy(
                        folded.at[i, :, pl.ds(0, 128)],
                        out.at[receiver, 2 * i + half],
                        out_sem.at[i, receiver, half],
                    ).wait()


def fold(shifts, facts, maps, tiles):
    rows, length = tiles[0].shape
    count = len(shifts)
    whole = pltpu.VMEM((count, rows, length), jnp.bfloat16)
    return pl.pallas_call(
        functools.partial(fold_body, shifts),
        in_specs=[pl.BlockSpec(memory_space=pltpu.SMEM), pl.BlockSpec(memory_space=pltpu.VMEM)]
        + [pl.BlockSpec(memory_space=pl.ANY)] * (2 * count),
        out_specs=pl.BlockSpec(memory_space=pl.ANY),
        out_shape=jax.ShapeDtypeStruct((8, 2 * count, rows, 128), jnp.bfloat16),
        scratch_shapes=[
            whole,
            whole,
            whole,
            pltpu.SemaphoreType.DMA((count,)),
            pltpu.SemaphoreType.DMA((count,)),
            pltpu.SemaphoreType.DMA((count, 8, 2)),
        ],
        compiler_params=pltpu.CompilerParams(vmem_limit_bytes=VMEM),
        cost_estimate=pl.CostEstimate(
            flops=2 * count * rows * length * length,
            bytes_accessed=count * rows * (4 * length + 16 * 256),
            transcendentals=0,
        ),
        name="fold",
    )(facts, maps, *tiles)


def ladder_body(facts, send_map, blocks, near, odd, opposite, ladder, sent, operand, rounded, sem):
    step = pl.program_id(0)
    slots = operand.shape[1] // 128
    length = rounded.shape[1]

    @pl.when(step == 0)
    def _():
        def place(k):
            return operand.at[:, pl.ds(k * 128, 128)]

        for k in range(slots):
            tile = facts[1 + k]
            z, ket = tile >> 3, tile & 7
            away, half = (z - facts[0] + 8) & 3, z >> 2

            @pl.when(away == 0)
            def _():
                pltpu.make_async_copy(near.at[ket, half], place(k), sem.at[k]).start()

            @pl.when((away & 1) == 1)
            def _():
                source = odd.at[ket, (away >> 1) * 2 + half]
                pltpu.make_async_copy(source, place(k), sem.at[k]).start()

            @pl.when(away == 2)
            def _():
                pltpu.make_async_copy(opposite.at[ket, half], place(k), sem.at[k]).start()

        for k in range(slots):
            pltpu.make_async_copy(near.at[0, 0], place(k), sem.at[k]).wait()

    total = jnp.dot(operand[...], blocks[...], preferred_element_type=jnp.float32)
    ladder[...] = total
    rounded[:, pl.ds(pl.multiple_of(step * COLS, COLS), COLS)] = total.astype(jnp.bfloat16)

    @pl.when(step == pl.num_programs(0) - 1)
    def _():
        def column(c, carry):
            start = pl.multiple_of(c * COLS, COLS)
            picks = one_hot(send_map[:, pl.ds(start, COLS)], length, COLS)
            moved = jnp.dot(rounded[...], picks, preferred_element_type=jnp.float32)
            sent[:, pl.ds(start, COLS)] = moved.astype(jnp.bfloat16)
            return carry

        lax.fori_loop(0, length // COLS, column, 0)


def ladder_of(facts, send_map, blocks, near, odd, opposite):
    depth, length = blocks.shape
    rows = near.shape[2]
    held = pl.BlockSpec(memory_space=pl.ANY)
    return pl.pallas_call(
        ladder_body,
        grid=(length // COLS,),
        in_specs=[
            pl.BlockSpec(memory_space=pltpu.SMEM),
            pl.BlockSpec((1, length), lambda n: (0, 0)),
            pl.BlockSpec((depth, COLS), lambda n: (0, n)),
            held,
            held,
            held,
        ],
        out_specs=[
            pl.BlockSpec((rows, COLS), lambda n: (0, n)),
            pl.BlockSpec((rows, length), lambda n: (0, 0)),
        ],
        out_shape=[
            jax.ShapeDtypeStruct((rows, length), jnp.float32),
            jax.ShapeDtypeStruct((rows, length), jnp.bfloat16),
        ],
        scratch_shapes=[
            pltpu.VMEM((rows, depth), jnp.bfloat16),
            pltpu.VMEM((rows, length), jnp.bfloat16),
            pltpu.SemaphoreType.DMA((depth // 128,)),
        ],
        compiler_params=pltpu.CompilerParams(
            vmem_limit_bytes=VMEM, dimension_semantics=("arbitrary",)
        ),
        cost_estimate=pl.CostEstimate(
            flops=2 * rows * depth * length,
            bytes_accessed=2 * depth * (rows + length),
            transcendentals=0,
        ),
        name="ladder",
    )(facts, send_map, blocks, near, odd, opposite)


def shifted(block, by):
    return lax.ppermute(block, "bra", [(i, (i + by) % 8) for i in range(8)])


def energies(table, indices):
    number = lax.broadcasted_iota(jnp.int32, (table.shape[0], 1), 0)
    return jnp.sum(jnp.where(number == indices[None, :], table[:, None], 0.0), axis=0)


def local(
    amplitudes, integrals, screen_list, block_owner, mirror_map, pair_virt, vir_energy, pair_energy
):
    z, ket = lax.axis_index("bra"), lax.axis_index("ket")
    own = amplitudes[:, 0, :]
    rows, length = own.shape
    all_blocks = lax.all_gather(integrals[0], "pair", axis=0, tiled=True).reshape(-1, length)

    wanted = lax.all_gather(block_owner[0] * 16 + screen_list[0], "ket", axis=0)
    served = jnp.arange(8, dtype=jnp.int32) * 8 + ket
    match = (wanted >> 4)[:, None, :] == served[None, :, None]
    asked = jnp.max(jnp.where(match, wanted[:, None, :] & 15, -1), axis=2)
    fold_facts = jnp.concatenate([z.astype(jnp.int32)[None], asked.reshape(-1)])
    ladder_facts = jnp.concatenate([z.astype(jnp.int32)[None], block_owner[0]])
    grid_maps = mirror_map.reshape(2, 4, 8, length)
    half_maps = lax.dynamic_index_in_dim(grid_maps, z >> 2, 0, keepdims=False)
    maps = lax.dynamic_index_in_dim(half_maps, ket, 1, keepdims=True)
    send_map = lax.dynamic_index_in_dim(mirror_map, ((z + 4) & 7) * 8 + ket, 0, keepdims=True)

    up1, down1 = shifted(own, -1), shifted(own, 1)
    up2, down2 = shifted(up1, -1), shifted(down1, 1)
    up3, down3 = shifted(up2, -1), shifted(down2, 1)
    cut = rows // 2
    far = jnp.concatenate([shifted(up3[:cut], -1), shifted(down3[cut:], 1)], axis=0)

    def exchange(block):
        return lax.all_to_all(block, "ket", split_axis=0, concat_axis=0, tiled=True)

    opposite = exchange(fold((2,), fold_facts, maps, (up2, down2)))
    odd = exchange(fold((1, 3), fold_facts, maps, (up1, down3, up3, down1)))
    near = exchange(fold((0,), fold_facts, maps, (own, far)))
    ladder, sent = ladder_of(ladder_facts, send_map, all_blocks, near, odd, opposite)
    partner = shifted(sent, 4)
    direction = jnp.where(z >= 4, 1.0, -1.0).astype(jnp.float32)
    residual = ladder + direction * partner.astype(jnp.float32)
    first = energies(vir_energy, pair_virt[0, 0])
    second = energies(vir_energy, pair_virt[0, 1])
    denominator = pair_energy[:, None] - first[None, :] - second[None, :]
    updated = own.astype(jnp.float32) + residual / denominator
    return updated.astype(jnp.bfloat16)[:, None, :]


def solution(mesh):
    placed = (
        P("pair", ("bra", "ket"), None),
        P(("bra", "ket"), "pair", None, None),
        P(("bra", "ket"), None),
        P(("bra", "ket"), None),
        P(),
        P(("bra", "ket"), None, None),
        P(),
        P("pair"),
    )
    return jax.shard_map(
        local,
        mesh=mesh,
        in_specs=placed,
        out_specs=P("pair", ("bra", "ket"), None),
        check_vma=False,
    )
```

time: 511 us -> 271 us (0.53)
  waiting for transfers between devices: 304 us -> 159 us
  local copies, waits for them, and re-layouts: 80.9 us -> 6.9 us
  Pallas kernels: 0 us -> 35.2 us
  blocking collectives: 39 us -> 10 us
  other arithmetic: 31.8 us -> 9.41 us
  matrix products: 9.45 us -> 0 us
  starting transfers between devices: 28.6 us -> 34.3 us
    all_to_all x2 -> x3, waiting for transfers between devices: 182 us -> 45.2 us  [exchange(): return lax.all_to_all(block, 'ket', split_axis=0, concat_axis=0, tiled=True)]
    reduce_scatter x1 -> x0, waiting for transfers between devices: 87.8 us -> none  [local(): lax.psum_scatter(jnp.dot(all_rows, flat_blocks, preferred_element_type=jn...]
    ppermute x2 -> x9, waiting for transfers between devices: 33.8 us -> 113 us  [shifted(): return lax.ppermute(block, 'bra', [(i, (i + by) % 8) for i in range(8)])]
    gather x11 -> x0, local copies, waits for them, and re-layouts: 58.1 us -> none  [the longest x6 25.6 us: permute_columns(): return jnp.take(tile_data, indices, axis=1)]
    all_to_all x1 -> x0, blocking collectives: 39 us -> none  [local(): lax.all_to_all(grouped, 'pair', split_axis=1, concat_axis=0, tiled=True)]
    pallas_call x0 -> x4, Pallas kernels: none -> 35.2 us  [the longest x3 19.6 us: fold(): pl.pallas_call(functools.partial(fold_body, shifts), in_specs=[pl.BlockSp...]
    select_n x10 -> x0, other arithmetic: 12 us -> none  [the longest x2 6.12 us: local(): outgoing = jnp.take(folded_both, slot_index, axis=1)]
    all_gather x0 -> x1, blocking collectives: none -> 10 us  [local(): wanted = lax.all_gather(block_owner[0] * 16 + screen_list[0], 'ket', axis=0)]
  transfers between devices with their start and end apart: 5 -> 13, of which waited for: 4 -> 10; matrix products, arithmetic and copies ran while one was open for 5% -> 3% of each run, Pallas kernels for 0% -> 7%
where the time goes in v1:
time: 271 us; the launch traced here: 268 us
  waiting for transfers between devices  159 us (59%)
  Pallas kernels  35.2 us (13%)
  starting transfers between devices  34.3 us (13%)
  between operations  13.5 us (5%)
  blocking collectives  10 us (4%)
  other arithmetic  9.41 us (3%)
  local copies, waits for them, and re-layouts  6.9 us (3%)
    ppermute x9, waiting for transfers between devices, shifted(): return lax.ppermute(block, 'bra', [(i, (i + by) % 8) for i in range(8)])  113 us
    all_to_all x3, waiting for transfers between devices, exchange(): return lax.all_to_all(block, 'ket', split_axis=0, concat_axis=0, tiled=True)  45.2 us
    all_to_all x3, starting transfers between devices, exchange(): return lax.all_to_all(block, 'ket', split_axis=0, concat_axis=0, tiled=True)  21.9 us
    pallas_call x3, Pallas kernels, fold(): pl.pallas_call(functools.partial(fold_body, shifts), in_specs=[pl.BlockSp...  19.6 us
    pallas_call x1, Pallas kernels, ladder_of(): pl.pallas_call(ladder_body, grid=(length // COLS,), in_specs=[pl.BlockSpe...  15.6 us
    ppermute x9, starting transfers between devices, shifted(): return lax.ppermute(block, 'bra', [(i, (i + by) % 8) for i in range(8)])  12.3 us
    all_gather x1, blocking collectives, local(): wanted = lax.all_gather(block_owner[0] * 16 + screen_list[0], 'ket', axis=0)  10 us
  transfers between devices with their start and end apart: 13, of which 10 were waited for; matrix products, arithmetic and copies ran while one was open for 3% of the time, Pallas kernels for 7%

profile of v1, /device:TPU:47, one launch (start us, length us, event | category | flops | bytes accessed | tf_op | source)
XLA Modules:
  0.0 268.4 jit_solution(7535589898372233517)
XLA Ops:
  6.5 0.0 copy-start
  6.5 0.0 all-gather.4.cloned.1.call-start
  6.6 0.7 all-gather.4.cloned.1.call-update
  7.3 0.6 copy-done.2
  7.9 0.0 collective-permute-start
  7.9 1.6 collective-permute-start.4
  9.5 25.7 %collective-permute-done.refs_0_ = bf16[384,1536]{1,0:T(8,128)(2,1)S(1)} collective-permute-done((bf16[384,1536]{1,0:T(8,128)(2,1)S(1)}, bf16[384,1536]{1,0:T(8,128)(2,1)S(1)}, u32[]{:S(2)}, u32[]{:S(2)}) %collective-permute-start) | collective-permute-done | bytes 1179680 | tf_op jit(solution)/shard_map/ppermute | solution.py:206
  35.2 2.7 %collective-permute-start.1 = (bf16[384,1536]{1,0:T(8,128)(2,1)S(1)}, bf16[384,1536]{1,0:T(8,128)(2,1)}, u32[]{:S(2)}, u32[]{:S(2)}) collective-permute-start(bf16[384,1536]{1,0:T(8,128)(2,1)S(1)} %collective-permute-done.refs_0_), channel_id=1, source_target_pairs={{0,224},{32,0},{64,32},{96,64},{128,96},{160,128},{192,160},{224,1... | collective-permute-start | bytes 3538952 | tf_op jit(solution)/shard_map/ppermute | solution.py:206
  37.9 0.8 collective-permute-done.4.refs_3_
  38.7 0.0 collective-permute-start.5
  38.7 0.0 copy-done.8
  38.8 10.0 %all-gather.1 = s32[8,1,32]{2,1,0:T(1,128)S(1)} all-gather(s32[1,1,32]{2,1,0:T(1,128)S(1)} %add_bitcast_fusion), channel_id=1, replica_groups=mesh['bra'=8,'ket'=8,'pair'=4] {'ket'}, dimensions={0}, use_global_device_ids=true | all-gather | bytes 1152 | tf_op jit(solution)/shard_map/all_gather | solution.py:222
  48.8 13.0 %collective-permute-done.1.refs_0_ = bf16[384,1536]{1,0:T(8,128)(2,1)} collective-permute-done((bf16[384,1536]{1,0:T(8,128)(2,1)S(1)}, bf16[384,1536]{1,0:T(8,128)(2,1)}, u32[]{:S(2)}, u32[]{:S(2)}) %collective-permute-start.1) | collective-permute-done | bytes 1179680 | tf_op jit(solution)/shard_map/ppermute | solution.py:206
  61.8 3.4 %collective-permute-start.2 = (bf16[384,1536]{1,0:T(8,128)(2,1)}, bf16[384,1536]{1,0:T(8,128)(2,1)}, u32[]{:S(2)}, u32[]{:S(2)}) collective-permute-start(bf16[384,1536]{1,0:T(8,128)(2,1)} %collective-permute-done.1.refs_0_), channel_id=1, source_target_pairs={{0,224},{32,0},{64,32},{96,64},{128,96},{160,128},{192,160},{224,1... | collective-permute-start | bytes 3538952 | tf_op jit(solution)/shard_map/ppermute | solution.py:206
  65.2 1.1 collective-permute-done.5.refs_1_
  66.3 0.0 collective-permute-start.6
  66.3 0.3 select_reduce_fusion.2
  66.6 0.1 reshape.25
  66.7 0.1 pad_add_fusion.1.facts
  66.8 6.2 %fold.5 = bf16[8,2,384,128]{3,2,1,0:T(8,128)(2,1)} custom-call(s32[65]{0:T(128)S(1)} %pad_add_fusion.1.facts, s32[4,1,1536]{2,1,0:T(1,128)S(1)} %dynamic-slice_bitcast_fusion.maps, bf16[384,1536]{1,0:T(8,128)(2,1)} %collective-permute-done.1.refs_0_, bf16[384,1536]{1,0:T(8,128)(2,1)} %collective-permute-done.5.refs_1_), custom_call_target="tpu_custom_call" | custom-call | flops 1811939328 | bytes 3932160 | tf_op jit(solution)/shard_map/fold/pallas_call | solution.py:94
  73.0 7.0 %all-to-all-start.2 = ((bf16[8,2,384,128]{3,2,1,0:T(8,128)(2,1)}), bf16[8,2,384,128]{3,2,1,0:T(8,128)(2,1)S(1)}, u32[]{:S(2)}, u32[]{:S(2)}) async-start(bf16[8,2,384,128]{3,2,1,0:T(8,128)(2,1)} %fold.5), calls=%async_computation.2 | async-start | bytes 3145728 | tf_op jit(solution)/shard_map/all_to_all | solution.py:240
  80.0 9.5 %collective-permute-done.2.refs_2_ = bf16[384,1536]{1,0:T(8,128)(2,1)} collective-permute-done((bf16[384,1536]{1,0:T(8,128)(2,1)}, bf16[384,1536]{1,0:T(8,128)(2,1)}, u32[]{:S(2)}, u32[]{:S(2)}) %collective-permute-start.2) | collective-permute-done | bytes 1179680 | tf_op jit(solution)/shard_map/ppermute | solution.py:206
  89.5 1.1 slice.16
  90.6 2.5 collective-permute-start.3
  93.2 0.0 collective-permute-done.6.refs_1_
  93.2 1.1 slice.17
  94.3 0.1 collective-permute-start.7
  94.4 9.4 %collective-permute-done.3 = bf16[192,1536]{1,0:T(8,128)(2,1)S(1)} collective-permute-done((bf16[192,1536]{1,0:T(8,128)(2,1)S(1)}, bf16[192,1536]{1,0:T(8,128)(2,1)S(1)}, u32[]{:S(2)}, u32[]{:S(2)}) %collective-permute-start.3) | collective-permute-done | bytes 589856 | tf_op jit(solution)/shard_map/ppermute | solution.py:206
  103.7 4.2 %collective-permute-done.7 = bf16[192,1536]{1,0:T(8,128)(2,1)S(1)} collective-permute-done((bf16[192,1536]{1,0:T(8,128)(2,1)S(1)}, bf16[192,1536]{1,0:T(8,128)(2,1)S(1)}, u32[]{:S(2)}, u32[]{:S(2)}) %collective-permute-start.7) | collective-permute-done | bytes 589856 | tf_op jit(solution)/shard_map/ppermute | solution.py:206
  107.9 0.1 pad_maximum_fusion.refs_1_
  108.0 0.0 copy-done.3
  108.0 4.5 %fold.3 = bf16[8,2,384,128]{3,2,1,0:T(8,128)(2,1)S(1)} custom-call(s32[65]{0:T(128)S(1)} %pad_add_fusion.1.facts, s32[4,1,1536]{2,1,0:T(1,128)S(1)} %dynamic-slice_bitcast_fusion.maps, bf16[384,1536]{1,0:T(8,128)(2,1)S(1)} %bitcast.18, bf16[384,1536]{1,0:T(8,128)(2,1)S(1)} %pad_maximum_fusion.refs_1_), custom_call_target="tpu_custom_call" | custom-call | flops 1811939328 | bytes 3932160 | tf_op jit(solution)/shard_map/fold/pallas_call | solution.py:94
  112.5 1.1 copy-done.1
  113.7 0.0 all-to-all-done.2.opposite
  113.7 8.6 %all-to-all-start = ((bf16[8,2,384,128]{3,2,1,0:T(8,128)(2,1)}), bf16[8,2,384,128]{3,2,1,0:T(8,128)(2,1)S(1)}, u32[]{:S(2)}, u32[]{:S(2)}) async-start(bf16[8,2,384,128]{3,2,1,0:T(8,128)(2,1)} %copy-done.1), calls=%async_computation | async-start | bytes 3145728 | tf_op jit(solution)/shard_map/all_to_all | solution.py:240
  122.3 0.7 copy-done.4
  123.0 1.3 copy-done.6
  124.3 8.9 %fold.4 = bf16[8,4,384,128]{3,2,1,0:T(8,128)(2,1)} custom-call(s32[65]{0:T(128)S(1)} %pad_add_fusion.1.facts, s32[4,1,1536]{2,1,0:T(1,128)S(1)} %copy-done.4, bf16[384,1536]{1,0:T(8,128)(2,1)S(1)} %copy-done.6, bf16[384,1536]{1,0:T(8,128)(2,1)} %collective-permute-done.6.refs_1_, bf16[384,1536]{1,0:T(8,128)(2,1)} %collective-permute-done.2.refs_2_, ...), custom_call_target="tpu_custom_call" | custom-call | flops 3623878656 | bytes 7864320 | tf_op jit(solution)/shard_map/fold/pallas_call | solution.py:94
  133.2 8.7 %all-to-all-done.near = bf16[8,2,384,128]{3,2,1,0:T(8,128)(2,1)S(1)} async-done(((bf16[8,2,384,128]{3,2,1,0:T(8,128)(2,1)}), bf16[8,2,384,128]{3,2,1,0:T(8,128)(2,1)S(1)}, u32[]{:S(2)}, u32[]{:S(2)}) %all-to-all-start) | async-done | bytes 1572896 | tf_op jit(solution)/shard_map/all_to_all | solution.py:240
  141.9 6.3 %all-to-all-start.1 = ((bf16[8,4,384,128]{3,2,1,0:T(8,128)(2,1)}), bf16[8,4,384,128]{3,2,1,0:T(8,128)(2,1)}, u32[]{:S(2)}, u32[]{:S(2)}) async-start(bf16[8,4,384,128]{3,2,1,0:T(8,128)(2,1)} %fold.4), calls=%async_computation.1 | async-start | bytes 6291456 | tf_op jit(solution)/shard_map/all_to_all | solution.py:240
  148.2 0.1 pad_add_fusion.facts
  148.3 36.5 %all-to-all-done.1.odd = bf16[8,4,384,128]{3,2,1,0:T(8,128)(2,1)} async-done(((bf16[8,4,384,128]{3,2,1,0:T(8,128)(2,1)}), bf16[8,4,384,128]{3,2,1,0:T(8,128)(2,1)}, u32[]{:S(2)}, u32[]{:S(2)}) %all-to-all-start.1) | async-done | bytes 3145760 | tf_op jit(solution)/shard_map/all_to_all | solution.py:240
  184.8 15.6 %ladder.1 = (f32[384,1536]{1,0:T(8,128)}, bf16[384,1536]{1,0:T(8,128)(2,1)}) custom-call(s32[33]{0:T(128)S(1)} %pad_add_fusion.facts, s32[1,1536]{1,0:T(1,128)S(1)} %constant_dynamic-slice_fusion.send_map, bf16[4096,1536]{1,0:T(8,128)(2,1)} %bitcast.19, bf16[8,2,384,128]{3,2,1,0:T(8,128)(2,1)S(1)} %all-to-all-done.near, ...), custom_call_target="tpu_custom_call" | custom-call | flops 4831838208 | bytes 15728640 | tf_op jit(solution)/shard_map/ladder/pallas_call | solution.py:169
  200.4 1.9 collective-permute-start.8
  202.3 0.8 slice_reduce_fusion.1
  203.1 5.1 %select_reduce_fusion.1 = (f32[1536]{0:T(1024)S(1)}, f32[1536]{0:T(1024)S(1)}) fusion(f32[2048]{0:T(1024)} %param.14, s32[1536]{0:T(1024)S(1)} %get-tuple-element.9, s32[1536]{0:T(1024)S(1)} %get-tuple-element.10), kind=kLoop, calls=%fused_computation.2 | loop fusion | flops 18871296 | bytes 32768 | tf_op jit(solution)/shard_map/reduce_sum | solution.py:211
  208.2 49.5 %collective-permute-done.8 = bf16[384,1536]{1,0:T(8,128)(2,1)S(1)} collective-permute-done((bf16[384,1536]{1,0:T(8,128)(2,1)}, bf16[384,1536]{1,0:T(8,128)(2,1)S(1)}, u32[]{:S(2)}, u32[]{:S(2)}) %collective-permute-start.8) | collective-permute-done | bytes 1179680 | tf_op jit(solution)/shard_map/ppermute | solution.py:206
  257.8 3.8 %fusion = bf16[384,1,1536]{2,0,1:T(8,128)(2,1)} fusion(f32[1536]{0:T(1024)S(1)} %get-tuple-element.12, f32[1536]{0:T(1024)S(1)} %get-tuple-element.11, f32[384]{0:T(512)S(1)} %copy-done.7, f32[384,1536]{1,0:T(8,128)} %get-tuple-element.7, bf16[384,1536]{1,0:T(8,128)(2,1)S(1)} %collective-permute-done.8, f32[]{:T(128)S(6)} %select_n.37, ...), kind=kLoop, calls=%fused_computation.6 | loop fusion | flops 5308416 | bytes 5912068 | tf_op jit(solution)/shard_map/broadcast_in_dim | solution.py:253
  (19 shorter events, 0.1 us)
Async XLA Ops:
  6.5 60.2 %copy-start = (s32[64,1536]{1,0:T(8,128)S(1)}, s32[64,1536]{1,0:T(8,128)}, u32[]{:S(2)}) copy-start(s32[64,1536]{1,0:T(8,128)} %param.12) | copy-start | bytes 1179652
  6.5 1.3 copy-start.2
  6.5 32.2 %copy-start.8 = (s32[1,32]{1,0:T(1,128)S(1)}, s32[1,32]{1,0:T(1,128)}, u32[]{:S(2)}) copy-start(s32[1,32]{1,0:T(1,128)} %param.10) | copy-start | bytes 388
  6.5 32.2 %copy-start.9 = (s32[1,32]{1,0:T(1,128)S(1)}, s32[1,32]{1,0:T(1,128)}, u32[]{:S(2)}) copy-start(s32[1,32]{1,0:T(1,128)} %param.11) | copy-start | bytes 388
  6.5 178.3 %all-gather.4.cloned.1.call-start = ((), (), s32[]{:S(2)}) async-start(), calls=%async_computation.3 | async-start | bytes 15728640 | tf_op jit(solution)/shard_map/all_gather | solution.py:220
  7.9 27.3 %collective-permute-start = (bf16[384,1536]{1,0:T(8,128)(2,1)S(1)}, bf16[384,1536]{1,0:T(8,128)(2,1)S(1)}, u32[]{:S(2)}, u32[]{:S(2)}) collective-permute-start(bf16[384,1536]{1,0:T(8,128)(2,1)S(1)} %bitcast.16), channel_id=1, source_target_pairs={{0,224},{32,0},{64,32},{96,64},{128,96},{160,128},{192,160},{224,1... | collective-permute-start | bytes 3538952 | tf_op jit(solution)/shard_map/ppermute | solution.py:206
  7.9 30.9 %collective-permute-start.4 = (bf16[384,1536]{1,0:T(8,128)(2,1)S(1)}, bf16[384,1536]{1,0:T(8,128)(2,1)}, u32[]{:S(2)}, u32[]{:S(2)}) collective-permute-start(bf16[384,1536]{1,0:T(8,128)(2,1)S(1)} %bitcast.17), channel_id=1, source_target_pairs={{0,32},{32,64},{64,96},{96,128},{128,160},{160,192},{192,224},{224... | collective-permute-start | bytes 3538952 | tf_op jit(solution)/shard_map/ppermute | solution.py:206
  35.2 37.8 %copy-start.5 = (bf16[384,1536]{1,0:T(8,128)(2,1)}, bf16[384,1536]{1,0:T(8,128)(2,1)S(1)}, u32[]{:S(2)}) copy-start(bf16[384,1536]{1,0:T(8,128)(2,1)S(1)} %collective-permute-done.refs_0_) | copy-start | bytes 3538948
  35.2 26.7 %collective-permute-start.1 = (bf16[384,1536]{1,0:T(8,128)(2,1)S(1)}, bf16[384,1536]{1,0:T(8,128)(2,1)}, u32[]{:S(2)}, u32[]{:S(2)}) collective-permute-start(bf16[384,1536]{1,0:T(8,128)(2,1)S(1)} %collective-permute-done.refs_0_), channel_id=1, source_target_pairs={{0,224},{32,0},{64,32},{96,64},{128,96},{160,128},{192,160},{224,1... | collective-permute-start | bytes 3538952 | tf_op jit(solution)/shard_map/ppermute | solution.py:206
  38.7 27.6 %collective-permute-start.5 = (bf16[384,1536]{1,0:T(8,128)(2,1)}, bf16[384,1536]{1,0:T(8,128)(2,1)}, u32[]{:S(2)}, u32[]{:S(2)}) collective-permute-start(bf16[384,1536]{1,0:T(8,128)(2,1)} %collective-permute-done.4.refs_3_), channel_id=1, source_target_pairs={{0,32},{32,64},{64,96},{96,128},{128,160},{160,192},{192,224},{224... | collective-permute-start | bytes 3538952 | tf_op jit(solution)/shard_map/ppermute | solution.py:206
  61.8 27.7 %collective-permute-start.2 = (bf16[384,1536]{1,0:T(8,128)(2,1)}, bf16[384,1536]{1,0:T(8,128)(2,1)}, u32[]{:S(2)}, u32[]{:S(2)}) collective-permute-start(bf16[384,1536]{1,0:T(8,128)(2,1)} %collective-permute-done.1.refs_0_), channel_id=1, source_target_pairs={{0,224},{32,0},{64,32},{96,64},{128,96},{160,128},{192,160},{224,1... | collective-permute-start | bytes 3538952 | tf_op jit(solution)/shard_map/ppermute | solution.py:206
  66.3 26.9 %collective-permute-start.6 = (bf16[384,1536]{1,0:T(8,128)(2,1)}, bf16[384,1536]{1,0:T(8,128)(2,1)}, u32[]{:S(2)}, u32[]{:S(2)}) collective-permute-start(bf16[384,1536]{1,0:T(8,128)(2,1)} %collective-permute-done.5.refs_1_), channel_id=1, source_target_pairs={{0,32},{32,64},{64,96},{96,128},{128,160},{160,192},{192,224},{224... | collective-permute-start | bytes 3538952 | tf_op jit(solution)/shard_map/ppermute | solution.py:206
  66.8 41.2 %copy-start.3 = (s32[4,1,1536]{2,1,0:T(1,128)}, s32[4,1,1536]{2,1,0:T(1,128)S(1)}, u32[]{:S(2)}) copy-start(s32[4,1,1536]{2,1,0:T(1,128)S(1)} %dynamic-slice_bitcast_fusion.maps) | copy-start | bytes 73732
  73.0 40.7 %all-to-all-start.2 = ((bf16[8,2,384,128]{3,2,1,0:T(8,128)(2,1)}), bf16[8,2,384,128]{3,2,1,0:T(8,128)(2,1)S(1)}, u32[]{:S(2)}, u32[]{:S(2)}) async-start(bf16[8,2,384,128]{3,2,1,0:T(8,128)(2,1)} %fold.5), calls=%async_computation.2 | async-start | bytes 3145728 | tf_op jit(solution)/shard_map/all_to_all | solution.py:240
  90.6 13.1 %collective-permute-start.3 = (bf16[192,1536]{1,0:T(8,128)(2,1)S(1)}, bf16[192,1536]{1,0:T(8,128)(2,1)S(1)}, u32[]{:S(2)}, u32[]{:S(2)}) collective-permute-start(bf16[192,1536]{1,0:T(8,128)(2,1)S(1)} %slice.16), channel_id=1, source_target_pairs={{0,224},{32,0},{64,32},{96,64},{128,96},{160,128},{192,160},{224,1... | collective-permute-start | bytes 1769480 | tf_op jit(solution)/shard_map/ppermute | solution.py:206
  94.3 13.7 %collective-permute-start.7 = (bf16[192,1536]{1,0:T(8,128)(2,1)S(1)}, bf16[192,1536]{1,0:T(8,128)(2,1)S(1)}, u32[]{:S(2)}, u32[]{:S(2)}) collective-permute-start(bf16[192,1536]{1,0:T(8,128)(2,1)S(1)} %slice.17), channel_id=1, source_target_pairs={{0,32},{32,64},{64,96},{96,128},{128,160},{160,192},{192,224},{224... | collective-permute-start | bytes 1769480 | tf_op jit(solution)/shard_map/ppermute | solution.py:206
  112.5 1.1 copy-start.1
  113.7 28.2 %all-to-all-start = ((bf16[8,2,384,128]{3,2,1,0:T(8,128)(2,1)}), bf16[8,2,384,128]{3,2,1,0:T(8,128)(2,1)S(1)}, u32[]{:S(2)}, u32[]{:S(2)}) async-start(bf16[8,2,384,128]{3,2,1,0:T(8,128)(2,1)} %copy-done.1), calls=%async_computation | async-start | bytes 3145728 | tf_op jit(solution)/shard_map/all_to_all | solution.py:240
  122.3 0.7 copy-start.4
  123.0 1.3 copy-start.6
  141.9 42.9 %all-to-all-start.1 = ((bf16[8,4,384,128]{3,2,1,0:T(8,128)(2,1)}), bf16[8,4,384,128]{3,2,1,0:T(8,128)(2,1)}, u32[]{:S(2)}, u32[]{:S(2)}) async-start(bf16[8,4,384,128]{3,2,1,0:T(8,128)(2,1)} %fold.4), calls=%async_computation.1 | async-start | bytes 6291456 | tf_op jit(solution)/shard_map/all_to_all | solution.py:240
  184.8 73.0 %copy-start.7 = (f32[384]{0:T(512)S(1)}, f32[384]{0:T(512)}, u32[]{:S(2)}) copy-start(f32[384]{0:T(512)} %param.15) | copy-start | bytes 4612
  200.4 57.3 %collective-permute-start.8 = (bf16[384,1536]{1,0:T(8,128)(2,1)}, bf16[384,1536]{1,0:T(8,128)(2,1)S(1)}, u32[]{:S(2)}, u32[]{:S(2)}) collective-permute-start(bf16[384,1536]{1,0:T(8,128)(2,1)} %get-tuple-element.8), channel_id=1, source_target_pairs={{0,128},{32,160},{64,192},{96,224},{128,0},{160,32},{192,64},{224,... | collective-permute-start | bytes 3538952 | tf_op jit(solution)/shard_map/ppermute | solution.py:206
Sparse Core Ops, SparseCore 0:
  9.2 122.6 all-gather.3

commit v2 on v1

--- a/solution.py
+++ b/solution.py
@@ -8,7 +8,7 @@
 from jax.sharding import PartitionSpec as P
 
 COLS = 256
-VMEM = 48 * 1024 * 1024
+VMEM = 40 * 1024 * 1024
 
 
 def one_hot(row, length, width):
@@ -18,19 +18,26 @@
 
 def fold_body(shifts, facts, maps, *refs):
     count = len(shifts)
-    tiles, out = refs[: 2 * count], refs[2 * count]
-    base, other, folded, base_sem, other_sem, out_sem = refs[2 * count + 1 :]
+    tiles = refs[: 3 if shifts == (0,) else 2 * count]
+    out, base, other, folded, base_sem, other_sem, out_sem = refs[-7:]
     z = facts[0]
     sign = jnp.where(z < 4, 1.0, -1.0).astype(jnp.float32)
     rows, length = folded.shape[1:]
 
     def fetch(i, turned):
+        if shifts[i] == 0:
+            cut = tiles[1].shape[0]
+            return (
+                pltpu.make_async_copy(tiles[0], base.at[i], base_sem.at[i]),
+                pltpu.make_async_copy(tiles[1], other.at[i, pl.ds(0, cut)], other_sem.at[i, 0]),
+                pltpu.make_async_copy(tiles[2], other.at[i, pl.ds(cut, cut)], other_sem.at[i, 1]),
+            )
         first, second = tiles[2 * i], tiles[2 * i + 1]
         if turned:
             first, second = second, first
         return (
             pltpu.make_async_copy(first, base.at[i], base_sem.at[i]),
-            pltpu.make_async_copy(second, other.at[i], other_sem.at[i]),
+            pltpu.make_async_copy(second, other.at[i], other_sem.at[i, 0]),
         )
 
     def straight(shift):
@@ -69,7 +76,7 @@
                     start = pl.multiple_of(segment * 128, 128)
                     pltpu.make_async_copy(
                         folded.at[i, :, pl.ds(start, 128)],
-                        out.at[receiver, 2 * i + half],
+                        out.at[receiver, 2 * (shift & 3) + half],
                         out_sem.at[i, receiver, half],
                     ).start()
 
@@ -82,27 +89,27 @@
                 def _():
                     pltpu.make_async_copy(
                         folded.at[i, :, pl.ds(0, 128)],
-                        out.at[receiver, 2 * i + half],
+                        out.at[receiver, 2 * (shift & 3) + half],
                         out_sem.at[i, receiver, half],
                     ).wait()
 
 
-def fold(shifts, facts, maps, tiles):
+def fold(shifts, facts, maps, tiles, before):
     rows, length = tiles[0].shape
     count = len(shifts)
     whole = pltpu.VMEM((count, rows, length), jnp.bfloat16)
     return pl.pallas_call(
         functools.partial(fold_body, shifts),
         in_specs=[pl.BlockSpec(memory_space=pltpu.SMEM), pl.BlockSpec(memory_space=pltpu.VMEM)]
-        + [pl.BlockSpec(memory_space=pl.ANY)] * (2 * count),
+        + [pl.BlockSpec(memory_space=pl.ANY)] * (len(tiles) + len(before)),
         out_specs=pl.BlockSpec(memory_space=pl.ANY),
-        out_shape=jax.ShapeDtypeStruct((8, 2 * count, rows, 128), jnp.bfloat16),
+        out_shape=pltpu.HBM((8, 8, rows, 128), jnp.bfloat16),
         scratch_shapes=[
             whole,
             whole,
             whole,
             pltpu.SemaphoreType.DMA((count,)),
-            pltpu.SemaphoreType.DMA((count,)),
+            pltpu.SemaphoreType.DMA((count, 2)),
             pltpu.SemaphoreType.DMA((count, 8, 2)),
         ],
         compiler_params=pltpu.CompilerParams(vmem_limit_bytes=VMEM),
@@ -111,11 +118,29 @@
             bytes_accessed=count * rows * (4 * length + 16 * 256),
             transcendentals=0,
         ),
+        input_output_aliases={2 + len(tiles): 0} if before else {},
         name="fold",
-    )(facts, maps, *tiles)
-
-
-def ladder_body(facts, send_map, blocks, near, odd, opposite, ladder, sent, operand, rounded, sem):
+    )(facts, maps, *tiles, *before)
+
+
+def nothing(*refs):
+    pass
+
+
+def joined(block, others, kind=jax.ShapeDtypeStruct):
+    held = pl.BlockSpec(memory_space=pl.ANY)
+    return pl.pallas_call(
+        nothing,
+        in_specs=[held] * (1 + len(others)),
+        out_specs=held,
+        out_shape=kind(block.shape, block.dtype),
+        input_output_aliases={0: 0},
+        compiler_params=pltpu.CompilerParams(vmem_limit_bytes=VMEM),
+        name="joined",
+    )(block, *others)
+
+
+def ladder_body(facts, send_map, blocks, received, ladder, sent, operand, rounded, sem):
     step = pl.program_id(0)
     slots = operand.shape[1] // 128
     length = rounded.shape[1]
@@ -125,26 +150,16 @@
         def place(k):
             return operand.at[:, pl.ds(k * 128, 128)]
 
-        for k in range(slots):
+        def copy(k):
             tile = facts[1 + k]
             z, ket = tile >> 3, tile & 7
-            away, half = (z - facts[0] + 8) & 3, z >> 2
-
-            @pl.when(away == 0)
-            def _():
-                pltpu.make_async_copy(near.at[ket, half], place(k), sem.at[k]).start()
-
-            @pl.when((away & 1) == 1)
-            def _():
-                source = odd.at[ket, (away >> 1) * 2 + half]
-                pltpu.make_async_copy(source, place(k), sem.at[k]).start()
-
-            @pl.when(away == 2)
-            def _():
-                pltpu.make_async_copy(opposite.at[ket, half], place(k), sem.at[k]).start()
+            slot = 2 * ((z - facts[0] + 8) & 3) + (z >> 2)
+            return pltpu.make_async_copy(received.at[ket, slot], place(k), sem.at[k])
 
         for k in range(slots):
-            pltpu.make_async_copy(near.at[0, 0], place(k), sem.at[k]).wait()
+            copy(k).start()
+        for k in range(slots):
+            copy(k).wait()
 
     total = jnp.dot(operand[...], blocks[...], preferred_element_type=jnp.float32)
     ladder[...] = total
@@ -162,10 +177,9 @@
         lax.fori_loop(0, length // COLS, column, 0)
 
 
-def ladder_of(facts, send_map, blocks, near, odd, opposite):
+def ladder_of(facts, send_map, blocks, received):
     depth, length = blocks.shape
-    rows = near.shape[2]
-    held = pl.BlockSpec(memory_space=pl.ANY)
+    rows = received.shape[2]
     return pl.pallas_call(
         ladder_body,
         grid=(length // COLS,),
@@ -173,16 +187,14 @@
             pl.BlockSpec(memory_space=pltpu.SMEM),
             pl.BlockSpec((1, length), lambda n: (0, 0)),
             pl.BlockSpec((depth, COLS), lambda n: (0, n)),
-            held,
-            held,
-            held,
+            pl.BlockSpec(memory_space=pl.ANY),
         ],
         out_specs=[
             pl.BlockSpec((rows, COLS), lambda n: (0, n)),
             pl.BlockSpec((rows, length), lambda n: (0, 0)),
         ],
         out_shape=[
-            jax.ShapeDtypeStruct((rows, length), jnp.float32),
+            pltpu.HBM((rows, length), jnp.float32),
             jax.ShapeDtypeStruct((rows, length), jnp.bfloat16),
         ],
         scratch_shapes=[
@@ -199,7 +211,7 @@
             transcendentals=0,
         ),
         name="ladder",
-    )(facts, send_map, blocks, near, odd, opposite)
+    )(facts, send_map, blocks, received)
 
 
 def shifted(block, by):
@@ -230,27 +242,38 @@
     maps = lax.dynamic_index_in_dim(half_maps, ket, 1, keepdims=True)
     send_map = lax.dynamic_index_in_dim(mirror_map, ((z + 4) & 7) * 8 + ket, 0, keepdims=True)
 
-    up1, down1 = shifted(own, -1), shifted(own, 1)
-    up2, down2 = shifted(up1, -1), shifted(down1, 1)
-    up3, down3 = shifted(up2, -1), shifted(down2, 1)
-    cut = rows // 2
-    far = jnp.concatenate([shifted(up3[:cut], -1), shifted(down3[cut:], 1)], axis=0)
-
-    def exchange(block):
-        return lax.all_to_all(block, "ket", split_axis=0, concat_axis=0, tiled=True)
-
-    opposite = exchange(fold((2,), fold_facts, maps, (up2, down2)))
-    odd = exchange(fold((1, 3), fold_facts, maps, (up1, down3, up3, down1)))
-    near = exchange(fold((0,), fold_facts, maps, (own, far)))
-    ladder, sent = ladder_of(ladder_facts, send_map, all_blocks, near, odd, opposite)
-    partner = shifted(sent, 4)
     direction = jnp.where(z >= 4, 1.0, -1.0).astype(jnp.float32)
-    residual = ladder + direction * partner.astype(jnp.float32)
     first = energies(vir_energy, pair_virt[0, 0])
     second = energies(vir_energy, pair_virt[0, 1])
-    denominator = pair_energy[:, None] - first[None, :] - second[None, :]
-    updated = own.astype(jnp.float32) + residual / denominator
-    return updated.astype(jnp.bfloat16)[:, None, :]
+    ends = (0, 224, rows)
+    parts = [own[low:high] for low, high in zip(ends, ends[1:])]
+    rings = []
+    for i, part in enumerate(parts):
+        if i:
+            part = joined(part, rings[i - 1][2], pltpu.HBM)
+        up1, down1 = shifted(part, -1), shifted(part, 1)
+        up2, down2 = shifted(up1, -1), shifted(down1, 1)
+        up3, down3 = shifted(up2, -1), shifted(down2, 1)
+        cut = part.shape[0] // 2
+        far = (shifted(up3[:cut], -1), shifted(down3[cut:], 1))
+        rings.append(((up1, down1), (up2, down2), (up3, down3), far))
+    updated = []
+    for i, part in enumerate(parts):
+        one, two, three, far = rings[i]
+        slots = fold((2,), fold_facts, maps, two, ())
+        slots = fold((1, 3), fold_facts, maps, (one[0], three[1], three[0], one[1]), (slots,))
+        slots = fold((0,), fold_facts, maps, (part, *far), (slots,))
+        if i + 1 < len(parts):
+            slots = joined(slots, rings[i + 1][0], pltpu.HBM)
+        received = lax.all_to_all(slots, "ket", split_axis=0, concat_axis=0, tiled=True)
+        ladder, sent = ladder_of(ladder_facts, send_map, all_blocks, received)
+        partner = shifted(sent, 4)
+        residual = ladder + direction * partner.astype(jnp.float32)
+        occupied = pair_energy[ends[i] : ends[i + 1]]
+        denominator = occupied[:, None] - first[None, :] - second[None, :]
+        fresh = part.astype(jnp.float32) + residual / denominator
+        updated.append(fresh.astype(jnp.bfloat16))
+    return jnp.concatenate(updated, axis=0)[:, None, :]
 
 
 def solution(mesh):

time: 271 us -> 228 us (0.84)
  waiting for transfers between devices: 159 us -> 94.7 us
  Pallas kernels: 35.2 us -> 54.5 us
  starting transfers between devices: 34.3 us -> 38.7 us
    ppermute x9 -> x18, waiting for transfers between devices: 113 us -> 77.5 us  [shifted(): return lax.ppermute(block, 'bra', [(i, (i + by) % 8) for i in range(8)])]
    all_to_all x3 -> x2, waiting for transfers between devices: 45.2 us -> 16.5 us  [local(): lax.all_to_all(slots, 'ket', split_axis=0, concat_axis=0, tiled=True)]
    pallas_call x3 -> x6, Pallas kernels: 19.6 us -> 30.8 us  [fold(): pl.pallas_call(functools.partial(fold_body, shifts), in_specs=[pl.BlockSp...]
    ppermute x9 -> x18, starting transfers between devices: 12.3 us -> 23.1 us  [shifted(): return lax.ppermute(block, 'bra', [(i, (i + by) % 8) for i in range(8)])]
    pallas_call x1 -> x2, Pallas kernels: 15.6 us -> 23.7 us  [ladder_of(): pl.pallas_call(ladder_body, grid=(length // COLS,), in_specs=[pl.BlockSpe...]
    all_to_all x3 -> x2, starting transfers between devices: 21.9 us -> 15.6 us  [local(): lax.all_to_all(slots, 'ket', split_axis=0, concat_axis=0, tiled=True)]
    convert_element_type x0 -> x2, other arithmetic: none -> 3.38 us  [local(): updated.append(fresh.astype(jnp.bfloat16))]
  transfers between devices with their start and end apart: 13 -> 21, of which waited for: 10 -> 12; matrix products, arithmetic and copies ran while one was open for 3% -> 4% of each run, Pallas kernels for 7% -> 24%
where the time goes in v2:
time: 228 us; the launch traced here: 227 us
  waiting for transfers between devices  94.7 us (42%)
  Pallas kernels  54.5 us (24%)
  starting transfers between devices  38.7 us (17%)
  between operations  13.7 us (6%)
  blocking collectives  10.3 us (5%)
  other arithmetic  9.45 us (4%)
  local copies, waits for them, and re-layouts  5.35 us (2%)
    ppermute x18, waiting for transfers between devices, shifted(): return lax.ppermute(block, 'bra', [(i, (i + by) % 8) for i in range(8)])  77.5 us
    pallas_call x6, Pallas kernels, fold(): pl.pallas_call(functools.partial(fold_body, shifts), in_specs=[pl.BlockSp...  30.8 us
    pallas_call x2, Pallas kernels, ladder_of(): pl.pallas_call(ladder_body, grid=(length // COLS,), in_specs=[pl.BlockSpe...  23.7 us
    ppermute x18, starting transfers between devices, shifted(): return lax.ppermute(block, 'bra', [(i, (i + by) % 8) for i in range(8)])  23.1 us
    all_to_all x2, waiting for transfers between devices, local(): lax.all_to_all(slots, 'ket', split_axis=0, concat_axis=0, tiled=True)  16.5 us
    all_to_all x2, starting transfers between devices, local(): lax.all_to_all(slots, 'ket', split_axis=0, concat_axis=0, tiled=True)  15.6 us
    all_gather x1, blocking collectives, local(): wanted = lax.all_gather(block_owner[0] * 16 + screen_list[0], 'ket', axis=0)  10.3 us
  transfers between devices with their start and end apart: 21, of which 12 were waited for; matrix products, arithmetic and copies ran while one was open for 4% of the time, Pallas kernels for 24%

profile of v2, /device:TPU:47, one launch (start us, length us, event | category | flops | bytes accessed | tf_op | source)
XLA Modules:
  0.0 226.8 jit_solution(696842064441165229)
XLA Ops:
  6.6 0.7 all-gather.4.cloned.1.call-update
  7.3 0.6 copy-done.7
  7.9 0.1 collective-permute-start
  8.0 1.7 collective-permute-start.4
  9.7 15.0 %collective-permute-done.refs_0_ = bf16[224,1536]{1,0:T(8,128)(2,1)S(1)} collective-permute-done((bf16[224,1536]{1,0:T(8,128)(2,1)S(1)}, bf16[224,1536]{1,0:T(8,128)(2,1)S(1)}, u32[]{:S(2)}, u32[]{:S(2)}) %collective-permute-start) | collective-permute-done | bytes 688160 | tf_op jit(solution)/shard_map/ppermute | solution.py:218
  24.7 2.8 %collective-permute-start.1 = (bf16[224,1536]{1,0:T(8,128)(2,1)S(1)}, bf16[224,1536]{1,0:T(8,128)(2,1)}, u32[]{:S(2)}, u32[]{:S(2)}) collective-permute-start(bf16[224,1536]{1,0:T(8,128)(2,1)S(1)} %collective-permute-done.refs_0_), channel_id=1, source_target_pairs={{0,224},{32,0},{64,32},{96,64},{128,96},{160,128},{192,160},{224,1... | collective-permute-start | bytes 2064392 | tf_op jit(solution)/shard_map/ppermute | solution.py:218
  27.5 0.8 copy-done.3
  28.4 0.9 copy-done.5
  29.2 10.3 %all-gather.1 = s32[8,1,32]{2,1,0:T(1,128)S(1)} all-gather(s32[1,1,32]{2,1,0:T(1,128)S(1)} %add_bitcast_fusion), channel_id=1, replica_groups=mesh['bra'=8,'ket'=8,'pair'=4] {'ket'}, dimensions={0}, use_global_device_ids=true | all-gather | bytes 1152 | tf_op jit(solution)/shard_map/all_gather | solution.py:234
  39.6 0.3 select_reduce_fusion.2
  39.9 0.8 collective-permute-done.1.refs_0_
  40.7 3.4 %collective-permute-start.2 = (bf16[224,1536]{1,0:T(8,128)(2,1)}, bf16[224,1536]{1,0:T(8,128)(2,1)S(1)}, u32[]{:S(2)}, u32[]{:S(2)}) collective-permute-start(bf16[224,1536]{1,0:T(8,128)(2,1)} %collective-permute-done.1.refs_0_), channel_id=1, source_target_pairs={{0,224},{32,0},{64,32},{96,64},{128,96},{160,128},{192,160},{224,1... | collective-permute-start | bytes 2064392 | tf_op jit(solution)/shard_map/ppermute | solution.py:218
  44.1 1.7 collective-permute-done.5.refs_1_
  45.8 1.1 slice_bitcast_fusion.1.refs_0_
  46.8 0.8 copy.17.refs_0_
  47.7 10.1 %collective-permute-done.2.refs_2_.refs_1_ = bf16[224,1536]{1,0:T(8,128)(2,1)S(1)} collective-permute-done((bf16[224,1536]{1,0:T(8,128)(2,1)}, bf16[224,1536]{1,0:T(8,128)(2,1)S(1)}, u32[]{:S(2)}, u32[]{:S(2)}) %collective-permute-start.2) | collective-permute-done | bytes 688160 | tf_op jit(solution)/shard_map/ppermute | solution.py:218
  57.7 3.7 %collective-permute-done.6.refs_1_.refs_2_ = bf16[224,1536]{1,0:T(8,128)(2,1)S(1)} collective-permute-done((bf16[224,1536]{1,0:T(8,128)(2,1)}, bf16[224,1536]{1,0:T(8,128)(2,1)S(1)}, u32[]{:S(2)}, u32[]{:S(2)}) %collective-permute-start.6) | collective-permute-done | bytes 688160 | tf_op jit(solution)/shard_map/ppermute | solution.py:218
  61.5 2.4 %collective-permute-start.8 = (bf16[160,1536]{1,0:T(8,128)(2,1)}, bf16[160,1536]{1,0:T(8,128)(2,1)S(1)}, u32[]{:S(2)}, u32[]{:S(2)}) collective-permute-start(bf16[160,1536]{1,0:T(8,128)(2,1)} %joined.2), channel_id=1, source_target_pairs={{0,224},{32,0},{64,32},{96,64},{128,96},{160,128},{192,160},{224,1... | collective-permute-start | bytes 1474568 | tf_op jit(solution)/shard_map/ppermute | solution.py:218
  63.9 1.5 collective-permute-start.3
  65.6 4.9 %fold.6.refs_4_ = bf16[8,8,224,128]{3,2,1,0:T(8,128)(2,1)} custom-call(s32[65]{0:T(128)S(1)} %pad_add_fusion.1.facts, s32[4,1,1536]{2,1,0:T(1,128)S(1)} %dynamic-slice_bitcast_fusion.maps, bf16[224,1536]{1,0:T(8,128)(2,1)} %collective-permute-done.1.refs_0_, bf16[224,1536]{1,0:T(8,128)(2,1)} %collective-permute-done.5.refs_1_), custom_call_target="tpu_custom_call" | custom-call | flops 1056964608 | bytes 2293760 | tf_op jit(solution)/shard_map/fold/pallas_call | solution.py:101
  70.6 7.0 %fold.7.refs_3_ = bf16[8,8,224,128]{3,2,1,0:T(8,128)(2,1)} custom-call(s32[65]{0:T(128)S(1)} %pad_add_fusion.1.facts, s32[4,1,1536]{2,1,0:T(1,128)S(1)} %dynamic-slice_bitcast_fusion.maps, bf16[224,1536]{1,0:T(8,128)(2,1)S(1)} %copy-done.4, bf16[224,1536]{1,0:T(8,128)(2,1)S(1)} %collective-permute-done.6.refs_1_.refs_2_, ...), custom_call_target="tpu_custom_call", output_to_operand_aliasing={{}: (6, {})} | custom-call | flops 2113929216 | bytes 4587520 | tf_op jit(solution)/shard_map/fold/pallas_call | solution.py:101
  77.7 0.9 collective-permute-done.3.refs_1_
  78.6 1.8 collective-permute-done.7.refs_2_
  80.4 4.1 %fold.8.refs_0_ = bf16[8,8,224,128]{3,2,1,0:T(8,128)(2,1)} custom-call(s32[65]{0:T(128)S(1)} %pad_add_fusion.1.facts, s32[4,1,1536]{2,1,0:T(1,128)S(1)} %dynamic-slice_bitcast_fusion.maps, bf16[224,1536]{1,0:T(8,128)(2,1)S(1)} %slice_bitcast_fusion.refs_0_, bf16[112,1536]{1,0:T(8,128)(2,1)S(1)} %collective-permute-done.3.refs_1_, ...), custom_call_target="tpu_custom_call", output_to_operand_aliasing={{}: (5, {})} | custom-call | flops 1056964608 | bytes 2293760 | tf_op jit(solution)/shard_map/fold/pallas_call | solution.py:101
  84.6 0.8 copy-done.1
  85.3 9.6 %all-to-all-start = ((bf16[8,8,224,128]{3,2,1,0:T(8,128)(2,1)}), bf16[8,8,224,128]{3,2,1,0:T(8,128)(2,1)}, u32[]{:S(2)}, u32[]{:S(2)}) async-start(bf16[8,8,224,128]{3,2,1,0:T(8,128)(2,1)} %joined.3), calls=%async_computation | async-start | bytes 7340032 | tf_op jit(solution)/shard_map/all_to_all | solution.py:268
  95.0 2.1 collective-permute-start.11
  97.1 10.4 %collective-permute-done.11.refs_0_ = bf16[160,1536]{1,0:T(8,128)(2,1)S(1)} collective-permute-done((bf16[160,1536]{1,0:T(8,128)(2,1)S(1)}, bf16[160,1536]{1,0:T(8,128)(2,1)S(1)}, u32[]{:S(2)}, u32[]{:S(2)}) %collective-permute-start.11) | collective-permute-done | bytes 491552 | tf_op jit(solution)/shard_map/ppermute | solution.py:218
  107.5 2.1 collective-permute-start.12
  109.7 0.2 collective-permute-start.15
  109.9 9.4 %collective-permute-done.12.refs_2_ = bf16[160,1536]{1,0:T(8,128)(2,1)S(1)} collective-permute-done((bf16[160,1536]{1,0:T(8,128)(2,1)S(1)}, bf16[160,1536]{1,0:T(8,128)(2,1)S(1)}, u32[]{:S(2)}, u32[]{:S(2)}) %collective-permute-start.12) | collective-permute-done | bytes 491552 | tf_op jit(solution)/shard_map/ppermute | solution.py:218
  119.3 2.2 collective-permute-start.13
  121.5 0.2 collective-permute-start.16
  121.7 3.9 %fold.9.refs_4_ = bf16[8,8,160,128]{3,2,1,0:T(8,128)(2,1)} custom-call(s32[65]{0:T(128)S(1)} %pad_add_fusion.1.facts, s32[4,1,1536]{2,1,0:T(1,128)S(1)} %dynamic-slice_bitcast_fusion.maps, bf16[160,1536]{1,0:T(8,128)(2,1)S(1)} %collective-permute-done.11.refs_0_, bf16[160,1536]{1,0:T(8,128)(2,1)S(1)} %collective-permute-done.14.refs_1_), custom_call_target="tpu_custom_call" | custom-call | flops 754974720 | bytes 1638400 | tf_op jit(solution)/shard_map/fold/pallas_call | solution.py:101
  125.6 6.6 %fold.10.refs_3_ = bf16[8,8,160,128]{3,2,1,0:T(8,128)(2,1)} custom-call(s32[65]{0:T(128)S(1)} %pad_add_fusion.1.facts, s32[4,1,1536]{2,1,0:T(1,128)S(1)} %dynamic-slice_bitcast_fusion.maps, bf16[160,1536]{1,0:T(8,128)(2,1)S(1)} %collective-permute-done.8.refs_1_.refs_0_, ...), custom_call_target="tpu_custom_call", output_to_operand_aliasing={{}: (6, {})} | custom-call | flops 1509949440 | bytes 3276800 | tf_op jit(solution)/shard_map/fold/pallas_call | solution.py:101
  132.3 4.2 %fold.11 = bf16[8,8,160,128]{3,2,1,0:T(8,128)(2,1)} custom-call(s32[65]{0:T(128)S(1)} %pad_add_fusion.1.facts, s32[4,1,1536]{2,1,0:T(1,128)S(1)} %dynamic-slice_bitcast_fusion.maps, bf16[160,1536]{1,0:T(8,128)(2,1)S(1)} %slice_bitcast_fusion.1.refs_0_, bf16[80,1536]{1,0:T(8,128)(2,1)S(1)} %collective-permute-done.13.refs_1_, ...), custom_call_target="tpu_custom_call", output_to_operand_aliasing={{}: (5, {})} | custom-call | flops 754974720 | bytes 1638400 | tf_op jit(solution)/shard_map/fold/pallas_call | solution.py:101
  136.5 0.6 all-to-all-done.received
  137.2 6.0 %all-to-all-start.1 = ((bf16[8,8,160,128]{3,2,1,0:T(8,128)(2,1)}), bf16[8,8,160,128]{3,2,1,0:T(8,128)(2,1)S(1)}, u32[]{:S(2)}, u32[]{:S(2)}) async-start(bf16[8,8,160,128]{3,2,1,0:T(8,128)(2,1)} %fold.11), calls=%async_computation.1 | async-start | bytes 5242880 | tf_op jit(solution)/shard_map/all_to_all | solution.py:268
  143.3 12.9 %ladder.2 = (f32[224,1536]{1,0:T(8,128)}, bf16[224,1536]{1,0:T(8,128)(2,1)}) custom-call(s32[33]{0:T(128)S(1)} %pad_add_fusion.facts, s32[1,1536]{1,0:T(1,128)S(1)} %constant_dynamic-slice_fusion.send_map, bf16[4096,1536]{1,0:T(8,128)(2,1)} %bitcast.22, bf16[8,8,224,128]{3,2,1,0:T(8,128)(2,1)} %all-to-all-done.received), custom_call_target="tpu_custom_call" | custom-call | flops 2818572288 | bytes 14417920 | tf_op jit(solution)/shard_map/ladder/pallas_call | solution.py:183
  156.2 2.1 collective-permute-start.10
  158.3 15.8 %all-to-all-done.1.received = bf16[8,8,160,128]{3,2,1,0:T(8,128)(2,1)S(1)} async-done(((bf16[8,8,160,128]{3,2,1,0:T(8,128)(2,1)}), bf16[8,8,160,128]{3,2,1,0:T(8,128)(2,1)S(1)}, u32[]{:S(2)}, u32[]{:S(2)}) %all-to-all-start.1) | async-done | bytes 2621472 | tf_op jit(solution)/shard_map/all_to_all | solution.py:268
  174.1 10.9 %ladder.3 = (f32[160,1536]{1,0:T(8,128)}, bf16[160,1536]{1,0:T(8,128)(2,1)S(1)}) custom-call(s32[33]{0:T(128)S(1)} %pad_add_fusion.facts, s32[1,1536]{1,0:T(1,128)S(1)} %constant_dynamic-slice_fusion.send_map, bf16[4096,1536]{1,0:T(8,128)(2,1)} %bitcast.23, bf16[8,8,160,128]{3,2,1,0:T(8,128)(2,1)S(1)} %all-to-all-done.1.received), custom_call_target="tpu_custom_call" | custom-call | flops 2013265920 | bytes 13893632 | tf_op jit(solution)/shard_map/ladder/pallas_call | solution.py:183
  185.0 2.1 collective-permute-start.17
  187.1 4.5 %select_reduce_fusion.1 = (f32[1536]{0:T(1024)S(1)}, f32[1536]{0:T(1024)S(1)}) fusion(f32[2048]{0:T(1024)S(1)} %copy-done.12, s32[1536]{0:T(1024)S(1)} %get-tuple-element.13, s32[1536]{0:T(1024)S(1)} %get-tuple-element.14), kind=kLoop, calls=%fused_computation.2 | loop fusion | flops 18871296 | bytes 32768 | tf_op jit(solution)/shard_map/reduce_sum | solution.py:223
  191.8 23.7 %collective-permute-done.17 = bf16[160,1536]{1,0:T(8,128)(2,1)} collective-permute-done((bf16[160,1536]{1,0:T(8,128)(2,1)S(1)}, bf16[160,1536]{1,0:T(8,128)(2,1)}, u32[]{:S(2)}, u32[]{:S(2)}) %collective-permute-start.17) | collective-permute-done | bytes 491552 | tf_op jit(solution)/shard_map/ppermute | solution.py:218
  215.4 1.8 add_convert_fusion.1
  217.3 1.6 add_convert_fusion
  218.9 1.1 maximum_bitcast_fusion
  (60 shorter events, 0.7 us)
Async XLA Ops:
  6.5 41.1 %copy-start = (s32[64,1536]{1,0:T(8,128)S(1)}, s32[64,1536]{1,0:T(8,128)}, u32[]{:S(2)}) copy-start(s32[64,1536]{1,0:T(8,128)} %param.12) | copy-start | bytes 1179652
  6.5 1.3 copy-start.7
  6.5 22.7 %copy-start.13 = (s32[1,32]{1,0:T(1,128)S(1)}, s32[1,32]{1,0:T(1,128)}, u32[]{:S(2)}) copy-start(s32[1,32]{1,0:T(1,128)} %param.10) | copy-start | bytes 388
  6.5 22.7 %copy-start.14 = (s32[1,32]{1,0:T(1,128)S(1)}, s32[1,32]{1,0:T(1,128)}, u32[]{:S(2)}) copy-start(s32[1,32]{1,0:T(1,128)} %param.11) | copy-start | bytes 388
  6.5 136.8 %all-gather.4.cloned.1.call-start = ((), (), s32[]{:S(2)}) async-start(), calls=%async_computation.2 | async-start | bytes 15728640 | tf_op jit(solution)/shard_map/all_gather | solution.py:232
  7.9 16.8 %collective-permute-start = (bf16[224,1536]{1,0:T(8,128)(2,1)S(1)}, bf16[224,1536]{1,0:T(8,128)(2,1)S(1)}, u32[]{:S(2)}, u32[]{:S(2)}) collective-permute-start(bf16[224,1536]{1,0:T(8,128)(2,1)S(1)} %slice_bitcast_fusion.refs_0_), channel_id=1, source_target_pairs={{0,224},{32,0},{64,32},{96,64},{128,96},{160,128},{192,160},{224,1... | collective-permute-start | bytes 2064392 | tf_op jit(solution)/shard_map/ppermute | solution.py:218
  8.0 20.3 %collective-permute-start.4 = (bf16[224,1536]{1,0:T(8,128)(2,1)S(1)}, bf16[224,1536]{1,0:T(8,128)(2,1)S(1)}, u32[]{:S(2)}, u32[]{:S(2)}) collective-permute-start(bf16[224,1536]{1,0:T(8,128)(2,1)S(1)} %slice_bitcast_fusion.refs_0_), channel_id=1, source_target_pairs={{0,32},{32,64},{64,96},{96,128},{128,160},{160,192},{192,224},{224... | collective-permute-start | bytes 2064392 | tf_op jit(solution)/shard_map/ppermute | solution.py:218
  24.7 16.0 %collective-permute-start.1 = (bf16[224,1536]{1,0:T(8,128)(2,1)S(1)}, bf16[224,1536]{1,0:T(8,128)(2,1)}, u32[]{:S(2)}, u32[]{:S(2)}) collective-permute-start(bf16[224,1536]{1,0:T(8,128)(2,1)S(1)} %collective-permute-done.refs_0_), channel_id=1, source_target_pairs={{0,224},{32,0},{64,32},{96,64},{128,96},{160,128},{192,160},{224,1... | collective-permute-start | bytes 2064392 | tf_op jit(solution)/shard_map/ppermute | solution.py:218
  27.5 0.8 copy-start.3
  28.3 17.4 %collective-permute-start.5 = (bf16[224,1536]{1,0:T(8,128)(2,1)S(1)}, bf16[224,1536]{1,0:T(8,128)(2,1)}, u32[]{:S(2)}, u32[]{:S(2)}) collective-permute-start(bf16[224,1536]{1,0:T(8,128)(2,1)S(1)} %collective-permute-done.4.refs_3_), channel_id=1, source_target_pairs={{0,32},{32,64},{64,96},{96,128},{128,160},{160,192},{192,224},{224... | collective-permute-start | bytes 2064392 | tf_op jit(solution)/shard_map/ppermute | solution.py:218
  28.3 0.9 copy-start.5
  40.7 17.0 %collective-permute-start.2 = (bf16[224,1536]{1,0:T(8,128)(2,1)}, bf16[224,1536]{1,0:T(8,128)(2,1)S(1)}, u32[]{:S(2)}, u32[]{:S(2)}) collective-permute-start(bf16[224,1536]{1,0:T(8,128)(2,1)} %collective-permute-done.1.refs_0_), channel_id=1, source_target_pairs={{0,224},{32,0},{64,32},{96,64},{128,96},{160,128},{192,160},{224,1... | collective-permute-start | bytes 2064392 | tf_op jit(solution)/shard_map/ppermute | solution.py:218
  45.8 15.7 %collective-permute-start.6 = (bf16[224,1536]{1,0:T(8,128)(2,1)}, bf16[224,1536]{1,0:T(8,128)(2,1)S(1)}, u32[]{:S(2)}, u32[]{:S(2)}) collective-permute-start(bf16[224,1536]{1,0:T(8,128)(2,1)} %collective-permute-done.5.refs_1_), channel_id=1, source_target_pairs={{0,32},{32,64},{64,96},{96,128},{128,160},{160,192},{192,224},{224... | collective-permute-start | bytes 2064392 | tf_op jit(solution)/shard_map/ppermute | solution.py:218
  61.5 23.0 %collective-permute-start.8 = (bf16[160,1536]{1,0:T(8,128)(2,1)}, bf16[160,1536]{1,0:T(8,128)(2,1)S(1)}, u32[]{:S(2)}, u32[]{:S(2)}) collective-permute-start(bf16[160,1536]{1,0:T(8,128)(2,1)} %joined.2), channel_id=1, source_target_pairs={{0,224},{32,0},{64,32},{96,64},{128,96},{160,128},{192,160},{224,1... | collective-permute-start | bytes 1474568 | tf_op jit(solution)/shard_map/ppermute | solution.py:218
  63.9 20.7 %collective-permute-start.9 = (bf16[160,1536]{1,0:T(8,128)(2,1)}, bf16[160,1536]{1,0:T(8,128)(2,1)S(1)}, u32[]{:S(2)}, u32[]{:S(2)}) collective-permute-start(bf16[160,1536]{1,0:T(8,128)(2,1)} %joined.2), channel_id=1, source_target_pairs={{0,32},{32,64},{64,96},{96,128},{128,160},{160,192},{192,224},{224... | collective-permute-start | bytes 1474568 | tf_op jit(solution)/shard_map/ppermute | solution.py:218
  63.9 14.7 %collective-permute-start.3 = (bf16[112,1536]{1,0:T(8,128)(2,1)S(1)}, bf16[112,1536]{1,0:T(8,128)(2,1)S(1)}, u32[]{:S(2)}, u32[]{:S(2)}) collective-permute-start(bf16[112,1536]{1,0:T(8,128)(2,1)S(1)} %slice.48), channel_id=1, source_target_pairs={{0,224},{32,0},{64,32},{96,64},{128,96},{160,128},{192,160},{224,1... | collective-permute-start | bytes 1032200 | tf_op jit(solution)/shard_map/ppermute | solution.py:218
  65.5 15.0 %collective-permute-start.7 = (bf16[112,1536]{1,0:T(8,128)(2,1)S(1)}, bf16[112,1536]{1,0:T(8,128)(2,1)S(1)}, u32[]{:S(2)}, u32[]{:S(2)}) collective-permute-start(bf16[112,1536]{1,0:T(8,128)(2,1)S(1)} %slice.49), channel_id=1, source_target_pairs={{0,32},{32,64},{64,96},{96,128},{128,160},{160,192},{192,224},{224... | collective-permute-start | bytes 1032200 | tf_op jit(solution)/shard_map/ppermute | solution.py:218
  65.6 4.9 %copy-start.4 = (bf16[224,1536]{1,0:T(8,128)(2,1)S(1)}, bf16[224,1536]{1,0:T(8,128)(2,1)}, u32[]{:S(2)}) copy-start(bf16[224,1536]{1,0:T(8,128)(2,1)} %copy-done.3) | copy-start | bytes 2064388
  65.6 5.0 %copy-start.6 = (bf16[224,1536]{1,0:T(8,128)(2,1)S(1)}, bf16[224,1536]{1,0:T(8,128)(2,1)}, u32[]{:S(2)}) copy-start(bf16[224,1536]{1,0:T(8,128)(2,1)} %copy-done.5) | copy-start | bytes 2064388
  84.6 0.8 copy-start.1
  85.3 51.9 %all-to-all-start = ((bf16[8,8,224,128]{3,2,1,0:T(8,128)(2,1)}), bf16[8,8,224,128]{3,2,1,0:T(8,128)(2,1)}, u32[]{:S(2)}, u32[]{:S(2)}) async-start(bf16[8,8,224,128]{3,2,1,0:T(8,128)(2,1)} %joined.3), calls=%async_computation | async-start | bytes 7340032 | tf_op jit(solution)/shard_map/all_to_all | solution.py:268
  95.0 30.7 %copy-start.2 = (bf16[160,1536]{1,0:T(8,128)(2,1)S(1)}, bf16[160,1536]{1,0:T(8,128)(2,1)}, u32[]{:S(2)}) copy-start(bf16[160,1536]{1,0:T(8,128)(2,1)} %copy-done.1) | copy-start | bytes 1474564
  95.0 12.6 %collective-permute-start.11 = (bf16[160,1536]{1,0:T(8,128)(2,1)S(1)}, bf16[160,1536]{1,0:T(8,128)(2,1)S(1)}, u32[]{:S(2)}, u32[]{:S(2)}) collective-permute-start(bf16[160,1536]{1,0:T(8,128)(2,1)S(1)} %collective-permute-done.8.refs_1_.refs_0_), channel_id=1, source_target_pairs={{0,224},{32,0},{64,32},{96,64},{128,96},{160,128},{192,160},{224,1... | collective-permute-start | bytes 1474568 | tf_op jit(solution)/shard_map/ppermute | solution.py:218
  97.1 12.6 %collective-permute-start.14 = (bf16[160,1536]{1,0:T(8,128)(2,1)}, bf16[160,1536]{1,0:T(8,128)(2,1)S(1)}, u32[]{:S(2)}, u32[]{:S(2)}) collective-permute-start(bf16[160,1536]{1,0:T(8,128)(2,1)} %copy-done.1), channel_id=1, source_target_pairs={{0,32},{32,64},{64,96},{96,128},{128,160},{160,192},{192,224},{224... | collective-permute-start | bytes 1474568 | tf_op jit(solution)/shard_map/ppermute | solution.py:218
  107.5 11.7 %collective-permute-start.12 = (bf16[160,1536]{1,0:T(8,128)(2,1)S(1)}, bf16[160,1536]{1,0:T(8,128)(2,1)S(1)}, u32[]{:S(2)}, u32[]{:S(2)}) collective-permute-start(bf16[160,1536]{1,0:T(8,128)(2,1)S(1)} %collective-permute-done.11.refs_0_), channel_id=1, source_target_pairs={{0,224},{32,0},{64,32},{96,64},{128,96},{160,128},{192,160},{224,1... | collective-permute-start | bytes 1474568 | tf_op jit(solution)/shard_map/ppermute | solution.py:218
  109.7 11.8 %collective-permute-start.15 = (bf16[160,1536]{1,0:T(8,128)(2,1)S(1)}, bf16[160,1536]{1,0:T(8,128)(2,1)S(1)}, u32[]{:S(2)}, u32[]{:S(2)}) collective-permute-start(bf16[160,1536]{1,0:T(8,128)(2,1)S(1)} %collective-permute-done.14.refs_1_), channel_id=1, source_target_pairs={{0,32},{32,64},{64,96},{96,128},{128,160},{160,192},{192,224},{224... | collective-permute-start | bytes 1474568 | tf_op jit(solution)/shard_map/ppermute | solution.py:218
  119.3 13.0 %collective-permute-start.13 = (bf16[80,1536]{1,0:T(8,128)(2,1)S(1)}, bf16[80,1536]{1,0:T(8,128)(2,1)S(1)}, u32[]{:S(2)}, u32[]{:S(2)}) collective-permute-start(bf16[80,1536]{1,0:T(8,128)(2,1)S(1)} %slice.50), channel_id=1, source_target_pairs={{0,224},{32,0},{64,32},{96,64},{128,96},{160,128},{192,160},{224,1... | collective-permute-start | bytes 737288 | tf_op jit(solution)/shard_map/ppermute | solution.py:218
  121.5 10.8 %collective-permute-start.16 = (bf16[80,1536]{1,0:T(8,128)(2,1)S(1)}, bf16[80,1536]{1,0:T(8,128)(2,1)S(1)}, u32[]{:S(2)}, u32[]{:S(2)}) collective-permute-start(bf16[80,1536]{1,0:T(8,128)(2,1)S(1)} %slice.51), channel_id=1, source_target_pairs={{0,32},{32,64},{64,96},{96,128},{128,160},{160,192},{192,224},{224... | collective-permute-start | bytes 737288 | tf_op jit(solution)/shard_map/ppermute | solution.py:218
  136.5 6.7 %copy-start.10 = (s32[1,2,1536]{2,1,0:T(2,128)S(1)}, s32[1,2,1536]{2,1,0:T(2,128)}, u32[]{:S(2)}) copy-start(s32[1,2,1536]{2,1,0:T(2,128)} %param.13) | copy-start | bytes 36868
  137.2 36.9 %all-to-all-start.1 = ((bf16[8,8,160,128]{3,2,1,0:T(8,128)(2,1)}), bf16[8,8,160,128]{3,2,1,0:T(8,128)(2,1)S(1)}, u32[]{:S(2)}, u32[]{:S(2)}) async-start(bf16[8,8,160,128]{3,2,1,0:T(8,128)(2,1)} %fold.11), calls=%async_computation.1 | async-start | bytes 5242880 | tf_op jit(solution)/shard_map/all_to_all | solution.py:268
  156.2 30.9 %copy-start.12 = (f32[2048]{0:T(1024)S(1)}, f32[2048]{0:T(1024)}, u32[]{:S(2)}) copy-start(f32[2048]{0:T(1024)} %param.14) | copy-start | bytes 24580
  156.2 35.5 %copy-start.11 = (f32[384]{0:T(512)S(1)}, f32[384]{0:T(512)}, u32[]{:S(2)}) copy-start(f32[384]{0:T(512)} %param.15) | copy-start | bytes 4612
  156.2 61.0 %collective-permute-start.10 = (bf16[224,1536]{1,0:T(8,128)(2,1)}, bf16[224,1536]{1,0:T(8,128)(2,1)}, u32[]{:S(2)}, u32[]{:S(2)}) collective-permute-start(bf16[224,1536]{1,0:T(8,128)(2,1)} %get-tuple-element.10), channel_id=1, source_target_pairs={{0,128},{32,160},{64,192},{96,224},{128,0},{160,32},{192,64},{224,... | collective-permute-start | bytes 2064392 | tf_op jit(solution)/shard_map/ppermute | solution.py:218
  185.0 32.3 %copy-start.8 = (bf16[384,1,1536]{2,0,1:T(8,128)(2,1)S(1)}, bf16[384,1,1536]{2,0,1:T(8,128)(2,1)}, u32[]{:S(2)}) copy-start(bf16[384,1,1536]{2,0,1:T(8,128)(2,1)} %param.8) | copy-start | bytes 3538948
  185.0 32.3 %copy-start.9 = (f32[224,1536]{1,0:T(8,128)S(1)}, f32[224,1536]{1,0:T(8,128)}, u32[]{:S(2)}) copy-start(f32[224,1536]{1,0:T(8,128)} %get-tuple-element.9) | copy-start | bytes 4128772
  185.0 32.3 %slice-start = ((f32[384]{0:T(512)}), f32[224]{0:T(256)S(1)}, s32[]{:S(2)}) async-start(f32[384]{0:T(512)} %param.15), calls=%async_computation.3 | async-start | bytes 2048 | tf_op jit(solution)/shard_map/slice | solution.py:272
  185.0 30.4 %collective-permute-start.17 = (bf16[160,1536]{1,0:T(8,128)(2,1)S(1)}, bf16[160,1536]{1,0:T(8,128)(2,1)}, u32[]{:S(2)}, u32[]{:S(2)}) collective-permute-start(bf16[160,1536]{1,0:T(8,128)(2,1)S(1)} %get-tuple-element.12), channel_id=1, source_target_pairs={{0,128},{32,160},{64,192},{96,224},{128,0},{160,32},{192,64},{224,... | collective-permute-start | bytes 1474568 | tf_op jit(solution)/shard_map/ppermute | solution.py:218
Sparse Core Ops, SparseCore 0:
  9.2 122.6 all-gather.3

commit v3 on v2

--- a/solution.py
+++ b/solution.py
@@ -19,7 +19,8 @@
 def fold_body(shifts, facts, maps, *refs):
     count = len(shifts)
     tiles = refs[: 3 if shifts == (0,) else 2 * count]
-    out, base, other, folded, base_sem, other_sem, out_sem = refs[-7:]
+    out, done, base, other, folded, base_sem, other_sem, out_sem = refs[-8:]
+    done[0] = 0
     z = facts[0]
     sign = jnp.where(z < 4, 1.0, -1.0).astype(jnp.float32)
     rows, length = folded.shape[1:]
@@ -65,7 +66,7 @@
             folded[i, :, pl.ds(start, COLS)] = ((mine + sign * turned) * 0.5).astype(jnp.bfloat16)
             return carry
 
-        lax.fori_loop(0, length // COLS, column, 0)
+        lax.fori_loop(0, length // COLS, column, 0, unroll=True)
 
         for receiver in range(8):
             for half in range(2):
@@ -102,8 +103,11 @@
         functools.partial(fold_body, shifts),
         in_specs=[pl.BlockSpec(memory_space=pltpu.SMEM), pl.BlockSpec(memory_space=pltpu.VMEM)]
         + [pl.BlockSpec(memory_space=pl.ANY)] * (len(tiles) + len(before)),
-        out_specs=pl.BlockSpec(memory_space=pl.ANY),
-        out_shape=pltpu.HBM((8, 8, rows, 128), jnp.bfloat16),
+        out_specs=[pl.BlockSpec(memory_space=pl.ANY), pl.BlockSpec(memory_space=pltpu.SMEM)],
+        out_shape=[
+            pltpu.HBM((8, 8, rows, 128), jnp.bfloat16),
+            jax.ShapeDtypeStruct((1,), jnp.int32),
+        ],
         scratch_shapes=[
             whole,
             whole,
@@ -140,6 +144,33 @@
     )(block, *others)
 
 
+def halves_body(first, second, _, first_out, second_out, sem):
+    cut = first_out.shape[0]
+    copies = (
+        pltpu.make_async_copy(first.at[pl.ds(0, cut)], first_out, sem.at[0]),
+        pltpu.make_async_copy(second.at[pl.ds(cut, cut)], second_out, sem.at[1]),
+    )
+    for copy in copies:
+        copy.start()
+    for copy in copies:
+        copy.wait()
+
+
+def halves(first, second, after):
+    rows, length = first.shape
+    held = pl.BlockSpec(memory_space=pl.ANY)
+    part = jax.ShapeDtypeStruct((rows // 2, length), first.dtype)
+    return pl.pallas_call(
+        halves_body,
+        in_specs=[held] * 3,
+        out_specs=[held] * 2,
+        out_shape=[part] * 2,
+        scratch_shapes=[pltpu.SemaphoreType.DMA((2,))],
+        compiler_params=pltpu.CompilerParams(vmem_limit_bytes=VMEM),
+        name="halves",
+    )(first, second, after)
+
+
 def ladder_body(facts, send_map, blocks, received, ladder, sent, operand, rounded, sem):
     step = pl.program_id(0)
     slots = operand.shape[1] // 128
@@ -174,7 +205,7 @@
             sent[:, pl.ds(start, COLS)] = moved.astype(jnp.bfloat16)
             return carry
 
-        lax.fori_loop(0, length // COLS, column, 0)
+        lax.fori_loop(0, length // COLS, column, 0, unroll=True)
 
 
 def ladder_of(facts, send_map, blocks, received):
@@ -212,6 +243,48 @@
         ),
         name="ladder",
     )(facts, send_map, blocks, received)
+
+
+def update_body(low, *refs):
+    own, ladder, partner, direction, occupied, virtual, out = refs[:7] if len(refs) == 7 else refs[:6] + refs[7:]
+    residual = ladder[...] + direction[0] * partner[...].astype(jnp.float32)
+    denominator = occupied[...] - virtual[0:1, :] - virtual[1:2, :]
+    out[...] = (own[...].astype(jnp.float32) + residual / denominator).astype(jnp.bfloat16)
+
+
+def update(low, own, ladder, partner, direction, occupied, virtual, before):
+    rows, length = ladder.shape
+    step = 32
+
+    def chunk(width):
+        return pl.BlockSpec((step, width), lambda n: (n, 0))
+
+    def whole(width):
+        return pl.BlockSpec((step, width), lambda n: (n + low // step, 0))
+
+    return pl.pallas_call(
+        functools.partial(update_body, low),
+        grid=(rows // step,),
+        in_specs=[
+            whole(length),
+            chunk(length),
+            chunk(length),
+            pl.BlockSpec(memory_space=pltpu.SMEM),
+            whole(1),
+            pl.BlockSpec((2, length), lambda n: (0, 0)),
+        ]
+        + [pl.BlockSpec(memory_space=pl.ANY)] * len(before),
+        out_specs=whole(length),
+        out_shape=jax.ShapeDtypeStruct(own.shape, jnp.bfloat16),
+        input_output_aliases={6: 0} if before else {},
+        compiler_params=pltpu.CompilerParams(
+            vmem_limit_bytes=VMEM, dimension_semantics=("arbitrary",)
+        ),
+        cost_estimate=pl.CostEstimate(
+            flops=8 * rows * length, bytes_accessed=10 * rows * length, transcendentals=0
+        ),
+        name="update",
+    )(own, ladder, partner, direction, occupied, virtual, *before)
 
 
 def shifted(block, by):
@@ -245,35 +318,34 @@
     direction = jnp.where(z >= 4, 1.0, -1.0).astype(jnp.float32)
     first = energies(vir_energy, pair_virt[0, 0])
     second = energies(vir_energy, pair_virt[0, 1])
+    virtual = jnp.stack([first, second])
     ends = (0, 224, rows)
-    parts = [own[low:high] for low, high in zip(ends, ends[1:])]
-    rings = []
-    for i, part in enumerate(parts):
-        if i:
-            part = joined(part, rings[i - 1][2], pltpu.HBM)
-        up1, down1 = shifted(part, -1), shifted(part, 1)
-        up2, down2 = shifted(up1, -1), shifted(down1, 1)
-        up3, down3 = shifted(up2, -1), shifted(down2, 1)
-        cut = part.shape[0] // 2
-        far = (shifted(up3[:cut], -1), shifted(down3[cut:], 1))
-        rings.append(((up1, down1), (up2, down2), (up3, down3), far))
-    updated = []
-    for i, part in enumerate(parts):
-        one, two, three, far = rings[i]
-        slots = fold((2,), fold_facts, maps, two, ())
-        slots = fold((1, 3), fold_facts, maps, (one[0], three[1], three[0], one[1]), (slots,))
-        slots = fold((0,), fold_facts, maps, (part, *far), (slots,))
-        if i + 1 < len(parts):
-            slots = joined(slots, rings[i + 1][0], pltpu.HBM)
+    steps, folds = [], []
+    for low, high in zip(ends, ends[1:]):
+        part = own[low:high]
+        if steps:
+            part = joined(part, steps[-1][2], pltpu.HBM)
+        one = (shifted(part, -1), shifted(part, 1))
+        two = (shifted(one[0], -1), shifted(one[1], 1))
+        slots, done = fold((2,), fold_facts, maps, two, ())
+        three = (shifted(two[0], -1), shifted(two[1], 1))
+        upper, lower = halves(*three, done if steps else fold_facts)
+        far = (shifted(upper, -1), shifted(lower, 1))
+        odd = (one[0], three[1], three[0], one[1])
+        slots, _ = fold((1, 3), fold_facts, maps, odd, (slots,))
+        steps.append((part, one, two, far))
+        folds.append(slots)
+    fresh = ()
+    for i, (part, one, two, far) in enumerate(steps):
+        slots, _ = fold((0,), fold_facts, maps, (part, *far), (folds[i],))
+        if i + 1 < len(steps):
+            slots = joined(slots, steps[i + 1][2], pltpu.HBM)
         received = lax.all_to_all(slots, "ket", split_axis=0, concat_axis=0, tiled=True)
         ladder, sent = ladder_of(ladder_facts, send_map, all_blocks, received)
         partner = shifted(sent, 4)
-        residual = ladder + direction * partner.astype(jnp.float32)
-        occupied = pair_energy[ends[i] : ends[i + 1]]
-        denominator = occupied[:, None] - first[None, :] - second[None, :]
-        fresh = part.astype(jnp.float32) + residual / denominator
-        updated.append(fresh.astype(jnp.bfloat16))
-    return jnp.concatenate(updated, axis=0)[:, None, :]
+        fresh = update(ends[i], own, ladder, partner, direction[None], pair_energy[:, None], virtual, fresh)
+        fresh = (fresh,)
+    return fresh[0][:, None, :]
 
 
 def solution(mesh):

time: 228 us -> 237 us (1.039)
  Pallas kernels: 54.5 us -> 62.6 us
  other arithmetic: 9.45 us -> 5 us
  waiting for transfers between devices: 94.7 us -> 97.8 us
    all_to_all x2, waiting for transfers between devices: 16.5 us -> 31.3 us  [local(): lax.all_to_all(slots, 'ket', split_axis=0, concat_axis=0, tiled=True)]
    ppermute x18, waiting for transfers between devices: 77.5 us -> 65.9 us  [shifted(): return lax.ppermute(block, 'bra', [(i, (i + by) % 8) for i in range(8)])]
    pallas_call x0 -> x4, Pallas kernels: none -> 11.2 us  [the longest x2 8.85 us: update(): pl.pallas_call(functools.partial(update_body, low), grid=(rows // step,),...]
    convert_element_type x2 -> x0, other arithmetic: 3.38 us -> none  [local(): updated.append(fresh.astype(jnp.bfloat16))]
  transfers between devices with their start and end apart: 21 -> 21, of which waited for: 12 -> 14; matrix products, arithmetic and copies ran while one was open for 4% -> 3% of each run, Pallas kernels for 24% -> 25%
where the time goes in v3:
time: 237 us; the launch traced here: 234 us
  waiting for transfers between devices  97.8 us (41%)
  Pallas kernels  62.6 us (26%)
  starting transfers between devices  38.9 us (16%)
  between operations  13.7 us (6%)
  blocking collectives  11.4 us (5%)
  other arithmetic  5 us (2%)
  local copies, waits for them, and re-layouts  4.11 us (2%)
    ppermute x18, waiting for transfers between devices, shifted(): return lax.ppermute(block, 'bra', [(i, (i + by) % 8) for i in range(8)])  65.9 us
    all_to_all x2, waiting for transfers between devices, local(): lax.all_to_all(slots, 'ket', split_axis=0, concat_axis=0, tiled=True)  31.3 us
    pallas_call x6, Pallas kernels, fold(): pl.pallas_call(functools.partial(fold_body, shifts), in_specs=[pl.BlockSp...  28.6 us
    ppermute x18, starting transfers between devices, shifted(): return lax.ppermute(block, 'bra', [(i, (i + by) % 8) for i in range(8)])  24.1 us
    pallas_call x2, Pallas kernels, ladder_of(): pl.pallas_call(ladder_body, grid=(length // COLS,), in_specs=[pl.BlockSpe...  22.8 us
    all_to_all x2, starting transfers between devices, local(): lax.all_to_all(slots, 'ket', split_axis=0, concat_axis=0, tiled=True)  14.8 us
    all_gather x1, blocking collectives, local(): wanted = lax.all_gather(block_owner[0] * 16 + screen_list[0], 'ket', axis=0)  11.4 us
    pallas_call x2, Pallas kernels, update(): pl.pallas_call(functools.partial(update_body, low), grid=(rows // step,),...  8.85 us
  transfers between devices with their start and end apart: 21, of which 14 were waited for; matrix products, arithmetic and copies ran while one was open for 3% of the time, Pallas kernels for 25%

profile of v3, /device:TPU:47, one launch (start us, length us, event | category | flops | bytes accessed | tf_op | source)
XLA Modules:
  0.0 233.5 jit_solution(8144083295544636363)
XLA Ops:
  6.6 0.7 all-gather.4.cloned.1.call-update
  7.3 1.1 slice_bitcast_fusion.refs_0_
  8.5 1.7 collective-permute-start.2
  10.2 15.1 %collective-permute-done.refs_0_ = bf16[224,1536]{1,0:T(8,128)(2,1)} collective-permute-done((bf16[224,1536]{1,0:T(8,128)(2,1)S(1)}, bf16[224,1536]{1,0:T(8,128)(2,1)}, u32[]{:S(2)}, u32[]{:S(2)}) %collective-permute-start) | collective-permute-done | bytes 688160 | tf_op jit(solution)/shard_map/ppermute | solution.py:291
  25.3 2.7 %collective-permute-start.1 = (bf16[224,1536]{1,0:T(8,128)(2,1)}, bf16[224,1536]{1,0:T(8,128)(2,1)S(1)}, u32[]{:S(2)}, u32[]{:S(2)}) collective-permute-start(bf16[224,1536]{1,0:T(8,128)(2,1)} %collective-permute-done.refs_0_), channel_id=1, source_target_pairs={{0,224},{32,0},{64,32},{96,64},{128,96},{160,128},{192,160},{224,1... | collective-permute-start | bytes 2064392 | tf_op jit(solution)/shard_map/ppermute | solution.py:291
  28.0 0.8 collective-permute-done.2.refs_3_
  28.9 0.8 slice_bitcast_fusion.1.refs_0_
  29.7 11.9 %collective-permute-done.1.refs_1_.refs_0_ = bf16[224,1536]{1,0:T(8,128)(2,1)S(1)} collective-permute-done((bf16[224,1536]{1,0:T(8,128)(2,1)}, bf16[224,1536]{1,0:T(8,128)(2,1)S(1)}, u32[]{:S(2)}, u32[]{:S(2)}) %collective-permute-start.1) | collective-permute-done | bytes 688160 | tf_op jit(solution)/shard_map/ppermute | solution.py:291
  41.5 3.5 %collective-permute-start.13 = (bf16[224,1536]{1,0:T(8,128)(2,1)S(1)}, bf16[224,1536]{1,0:T(8,128)(2,1)}, u32[]{:S(2)}, u32[]{:S(2)}) collective-permute-start(bf16[224,1536]{1,0:T(8,128)(2,1)S(1)} %collective-permute-done.1.refs_1_.refs_0_), channel_id=1, source_target_pairs={{0,224},{32,0},{64,32},{96,64},{128,96},{160,128},{192,160},{224,1... | collective-permute-start | bytes 2064392 | tf_op jit(solution)/shard_map/ppermute | solution.py:291
  45.0 0.7 collective-permute-done.3.refs_2_.refs_1_
  45.8 2.8 %collective-permute-start.4 = (bf16[160,1536]{1,0:T(8,128)(2,1)}, bf16[160,1536]{1,0:T(8,128)(2,1)}, u32[]{:S(2)}, u32[]{:S(2)}) collective-permute-start(bf16[160,1536]{1,0:T(8,128)(2,1)} %joined.2.refs_0_), channel_id=1, source_target_pairs={{0,224},{32,0},{64,32},{96,64},{128,96},{160,128},{192,160},{224,1... | collective-permute-start | bytes 1474568 | tf_op jit(solution)/shard_map/ppermute | solution.py:291
  48.6 11.4 %all-gather.1 = s32[8,1,32]{2,1,0:T(1,128)S(1)} all-gather(s32[1,1,32]{2,1,0:T(1,128)S(1)} %add_bitcast_fusion), channel_id=1, replica_groups=mesh['bra'=8,'ket'=8,'pair'=4] {'ket'}, dimensions={0}, use_global_device_ids=true | all-gather | bytes 1152 | tf_op jit(solution)/shard_map/all_gather | solution.py:307
  60.0 0.3 select_reduce_fusion.2
  60.4 8.6 %collective-permute-done.4.refs_0_ = bf16[160,1536]{1,0:T(8,128)(2,1)} collective-permute-done((bf16[160,1536]{1,0:T(8,128)(2,1)}, bf16[160,1536]{1,0:T(8,128)(2,1)}, u32[]{:S(2)}, u32[]{:S(2)}) %collective-permute-start.4) | collective-permute-done | bytes 491552 | tf_op jit(solution)/shard_map/ppermute | solution.py:291
  69.0 2.4 %collective-permute-start.5 = (bf16[160,1536]{1,0:T(8,128)(2,1)}, bf16[160,1536]{1,0:T(8,128)(2,1)S(1)}, u32[]{:S(2)}, u32[]{:S(2)}) collective-permute-start(bf16[160,1536]{1,0:T(8,128)(2,1)} %collective-permute-done.4.refs_0_), channel_id=1, source_target_pairs={{0,224},{32,0},{64,32},{96,64},{128,96},{160,128},{192,160},{224,1... | collective-permute-start | bytes 1474568 | tf_op jit(solution)/shard_map/ppermute | solution.py:291
  71.4 0.9 collective-permute-done.7.refs_3_
  72.4 1.1 halves.3
  73.5 2.6 %collective-permute-start.15 = (bf16[112,1536]{1,0:T(8,128)(2,1)S(1)}, bf16[112,1536]{1,0:T(8,128)(2,1)S(1)}, u32[]{:S(2)}, u32[]{:S(2)}) collective-permute-start(bf16[112,1536]{1,0:T(8,128)(2,1)S(1)} %get-tuple-element.28), channel_id=1, source_target_pairs={{0,224},{32,0},{64,32},{96,64},{128,96},{160,128},{192,160},{224,1... | collective-permute-start | bytes 1032200 | tf_op jit(solution)/shard_map/ppermute | solution.py:291
  76.1 4.8 %fold.9 = (bf16[8,8,224,128]{3,2,1,0:T(8,128)(2,1)}, s32[1]{0:T(128)}) custom-call(s32[65]{0:T(128)S(1)} %pad_add_fusion.1.facts._, s32[4,1,1536]{2,1,0:T(1,128)S(1)} %dynamic-slice_bitcast_fusion.maps, bf16[224,1536]{1,0:T(8,128)(2,1)S(1)} %collective-permute-done.1.refs_1_.refs_0_, bf16[224,1536]{1,0:T(8,128)(2,1)} %collective-permute-done.3.refs_2_.refs_1_), custom_call_target="tpu_custom_call" | custom-call | flops 1056964608 | bytes 2293760 | tf_op jit(solution)/shard_map/fold/pallas_call | solution.py:102
  80.9 6.2 %fold.10 = (bf16[8,8,224,128]{3,2,1,0:T(8,128)(2,1)}, s32[1]{0:T(128)}) custom-call(s32[65]{0:T(128)S(1)} %pad_add_fusion.1.facts._, s32[4,1,1536]{2,1,0:T(1,128)S(1)} %dynamic-slice_bitcast_fusion.maps, bf16[224,1536]{1,0:T(8,128)(2,1)} %collective-permute-done.refs_0_, ...), custom_call_target="tpu_custom_call", output_to_operand_aliasing={{0}: (6, {})} | custom-call | flops 2113929216 | bytes 4587520 | tf_op jit(solution)/shard_map/fold/pallas_call | solution.py:102
  87.2 0.3 collective-permute-done.15.refs_1_
  87.5 3.0 %collective-permute-done.16.refs_2_ = bf16[112,1536]{1,0:T(8,128)(2,1)S(1)} collective-permute-done((bf16[112,1536]{1,0:T(8,128)(2,1)S(1)}, bf16[112,1536]{1,0:T(8,128)(2,1)S(1)}, u32[]{:S(2)}, u32[]{:S(2)}) %collective-permute-start.16) | collective-permute-done | bytes 344096 | tf_op jit(solution)/shard_map/ppermute | solution.py:291
  90.5 4.1 %fold.11 = (bf16[8,8,224,128]{3,2,1,0:T(8,128)(2,1)}, s32[1]{0:T(128)}) custom-call(s32[65]{0:T(128)S(1)} %pad_add_fusion.1.facts._, s32[4,1,1536]{2,1,0:T(1,128)S(1)} %dynamic-slice_bitcast_fusion.maps, bf16[224,1536]{1,0:T(8,128)(2,1)S(1)} %slice_bitcast_fusion.refs_0_, ...), custom_call_target="tpu_custom_call", output_to_operand_aliasing={{0}: (5, {})} | custom-call | flops 1056964608 | bytes 2293760 | tf_op jit(solution)/shard_map/fold/pallas_call | solution.py:102
  94.6 0.8 copy-done.5
  95.4 8.5 %all-to-all-start.1 = ((bf16[8,8,224,128]{3,2,1,0:T(8,128)(2,1)}), bf16[8,8,224,128]{3,2,1,0:T(8,128)(2,1)}, u32[]{:S(2)}, u32[]{:S(2)}) async-start(bf16[8,8,224,128]{3,2,1,0:T(8,128)(2,1)} %joined.3), calls=%async_computation.1 | async-start | bytes 7340032 | tf_op jit(solution)/shard_map/all_to_all | solution.py:343
  103.9 2.6 %collective-permute-start.6 = (bf16[160,1536]{1,0:T(8,128)(2,1)S(1)}, bf16[160,1536]{1,0:T(8,128)(2,1)S(1)}, u32[]{:S(2)}, u32[]{:S(2)}) collective-permute-start(bf16[160,1536]{1,0:T(8,128)(2,1)S(1)} %collective-permute-done.5.refs_0_.refs_1_), channel_id=1, source_target_pairs={{0,224},{32,0},{64,32},{96,64},{128,96},{160,128},{192,160},{224,1... | collective-permute-start | bytes 1474568 | tf_op jit(solution)/shard_map/ppermute | solution.py:291
  106.5 1.1 copy-done.6
  107.6 3.8 %fold.6 = (bf16[8,8,160,128]{3,2,1,0:T(8,128)(2,1)}, s32[1]{0:T(128)}) custom-call(s32[65]{0:T(128)S(1)} %pad_add_fusion.1.facts._, s32[4,1,1536]{2,1,0:T(1,128)S(1)} %dynamic-slice_bitcast_fusion.maps, bf16[160,1536]{1,0:T(8,128)(2,1)S(1)} %collective-permute-done.5.refs_0_.refs_1_, bf16[160,1536]{1,0:T(8,128)(2,1)S(1)} %copy-done.6), custom_call_target="tpu_custom_call" | custom-call | flops 754974720 | bytes 1638400 | tf_op jit(solution)/shard_map/fold/pallas_call | solution.py:102
  111.4 5.4 %collective-permute-done.6.first.refs_2_ = bf16[160,1536]{1,0:T(8,128)(2,1)S(1)} collective-permute-done((bf16[160,1536]{1,0:T(8,128)(2,1)S(1)}, bf16[160,1536]{1,0:T(8,128)(2,1)S(1)}, u32[]{:S(2)}, u32[]{:S(2)}) %collective-permute-start.6) | collective-permute-done | bytes 491552 | tf_op jit(solution)/shard_map/ppermute | solution.py:291
  116.8 2.2 collective-permute-done.9.second.refs_1_
  119.0 1.3 halves.2
  120.2 1.3 collective-permute-start.10
  121.6 0.2 collective-permute-start.11
  121.8 5.5 %fold.7 = (bf16[8,8,160,128]{3,2,1,0:T(8,128)(2,1)}, s32[1]{0:T(128)}) custom-call(s32[65]{0:T(128)S(1)} %pad_add_fusion.1.facts._, s32[4,1,1536]{2,1,0:T(1,128)S(1)} %dynamic-slice_bitcast_fusion.maps, bf16[160,1536]{1,0:T(8,128)(2,1)} %collective-permute-done.4.refs_0_, ...), custom_call_target="tpu_custom_call", output_to_operand_aliasing={{0}: (6, {})} | custom-call | flops 1509949440 | bytes 3276800 | tf_op jit(solution)/shard_map/fold/pallas_call | solution.py:102
  127.3 0.2 collective-permute-done.11.refs_2_
  127.4 4.2 %fold.8 = (bf16[8,8,160,128]{3,2,1,0:T(8,128)(2,1)}, s32[1]{0:T(128)}) custom-call(s32[65]{0:T(128)S(1)} %pad_add_fusion.1.facts._, s32[4,1,1536]{2,1,0:T(1,128)S(1)} %dynamic-slice_bitcast_fusion.maps, bf16[160,1536]{1,0:T(8,128)(2,1)S(1)} %copy-done.2, bf16[80,1536]{1,0:T(8,128)(2,1)S(1)} %collective-permute-done.10.refs_1_, ...), custom_call_target="tpu_custom_call", output_to_operand_aliasing={{0}: (5, {})} | custom-call | flops 754974720 | bytes 1638400 | tf_op jit(solution)/shard_map/fold/pallas_call | solution.py:102
  131.6 14.5 %all-to-all-done.1.received = bf16[8,8,224,128]{3,2,1,0:T(8,128)(2,1)} async-done(((bf16[8,8,224,128]{3,2,1,0:T(8,128)(2,1)}), bf16[8,8,224,128]{3,2,1,0:T(8,128)(2,1)}, u32[]{:S(2)}, u32[]{:S(2)}) %all-to-all-start.1) | async-done | bytes 3670048 | tf_op jit(solution)/shard_map/all_to_all | solution.py:343
  146.1 6.2 %all-to-all-start = ((bf16[8,8,160,128]{3,2,1,0:T(8,128)(2,1)}), bf16[8,8,160,128]{3,2,1,0:T(8,128)(2,1)}, u32[]{:S(2)}, u32[]{:S(2)}) async-start(bf16[8,8,160,128]{3,2,1,0:T(8,128)(2,1)} %get-tuple-element.25), calls=%async_computation | async-start | bytes 5242880 | tf_op jit(solution)/shard_map/all_to_all | solution.py:343
  152.5 11.9 %ladder.3 = (f32[224,1536]{1,0:T(8,128)}, bf16[224,1536]{1,0:T(8,128)(2,1)}) custom-call(s32[33]{0:T(128)S(1)} %pad_add_fusion.facts, s32[1,1536]{1,0:T(1,128)S(1)} %constant_dynamic-slice_fusion.send_map, bf16[4096,1536]{1,0:T(8,128)(2,1)} %bitcast.21, bf16[8,8,224,128]{3,2,1,0:T(8,128)(2,1)} %all-to-all-done.1.received), custom_call_target="tpu_custom_call" | custom-call | flops 2818572288 | bytes 14417920 | tf_op jit(solution)/shard_map/ladder/pallas_call | solution.py:214
  164.4 2.1 collective-permute-start.17
  166.5 16.8 %all-to-all-done.received = bf16[8,8,160,128]{3,2,1,0:T(8,128)(2,1)} async-done(((bf16[8,8,160,128]{3,2,1,0:T(8,128)(2,1)}), bf16[8,8,160,128]{3,2,1,0:T(8,128)(2,1)}, u32[]{:S(2)}, u32[]{:S(2)}) %all-to-all-start) | async-done | bytes 2621472 | tf_op jit(solution)/shard_map/all_to_all | solution.py:343
  183.3 10.9 %ladder.2 = (f32[160,1536]{1,0:T(8,128)}, bf16[160,1536]{1,0:T(8,128)(2,1)}) custom-call(s32[33]{0:T(128)S(1)} %pad_add_fusion.facts, s32[1,1536]{1,0:T(1,128)S(1)} %constant_dynamic-slice_fusion.send_map, bf16[4096,1536]{1,0:T(8,128)(2,1)} %bitcast.22, bf16[8,8,160,128]{3,2,1,0:T(8,128)(2,1)} %all-to-all-done.received), custom_call_target="tpu_custom_call" | custom-call | flops 2013265920 | bytes 13893632 | tf_op jit(solution)/shard_map/ladder/pallas_call | solution.py:214
  194.2 2.1 collective-permute-start.12
  196.3 4.5 %select_reduce_fusion.1 = (f32[1536]{0:T(1024)S(1)}, f32[1536]{0:T(1024)S(1)}) fusion(f32[2048]{0:T(1024)S(1)} %copy-done.9, s32[1536]{0:T(1024)S(1)} %get-tuple-element.35, s32[1536]{0:T(1024)S(1)} %get-tuple-element.36), kind=kLoop, calls=%fused_computation.2 | loop fusion | flops 18871296 | bytes 32768 | tf_op jit(solution)/shard_map/reduce_sum | solution.py:296
  200.9 0.1 broadcast_in_dim.56.refs_4_
  201.1 5.1 %update.2.refs_6_ = bf16[384,1536]{1,0:T(8,128)(2,1)} custom-call(bf16[384,1536]{1,0:T(8,128)(2,1)S(1)} %bitcast.19, f32[224,1536]{1,0:T(8,128)S(1)} %copy-done.3, bf16[224,1536]{1,0:T(8,128)(2,1)} %collective-permute-done.17.refs_2_, f32[1]{0:T(128)} %bitcast.12.refs_3_, f32[384,1]{1,0:T(8,128)S(1)} %broadcast_in_dim.56.refs_4_, ...), custom_call_target="tpu_custom_call" | custom-call | flops 2752512 | bytes 3440640 | tf_op jit(solution)/shard_map/update/pallas_call | solution.py:265
  206.1 16.8 %collective-permute-done.12.refs_2_ = bf16[160,1536]{1,0:T(8,128)(2,1)} collective-permute-done((bf16[160,1536]{1,0:T(8,128)(2,1)}, bf16[160,1536]{1,0:T(8,128)(2,1)}, u32[]{:S(2)}, u32[]{:S(2)}) %collective-permute-start.12) | collective-permute-done | bytes 491552 | tf_op jit(solution)/shard_map/ppermute | solution.py:291
  222.9 3.8 %update.3 = bf16[384,1536]{1,0:T(8,128)(2,1)} custom-call(bf16[384,1536]{1,0:T(8,128)(2,1)S(1)} %bitcast.20, f32[160,1536]{1,0:T(8,128)S(1)} %copy-done.4, bf16[160,1536]{1,0:T(8,128)(2,1)} %collective-permute-done.12.refs_2_, f32[1]{0:T(128)} %bitcast.12.refs_3_, f32[384,1]{1,0:T(8,128)S(1)} %broadcast_in_dim.56.refs_4_, ...), custom_call_target="tpu_custom_call", output_to_operand_aliasing={{}: (6, {})} | custom-call | flops 1966080 | bytes 2457600 | tf_op jit(solution)/shard_map/update/pallas_call | solution.py:265
  (51 shorter events, 0.6 us)
Async XLA Ops:
  6.5 69.5 %copy-start = (s32[64,1536]{1,0:T(8,128)S(1)}, s32[64,1536]{1,0:T(8,128)}, u32[]{:S(2)}) copy-start(s32[64,1536]{1,0:T(8,128)} %param.12) | copy-start | bytes 1179652
  6.5 22.3 %copy-start.1 = (bf16[384,1,1536]{2,0,1:T(8,128)(2,1)S(1)}, bf16[384,1,1536]{2,0,1:T(8,128)(2,1)}, u32[]{:S(2)}) copy-start(bf16[384,1,1536]{2,0,1:T(8,128)(2,1)} %param.8) | copy-start | bytes 3538948
  6.5 39.2 %copy-start.10 = (s32[1,32]{1,0:T(1,128)S(1)}, s32[1,32]{1,0:T(1,128)}, u32[]{:S(2)}) copy-start(s32[1,32]{1,0:T(1,128)} %param.10) | copy-start | bytes 388
  6.5 39.2 %copy-start.11 = (s32[1,32]{1,0:T(1,128)S(1)}, s32[1,32]{1,0:T(1,128)}, u32[]{:S(2)}) copy-start(s32[1,32]{1,0:T(1,128)} %param.11) | copy-start | bytes 388
  6.5 146.0 %all-gather.4.cloned.1.call-start = ((), (), s32[]{:S(2)}) async-start(), calls=%async_computation.2 | async-start | bytes 15728640 | tf_op jit(solution)/shard_map/all_gather | solution.py:305
  8.4 16.9 %collective-permute-start = (bf16[224,1536]{1,0:T(8,128)(2,1)S(1)}, bf16[224,1536]{1,0:T(8,128)(2,1)}, u32[]{:S(2)}, u32[]{:S(2)}) collective-permute-start(bf16[224,1536]{1,0:T(8,128)(2,1)S(1)} %slice_bitcast_fusion.refs_0_), channel_id=1, source_target_pairs={{0,224},{32,0},{64,32},{96,64},{128,96},{160,128},{192,160},{224,1... | collective-permute-start | bytes 2064392 | tf_op jit(solution)/shard_map/ppermute | solution.py:291
  8.5 20.3 %collective-permute-start.2 = (bf16[224,1536]{1,0:T(8,128)(2,1)S(1)}, bf16[224,1536]{1,0:T(8,128)(2,1)}, u32[]{:S(2)}, u32[]{:S(2)}) collective-permute-start(bf16[224,1536]{1,0:T(8,128)(2,1)S(1)} %slice_bitcast_fusion.refs_0_), channel_id=1, source_target_pairs={{0,32},{32,64},{64,96},{96,128},{128,160},{160,192},{192,224},{224... | collective-permute-start | bytes 2064392 | tf_op jit(solution)/shard_map/ppermute | solution.py:291
  25.3 16.2 %collective-permute-start.1 = (bf16[224,1536]{1,0:T(8,128)(2,1)}, bf16[224,1536]{1,0:T(8,128)(2,1)S(1)}, u32[]{:S(2)}, u32[]{:S(2)}) collective-permute-start(bf16[224,1536]{1,0:T(8,128)(2,1)} %collective-permute-done.refs_0_), channel_id=1, source_target_pairs={{0,224},{32,0},{64,32},{96,64},{128,96},{160,128},{192,160},{224,1... | collective-permute-start | bytes 2064392 | tf_op jit(solution)/shard_map/ppermute | solution.py:291
  28.8 16.9 %collective-permute-start.3 = (bf16[224,1536]{1,0:T(8,128)(2,1)}, bf16[224,1536]{1,0:T(8,128)(2,1)}, u32[]{:S(2)}, u32[]{:S(2)}) collective-permute-start(bf16[224,1536]{1,0:T(8,128)(2,1)} %collective-permute-done.2.refs_3_), channel_id=1, source_target_pairs={{0,32},{32,64},{64,96},{96,128},{128,160},{160,192},{192,224},{224... | collective-permute-start | bytes 2064392 | tf_op jit(solution)/shard_map/ppermute | solution.py:291
  41.5 30.9 %collective-permute-start.13 = (bf16[224,1536]{1,0:T(8,128)(2,1)S(1)}, bf16[224,1536]{1,0:T(8,128)(2,1)}, u32[]{:S(2)}, u32[]{:S(2)}) collective-permute-start(bf16[224,1536]{1,0:T(8,128)(2,1)S(1)} %collective-permute-done.1.refs_1_.refs_0_), channel_id=1, source_target_pairs={{0,224},{32,0},{64,32},{96,64},{128,96},{160,128},{192,160},{224,1... | collective-permute-start | bytes 2064392 | tf_op jit(solution)/shard_map/ppermute | solution.py:291
  45.8 26.6 %collective-permute-start.14 = (bf16[224,1536]{1,0:T(8,128)(2,1)}, bf16[224,1536]{1,0:T(8,128)(2,1)}, u32[]{:S(2)}, u32[]{:S(2)}) collective-permute-start(bf16[224,1536]{1,0:T(8,128)(2,1)} %collective-permute-done.3.refs_2_.refs_1_), channel_id=1, source_target_pairs={{0,32},{32,64},{64,96},{96,128},{128,160},{160,192},{192,224},{224... | collective-permute-start | bytes 2064392 | tf_op jit(solution)/shard_map/ppermute | solution.py:291
  45.8 23.2 %collective-permute-start.4 = (bf16[160,1536]{1,0:T(8,128)(2,1)}, bf16[160,1536]{1,0:T(8,128)(2,1)}, u32[]{:S(2)}, u32[]{:S(2)}) collective-permute-start(bf16[160,1536]{1,0:T(8,128)(2,1)} %joined.2.refs_0_), channel_id=1, source_target_pairs={{0,224},{32,0},{64,32},{96,64},{128,96},{160,128},{192,160},{224,1... | collective-permute-start | bytes 1474568 | tf_op jit(solution)/shard_map/ppermute | solution.py:291
  48.6 23.8 %collective-permute-start.7 = (bf16[160,1536]{1,0:T(8,128)(2,1)}, bf16[160,1536]{1,0:T(8,128)(2,1)}, u32[]{:S(2)}, u32[]{:S(2)}) collective-permute-start(bf16[160,1536]{1,0:T(8,128)(2,1)} %joined.2.refs_0_), channel_id=1, source_target_pairs={{0,32},{32,64},{64,96},{96,128},{128,160},{160,192},{192,224},{224... | collective-permute-start | bytes 1474568 | tf_op jit(solution)/shard_map/ppermute | solution.py:291
  69.0 25.6 %collective-permute-start.5 = (bf16[160,1536]{1,0:T(8,128)(2,1)}, bf16[160,1536]{1,0:T(8,128)(2,1)S(1)}, u32[]{:S(2)}, u32[]{:S(2)}) collective-permute-start(bf16[160,1536]{1,0:T(8,128)(2,1)} %collective-permute-done.4.refs_0_), channel_id=1, source_target_pairs={{0,224},{32,0},{64,32},{96,64},{128,96},{160,128},{192,160},{224,1... | collective-permute-start | bytes 1474568 | tf_op jit(solution)/shard_map/ppermute | solution.py:291
  72.4 22.2 %collective-permute-start.8 = (bf16[160,1536]{1,0:T(8,128)(2,1)}, bf16[160,1536]{1,0:T(8,128)(2,1)S(1)}, u32[]{:S(2)}, u32[]{:S(2)}) collective-permute-start(bf16[160,1536]{1,0:T(8,128)(2,1)} %collective-permute-done.7.refs_3_), channel_id=1, source_target_pairs={{0,32},{32,64},{64,96},{96,128},{128,160},{160,192},{192,224},{224... | collective-permute-start | bytes 1474568 | tf_op jit(solution)/shard_map/ppermute | solution.py:291
  73.5 14.0 %collective-permute-start.15 = (bf16[112,1536]{1,0:T(8,128)(2,1)S(1)}, bf16[112,1536]{1,0:T(8,128)(2,1)S(1)}, u32[]{:S(2)}, u32[]{:S(2)}) collective-permute-start(bf16[112,1536]{1,0:T(8,128)(2,1)S(1)} %get-tuple-element.28), channel_id=1, source_target_pairs={{0,224},{32,0},{64,32},{96,64},{128,96},{160,128},{192,160},{224,1... | collective-permute-start | bytes 1032200 | tf_op jit(solution)/shard_map/ppermute | solution.py:291
  76.1 14.4 %collective-permute-start.16 = (bf16[112,1536]{1,0:T(8,128)(2,1)S(1)}, bf16[112,1536]{1,0:T(8,128)(2,1)S(1)}, u32[]{:S(2)}, u32[]{:S(2)}) collective-permute-start(bf16[112,1536]{1,0:T(8,128)(2,1)S(1)} %get-tuple-element.29), channel_id=1, source_target_pairs={{0,32},{32,64},{64,96},{96,128},{128,160},{160,192},{192,224},{224... | collective-permute-start | bytes 1032200 | tf_op jit(solution)/shard_map/ppermute | solution.py:291
  94.6 0.8 copy-start.5
  95.4 50.7 %all-to-all-start.1 = ((bf16[8,8,224,128]{3,2,1,0:T(8,128)(2,1)}), bf16[8,8,224,128]{3,2,1,0:T(8,128)(2,1)}, u32[]{:S(2)}, u32[]{:S(2)}) async-start(bf16[8,8,224,128]{3,2,1,0:T(8,128)(2,1)} %joined.3), calls=%async_computation.1 | async-start | bytes 7340032 | tf_op jit(solution)/shard_map/all_to_all | solution.py:343
  103.9 12.9 %collective-permute-start.6 = (bf16[160,1536]{1,0:T(8,128)(2,1)S(1)}, bf16[160,1536]{1,0:T(8,128)(2,1)S(1)}, u32[]{:S(2)}, u32[]{:S(2)}) collective-permute-start(bf16[160,1536]{1,0:T(8,128)(2,1)S(1)} %collective-permute-done.5.refs_0_.refs_1_), channel_id=1, source_target_pairs={{0,224},{32,0},{64,32},{96,64},{128,96},{160,128},{192,160},{224,1... | collective-permute-start | bytes 1474568 | tf_op jit(solution)/shard_map/ppermute | solution.py:291
  106.5 12.4 %collective-permute-start.9 = (bf16[160,1536]{1,0:T(8,128)(2,1)}, bf16[160,1536]{1,0:T(8,128)(2,1)S(1)}, u32[]{:S(2)}, u32[]{:S(2)}) collective-permute-start(bf16[160,1536]{1,0:T(8,128)(2,1)} %copy-done.5), channel_id=1, source_target_pairs={{0,32},{32,64},{64,96},{96,128},{128,160},{160,192},{192,224},{224... | collective-permute-start | bytes 1474568 | tf_op jit(solution)/shard_map/ppermute | solution.py:291
  106.5 1.1 copy-start.6
  111.4 16.0 %copy-start.2 = (bf16[160,1536]{1,0:T(8,128)(2,1)S(1)}, bf16[160,1536]{1,0:T(8,128)(2,1)}, u32[]{:S(2)}) copy-start(bf16[160,1536]{1,0:T(8,128)(2,1)} %joined.2.refs_0_) | copy-start | bytes 1474564
  120.2 7.0 %collective-permute-start.10 = (bf16[80,1536]{1,0:T(8,128)(2,1)S(1)}, bf16[80,1536]{1,0:T(8,128)(2,1)S(1)}, u32[]{:S(2)}, u32[]{:S(2)}) collective-permute-start(bf16[80,1536]{1,0:T(8,128)(2,1)S(1)} %get-tuple-element.21), channel_id=1, source_target_pairs={{0,224},{32,0},{64,32},{96,64},{128,96},{160,128},{192,160},{224,1... | collective-permute-start | bytes 737288 | tf_op jit(solution)/shard_map/ppermute | solution.py:291
  121.6 5.9 %collective-permute-start.11 = (bf16[80,1536]{1,0:T(8,128)(2,1)S(1)}, bf16[80,1536]{1,0:T(8,128)(2,1)S(1)}, u32[]{:S(2)}, u32[]{:S(2)}) collective-permute-start(bf16[80,1536]{1,0:T(8,128)(2,1)S(1)} %get-tuple-element.22), channel_id=1, source_target_pairs={{0,32},{32,64},{64,96},{96,128},{128,160},{160,192},{192,224},{224... | collective-permute-start | bytes 737288 | tf_op jit(solution)/shard_map/ppermute | solution.py:291
  127.4 25.0 %copy-start.7 = (s32[1,2,1536]{2,1,0:T(2,128)S(1)}, s32[1,2,1536]{2,1,0:T(2,128)}, u32[]{:S(2)}) copy-start(s32[1,2,1536]{2,1,0:T(2,128)} %param.13) | copy-start | bytes 36868
  146.1 37.2 %all-to-all-start = ((bf16[8,8,160,128]{3,2,1,0:T(8,128)(2,1)}), bf16[8,8,160,128]{3,2,1,0:T(8,128)(2,1)}, u32[]{:S(2)}, u32[]{:S(2)}) async-start(bf16[8,8,160,128]{3,2,1,0:T(8,128)(2,1)} %get-tuple-element.25), calls=%async_computation | async-start | bytes 5242880 | tf_op jit(solution)/shard_map/all_to_all | solution.py:343
  164.4 31.9 %copy-start.9 = (f32[2048]{0:T(1024)S(1)}, f32[2048]{0:T(1024)}, u32[]{:S(2)}) copy-start(f32[2048]{0:T(1024)} %param.14) | copy-start | bytes 24580
  164.4 36.5 %copy-start.8 = (f32[384]{0:T(512)S(1)}, f32[384]{0:T(512)}, u32[]{:S(2)}) copy-start(f32[384]{0:T(512)} %param.15) | copy-start | bytes 4612
  164.4 36.6 %copy-start.3 = (f32[224,1536]{1,0:T(8,128)S(1)}, f32[224,1536]{1,0:T(8,128)}, u32[]{:S(2)}) copy-start(f32[224,1536]{1,0:T(8,128)} %get-tuple-element.33.refs_1_) | copy-start | bytes 4128772
  164.4 36.6 %collective-permute-start.17 = (bf16[224,1536]{1,0:T(8,128)(2,1)}, bf16[224,1536]{1,0:T(8,128)(2,1)}, u32[]{:S(2)}, u32[]{:S(2)}) collective-permute-start(bf16[224,1536]{1,0:T(8,128)(2,1)} %get-tuple-element.34), channel_id=1, source_target_pairs={{0,128},{32,160},{64,192},{96,224},{128,0},{160,32},{192,64},{224,... | collective-permute-start | bytes 2064392 | tf_op jit(solution)/shard_map/ppermute | solution.py:291
  194.2 28.7 %collective-permute-start.12 = (bf16[160,1536]{1,0:T(8,128)(2,1)}, bf16[160,1536]{1,0:T(8,128)(2,1)}, u32[]{:S(2)}, u32[]{:S(2)}) collective-permute-start(bf16[160,1536]{1,0:T(8,128)(2,1)} %get-tuple-element.27), channel_id=1, source_target_pairs={{0,128},{32,160},{64,192},{96,224},{128,0},{160,32},{192,64},{224,... | collective-permute-start | bytes 1474568 | tf_op jit(solution)/shard_map/ppermute | solution.py:291
  201.0 21.9 %copy-start.4 = (f32[160,1536]{1,0:T(8,128)S(1)}, f32[160,1536]{1,0:T(8,128)}, u32[]{:S(2)}) copy-start(f32[160,1536]{1,0:T(8,128)} %get-tuple-element.26.refs_1_) | copy-start | bytes 2949124
Sparse Core Ops, SparseCore 0:
  9.2 122.6 all-gather.3

commit v4 on v3

--- a/solution.py
+++ b/solution.py
@@ -171,71 +171,72 @@
     )(first, second, after)
 
 
-def ladder_body(facts, send_map, blocks, received, ladder, sent, operand, rounded, sem):
-    step = pl.program_id(0)
-    slots = operand.shape[1] // 128
+def ladder_body(facts, send_map, blocks, received, ladder, sent, operand, rounded, held, sem, held_sem):
     length = rounded.shape[1]
-
-    @pl.when(step == 0)
-    def _():
-        def place(k):
-            return operand.at[:, pl.ds(k * 128, 128)]
-
-        def copy(k):
-            tile = facts[1 + k]
-            z, ket = tile >> 3, tile & 7
-            slot = 2 * ((z - facts[0] + 8) & 3) + (z >> 2)
-            return pltpu.make_async_copy(received.at[ket, slot], place(k), sem.at[k])
-
-        for k in range(slots):
-            copy(k).start()
-        for k in range(slots):
-            copy(k).wait()
-
-    total = jnp.dot(operand[...], blocks[...], preferred_element_type=jnp.float32)
-    ladder[...] = total
-    rounded[:, pl.ds(pl.multiple_of(step * COLS, COLS), COLS)] = total.astype(jnp.bfloat16)
-
-    @pl.when(step == pl.num_programs(0) - 1)
-    def _():
-        def column(c, carry):
-            start = pl.multiple_of(c * COLS, COLS)
-            picks = one_hot(send_map[:, pl.ds(start, COLS)], length, COLS)
-            moved = jnp.dot(rounded[...], picks, preferred_element_type=jnp.float32)
-            sent[:, pl.ds(start, COLS)] = moved.astype(jnp.bfloat16)
-            return carry
-
-        lax.fori_loop(0, length // COLS, column, 0, unroll=True)
+    parts = held_sem.shape[0]
+    depth = held.shape[0] // parts
+
+    def place(k):
+        tile = facts[1 + k]
+        z, ket = tile >> 3, tile & 7
+        slot = 2 * ((z - facts[0] + 8) & 3) + (z >> 2)
+        where = operand.at[:, pl.ds(k * 128, 128)]
+        return pltpu.make_async_copy(received.at[ket, slot], where, sem.at[k])
+
+    def bring(i):
+        rows = pl.ds(i * depth, depth)
+        return pltpu.make_async_copy(blocks.at[rows], held.at[rows], held_sem.at[i])
+
+    each = depth // 128
+    for i in range(parts):
+        for k in range(i * each, (i + 1) * each):
+            place(k).start()
+        bring(i).start()
+    for i in range(parts):
+        for k in range(i * each, (i + 1) * each):
+            place(k).wait()
+        bring(i).wait()
+        rows = slice(i * depth, (i + 1) * depth)
+        for low in range(0, length, COLS):
+            columns = slice(low, low + COLS)
+            total = jnp.dot(operand[:, rows], held[rows, columns], preferred_element_type=jnp.float32)
+            if i:
+                total += ladder[:, columns]
+            ladder[:, columns] = total
+            if i == parts - 1:
+                rounded[:, columns] = total.astype(jnp.bfloat16)
+    for low in range(0, length, COLS):
+        columns = slice(low, low + COLS)
+        picks = one_hot(send_map[:, columns], length, COLS)
+        moved = jnp.dot(rounded[...], picks, preferred_element_type=jnp.float32)
+        sent[:, columns] = moved.astype(jnp.bfloat16)
 
 
 def ladder_of(facts, send_map, blocks, received):
     depth, length = blocks.shape
     rows = received.shape[2]
+    vmem = pl.BlockSpec(memory_space=pltpu.VMEM)
     return pl.pallas_call(
         ladder_body,
-        grid=(length // COLS,),
         in_specs=[
             pl.BlockSpec(memory_space=pltpu.SMEM),
-            pl.BlockSpec((1, length), lambda n: (0, 0)),
-            pl.BlockSpec((depth, COLS), lambda n: (0, n)),
+            vmem,
             pl.BlockSpec(memory_space=pl.ANY),
-        ],
-        out_specs=[
-            pl.BlockSpec((rows, COLS), lambda n: (0, n)),
-            pl.BlockSpec((rows, length), lambda n: (0, 0)),
-        ],
+            pl.BlockSpec(memory_space=pl.ANY),
+        ],
+        out_specs=[vmem, vmem],
         out_shape=[
-            pltpu.HBM((rows, length), jnp.float32),
+            jax.ShapeDtypeStruct((rows, length), jnp.float32),
             jax.ShapeDtypeStruct((rows, length), jnp.bfloat16),
         ],
         scratch_shapes=[
             pltpu.VMEM((rows, depth), jnp.bfloat16),
             pltpu.VMEM((rows, length), jnp.bfloat16),
+            pltpu.VMEM((depth, length), jnp.bfloat16),
             pltpu.SemaphoreType.DMA((depth // 128,)),
-        ],
-        compiler_params=pltpu.CompilerParams(
-            vmem_limit_bytes=VMEM, dimension_semantics=("arbitrary",)
-        ),
+            pltpu.SemaphoreType.DMA((4,)),
+        ],
+        compiler_params=pltpu.CompilerParams(vmem_limit_bytes=VMEM),
         cost_estimate=pl.CostEstimate(
             flops=2 * rows * depth * length,
             bytes_accessed=2 * depth * (rows + length),
@@ -254,7 +255,7 @@
 
 def update(low, own, ladder, partner, direction, occupied, virtual, before):
     rows, length = ladder.shape
-    step = 32
+    step = 64
 
     def chunk(width):
         return pl.BlockSpec((step, width), lambda n: (n, 0))
@@ -319,7 +320,7 @@
     first = energies(vir_energy, pair_virt[0, 0])
     second = energies(vir_energy, pair_virt[0, 1])
     virtual = jnp.stack([first, second])
-    ends = (0, 224, rows)
+    ends = (0, 192, rows)
     steps, folds = [], []
     for low, high in zip(ends, ends[1:]):
         part = own[low:high]
@@ -333,13 +334,13 @@
         far = (shifted(upper, -1), shifted(lower, 1))
         odd = (one[0], three[1], three[0], one[1])
         slots, _ = fold((1, 3), fold_facts, maps, odd, (slots,))
-        steps.append((part, one, two, far))
+        steps.append((part, one, three, far))
         folds.append(slots)
     fresh = ()
-    for i, (part, one, two, far) in enumerate(steps):
+    for i, (part, one, three, far) in enumerate(steps):
         slots, _ = fold((0,), fold_facts, maps, (part, *far), (folds[i],))
         if i + 1 < len(steps):
-            slots = joined(slots, steps[i + 1][2], pltpu.HBM)
+            slots = joined(slots, steps[i + 1][1], pltpu.HBM)
         received = lax.all_to_all(slots, "ket", split_axis=0, concat_axis=0, tiled=True)
         ladder, sent = ladder_of(ladder_facts, send_map, all_blocks, received)
         partner = shifted(sent, 4)

time: 237 us -> 233 us (0.983)
  the two profiles are of different devices: /device:TPU:47 before, /device:TPU:1 now
where the time goes in v4:
time: 233 us
  waiting for transfers between devices  98.4 us (42%)
  Pallas kernels  47.7 us (20%)
  starting transfers between devices  42.3 us (18%)
  between operations  13.8 us (6%)
  blocking collectives  13.2 us (6%)
  local copies, waits for them, and re-layouts  12.4 us (5%)
  other arithmetic  5.01 us (2%)
    ppermute x18, waiting for transfers between devices, shifted(): return lax.ppermute(block, 'bra', [(i, (i + by) % 8) for i in range(8)])  72.7 us
    ppermute x18, starting transfers between devices, shifted(): return lax.ppermute(block, 'bra', [(i, (i + by) % 8) for i in range(8)])  30.3 us
    pallas_call x6, Pallas kernels, fold(): pl.pallas_call(functools.partial(fold_body, shifts), in_specs=[pl.BlockSp...  25.1 us
    all_to_all x2, waiting for transfers between devices, local(): lax.all_to_all(slots, 'ket', split_axis=0, concat_axis=0, tiled=True)  25 us
    pallas_call x2, Pallas kernels, ladder_of(): pl.pallas_call(ladder_body, in_specs=[pl.BlockSpec(memory_space=pltpu.SME...  17.2 us
    all_gather x1, blocking collectives, local(): wanted = lax.all_gather(block_owner[0] * 16 + screen_list[0], 'ket', axis=0)  13.2 us
    all_to_all x2, starting transfers between devices, local(): lax.all_to_all(slots, 'ket', split_axis=0, concat_axis=0, tiled=True)  12 us
    unnamed x52, local copies, waits for them, and re-layouts  9.22 us
  transfers between devices with their start and end apart: 21, of which 9 were waited for; matrix products, arithmetic and copies ran while one was open for 4% of the time, Pallas kernels for 20%

profile of v4, /device:TPU:1, one launch (start us, length us, event | category | flops | bytes accessed | tf_op | source)
XLA Modules:
  0.0 232.8 jit_solution(15142778398443120092)
XLA Ops:
  6.6 0.7 all-gather.4.cloned.1.call-update
  7.3 0.6 copy-done.1
  7.9 0.9 slice_bitcast_fusion
  8.8 6.4 %collective-permute-start = (bf16[192,1536]{1,0:T(8,128)(2,1)S(1)}, bf16[192,1536]{1,0:T(8,128)(2,1)S(1)}, u32[]{:S(2)}, u32[]{:S(2)}) collective-permute-start(bf16[192,1536]{1,0:T(8,128)(2,1)S(1)} %get-tuple-element.39.refs_0_), channel_id=1, source_target_pairs={{0,224},{32,0},{64,32},{96,64},{128,96},{160,128},{192,160},{224,1... | collective-permute-start | bytes 1769480 | tf_op jit(solution)/shard_map/ppermute | solution.py:292
  15.2 12.0 %collective-permute-done.refs_0_ = bf16[192,1536]{1,0:T(8,128)(2,1)S(1)} collective-permute-done((bf16[192,1536]{1,0:T(8,128)(2,1)S(1)}, bf16[192,1536]{1,0:T(8,128)(2,1)S(1)}, u32[]{:S(2)}, u32[]{:S(2)}) %collective-permute-start) | collective-permute-done | bytes 589856 | tf_op jit(solution)/shard_map/ppermute | solution.py:292
  27.2 3.4 %collective-permute-start.1 = (bf16[192,1536]{1,0:T(8,128)(2,1)S(1)}, bf16[192,1536]{1,0:T(8,128)(2,1)S(1)}, u32[]{:S(2)}, u32[]{:S(2)}) collective-permute-start(bf16[192,1536]{1,0:T(8,128)(2,1)S(1)} %collective-permute-done.refs_0_), channel_id=1, source_target_pairs={{0,224},{32,0},{64,32},{96,64},{128,96},{160,128},{192,160},{224,1... | collective-permute-start | bytes 1769480 | tf_op jit(solution)/shard_map/ppermute | solution.py:292
  30.6 0.8 copy-done.13
  31.4 0.8 copy-done.15
  32.2 9.4 %collective-permute-done.1.refs_0_ = bf16[192,1536]{1,0:T(8,128)(2,1)S(1)} collective-permute-done((bf16[192,1536]{1,0:T(8,128)(2,1)S(1)}, bf16[192,1536]{1,0:T(8,128)(2,1)S(1)}, u32[]{:S(2)}, u32[]{:S(2)}) %collective-permute-start.1) | collective-permute-done | bytes 589856 | tf_op jit(solution)/shard_map/ppermute | solution.py:292
  41.6 3.5 %collective-permute-start.2 = (bf16[192,1536]{1,0:T(8,128)(2,1)S(1)}, bf16[192,1536]{1,0:T(8,128)(2,1)S(1)}, u32[]{:S(2)}, u32[]{:S(2)}) collective-permute-start(bf16[192,1536]{1,0:T(8,128)(2,1)S(1)} %collective-permute-done.1.refs_0_), channel_id=1, source_target_pairs={{0,224},{32,0},{64,32},{96,64},{128,96},{160,128},{192,160},{224,1... | collective-permute-start | bytes 1769480 | tf_op jit(solution)/shard_map/ppermute | solution.py:292
  45.2 0.8 copy-done.17
  46.0 13.2 %all-gather.1 = s32[8,1,32]{2,1,0:T(1,128)S(1)} all-gather(s32[1,1,32]{2,1,0:T(1,128)S(1)} %add_bitcast_fusion), channel_id=1, replica_groups=mesh['bra'=8,'ket'=8,'pair'=4] {'ket'}, dimensions={0}, use_global_device_ids=true | all-gather | bytes 1152 | tf_op jit(solution)/shard_map/all_gather | solution.py:308
  59.6 3.0 %collective-permute-start.6 = (bf16[192,1536]{1,0:T(8,128)(2,1)}, bf16[192,1536]{1,0:T(8,128)(2,1)S(1)}, u32[]{:S(2)}, u32[]{:S(2)}) collective-permute-start(bf16[192,1536]{1,0:T(8,128)(2,1)} %joined.2.refs_0_), channel_id=1, source_target_pairs={{0,224},{32,0},{64,32},{96,64},{128,96},{160,128},{192,160},{224,1... | collective-permute-start | bytes 1769480 | tf_op jit(solution)/shard_map/ppermute | solution.py:292
  62.9 2.7 %collective-permute-start.15 = (bf16[96,1536]{1,0:T(8,128)(2,1)S(1)}, bf16[96,1536]{1,0:T(8,128)(2,1)S(1)}, u32[]{:S(2)}, u32[]{:S(2)}) collective-permute-start(bf16[96,1536]{1,0:T(8,128)(2,1)S(1)} %get-tuple-element.28), channel_id=1, source_target_pairs={{0,224},{32,0},{64,32},{96,64},{128,96},{160,128},{192,160},{224,1... | collective-permute-start | bytes 884744 | tf_op jit(solution)/shard_map/ppermute | solution.py:292
  65.7 1.1 copy-done.18
  66.7 1.1 copy-done.20
  67.8 3.5 %fold.9 = (bf16[8,8,192,128]{3,2,1,0:T(8,128)(2,1)}, s32[1]{0:T(128)}) custom-call(s32[65]{0:T(128)S(1)} %pad_add_fusion.1.facts._, s32[4,1,1536]{2,1,0:T(1,128)S(1)} %dynamic-slice_bitcast_fusion.maps, bf16[192,1536]{1,0:T(8,128)(2,1)S(1)} %copy-done.18, bf16[192,1536]{1,0:T(8,128)(2,1)S(1)} %copy-done.20), custom_call_target="tpu_custom_call" | custom-call | flops 905969664 | bytes 1966080 | tf_op jit(solution)/shard_map/fold/pallas_call | solution.py:102
  71.3 5.4 %fold.10 = (bf16[8,8,192,128]{3,2,1,0:T(8,128)(2,1)}, s32[1]{0:T(128)}) custom-call(s32[65]{0:T(128)S(1)} %pad_add_fusion.1.facts._, s32[4,1,1536]{2,1,0:T(1,128)S(1)} %dynamic-slice_bitcast_fusion.maps, bf16[192,1536]{1,0:T(8,128)(2,1)S(1)} %copy-done.14, ...), custom_call_target="tpu_custom_call", output_to_operand_aliasing={{0}: (6, {})} | custom-call | flops 1811939328 | bytes 3932160 | tf_op jit(solution)/shard_map/fold/pallas_call | solution.py:102
  76.7 5.0 %collective-permute-done.15.refs_1_ = bf16[96,1536]{1,0:T(8,128)(2,1)S(1)} collective-permute-done((bf16[96,1536]{1,0:T(8,128)(2,1)S(1)}, bf16[96,1536]{1,0:T(8,128)(2,1)S(1)}, u32[]{:S(2)}, u32[]{:S(2)}) %collective-permute-start.15) | collective-permute-done | bytes 294944 | tf_op jit(solution)/shard_map/ppermute | solution.py:292
  81.7 3.2 %collective-permute-done.16.refs_2_ = bf16[96,1536]{1,0:T(8,128)(2,1)S(1)} collective-permute-done((bf16[96,1536]{1,0:T(8,128)(2,1)S(1)}, bf16[96,1536]{1,0:T(8,128)(2,1)S(1)}, u32[]{:S(2)}, u32[]{:S(2)}) %collective-permute-start.16) | collective-permute-done | bytes 294944 | tf_op jit(solution)/shard_map/ppermute | solution.py:292
  84.9 3.6 %fold.11 = (bf16[8,8,192,128]{3,2,1,0:T(8,128)(2,1)}, s32[1]{0:T(128)}) custom-call(s32[65]{0:T(128)S(1)} %pad_add_fusion.1.facts._, s32[4,1,1536]{2,1,0:T(1,128)S(1)} %dynamic-slice_bitcast_fusion.maps, bf16[192,1536]{1,0:T(8,128)(2,1)S(1)} %get-tuple-element.39.refs_0_, ...), custom_call_target="tpu_custom_call", output_to_operand_aliasing={{0}: (5, {})} | custom-call | flops 905969664 | bytes 1966080 | tf_op jit(solution)/shard_map/fold/pallas_call | solution.py:102
  88.6 0.8 copy-done.6
  89.5 4.6 %all-to-all-start.1 = ((bf16[8,8,192,128]{3,2,1,0:T(8,128)(2,1)}), bf16[8,8,192,128]{3,2,1,0:T(8,128)(2,1)S(1)}, u32[]{:S(2)}, u32[]{:S(2)}) async-start(bf16[8,8,192,128]{3,2,1,0:T(8,128)(2,1)} %joined.3), calls=%async_computation.1 | async-start | bytes 6291456 | tf_op jit(solution)/shard_map/all_to_all | solution.py:344
  94.2 2.7 %collective-permute-start.7 = (bf16[192,1536]{1,0:T(8,128)(2,1)}, bf16[192,1536]{1,0:T(8,128)(2,1)S(1)}, u32[]{:S(2)}, u32[]{:S(2)}) collective-permute-start(bf16[192,1536]{1,0:T(8,128)(2,1)} %copy-done.6), channel_id=1, source_target_pairs={{0,224},{32,0},{64,32},{96,64},{128,96},{160,128},{192,160},{224,1... | collective-permute-start | bytes 1769480 | tf_op jit(solution)/shard_map/ppermute | solution.py:292
  96.8 13.6 %collective-permute-done.10.refs_1_ = bf16[192,1536]{1,0:T(8,128)(2,1)S(1)} collective-permute-done((bf16[192,1536]{1,0:T(8,128)(2,1)}, bf16[192,1536]{1,0:T(8,128)(2,1)S(1)}, u32[]{:S(2)}, u32[]{:S(2)}) %collective-permute-start.10) | collective-permute-done | bytes 589856 | tf_op jit(solution)/shard_map/ppermute | solution.py:292
  110.4 2.7 %collective-permute-start.8 = (bf16[192,1536]{1,0:T(8,128)(2,1)S(1)}, bf16[192,1536]{1,0:T(8,128)(2,1)S(1)}, u32[]{:S(2)}, u32[]{:S(2)}) collective-permute-start(bf16[192,1536]{1,0:T(8,128)(2,1)S(1)} %collective-permute-done.7.refs_0_), channel_id=1, source_target_pairs={{0,224},{32,0},{64,32},{96,64},{128,96},{160,128},{192,160},{224,1... | collective-permute-start | bytes 1769480 | tf_op jit(solution)/shard_map/ppermute | solution.py:292
  113.1 0.7 copy-done.11
  113.8 3.5 %fold.6 = (bf16[8,8,192,128]{3,2,1,0:T(8,128)(2,1)}, s32[1]{0:T(128)}) custom-call(s32[65]{0:T(128)S(1)} %pad_add_fusion.1.facts._, s32[4,1,1536]{2,1,0:T(1,128)S(1)} %copy-done.11, bf16[192,1536]{1,0:T(8,128)(2,1)S(1)} %collective-permute-done.7.refs_0_, bf16[192,1536]{1,0:T(8,128)(2,1)S(1)} %collective-permute-done.10.refs_1_), custom_call_target="tpu_custom_call" | custom-call | flops 905969664 | bytes 1966080 | tf_op jit(solution)/shard_map/fold/pallas_call | solution.py:102
  117.4 8.3 %collective-permute-done.11.second.refs_1_ = bf16[192,1536]{1,0:T(8,128)(2,1)S(1)} collective-permute-done((bf16[192,1536]{1,0:T(8,128)(2,1)S(1)}, bf16[192,1536]{1,0:T(8,128)(2,1)S(1)}, u32[]{:S(2)}, u32[]{:S(2)}) %collective-permute-start.11) | collective-permute-done | bytes 589856 | tf_op jit(solution)/shard_map/ppermute | solution.py:292
  125.7 0.7 halves.2
  126.4 2.5 %collective-permute-start.12 = (bf16[96,1536]{1,0:T(8,128)(2,1)S(1)}, bf16[96,1536]{1,0:T(8,128)(2,1)S(1)}, u32[]{:S(2)}, u32[]{:S(2)}) collective-permute-start(bf16[96,1536]{1,0:T(8,128)(2,1)S(1)} %get-tuple-element.21), channel_id=1, source_target_pairs={{0,224},{32,0},{64,32},{96,64},{128,96},{160,128},{192,160},{224,1... | collective-permute-start | bytes 884744 | tf_op jit(solution)/shard_map/ppermute | solution.py:292
  128.9 5.4 %fold.7 = (bf16[8,8,192,128]{3,2,1,0:T(8,128)(2,1)}, s32[1]{0:T(128)}) custom-call(s32[65]{0:T(128)S(1)} %pad_add_fusion.1.facts._, s32[4,1,1536]{2,1,0:T(1,128)S(1)} %copy-done.12, bf16[192,1536]{1,0:T(8,128)(2,1)S(1)} %copy-done.7, bf16[192,1536]{1,0:T(8,128)(2,1)S(1)} %collective-permute-done.11.second.refs_1_, ...), custom_call_target="tpu_custom_call", output_to_operand_aliasing={{0}: (6, {})} | custom-call | flops 1811939328 | bytes 3932160 | tf_op jit(solution)/shard_map/fold/pallas_call | solution.py:102
  134.3 2.0 collective-permute-done.13.refs_2_
  136.3 3.7 %fold.8 = (bf16[8,8,192,128]{3,2,1,0:T(8,128)(2,1)}, s32[1]{0:T(128)}) custom-call(s32[65]{0:T(128)S(1)} %pad_add_fusion.1.facts._, s32[4,1,1536]{2,1,0:T(1,128)S(1)} %copy-done.12, bf16[192,1536]{1,0:T(8,128)(2,1)S(1)} %copy-done.3, bf16[96,1536]{1,0:T(8,128)(2,1)S(1)} %collective-permute-done.12.refs_1_, ...), custom_call_target="tpu_custom_call", output_to_operand_aliasing={{0}: (5, {})} | custom-call | flops 905969664 | bytes 1966080 | tf_op jit(solution)/shard_map/fold/pallas_call | solution.py:102
  140.0 7.4 %all-to-all-start = ((bf16[8,8,192,128]{3,2,1,0:T(8,128)(2,1)}), bf16[8,8,192,128]{3,2,1,0:T(8,128)(2,1)}, u32[]{:S(2)}, u32[]{:S(2)}) async-start(bf16[8,8,192,128]{3,2,1,0:T(8,128)(2,1)} %get-tuple-element.25), calls=%async_computation | async-start | bytes 6291456 | tf_op jit(solution)/shard_map/all_to_all | solution.py:344
  147.4 1.4 slice_reduce_fusion.1
  148.9 8.4 %ladder.3 = (f32[192,1536]{1,0:T(8,128)S(1)}, bf16[192,1536]{1,0:T(8,128)(2,1)}) custom-call(s32[33]{0:T(128)S(1)} %pad_add_fusion.facts, s32[1,1536]{1,0:T(1,128)S(1)} %constant_dynamic-slice_fusion.send_map, bf16[4096,1536]{1,0:T(8,128)(2,1)} %bitcast.21, bf16[8,8,192,128]{3,2,1,0:T(8,128)(2,1)S(1)} %all-to-all-done.1.received), custom_call_target="tpu_custom_call" | custom-call | flops 2415919104 | bytes 14155776 | tf_op jit(solution)/shard_map/ladder/pallas_call | solution.py:219
  157.3 1.0 copy-done.4
  158.3 1.7 collective-permute-start.17
  160.0 25.0 %all-to-all-done.received = bf16[8,8,192,128]{3,2,1,0:T(8,128)(2,1)} async-done(((bf16[8,8,192,128]{3,2,1,0:T(8,128)(2,1)}), bf16[8,8,192,128]{3,2,1,0:T(8,128)(2,1)}, u32[]{:S(2)}, u32[]{:S(2)}) %all-to-all-start) | async-done | bytes 3145760 | tf_op jit(solution)/shard_map/all_to_all | solution.py:344
  185.1 8.8 %ladder.2 = (f32[192,1536]{1,0:T(8,128)S(1)}, bf16[192,1536]{1,0:T(8,128)(2,1)}) custom-call(s32[33]{0:T(128)S(1)} %pad_add_fusion.facts, s32[1,1536]{1,0:T(1,128)S(1)} %constant_dynamic-slice_fusion.send_map, bf16[4096,1536]{1,0:T(8,128)(2,1)} %bitcast.22, bf16[8,8,192,128]{3,2,1,0:T(8,128)(2,1)} %all-to-all-done.received), custom_call_target="tpu_custom_call" | custom-call | flops 2415919104 | bytes 14155776 | tf_op jit(solution)/shard_map/ladder/pallas_call | solution.py:219
  193.8 1.7 collective-permute-start.14
  195.5 4.6 %select_reduce_fusion.1 = (f32[1536]{0:T(1024)S(1)}, f32[1536]{0:T(1024)S(1)}) fusion(f32[2048]{0:T(1024)S(1)} %copy-done.23, s32[1536]{0:T(1024)S(1)} %copy-done.21, s32[1536]{0:T(1024)S(1)} %copy-done.22), kind=kLoop, calls=%fused_computation.2 | loop fusion | flops 18871296 | bytes 32768 | tf_op jit(solution)/shard_map/reduce_sum | solution.py:297
  200.1 0.8 broadcast_in_dim.56.refs_4_
  201.0 1.3 copy-done.5
  202.2 2.9 %update.2.refs_6_ = bf16[384,1536]{1,0:T(8,128)(2,1)} custom-call(bf16[384,1536]{1,0:T(8,128)(2,1)S(1)} %bitcast.19, f32[192,1536]{1,0:T(8,128)S(1)} %copy-done.5, bf16[192,1536]{1,0:T(8,128)(2,1)} %collective-permute-done.17.refs_2_, f32[1]{0:T(128)} %bitcast.12.refs_3_, f32[384,1]{1,0:T(8,128)S(1)} %broadcast_in_dim.56.refs_4_, ...), custom_call_target="tpu_custom_call" | custom-call | flops 2359296 | bytes 2949120 | tf_op jit(solution)/shard_map/update/pallas_call | solution.py:266
  205.2 19.1 %collective-permute-done.14.refs_2_ = bf16[192,1536]{1,0:T(8,128)(2,1)S(1)} collective-permute-done((bf16[192,1536]{1,0:T(8,128)(2,1)}, bf16[192,1536]{1,0:T(8,128)(2,1)S(1)}, u32[]{:S(2)}, u32[]{:S(2)}) %collective-permute-start.14) | collective-permute-done | bytes 589856 | tf_op jit(solution)/shard_map/ppermute | solution.py:292
  224.3 1.7 update.3
  (78 shorter events, 1.1 us)
Async XLA Ops:
  6.5 59.1 %copy-start = (s32[64,1536]{1,0:T(8,128)S(1)}, s32[64,1536]{1,0:T(8,128)}, u32[]{:S(2)}) copy-start(s32[64,1536]{1,0:T(8,128)} %param.12) | copy-start | bytes 1179652
  6.5 1.3 copy-start.1
  6.5 39.5 %copy-start.24 = (s32[1,32]{1,0:T(1,128)S(1)}, s32[1,32]{1,0:T(1,128)}, u32[]{:S(2)}) copy-start(s32[1,32]{1,0:T(1,128)} %param.10) | copy-start | bytes 388
  6.5 39.5 %copy-start.25 = (s32[1,32]{1,0:T(1,128)S(1)}, s32[1,32]{1,0:T(1,128)}, u32[]{:S(2)}) copy-start(s32[1,32]{1,0:T(1,128)} %param.11) | copy-start | bytes 388
  6.5 142.3 %all-gather.4.cloned.1.call-start = ((), (), s32[]{:S(2)}) async-start(), calls=%async_computation.2 | async-start | bytes 15728640 | tf_op jit(solution)/shard_map/all_gather | solution.py:306
  8.8 18.4 %collective-permute-start = (bf16[192,1536]{1,0:T(8,128)(2,1)S(1)}, bf16[192,1536]{1,0:T(8,128)(2,1)S(1)}, u32[]{:S(2)}, u32[]{:S(2)}) collective-permute-start(bf16[192,1536]{1,0:T(8,128)(2,1)S(1)} %get-tuple-element.39.refs_0_), channel_id=1, source_target_pairs={{0,224},{32,0},{64,32},{96,64},{128,96},{160,128},{192,160},{224,1... | collective-permute-start | bytes 1769480 | tf_op jit(solution)/shard_map/ppermute | solution.py:292
  15.2 16.2 %collective-permute-start.3 = (bf16[192,1536]{1,0:T(8,128)(2,1)S(1)}, bf16[192,1536]{1,0:T(8,128)(2,1)S(1)}, u32[]{:S(2)}, u32[]{:S(2)}) collective-permute-start(bf16[192,1536]{1,0:T(8,128)(2,1)S(1)} %get-tuple-element.39.refs_0_), channel_id=1, source_target_pairs={{0,32},{32,64},{64,96},{96,128},{128,160},{160,192},{192,224},{224... | collective-permute-start | bytes 1769480 | tf_op jit(solution)/shard_map/ppermute | solution.py:292
  27.2 14.5 %collective-permute-start.1 = (bf16[192,1536]{1,0:T(8,128)(2,1)S(1)}, bf16[192,1536]{1,0:T(8,128)(2,1)S(1)}, u32[]{:S(2)}, u32[]{:S(2)}) collective-permute-start(bf16[192,1536]{1,0:T(8,128)(2,1)S(1)} %collective-permute-done.refs_0_), channel_id=1, source_target_pairs={{0,224},{32,0},{64,32},{96,64},{128,96},{160,128},{192,160},{224,1... | collective-permute-start | bytes 1769480 | tf_op jit(solution)/shard_map/ppermute | solution.py:292
  30.6 0.8 copy-start.13
  31.4 14.6 %collective-permute-start.4 = (bf16[192,1536]{1,0:T(8,128)(2,1)S(1)}, bf16[192,1536]{1,0:T(8,128)(2,1)S(1)}, u32[]{:S(2)}, u32[]{:S(2)}) collective-permute-start(bf16[192,1536]{1,0:T(8,128)(2,1)S(1)} %collective-permute-done.3.refs_3_), channel_id=1, source_target_pairs={{0,32},{32,64},{64,96},{96,128},{128,160},{160,192},{192,224},{224... | collective-permute-start | bytes 1769480 | tf_op jit(solution)/shard_map/ppermute | solution.py:292
  31.4 0.8 copy-start.15
  41.6 18.0 %collective-permute-start.2 = (bf16[192,1536]{1,0:T(8,128)(2,1)S(1)}, bf16[192,1536]{1,0:T(8,128)(2,1)S(1)}, u32[]{:S(2)}, u32[]{:S(2)}) collective-permute-start(bf16[192,1536]{1,0:T(8,128)(2,1)S(1)} %collective-permute-done.1.refs_0_), channel_id=1, source_target_pairs={{0,224},{32,0},{64,32},{96,64},{128,96},{160,128},{192,160},{224,1... | collective-permute-start | bytes 1769480 | tf_op jit(solution)/shard_map/ppermute | solution.py:292
  45.2 0.8 copy-start.17
  46.0 13.6 %copy-start.19 = (bf16[192,1536]{1,0:T(8,128)(2,1)}, bf16[192,1536]{1,0:T(8,128)(2,1)S(1)}, u32[]{:S(2)}) copy-start(bf16[192,1536]{1,0:T(8,128)(2,1)S(1)} %collective-permute-done.4.refs_1_) | copy-start | bytes 1769476
  46.0 13.6 %collective-permute-start.5 = (bf16[192,1536]{1,0:T(8,128)(2,1)S(1)}, bf16[192,1536]{1,0:T(8,128)(2,1)S(1)}, u32[]{:S(2)}, u32[]{:S(2)}) collective-permute-start(bf16[192,1536]{1,0:T(8,128)(2,1)S(1)} %collective-permute-done.4.refs_1_), channel_id=1, source_target_pairs={{0,32},{32,64},{64,96},{96,128},{128,160},{160,192},{192,224},{224... | collective-permute-start | bytes 1769480 | tf_op jit(solution)/shard_map/ppermute | solution.py:292
  59.6 28.9 %collective-permute-start.6 = (bf16[192,1536]{1,0:T(8,128)(2,1)}, bf16[192,1536]{1,0:T(8,128)(2,1)S(1)}, u32[]{:S(2)}, u32[]{:S(2)}) collective-permute-start(bf16[192,1536]{1,0:T(8,128)(2,1)} %joined.2.refs_0_), channel_id=1, source_target_pairs={{0,224},{32,0},{64,32},{96,64},{128,96},{160,128},{192,160},{224,1... | collective-permute-start | bytes 1769480 | tf_op jit(solution)/shard_map/ppermute | solution.py:292
  62.6 25.9 %collective-permute-start.9 = (bf16[192,1536]{1,0:T(8,128)(2,1)}, bf16[192,1536]{1,0:T(8,128)(2,1)S(1)}, u32[]{:S(2)}, u32[]{:S(2)}) collective-permute-start(bf16[192,1536]{1,0:T(8,128)(2,1)} %joined.2.refs_0_), channel_id=1, source_target_pairs={{0,32},{32,64},{64,96},{96,128},{128,160},{160,192},{192,224},{224... | collective-permute-start | bytes 1769480 | tf_op jit(solution)/shard_map/ppermute | solution.py:292
  62.7 8.6 %copy-start.14 = (bf16[192,1536]{1,0:T(8,128)(2,1)S(1)}, bf16[192,1536]{1,0:T(8,128)(2,1)}, u32[]{:S(2)}) copy-start(bf16[192,1536]{1,0:T(8,128)(2,1)} %copy-done.13) | copy-start | bytes 1769476
  62.7 8.6 %copy-start.16 = (bf16[192,1536]{1,0:T(8,128)(2,1)S(1)}, bf16[192,1536]{1,0:T(8,128)(2,1)}, u32[]{:S(2)}) copy-start(bf16[192,1536]{1,0:T(8,128)(2,1)} %copy-done.15) | copy-start | bytes 1769476
  62.9 18.8 %collective-permute-start.15 = (bf16[96,1536]{1,0:T(8,128)(2,1)S(1)}, bf16[96,1536]{1,0:T(8,128)(2,1)S(1)}, u32[]{:S(2)}, u32[]{:S(2)}) collective-permute-start(bf16[96,1536]{1,0:T(8,128)(2,1)S(1)} %get-tuple-element.28), channel_id=1, source_target_pairs={{0,224},{32,0},{64,32},{96,64},{128,96},{160,128},{192,160},{224,1... | collective-permute-start | bytes 884744 | tf_op jit(solution)/shard_map/ppermute | solution.py:292
  65.6 19.3 %collective-permute-start.16 = (bf16[96,1536]{1,0:T(8,128)(2,1)S(1)}, bf16[96,1536]{1,0:T(8,128)(2,1)S(1)}, u32[]{:S(2)}, u32[]{:S(2)}) collective-permute-start(bf16[96,1536]{1,0:T(8,128)(2,1)S(1)} %get-tuple-element.29), channel_id=1, source_target_pairs={{0,32},{32,64},{64,96},{96,128},{128,160},{160,192},{192,224},{224... | collective-permute-start | bytes 884744 | tf_op jit(solution)/shard_map/ppermute | solution.py:292
  65.6 1.1 copy-start.18
  66.7 1.1 copy-start.20
  67.8 17.1 %copy-start.10 = (s32[4,1,1536]{2,1,0:T(1,128)}, s32[4,1,1536]{2,1,0:T(1,128)S(1)}, u32[]{:S(2)}) copy-start(s32[4,1,1536]{2,1,0:T(1,128)S(1)} %dynamic-slice_bitcast_fusion.maps) | copy-start | bytes 73732
  88.5 0.8 copy-start.6
  88.5 1.0 copy-start.8
  89.5 50.4 %all-to-all-start.1 = ((bf16[8,8,192,128]{3,2,1,0:T(8,128)(2,1)}), bf16[8,8,192,128]{3,2,1,0:T(8,128)(2,1)S(1)}, u32[]{:S(2)}, u32[]{:S(2)}) async-start(bf16[8,8,192,128]{3,2,1,0:T(8,128)(2,1)} %joined.3), calls=%async_computation.1 | async-start | bytes 6291456 | tf_op jit(solution)/shard_map/all_to_all | solution.py:344
  94.2 34.7 %copy-start.7 = (bf16[192,1536]{1,0:T(8,128)(2,1)S(1)}, bf16[192,1536]{1,0:T(8,128)(2,1)}, u32[]{:S(2)}) copy-start(bf16[192,1536]{1,0:T(8,128)(2,1)} %copy-done.6) | copy-start | bytes 1769476
  94.2 34.7 %copy-start.9 = (bf16[192,1536]{1,0:T(8,128)(2,1)S(1)}, bf16[192,1536]{1,0:T(8,128)(2,1)}, u32[]{:S(2)}) copy-start(bf16[192,1536]{1,0:T(8,128)(2,1)} %copy-done.8) | copy-start | bytes 1769476
  94.2 16.3 %collective-permute-start.10 = (bf16[192,1536]{1,0:T(8,128)(2,1)}, bf16[192,1536]{1,0:T(8,128)(2,1)S(1)}, u32[]{:S(2)}, u32[]{:S(2)}) collective-permute-start(bf16[192,1536]{1,0:T(8,128)(2,1)} %copy-done.8), channel_id=1, source_target_pairs={{0,32},{32,64},{64,96},{96,128},{128,160},{160,192},{192,224},{224... | collective-permute-start | bytes 1769480 | tf_op jit(solution)/shard_map/ppermute | solution.py:292
  94.2 16.3 %collective-permute-start.7 = (bf16[192,1536]{1,0:T(8,128)(2,1)}, bf16[192,1536]{1,0:T(8,128)(2,1)S(1)}, u32[]{:S(2)}, u32[]{:S(2)}) collective-permute-start(bf16[192,1536]{1,0:T(8,128)(2,1)} %copy-done.6), channel_id=1, source_target_pairs={{0,224},{32,0},{64,32},{96,64},{128,96},{160,128},{192,160},{224,1... | collective-permute-start | bytes 1769480 | tf_op jit(solution)/shard_map/ppermute | solution.py:292
  110.4 15.2 %collective-permute-start.11 = (bf16[192,1536]{1,0:T(8,128)(2,1)S(1)}, bf16[192,1536]{1,0:T(8,128)(2,1)S(1)}, u32[]{:S(2)}, u32[]{:S(2)}) collective-permute-start(bf16[192,1536]{1,0:T(8,128)(2,1)S(1)} %collective-permute-done.10.refs_1_), channel_id=1, source_target_pairs={{0,32},{32,64},{64,96},{96,128},{128,160},{160,192},{192,224},{224... | collective-permute-start | bytes 1769480 | tf_op jit(solution)/shard_map/ppermute | solution.py:292
  110.4 15.2 %collective-permute-start.8 = (bf16[192,1536]{1,0:T(8,128)(2,1)S(1)}, bf16[192,1536]{1,0:T(8,128)(2,1)S(1)}, u32[]{:S(2)}, u32[]{:S(2)}) collective-permute-start(bf16[192,1536]{1,0:T(8,128)(2,1)S(1)} %collective-permute-done.7.refs_0_), channel_id=1, source_target_pairs={{0,224},{32,0},{64,32},{96,64},{128,96},{160,128},{192,160},{224,1... | collective-permute-start | bytes 1769480 | tf_op jit(solution)/shard_map/ppermute | solution.py:292
  113.1 0.7 copy-start.11
  113.8 15.0 %copy-start.12 = (s32[4,1,1536]{2,1,0:T(1,128)S(1)}, s32[4,1,1536]{2,1,0:T(1,128)}, u32[]{:S(2)}) copy-start(s32[4,1,1536]{2,1,0:T(1,128)} %copy-done.10) | copy-start | bytes 73732
  126.4 7.9 %collective-permute-start.12 = (bf16[96,1536]{1,0:T(8,128)(2,1)S(1)}, bf16[96,1536]{1,0:T(8,128)(2,1)S(1)}, u32[]{:S(2)}, u32[]{:S(2)}) collective-permute-start(bf16[96,1536]{1,0:T(8,128)(2,1)S(1)} %get-tuple-element.21), channel_id=1, source_target_pairs={{0,224},{32,0},{64,32},{96,64},{128,96},{160,128},{192,160},{224,1... | collective-permute-start | bytes 884744 | tf_op jit(solution)/shard_map/ppermute | solution.py:292
  128.9 7.4 %collective-permute-start.13 = (bf16[96,1536]{1,0:T(8,128)(2,1)S(1)}, bf16[96,1536]{1,0:T(8,128)(2,1)S(1)}, u32[]{:S(2)}, u32[]{:S(2)}) collective-permute-start(bf16[96,1536]{1,0:T(8,128)(2,1)S(1)} %get-tuple-element.22), channel_id=1, source_target_pairs={{0,32},{32,64},{64,96},{96,128},{128,160},{160,192},{192,224},{224... | collective-permute-start | bytes 884744 | tf_op jit(solution)/shard_map/ppermute | solution.py:292
  128.9 7.4 %copy-start.3 = (bf16[192,1536]{1,0:T(8,128)(2,1)S(1)}, bf16[192,1536]{1,0:T(8,128)(2,1)}, u32[]{:S(2)}) copy-start(bf16[192,1536]{1,0:T(8,128)(2,1)} %joined.2.refs_0_) | copy-start | bytes 1769476
  140.0 45.1 %all-to-all-start = ((bf16[8,8,192,128]{3,2,1,0:T(8,128)(2,1)}), bf16[8,8,192,128]{3,2,1,0:T(8,128)(2,1)}, u32[]{:S(2)}, u32[]{:S(2)}) async-start(bf16[8,8,192,128]{3,2,1,0:T(8,128)(2,1)} %get-tuple-element.25), calls=%async_computation | async-start | bytes 6291456 | tf_op jit(solution)/shard_map/all_to_all | solution.py:344
  157.3 1.0 copy-start.4
  158.3 37.2 %copy-start.21 = (s32[1536]{0:T(1024)S(1)}, s32[1536]{0:T(1024)}, u32[]{:S(2)}) copy-start(s32[1536]{0:T(1024)} %get-tuple-element.35) | copy-start | bytes 18436
  158.3 37.2 %copy-start.22 = (s32[1536]{0:T(1024)S(1)}, s32[1536]{0:T(1024)}, u32[]{:S(2)}) copy-start(s32[1536]{0:T(1024)} %get-tuple-element.36) | copy-start | bytes 18436
  158.3 37.2 %copy-start.23 = (f32[2048]{0:T(1024)S(1)}, f32[2048]{0:T(1024)}, u32[]{:S(2)}) copy-start(f32[2048]{0:T(1024)} %param.14) | copy-start | bytes 24580
  158.3 42.6 %copy-start.2 = (bf16[384,1,1536]{2,0,1:T(8,128)(2,1)S(1)}, bf16[384,1,1536]{2,0,1:T(8,128)(2,1)}, u32[]{:S(2)}) copy-start(bf16[384,1,1536]{2,0,1:T(8,128)(2,1)} %param.8) | copy-start | bytes 3538948
  158.3 42.6 %collective-permute-start.17 = (bf16[192,1536]{1,0:T(8,128)(2,1)}, bf16[192,1536]{1,0:T(8,128)(2,1)}, u32[]{:S(2)}, u32[]{:S(2)}) collective-permute-start(bf16[192,1536]{1,0:T(8,128)(2,1)} %get-tuple-element.34), channel_id=1, source_target_pairs={{0,128},{32,160},{64,192},{96,224},{128,0},{160,32},{192,64},{224,... | collective-permute-start | bytes 1769480 | tf_op jit(solution)/shard_map/ppermute | solution.py:292
  193.8 30.5 %collective-permute-start.14 = (bf16[192,1536]{1,0:T(8,128)(2,1)}, bf16[192,1536]{1,0:T(8,128)(2,1)S(1)}, u32[]{:S(2)}, u32[]{:S(2)}) collective-permute-start(bf16[192,1536]{1,0:T(8,128)(2,1)} %get-tuple-element.27), channel_id=1, source_target_pairs={{0,128},{32,160},{64,192},{96,224},{128,0},{160,32},{192,64},{224,... | collective-permute-start | bytes 1769480 | tf_op jit(solution)/shard_map/ppermute | solution.py:292
  201.0 1.3 copy-start.5
Sparse Core Ops, SparseCore 0:
  9.2 124.9 all-gather.3

commit v5 on v4

--- a/solution.py
+++ b/solution.py
@@ -1,4 +1,5 @@
 import functools
+import math
 
 import jax
 import jax.numpy as jnp
@@ -16,10 +17,11 @@
     return jnp.where(number == row, 1.0, 0.0).astype(jnp.bfloat16)
 
 
-def fold_body(shifts, facts, maps, *refs):
+def fold_body(shifts, pieces, facts, maps, *refs):
     count = len(shifts)
     tiles = refs[: 3 if shifts == (0,) else 2 * count]
-    out, done, base, other, folded, base_sem, other_sem, out_sem = refs[-8:]
+    done, base, other, folded, base_sem, other_sem, out_sem = refs[-7:]
+    outs = refs[-7 - len(pieces) : -7]
     done[0] = 0
     z = facts[0]
     sign = jnp.where(z < 4, 1.0, -1.0).astype(jnp.float32)
@@ -53,6 +55,7 @@
                 for copy in fetch(i, turned):
                     copy.start()
 
+    sends = []
     for i, shift in enumerate(shifts):
         low = (z + shift + 8) & 3
         for copy in fetch(i, False):
@@ -68,18 +71,26 @@
 
         lax.fori_loop(0, length // COLS, column, 0, unroll=True)
 
+        def send(receiver, half, start, i=i, shift=shift):
+            copies, low = [], 0
+            for p, (out, count) in enumerate(zip(outs, pieces)):
+                source = folded.at[i, pl.ds(low, count), pl.ds(start, 128)]
+                place = out.at[receiver, 2 * (shift & 3) + half]
+                copies.append(
+                    pltpu.make_async_copy(source, place, out_sem.at[i, receiver, 2 * p + half])
+                )
+                low += count
+            return copies
+
+        sends.append(send)
         for receiver in range(8):
             for half in range(2):
                 segment = facts[1 + receiver * 8 + low + 4 * half]
 
                 @pl.when(segment >= 0)
                 def _():
-                    start = pl.multiple_of(segment * 128, 128)
-                    pltpu.make_async_copy(
-                        folded.at[i, :, pl.ds(start, 128)],
-                        out.at[receiver, 2 * (shift & 3) + half],
-                        out_sem.at[i, receiver, half],
-                    ).start()
+                    for copy in send(receiver, half, pl.multiple_of(segment * 128, 128)):
+                        copy.start()
 
     for i, shift in enumerate(shifts):
         low = (z + shift + 8) & 3
@@ -88,33 +99,29 @@
 
                 @pl.when(facts[1 + receiver * 8 + low + 4 * half] >= 0)
                 def _():
-                    pltpu.make_async_copy(
-                        folded.at[i, :, pl.ds(0, 128)],
-                        out.at[receiver, 2 * (shift & 3) + half],
-                        out_sem.at[i, receiver, half],
-                    ).wait()
-
-
-def fold(shifts, facts, maps, tiles, before):
+                    for copy in sends[i](receiver, half, 0):
+                        copy.wait()
+
+
+def fold(shifts, facts, maps, tiles, pieces, before):
     rows, length = tiles[0].shape
     count = len(shifts)
     whole = pltpu.VMEM((count, rows, length), jnp.bfloat16)
     return pl.pallas_call(
-        functools.partial(fold_body, shifts),
+        functools.partial(fold_body, shifts, pieces),
         in_specs=[pl.BlockSpec(memory_space=pltpu.SMEM), pl.BlockSpec(memory_space=pltpu.VMEM)]
         + [pl.BlockSpec(memory_space=pl.ANY)] * (len(tiles) + len(before)),
-        out_specs=[pl.BlockSpec(memory_space=pl.ANY), pl.BlockSpec(memory_space=pltpu.SMEM)],
-        out_shape=[
-            pltpu.HBM((8, 8, rows, 128), jnp.bfloat16),
-            jax.ShapeDtypeStruct((1,), jnp.int32),
-        ],
+        out_specs=[pl.BlockSpec(memory_space=pl.ANY)] * len(pieces)
+        + [pl.BlockSpec(memory_space=pltpu.SMEM)],
+        out_shape=[pltpu.HBM((8, 8, piece, 128), jnp.bfloat16) for piece in pieces]
+        + [jax.ShapeDtypeStruct((1,), jnp.int32)],
         scratch_shapes=[
             whole,
             whole,
             whole,
             pltpu.SemaphoreType.DMA((count,)),
             pltpu.SemaphoreType.DMA((count, 2)),
-            pltpu.SemaphoreType.DMA((count, 8, 2)),
+            pltpu.SemaphoreType.DMA((count, 8, 2 * len(pieces))),
         ],
         compiler_params=pltpu.CompilerParams(vmem_limit_bytes=VMEM),
         cost_estimate=pl.CostEstimate(
@@ -122,7 +129,7 @@
             bytes_accessed=count * rows * (4 * length + 16 * 256),
             transcendentals=0,
         ),
-        input_output_aliases={2 + len(tiles): 0} if before else {},
+        input_output_aliases={2 + len(tiles) + p: p for p in range(len(before))},
         name="fold",
     )(facts, maps, *tiles, *before)
 
@@ -226,7 +233,7 @@
         ],
         out_specs=[vmem, vmem],
         out_shape=[
-            jax.ShapeDtypeStruct((rows, length), jnp.float32),
+            pltpu.HBM((rows, length), jnp.float32),
             jax.ShapeDtypeStruct((rows, length), jnp.bfloat16),
         ],
         scratch_shapes=[
@@ -236,7 +243,7 @@
             pltpu.SemaphoreType.DMA((depth // 128,)),
             pltpu.SemaphoreType.DMA((4,)),
         ],
-        compiler_params=pltpu.CompilerParams(vmem_limit_bytes=VMEM),
+        compiler_params=pltpu.CompilerParams(vmem_limit_bytes=60 * 1024 * 1024),
         cost_estimate=pl.CostEstimate(
             flops=2 * rows * depth * length,
             bytes_accessed=2 * depth * (rows + length),
@@ -255,7 +262,7 @@
 
 def update(low, own, ladder, partner, direction, occupied, virtual, before):
     rows, length = ladder.shape
-    step = 64
+    step = math.gcd(low, rows) if low else rows // 2
 
     def chunk(width):
         return pl.BlockSpec((step, width), lambda n: (n, 0))
@@ -320,33 +327,38 @@
     first = energies(vir_energy, pair_virt[0, 0])
     second = energies(vir_energy, pair_virt[0, 1])
     virtual = jnp.stack([first, second])
-    ends = (0, 192, rows)
-    steps, folds = [], []
-    for low, high in zip(ends, ends[1:]):
-        part = own[low:high]
+    chunks = ((224,), (160,))
+    steps, folds, low = [], [], 0
+    for pieces in chunks:
+        part = own[low : low + sum(pieces)]
+        low += sum(pieces)
         if steps:
             part = joined(part, steps[-1][2], pltpu.HBM)
         one = (shifted(part, -1), shifted(part, 1))
         two = (shifted(one[0], -1), shifted(one[1], 1))
-        slots, done = fold((2,), fold_facts, maps, two, ())
+        *slots, done = fold((2,), fold_facts, maps, two, pieces, ())
         three = (shifted(two[0], -1), shifted(two[1], 1))
         upper, lower = halves(*three, done if steps else fold_facts)
         far = (shifted(upper, -1), shifted(lower, 1))
         odd = (one[0], three[1], three[0], one[1])
-        slots, _ = fold((1, 3), fold_facts, maps, odd, (slots,))
+        *slots, _ = fold((1, 3), fold_facts, maps, odd, pieces, slots)
         steps.append((part, one, three, far))
         folds.append(slots)
-    fresh = ()
+    fresh, low, last, sents = (), 0, (), ()
     for i, (part, one, three, far) in enumerate(steps):
-        slots, _ = fold((0,), fold_facts, maps, (part, *far), (folds[i],))
-        if i + 1 < len(steps):
-            slots = joined(slots, steps[i + 1][1], pltpu.HBM)
-        received = lax.all_to_all(slots, "ket", split_axis=0, concat_axis=0, tiled=True)
-        ladder, sent = ladder_of(ladder_facts, send_map, all_blocks, received)
-        partner = shifted(sent, 4)
-        fresh = update(ends[i], own, ladder, partner, direction[None], pair_energy[:, None], virtual, fresh)
-        fresh = (fresh,)
-    return fresh[0][:, None, :]
+        *slots, _ = fold((0,), fold_facts, maps, (part, *far), chunks[i], folds[i])
+        later = steps[i + 1][1] if i + 1 < len(steps) else ()
+        for piece in slots:
+            piece = joined(piece, (*later, *last), pltpu.HBM)
+            received = lax.all_to_all(piece, "ket", split_axis=0, concat_axis=0, tiled=True)
+            ladder, sent = ladder_of(ladder_facts, send_map, all_blocks, received)
+            last = (received, *sents)
+            sents = (sent,)
+            partner = shifted(sent, 4)
+            new = update(low, own, ladder, partner, direction[None], pair_energy[:, None], virtual, fresh)
+            fresh = (new,)
+            low += piece.shape[2]
+    return new[:, None, :]
 
 
 def solution(mesh):

time: 233 us -> 224 us (0.961)
  the two profiles are of different devices: /device:TPU:1 before, /device:TPU:47 now
where the time goes in v5:
time: 224 us
  waiting for transfers between devices  95.3 us (43%)
  Pallas kernels  54.6 us (24%)
  starting transfers between devices  38.3 us (17%)
  between operations  13.7 us (6%)
  blocking collectives  10.3 us (5%)
  local copies, waits for them, and re-layouts  6.24 us (3%)
  other arithmetic  5.5 us (2%)
    ppermute x18, waiting for transfers between devices, shifted(): return lax.ppermute(block, 'bra', [(i, (i + by) % 8) for i in range(8)])  74.6 us
    pallas_call x6, Pallas kernels, fold(): pl.pallas_call(functools.partial(fold_body, shifts, pieces), in_specs=[pl...  29 us
    ppermute x18, starting transfers between devices, shifted(): return lax.ppermute(block, 'bra', [(i, (i + by) % 8) for i in range(8)])  22.8 us
    all_to_all x2, waiting for transfers between devices, local(): lax.all_to_all(piece, 'ket', split_axis=0, concat_axis=0, tiled=True)  20 us
    pallas_call x2, Pallas kernels, ladder_of(): pl.pallas_call(ladder_body, in_specs=[pl.BlockSpec(memory_space=pltpu.SME...  17.8 us
    all_to_all x2, starting transfers between devices, local(): lax.all_to_all(piece, 'ket', split_axis=0, concat_axis=0, tiled=True)  15.6 us
    all_gather x1, blocking collectives, local(): wanted = lax.all_gather(block_owner[0] * 16 + screen_list[0], 'ket', axis=0)  10.3 us
    pallas_call x2, Pallas kernels, update(): pl.pallas_call(functools.partial(update_body, low), grid=(rows // step,),...  6.18 us
  transfers between devices with their start and end apart: 21, of which 13 were waited for; matrix products, arithmetic and copies ran while one was open for 4% of the time, Pallas kernels for 23%

profile of v5, /device:TPU:47, one launch (start us, length us, event | category | flops | bytes accessed | tf_op | source)
XLA Modules:
  0.0 223.9 jit_solution(9604606516233601435)
XLA Ops:
  6.6 0.7 all-gather.4.cloned.1.call-update
  7.3 1.1 slice_bitcast_fusion.refs_0_
  8.5 1.7 collective-permute-start.3
  10.2 0.8 copy-done.3
  11.1 14.1 %collective-permute-done.refs_0_ = bf16[224,1536]{1,0:T(8,128)(2,1)S(1)} collective-permute-done((bf16[224,1536]{1,0:T(8,128)(2,1)S(1)}, bf16[224,1536]{1,0:T(8,128)(2,1)S(1)}, u32[]{:S(2)}, u32[]{:S(2)}) %collective-permute-start) | collective-permute-done | bytes 688160 | tf_op jit(solution)/shard_map/ppermute | solution.py:299
  25.2 2.8 %collective-permute-start.1 = (bf16[224,1536]{1,0:T(8,128)(2,1)S(1)}, bf16[224,1536]{1,0:T(8,128)(2,1)}, u32[]{:S(2)}, u32[]{:S(2)}) collective-permute-start(bf16[224,1536]{1,0:T(8,128)(2,1)S(1)} %collective-permute-done.refs_0_), channel_id=1, source_target_pairs={{0,224},{32,0},{64,32},{96,64},{128,96},{160,128},{192,160},{224,1... | collective-permute-start | bytes 2064392 | tf_op jit(solution)/shard_map/ppermute | solution.py:299
  28.0 0.9 copy-done.9
  28.9 0.8 copy-done.11
  29.7 10.3 %all-gather.1 = s32[8,1,32]{2,1,0:T(1,128)S(1)} all-gather(s32[1,1,32]{2,1,0:T(1,128)S(1)} %add_bitcast_fusion), channel_id=1, replica_groups=mesh['bra'=8,'ket'=8,'pair'=4] {'ket'}, dimensions={0}, use_global_device_ids=true | all-gather | bytes 1152 | tf_op jit(solution)/shard_map/all_gather | solution.py:315
  40.1 1.1 collective-permute-done.1.refs_0_
  41.2 3.4 %collective-permute-start.2 = (bf16[224,1536]{1,0:T(8,128)(2,1)}, bf16[224,1536]{1,0:T(8,128)(2,1)S(1)}, u32[]{:S(2)}, u32[]{:S(2)}) collective-permute-start(bf16[224,1536]{1,0:T(8,128)(2,1)} %collective-permute-done.1.refs_0_), channel_id=1, source_target_pairs={{0,224},{32,0},{64,32},{96,64},{128,96},{160,128},{192,160},{224,1... | collective-permute-start | bytes 2064392 | tf_op jit(solution)/shard_map/ppermute | solution.py:299
  44.6 1.7 collective-permute-done.4.refs_1_
  46.3 0.3 select_reduce_fusion.2
  46.8 0.8 slice_bitcast_fusion.1.refs_0_
  47.6 10.7 %collective-permute-done.2.refs_1_.first.refs_2_ = bf16[224,1536]{1,0:T(8,128)(2,1)S(1)} collective-permute-done((bf16[224,1536]{1,0:T(8,128)(2,1)}, bf16[224,1536]{1,0:T(8,128)(2,1)S(1)}, u32[]{:S(2)}, u32[]{:S(2)}) %collective-permute-start.2) | collective-permute-done | bytes 688160 | tf_op jit(solution)/shard_map/ppermute | solution.py:299
  58.2 3.8 %collective-permute-done.5.refs_2_.second.refs_1_ = bf16[224,1536]{1,0:T(8,128)(2,1)S(1)} collective-permute-done((bf16[224,1536]{1,0:T(8,128)(2,1)}, bf16[224,1536]{1,0:T(8,128)(2,1)S(1)}, u32[]{:S(2)}, u32[]{:S(2)}) %collective-permute-start.5) | collective-permute-done | bytes 688160 | tf_op jit(solution)/shard_map/ppermute | solution.py:299
  62.0 2.4 %collective-permute-start.6 = (bf16[160,1536]{1,0:T(8,128)(2,1)}, bf16[160,1536]{1,0:T(8,128)(2,1)S(1)}, u32[]{:S(2)}, u32[]{:S(2)}) collective-permute-start(bf16[160,1536]{1,0:T(8,128)(2,1)} %joined.3.refs_0_), channel_id=1, source_target_pairs={{0,224},{32,0},{64,32},{96,64},{128,96},{160,128},{192,160},{224,1... | collective-permute-start | bytes 1474568 | tf_op jit(solution)/shard_map/ppermute | solution.py:299
  64.7 1.5 collective-permute-start.14
  66.3 4.8 %fold.9 = (bf16[8,8,224,128]{3,2,1,0:T(8,128)(2,1)}, s32[1]{0:T(128)}) custom-call(s32[65]{0:T(128)S(1)} %pad_add_fusion.1.facts._, s32[4,1,1536]{2,1,0:T(1,128)S(1)} %dynamic-slice_bitcast_fusion.maps, bf16[224,1536]{1,0:T(8,128)(2,1)} %collective-permute-done.1.refs_0_, bf16[224,1536]{1,0:T(8,128)(2,1)} %collective-permute-done.4.refs_1_), custom_call_target="tpu_custom_call" | custom-call | flops 1056964608 | bytes 2293760 | tf_op jit(solution)/shard_map/fold/pallas_call | solution.py:110
  71.1 6.2 %fold.10 = (bf16[8,8,224,128]{3,2,1,0:T(8,128)(2,1)}, s32[1]{0:T(128)}) custom-call(s32[65]{0:T(128)S(1)} %pad_add_fusion.1.facts._, s32[4,1,1536]{2,1,0:T(1,128)S(1)} %dynamic-slice_bitcast_fusion.maps, bf16[224,1536]{1,0:T(8,128)(2,1)S(1)} %copy-done.10, ...), custom_call_target="tpu_custom_call", output_to_operand_aliasing={{0}: (6, {})} | custom-call | flops 2113929216 | bytes 4587520 | tf_op jit(solution)/shard_map/fold/pallas_call | solution.py:110
  77.3 1.8 collective-permute-done.14.refs_1_
  79.1 1.8 collective-permute-done.15.refs_2_
  81.0 4.0 %fold.11 = (bf16[8,8,224,128]{3,2,1,0:T(8,128)(2,1)}, s32[1]{0:T(128)}) custom-call(s32[65]{0:T(128)S(1)} %pad_add_fusion.1.facts._, s32[4,1,1536]{2,1,0:T(1,128)S(1)} %dynamic-slice_bitcast_fusion.maps, bf16[224,1536]{1,0:T(8,128)(2,1)S(1)} %copy-done.4, bf16[112,1536]{1,0:T(8,128)(2,1)S(1)} %collective-permute-done.14.refs_1_, ...), custom_call_target="tpu_custom_call", output_to_operand_aliasing={{0}: (5, {})} | custom-call | flops 1056964608 | bytes 2293760 | tf_op jit(solution)/shard_map/fold/pallas_call | solution.py:110
  85.0 0.8 copy-done.7
  85.7 9.2 %all-to-all-start = ((bf16[8,8,224,128]{3,2,1,0:T(8,128)(2,1)}), bf16[8,8,224,128]{3,2,1,0:T(8,128)(2,1)}, u32[]{:S(2)}, u32[]{:S(2)}) async-start(bf16[8,8,224,128]{3,2,1,0:T(8,128)(2,1)} %joined.4), calls=%async_computation | async-start | bytes 7340032 | tf_op jit(solution)/shard_map/all_to_all | solution.py:353
  95.1 1.6 collective-permute-start.7
  96.8 11.6 %collective-permute-done.10.refs_1_ = bf16[160,1536]{1,0:T(8,128)(2,1)S(1)} collective-permute-done((bf16[160,1536]{1,0:T(8,128)(2,1)}, bf16[160,1536]{1,0:T(8,128)(2,1)S(1)}, u32[]{:S(2)}, u32[]{:S(2)}) %collective-permute-start.10) | collective-permute-done | bytes 491552 | tf_op jit(solution)/shard_map/ppermute | solution.py:299
  108.4 2.3 %collective-permute-start.8 = (bf16[160,1536]{1,0:T(8,128)(2,1)S(1)}, bf16[160,1536]{1,0:T(8,128)(2,1)S(1)}, u32[]{:S(2)}, u32[]{:S(2)}) collective-permute-start(bf16[160,1536]{1,0:T(8,128)(2,1)S(1)} %collective-permute-done.7.refs_0_), channel_id=1, source_target_pairs={{0,224},{32,0},{64,32},{96,64},{128,96},{160,128},{192,160},{224,1... | collective-permute-start | bytes 1474568 | tf_op jit(solution)/shard_map/ppermute | solution.py:299
  110.7 3.8 %fold.6 = (bf16[8,8,160,128]{3,2,1,0:T(8,128)(2,1)}, s32[1]{0:T(128)}) custom-call(s32[65]{0:T(128)S(1)} %pad_add_fusion.1.facts._, s32[4,1,1536]{2,1,0:T(1,128)S(1)} %dynamic-slice_bitcast_fusion.maps, bf16[160,1536]{1,0:T(8,128)(2,1)S(1)} %collective-permute-done.7.refs_0_, bf16[160,1536]{1,0:T(8,128)(2,1)S(1)} %collective-permute-done.10.refs_1_), custom_call_target="tpu_custom_call" | custom-call | flops 754974720 | bytes 1638400 | tf_op jit(solution)/shard_map/fold/pallas_call | solution.py:110
  114.5 6.7 %collective-permute-done.11.second.refs_1_ = bf16[160,1536]{1,0:T(8,128)(2,1)S(1)} collective-permute-done((bf16[160,1536]{1,0:T(8,128)(2,1)S(1)}, bf16[160,1536]{1,0:T(8,128)(2,1)S(1)}, u32[]{:S(2)}, u32[]{:S(2)}) %collective-permute-start.11) | collective-permute-done | bytes 491552 | tf_op jit(solution)/shard_map/ppermute | solution.py:299
  121.3 1.3 halves.2
  122.5 2.4 %collective-permute-start.12 = (bf16[80,1536]{1,0:T(8,128)(2,1)S(1)}, bf16[80,1536]{1,0:T(8,128)(2,1)S(1)}, u32[]{:S(2)}, u32[]{:S(2)}) collective-permute-start(bf16[80,1536]{1,0:T(8,128)(2,1)S(1)} %get-tuple-element.21), channel_id=1, source_target_pairs={{0,224},{32,0},{64,32},{96,64},{128,96},{160,128},{192,160},{224,1... | collective-permute-start | bytes 737288 | tf_op jit(solution)/shard_map/ppermute | solution.py:299
  125.0 6.1 %fold.7 = (bf16[8,8,160,128]{3,2,1,0:T(8,128)(2,1)}, s32[1]{0:T(128)}) custom-call(s32[65]{0:T(128)S(1)} %pad_add_fusion.1.facts._, s32[4,1,1536]{2,1,0:T(1,128)S(1)} %dynamic-slice_bitcast_fusion.maps, bf16[160,1536]{1,0:T(8,128)(2,1)S(1)} %collective-permute-done.6.refs_0_.refs_1_, ...), custom_call_target="tpu_custom_call", output_to_operand_aliasing={{0}: (6, {})} | custom-call | flops 1509949440 | bytes 3276800 | tf_op jit(solution)/shard_map/fold/pallas_call | solution.py:110
  131.1 0.3 collective-permute-done.13.refs_2_
  131.4 4.1 %fold.8 = (bf16[8,8,160,128]{3,2,1,0:T(8,128)(2,1)}, s32[1]{0:T(128)}) custom-call(s32[65]{0:T(128)S(1)} %pad_add_fusion.1.facts._, s32[4,1,1536]{2,1,0:T(1,128)S(1)} %dynamic-slice_bitcast_fusion.maps, bf16[160,1536]{1,0:T(8,128)(2,1)S(1)} %copy-done.2, bf16[80,1536]{1,0:T(8,128)(2,1)S(1)} %collective-permute-done.12.refs_1_, ...), custom_call_target="tpu_custom_call", output_to_operand_aliasing={{0}: (5, {})} | custom-call | flops 754974720 | bytes 1638400 | tf_op jit(solution)/shard_map/fold/pallas_call | solution.py:110
  135.5 1.7 all-to-all-done.refs_1_.received
  137.2 6.4 %all-to-all-start.1 = ((bf16[8,8,160,128]{3,2,1,0:T(8,128)(2,1)}), bf16[8,8,160,128]{3,2,1,0:T(8,128)(2,1)}, u32[]{:S(2)}, u32[]{:S(2)}) async-start(bf16[8,8,160,128]{3,2,1,0:T(8,128)(2,1)} %joined.5), calls=%async_computation.1 | async-start | bytes 5242880 | tf_op jit(solution)/shard_map/all_to_all | solution.py:353
  143.5 0.6 pad_add_fusion.facts
  144.1 0.6 constant_dynamic-slice_fusion.send_map
  144.8 9.3 %ladder.3 = (f32[224,1536]{1,0:T(8,128)}, bf16[224,1536]{1,0:T(8,128)(2,1)}) custom-call(s32[33]{0:T(128)} %pad_add_fusion.facts, s32[1,1536]{1,0:T(1,128)} %constant_dynamic-slice_fusion.send_map, bf16[4096,1536]{1,0:T(8,128)(2,1)} %bitcast.21, bf16[8,8,224,128]{3,2,1,0:T(8,128)(2,1)} %all-to-all-done.refs_1_.received), custom_call_target="tpu_custom_call" | custom-call | flops 2818572288 | bytes 14417920 | tf_op jit(solution)/shard_map/ladder/pallas_call | solution.py:226
  154.1 2.1 collective-permute-start.17
  156.2 18.3 %all-to-all-done.1.received = bf16[8,8,160,128]{3,2,1,0:T(8,128)(2,1)} async-done(((bf16[8,8,160,128]{3,2,1,0:T(8,128)(2,1)}), bf16[8,8,160,128]{3,2,1,0:T(8,128)(2,1)}, u32[]{:S(2)}, u32[]{:S(2)}) %all-to-all-start.1) | async-done | bytes 2621472 | tf_op jit(solution)/shard_map/all_to_all | solution.py:353
  174.5 8.5 %ladder.2 = (f32[160,1536]{1,0:T(8,128)}, bf16[160,1536]{1,0:T(8,128)(2,1)}) custom-call(s32[33]{0:T(128)} %pad_add_fusion.facts, s32[1,1536]{1,0:T(1,128)} %constant_dynamic-slice_fusion.send_map, bf16[4096,1536]{1,0:T(8,128)(2,1)} %bitcast.22, bf16[8,8,160,128]{3,2,1,0:T(8,128)(2,1)} %all-to-all-done.1.received), custom_call_target="tpu_custom_call" | custom-call | flops 2013265920 | bytes 13893632 | tf_op jit(solution)/shard_map/ladder/pallas_call | solution.py:226
  183.1 2.1 collective-permute-start.16
  185.2 4.5 %select_reduce_fusion.1 = (f32[1536]{0:T(1024)S(1)}, f32[1536]{0:T(1024)S(1)}) fusion(f32[2048]{0:T(1024)S(1)} %copy-done.15, s32[1536]{0:T(1024)S(1)} %get-tuple-element.35, s32[1536]{0:T(1024)S(1)} %get-tuple-element.36), kind=kLoop, calls=%fused_computation.2 | loop fusion | flops 18871296 | bytes 32768 | tf_op jit(solution)/shard_map/reduce_sum | solution.py:304
  189.9 2.4 %update.2.refs_6_ = bf16[384,1536]{1,0:T(8,128)(2,1)} custom-call(bf16[384,1536]{1,0:T(8,128)(2,1)S(1)} %bitcast.19, f32[224,1536]{1,0:T(8,128)S(1)} %copy-done.5, bf16[224,1536]{1,0:T(8,128)(2,1)} %collective-permute-done.17.refs_2_, f32[1]{0:T(128)} %bitcast.12.refs_3_, f32[384,1]{1,0:T(8,128)S(1)} %broadcast_in_dim.56.refs_4_, ...), custom_call_target="tpu_custom_call" | custom-call | flops 2752512 | bytes 3440640 | tf_op jit(solution)/shard_map/update/pallas_call | solution.py:273
  192.3 21.0 %collective-permute-done.16.refs_2_ = bf16[160,1536]{1,0:T(8,128)(2,1)} collective-permute-done((bf16[160,1536]{1,0:T(8,128)(2,1)}, bf16[160,1536]{1,0:T(8,128)(2,1)}, u32[]{:S(2)}, u32[]{:S(2)}) %collective-permute-start.16) | collective-permute-done | bytes 491552 | tf_op jit(solution)/shard_map/ppermute | solution.py:299
  213.3 3.8 %update.3 = bf16[384,1536]{1,0:T(8,128)(2,1)} custom-call(bf16[384,1536]{1,0:T(8,128)(2,1)S(1)} %bitcast.20, f32[160,1536]{1,0:T(8,128)S(1)} %copy-done.6, bf16[160,1536]{1,0:T(8,128)(2,1)} %collective-permute-done.16.refs_2_, f32[1]{0:T(128)} %bitcast.12.refs_3_, f32[384,1]{1,0:T(8,128)S(1)} %broadcast_in_dim.56.refs_4_, ...), custom_call_target="tpu_custom_call", output_to_operand_aliasing={{}: (6, {})} | custom-call | flops 1966080 | bytes 2457600 | tf_op jit(solution)/shard_map/update/pallas_call | solution.py:273
  (64 shorter events, 1.0 us)
Async XLA Ops:
  6.5 59.7 %copy-start = (s32[64,1536]{1,0:T(8,128)S(1)}, s32[64,1536]{1,0:T(8,128)}, u32[]{:S(2)}) copy-start(s32[64,1536]{1,0:T(8,128)} %param.12) | copy-start | bytes 1179652
  6.5 40.2 %copy-start.1 = (bf16[384,1,1536]{2,0,1:T(8,128)(2,1)S(1)}, bf16[384,1,1536]{2,0,1:T(8,128)(2,1)}, u32[]{:S(2)}) copy-start(bf16[384,1,1536]{2,0,1:T(8,128)(2,1)} %param.8) | copy-start | bytes 3538948
  6.5 23.2 %copy-start.16 = (s32[1,32]{1,0:T(1,128)S(1)}, s32[1,32]{1,0:T(1,128)}, u32[]{:S(2)}) copy-start(s32[1,32]{1,0:T(1,128)} %param.10) | copy-start | bytes 388
  6.5 23.2 %copy-start.17 = (s32[1,32]{1,0:T(1,128)S(1)}, s32[1,32]{1,0:T(1,128)}, u32[]{:S(2)}) copy-start(s32[1,32]{1,0:T(1,128)} %param.11) | copy-start | bytes 388
  6.5 138.2 %all-gather.4.cloned.1.call-start = ((), (), s32[]{:S(2)}) async-start(), calls=%async_computation.2 | async-start | bytes 15728640 | tf_op jit(solution)/shard_map/all_gather | solution.py:313
  8.4 16.8 %collective-permute-start = (bf16[224,1536]{1,0:T(8,128)(2,1)S(1)}, bf16[224,1536]{1,0:T(8,128)(2,1)S(1)}, u32[]{:S(2)}, u32[]{:S(2)}) collective-permute-start(bf16[224,1536]{1,0:T(8,128)(2,1)S(1)} %slice_bitcast_fusion.refs_0_), channel_id=1, source_target_pairs={{0,224},{32,0},{64,32},{96,64},{128,96},{160,128},{192,160},{224,1... | collective-permute-start | bytes 2064392 | tf_op jit(solution)/shard_map/ppermute | solution.py:299
  8.5 20.4 %collective-permute-start.3 = (bf16[224,1536]{1,0:T(8,128)(2,1)S(1)}, bf16[224,1536]{1,0:T(8,128)(2,1)S(1)}, u32[]{:S(2)}, u32[]{:S(2)}) collective-permute-start(bf16[224,1536]{1,0:T(8,128)(2,1)S(1)} %slice_bitcast_fusion.refs_0_), channel_id=1, source_target_pairs={{0,32},{32,64},{64,96},{96,128},{128,160},{160,192},{192,224},{224... | collective-permute-start | bytes 2064392 | tf_op jit(solution)/shard_map/ppermute | solution.py:299
  10.2 0.8 copy-start.3
  25.2 16.0 %collective-permute-start.1 = (bf16[224,1536]{1,0:T(8,128)(2,1)S(1)}, bf16[224,1536]{1,0:T(8,128)(2,1)}, u32[]{:S(2)}, u32[]{:S(2)}) collective-permute-start(bf16[224,1536]{1,0:T(8,128)(2,1)S(1)} %collective-permute-done.refs_0_), channel_id=1, source_target_pairs={{0,224},{32,0},{64,32},{96,64},{128,96},{160,128},{192,160},{224,1... | collective-permute-start | bytes 2064392 | tf_op jit(solution)/shard_map/ppermute | solution.py:299
  28.0 0.9 copy-start.9
  28.9 17.4 %collective-permute-start.4 = (bf16[224,1536]{1,0:T(8,128)(2,1)S(1)}, bf16[224,1536]{1,0:T(8,128)(2,1)}, u32[]{:S(2)}, u32[]{:S(2)}) collective-permute-start(bf16[224,1536]{1,0:T(8,128)(2,1)S(1)} %collective-permute-done.3.refs_3_), channel_id=1, source_target_pairs={{0,32},{32,64},{64,96},{96,128},{128,160},{160,192},{192,224},{224... | collective-permute-start | bytes 2064392 | tf_op jit(solution)/shard_map/ppermute | solution.py:299
  28.9 0.9 copy-start.11
  41.2 17.0 %collective-permute-start.2 = (bf16[224,1536]{1,0:T(8,128)(2,1)}, bf16[224,1536]{1,0:T(8,128)(2,1)S(1)}, u32[]{:S(2)}, u32[]{:S(2)}) collective-permute-start(bf16[224,1536]{1,0:T(8,128)(2,1)} %collective-permute-done.1.refs_0_), channel_id=1, source_target_pairs={{0,224},{32,0},{64,32},{96,64},{128,96},{160,128},{192,160},{224,1... | collective-permute-start | bytes 2064392 | tf_op jit(solution)/shard_map/ppermute | solution.py:299
  46.3 15.7 %collective-permute-start.5 = (bf16[224,1536]{1,0:T(8,128)(2,1)}, bf16[224,1536]{1,0:T(8,128)(2,1)S(1)}, u32[]{:S(2)}, u32[]{:S(2)}) collective-permute-start(bf16[224,1536]{1,0:T(8,128)(2,1)} %collective-permute-done.4.refs_1_), channel_id=1, source_target_pairs={{0,32},{32,64},{64,96},{96,128},{128,160},{160,192},{192,224},{224... | collective-permute-start | bytes 2064392 | tf_op jit(solution)/shard_map/ppermute | solution.py:299
  47.6 23.5 %copy-start.10 = (bf16[224,1536]{1,0:T(8,128)(2,1)S(1)}, bf16[224,1536]{1,0:T(8,128)(2,1)}, u32[]{:S(2)}) copy-start(bf16[224,1536]{1,0:T(8,128)(2,1)} %copy-done.9) | copy-start | bytes 2064388
  47.6 23.5 %copy-start.12 = (bf16[224,1536]{1,0:T(8,128)(2,1)S(1)}, bf16[224,1536]{1,0:T(8,128)(2,1)}, u32[]{:S(2)}) copy-start(bf16[224,1536]{1,0:T(8,128)(2,1)} %copy-done.11) | copy-start | bytes 2064388
  62.0 22.9 %collective-permute-start.6 = (bf16[160,1536]{1,0:T(8,128)(2,1)}, bf16[160,1536]{1,0:T(8,128)(2,1)S(1)}, u32[]{:S(2)}, u32[]{:S(2)}) collective-permute-start(bf16[160,1536]{1,0:T(8,128)(2,1)} %joined.3.refs_0_), channel_id=1, source_target_pairs={{0,224},{32,0},{64,32},{96,64},{128,96},{160,128},{192,160},{224,1... | collective-permute-start | bytes 1474568 | tf_op jit(solution)/shard_map/ppermute | solution.py:299
  64.4 20.5 %collective-permute-start.9 = (bf16[160,1536]{1,0:T(8,128)(2,1)}, bf16[160,1536]{1,0:T(8,128)(2,1)S(1)}, u32[]{:S(2)}, u32[]{:S(2)}) collective-permute-start(bf16[160,1536]{1,0:T(8,128)(2,1)} %joined.3.refs_0_), channel_id=1, source_target_pairs={{0,32},{32,64},{64,96},{96,128},{128,160},{160,192},{192,224},{224... | collective-permute-start | bytes 1474568 | tf_op jit(solution)/shard_map/ppermute | solution.py:299
  64.7 14.4 %collective-permute-start.14 = (bf16[112,1536]{1,0:T(8,128)(2,1)S(1)}, bf16[112,1536]{1,0:T(8,128)(2,1)S(1)}, u32[]{:S(2)}, u32[]{:S(2)}) collective-permute-start(bf16[112,1536]{1,0:T(8,128)(2,1)S(1)} %get-tuple-element.26), channel_id=1, source_target_pairs={{0,224},{32,0},{64,32},{96,64},{128,96},{160,128},{192,160},{224,1... | collective-permute-start | bytes 1032200 | tf_op jit(solution)/shard_map/ppermute | solution.py:299
  66.2 14.7 %collective-permute-start.15 = (bf16[112,1536]{1,0:T(8,128)(2,1)S(1)}, bf16[112,1536]{1,0:T(8,128)(2,1)S(1)}, u32[]{:S(2)}, u32[]{:S(2)}) collective-permute-start(bf16[112,1536]{1,0:T(8,128)(2,1)S(1)} %get-tuple-element.27), channel_id=1, source_target_pairs={{0,32},{32,64},{64,96},{96,128},{128,160},{160,192},{192,224},{224... | collective-permute-start | bytes 1032200 | tf_op jit(solution)/shard_map/ppermute | solution.py:299
  71.1 9.9 %copy-start.4 = (bf16[224,1536]{1,0:T(8,128)(2,1)S(1)}, bf16[224,1536]{1,0:T(8,128)(2,1)}, u32[]{:S(2)}) copy-start(bf16[224,1536]{1,0:T(8,128)(2,1)} %copy-done.3) | copy-start | bytes 2064388
  85.0 0.8 copy-start.7
  85.7 51.4 %all-to-all-start = ((bf16[8,8,224,128]{3,2,1,0:T(8,128)(2,1)}), bf16[8,8,224,128]{3,2,1,0:T(8,128)(2,1)}, u32[]{:S(2)}, u32[]{:S(2)}) async-start(bf16[8,8,224,128]{3,2,1,0:T(8,128)(2,1)} %joined.4), calls=%async_computation | async-start | bytes 7340032 | tf_op jit(solution)/shard_map/all_to_all | solution.py:353
  94.9 30.0 %copy-start.8 = (bf16[160,1536]{1,0:T(8,128)(2,1)S(1)}, bf16[160,1536]{1,0:T(8,128)(2,1)}, u32[]{:S(2)}) copy-start(bf16[160,1536]{1,0:T(8,128)(2,1)} %copy-done.7) | copy-start | bytes 1474564
  94.9 13.4 %collective-permute-start.10 = (bf16[160,1536]{1,0:T(8,128)(2,1)}, bf16[160,1536]{1,0:T(8,128)(2,1)S(1)}, u32[]{:S(2)}, u32[]{:S(2)}) collective-permute-start(bf16[160,1536]{1,0:T(8,128)(2,1)} %copy-done.7), channel_id=1, source_target_pairs={{0,32},{32,64},{64,96},{96,128},{128,160},{160,192},{192,224},{224... | collective-permute-start | bytes 1474568 | tf_op jit(solution)/shard_map/ppermute | solution.py:299
  95.1 13.3 %collective-permute-start.7 = (bf16[160,1536]{1,0:T(8,128)(2,1)S(1)}, bf16[160,1536]{1,0:T(8,128)(2,1)S(1)}, u32[]{:S(2)}, u32[]{:S(2)}) collective-permute-start(bf16[160,1536]{1,0:T(8,128)(2,1)S(1)} %collective-permute-done.6.refs_0_.refs_1_), channel_id=1, source_target_pairs={{0,224},{32,0},{64,32},{96,64},{128,96},{160,128},{192,160},{224,1... | collective-permute-start | bytes 1474568 | tf_op jit(solution)/shard_map/ppermute | solution.py:299
  108.4 12.9 %collective-permute-start.11 = (bf16[160,1536]{1,0:T(8,128)(2,1)S(1)}, bf16[160,1536]{1,0:T(8,128)(2,1)S(1)}, u32[]{:S(2)}, u32[]{:S(2)}) collective-permute-start(bf16[160,1536]{1,0:T(8,128)(2,1)S(1)} %collective-permute-done.10.refs_1_), channel_id=1, source_target_pairs={{0,32},{32,64},{64,96},{96,128},{128,160},{160,192},{192,224},{224... | collective-permute-start | bytes 1474568 | tf_op jit(solution)/shard_map/ppermute | solution.py:299
  108.4 12.9 %collective-permute-start.8 = (bf16[160,1536]{1,0:T(8,128)(2,1)S(1)}, bf16[160,1536]{1,0:T(8,128)(2,1)S(1)}, u32[]{:S(2)}, u32[]{:S(2)}) collective-permute-start(bf16[160,1536]{1,0:T(8,128)(2,1)S(1)} %collective-permute-done.7.refs_0_), channel_id=1, source_target_pairs={{0,224},{32,0},{64,32},{96,64},{128,96},{160,128},{192,160},{224,1... | collective-permute-start | bytes 1474568 | tf_op jit(solution)/shard_map/ppermute | solution.py:299
  114.5 16.8 %copy-start.2 = (bf16[160,1536]{1,0:T(8,128)(2,1)S(1)}, bf16[160,1536]{1,0:T(8,128)(2,1)}, u32[]{:S(2)}) copy-start(bf16[160,1536]{1,0:T(8,128)(2,1)} %joined.3.refs_0_) | copy-start | bytes 1474564
  122.5 8.5 %collective-permute-start.12 = (bf16[80,1536]{1,0:T(8,128)(2,1)S(1)}, bf16[80,1536]{1,0:T(8,128)(2,1)S(1)}, u32[]{:S(2)}, u32[]{:S(2)}) collective-permute-start(bf16[80,1536]{1,0:T(8,128)(2,1)S(1)} %get-tuple-element.21), channel_id=1, source_target_pairs={{0,224},{32,0},{64,32},{96,64},{128,96},{160,128},{192,160},{224,1... | collective-permute-start | bytes 737288 | tf_op jit(solution)/shard_map/ppermute | solution.py:299
  125.0 6.4 %collective-permute-start.13 = (bf16[80,1536]{1,0:T(8,128)(2,1)S(1)}, bf16[80,1536]{1,0:T(8,128)(2,1)S(1)}, u32[]{:S(2)}, u32[]{:S(2)}) collective-permute-start(bf16[80,1536]{1,0:T(8,128)(2,1)S(1)} %get-tuple-element.22), channel_id=1, source_target_pairs={{0,32},{32,64},{64,96},{96,128},{128,160},{160,192},{192,224},{224... | collective-permute-start | bytes 737288 | tf_op jit(solution)/shard_map/ppermute | solution.py:299
  137.2 7.0 %copy-start.13 = (s32[1,2,1536]{2,1,0:T(2,128)S(1)}, s32[1,2,1536]{2,1,0:T(2,128)}, u32[]{:S(2)}) copy-start(s32[1,2,1536]{2,1,0:T(2,128)} %param.13) | copy-start | bytes 36868
  137.2 37.3 %all-to-all-start.1 = ((bf16[8,8,160,128]{3,2,1,0:T(8,128)(2,1)}), bf16[8,8,160,128]{3,2,1,0:T(8,128)(2,1)}, u32[]{:S(2)}, u32[]{:S(2)}) async-start(bf16[8,8,160,128]{3,2,1,0:T(8,128)(2,1)} %joined.5), calls=%async_computation.1 | async-start | bytes 5242880 | tf_op jit(solution)/shard_map/all_to_all | solution.py:353
  154.1 31.1 %copy-start.15 = (f32[2048]{0:T(1024)S(1)}, f32[2048]{0:T(1024)}, u32[]{:S(2)}) copy-start(f32[2048]{0:T(1024)} %param.14) | copy-start | bytes 24580
  154.1 35.7 %copy-start.14 = (f32[384]{0:T(512)S(1)}, f32[384]{0:T(512)}, u32[]{:S(2)}) copy-start(f32[384]{0:T(512)} %param.15) | copy-start | bytes 4612
  154.1 35.8 %copy-start.5 = (f32[224,1536]{1,0:T(8,128)S(1)}, f32[224,1536]{1,0:T(8,128)}, u32[]{:S(2)}) copy-start(f32[224,1536]{1,0:T(8,128)} %get-tuple-element.33.refs_1_) | copy-start | bytes 4128772
  154.1 35.8 %collective-permute-start.17 = (bf16[224,1536]{1,0:T(8,128)(2,1)}, bf16[224,1536]{1,0:T(8,128)(2,1)}, u32[]{:S(2)}, u32[]{:S(2)}) collective-permute-start(bf16[224,1536]{1,0:T(8,128)(2,1)} %get-tuple-element.34), channel_id=1, source_target_pairs={{0,128},{32,160},{64,192},{96,224},{128,0},{160,32},{192,64},{224,... | collective-permute-start | bytes 2064392 | tf_op jit(solution)/shard_map/ppermute | solution.py:299
  183.1 30.3 %collective-permute-start.16 = (bf16[160,1536]{1,0:T(8,128)(2,1)}, bf16[160,1536]{1,0:T(8,128)(2,1)}, u32[]{:S(2)}, u32[]{:S(2)}) collective-permute-start(bf16[160,1536]{1,0:T(8,128)(2,1)} %get-tuple-element.32), channel_id=1, source_target_pairs={{0,128},{32,160},{64,192},{96,224},{128,0},{160,32},{192,64},{224,... | collective-permute-start | bytes 1474568 | tf_op jit(solution)/shard_map/ppermute | solution.py:299
  189.9 23.4 %copy-start.6 = (f32[160,1536]{1,0:T(8,128)S(1)}, f32[160,1536]{1,0:T(8,128)}, u32[]{:S(2)}) copy-start(f32[160,1536]{1,0:T(8,128)} %get-tuple-element.31.refs_1_) | copy-start | bytes 2949124
Sparse Core Ops, SparseCore 0:
  9.2 122.6 all-gather.3

commit v6 on v4

--- a/solution.py
+++ b/solution.py
@@ -8,6 +8,7 @@
 from jax.sharding import PartitionSpec as P
 
 COLS = 256
+FIRST = 224
 VMEM = 40 * 1024 * 1024
 
 
@@ -16,7 +17,7 @@
     return jnp.where(number == row, 1.0, 0.0).astype(jnp.bfloat16)
 
 
-def fold_body(shifts, facts, maps, *refs):
+def fold_body(shifts, first, facts, maps, *refs):
     count = len(shifts)
     tiles = refs[: 3 if shifts == (0,) else 2 * count]
     out, done, base, other, folded, base_sem, other_sem, out_sem = refs[-8:]
@@ -77,7 +78,7 @@
                     start = pl.multiple_of(segment * 128, 128)
                     pltpu.make_async_copy(
                         folded.at[i, :, pl.ds(start, 128)],
-                        out.at[receiver, 2 * (shift & 3) + half],
+                        out.at[receiver, 2 * ((shift & 3) - first) + half],
                         out_sem.at[i, receiver, half],
                     ).start()
 
@@ -90,22 +91,22 @@
                 def _():
                     pltpu.make_async_copy(
                         folded.at[i, :, pl.ds(0, 128)],
-                        out.at[receiver, 2 * (shift & 3) + half],
+                        out.at[receiver, 2 * ((shift & 3) - first) + half],
                         out_sem.at[i, receiver, half],
                     ).wait()
 
 
-def fold(shifts, facts, maps, tiles, before):
+def fold(shifts, facts, maps, tiles, classes, before=(), after=()):
     rows, length = tiles[0].shape
     count = len(shifts)
     whole = pltpu.VMEM((count, rows, length), jnp.bfloat16)
     return pl.pallas_call(
-        functools.partial(fold_body, shifts),
+        functools.partial(fold_body, shifts, classes[0]),
         in_specs=[pl.BlockSpec(memory_space=pltpu.SMEM), pl.BlockSpec(memory_space=pltpu.VMEM)]
-        + [pl.BlockSpec(memory_space=pl.ANY)] * (len(tiles) + len(before)),
+        + [pl.BlockSpec(memory_space=pl.ANY)] * (len(tiles) + len(before) + len(after)),
         out_specs=[pl.BlockSpec(memory_space=pl.ANY), pl.BlockSpec(memory_space=pltpu.SMEM)],
         out_shape=[
-            pltpu.HBM((8, 8, rows, 128), jnp.bfloat16),
+            pltpu.HBM((8, 2 * len(classes), rows, 128), jnp.bfloat16),
             jax.ShapeDtypeStruct((1,), jnp.int32),
         ],
         scratch_shapes=[
@@ -124,7 +125,7 @@
         ),
         input_output_aliases={2 + len(tiles): 0} if before else {},
         name="fold",
-    )(facts, maps, *tiles, *before)
+    )(facts, maps, *tiles, *before, *after)
 
 
 def nothing(*refs):
@@ -171,17 +172,27 @@
     )(first, second, after)
 
 
-def ladder_body(facts, send_map, blocks, received, ladder, sent, operand, rounded, held, sem, held_sem):
+def ladder_body(classes, facts, send_map, blocks, *refs):
+    received = refs[: len(classes)]
+    ladder, sent, operand, rounded, held, sem, held_sem = refs[len(classes) :]
     length = rounded.shape[1]
     parts = held_sem.shape[0]
     depth = held.shape[0] // parts
 
-    def place(k):
+    def place(k, source=None):
+        source = received[0].at[0, 0] if source is None else source
+        return pltpu.make_async_copy(source, operand.at[:, pl.ds(k * 128, 128)], sem.at[k])
+
+    def begin(k):
         tile = facts[1 + k]
         z, ket = tile >> 3, tile & 7
-        slot = 2 * ((z - facts[0] + 8) & 3) + (z >> 2)
-        where = operand.at[:, pl.ds(k * 128, 128)]
-        return pltpu.make_async_copy(received.at[ket, slot], where, sem.at[k])
+        away = (z - facts[0] + 8) & 3
+        for held_classes, array in zip(classes, received):
+
+            @pl.when((away >= held_classes[0]) & (away <= held_classes[-1]))
+            def _():
+                slot = 2 * (away - held_classes[0]) + (z >> 2)
+                place(k, array.at[ket, slot]).start()
 
     def bring(i):
         rows = pl.ds(i * depth, depth)
@@ -190,7 +201,7 @@
     each = depth // 128
     for i in range(parts):
         for k in range(i * each, (i + 1) * each):
-            place(k).start()
+            begin(k)
         bring(i).start()
     for i in range(parts):
         for k in range(i * each, (i + 1) * each):
@@ -212,21 +223,20 @@
         sent[:, columns] = moved.astype(jnp.bfloat16)
 
 
-def ladder_of(facts, send_map, blocks, received):
+def ladder_of(facts, send_map, blocks, classes, received):
     depth, length = blocks.shape
-    rows = received.shape[2]
+    rows = received[0].shape[2]
     vmem = pl.BlockSpec(memory_space=pltpu.VMEM)
     return pl.pallas_call(
-        ladder_body,
+        functools.partial(ladder_body, classes),
         in_specs=[
             pl.BlockSpec(memory_space=pltpu.SMEM),
             vmem,
-            pl.BlockSpec(memory_space=pl.ANY),
-            pl.BlockSpec(memory_space=pl.ANY),
-        ],
+        ]
+        + [pl.BlockSpec(memory_space=pl.ANY)] * (1 + len(received)),
         out_specs=[vmem, vmem],
         out_shape=[
-            jax.ShapeDtypeStruct((rows, length), jnp.float32),
+            pltpu.HBM((rows, length), jnp.float32),
             jax.ShapeDtypeStruct((rows, length), jnp.bfloat16),
         ],
         scratch_shapes=[
@@ -236,51 +246,50 @@
             pltpu.SemaphoreType.DMA((depth // 128,)),
             pltpu.SemaphoreType.DMA((4,)),
         ],
-        compiler_params=pltpu.CompilerParams(vmem_limit_bytes=VMEM),
+        compiler_params=pltpu.CompilerParams(vmem_limit_bytes=60 * 1024 * 1024),
         cost_estimate=pl.CostEstimate(
             flops=2 * rows * depth * length,
             bytes_accessed=2 * depth * (rows + length),
             transcendentals=0,
         ),
         name="ladder",
-    )(facts, send_map, blocks, received)
+    )(facts, send_map, blocks, *received)
 
 
 def update_body(low, *refs):
-    own, ladder, partner, direction, occupied, virtual, out = refs[:7] if len(refs) == 7 else refs[:6] + refs[7:]
-    residual = ladder[...] + direction[0] * partner[...].astype(jnp.float32)
-    denominator = occupied[...] - virtual[0:1, :] - virtual[1:2, :]
-    out[...] = (own[...].astype(jnp.float32) + residual / denominator).astype(jnp.bfloat16)
-
-
-def update(low, own, ladder, partner, direction, occupied, virtual, before):
+    own, ladder, partner, direction, occupied, virtual = refs[:6]
+    out, fresh, sem = refs[-3:]
+    rows = fresh.shape[0]
+    step = 32
+    copies = []
+    for start in range(0, rows, step):
+        block = slice(start, start + step)
+        residual = ladder[block] + direction[0] * partner[block].astype(jnp.float32)
+        denominator = occupied[block] - virtual[0:1, :] - virtual[1:2, :]
+        new = own[block].astype(jnp.float32) + residual / denominator
+        fresh[block] = new.astype(jnp.bfloat16)
+        copies.append(
+            pltpu.make_async_copy(
+                fresh.at[pl.ds(start, step)], out.at[pl.ds(low + start, step)], sem.at[start // step]
+            )
+        )
+        copies[-1].start()
+    for copy in copies:
+        copy.wait()
+
+
+def update(low, total, own, ladder, partner, direction, occupied, virtual, before):
     rows, length = ladder.shape
-    step = 64
-
-    def chunk(width):
-        return pl.BlockSpec((step, width), lambda n: (n, 0))
-
-    def whole(width):
-        return pl.BlockSpec((step, width), lambda n: (n + low // step, 0))
-
+    vmem, held = pl.BlockSpec(memory_space=pltpu.VMEM), pl.BlockSpec(memory_space=pl.ANY)
     return pl.pallas_call(
         functools.partial(update_body, low),
-        grid=(rows // step,),
-        in_specs=[
-            whole(length),
-            chunk(length),
-            chunk(length),
-            pl.BlockSpec(memory_space=pltpu.SMEM),
-            whole(1),
-            pl.BlockSpec((2, length), lambda n: (0, 0)),
-        ]
-        + [pl.BlockSpec(memory_space=pl.ANY)] * len(before),
-        out_specs=whole(length),
-        out_shape=jax.ShapeDtypeStruct(own.shape, jnp.bfloat16),
+        in_specs=[vmem, vmem, vmem, pl.BlockSpec(memory_space=pltpu.SMEM), vmem, vmem]
+        + [held] * len(before),
+        out_specs=held,
+        out_shape=pltpu.HBM((total, length), jnp.bfloat16),
+        scratch_shapes=[pltpu.VMEM((rows, length), jnp.bfloat16), pltpu.SemaphoreType.DMA((rows // 32,))],
         input_output_aliases={6: 0} if before else {},
-        compiler_params=pltpu.CompilerParams(
-            vmem_limit_bytes=VMEM, dimension_semantics=("arbitrary",)
-        ),
+        compiler_params=pltpu.CompilerParams(vmem_limit_bytes=VMEM),
         cost_estimate=pl.CostEstimate(
             flops=8 * rows * length, bytes_accessed=10 * rows * length, transcendentals=0
         ),
@@ -320,33 +329,46 @@
     first = energies(vir_energy, pair_virt[0, 0])
     second = energies(vir_energy, pair_virt[0, 1])
     virtual = jnp.stack([first, second])
-    ends = (0, 192, rows)
-    steps, folds = [], []
-    for low, high in zip(ends, ends[1:]):
-        part = own[low:high]
-        if steps:
-            part = joined(part, steps[-1][2], pltpu.HBM)
+    cut = FIRST
+    everything, later, near = (0, 1, 2, 3), (1, 2, 3), (0,)
+
+    def climb(part, classes):
         one = (shifted(part, -1), shifted(part, 1))
         two = (shifted(one[0], -1), shifted(one[1], 1))
-        slots, done = fold((2,), fold_facts, maps, two, ())
+        slots, done = fold((2,), fold_facts, maps, two, classes)
         three = (shifted(two[0], -1), shifted(two[1], 1))
-        upper, lower = halves(*three, done if steps else fold_facts)
+        upper, lower = halves(*three, done)
         far = (shifted(upper, -1), shifted(lower, 1))
         odd = (one[0], three[1], three[0], one[1])
-        slots, _ = fold((1, 3), fold_facts, maps, odd, (slots,))
-        steps.append((part, one, three, far))
-        folds.append(slots)
-    fresh = ()
-    for i, (part, one, three, far) in enumerate(steps):
-        slots, _ = fold((0,), fold_facts, maps, (part, *far), (folds[i],))
-        if i + 1 < len(steps):
-            slots = joined(slots, steps[i + 1][1], pltpu.HBM)
-        received = lax.all_to_all(slots, "ket", split_axis=0, concat_axis=0, tiled=True)
-        ladder, sent = ladder_of(ladder_facts, send_map, all_blocks, received)
+        slots, _ = fold((1, 3), fold_facts, maps, odd, classes, (slots,))
+        return one, far, slots
+
+    def exchange(slots, *others):
+        slots = joined(slots, others, pltpu.HBM)
+        return lax.all_to_all(slots, "ket", split_axis=0, concat_axis=0, tiled=True)
+
+    part = own[:cut]
+    _, far, slots = climb(part, later)
+    first_received = exchange(slots, *far)
+    next_part = joined(own[cut:], far, pltpu.HBM)
+    next_one, next_far, next_slots = climb(next_part, everything)
+    slots, _ = fold((0,), fold_facts, maps, (part, *far), near, (), next_one)
+    second_received = exchange(slots, first_received)
+    next_slots, _ = fold((0,), fold_facts, maps, (next_part, *next_far), everything, (next_slots,))
+    third_received = exchange(next_slots, second_received)
+
+    work = (
+        (0, part, (later, near), (first_received, second_received)),
+        (cut, next_part, (everything,), (third_received,)),
+    )
+    before = ()
+    for low, chunk, classes, received in work:
+        ladder, sent = ladder_of(ladder_facts, send_map, all_blocks, classes, received)
         partner = shifted(sent, 4)
-        fresh = update(ends[i], own, ladder, partner, direction[None], pair_energy[:, None], virtual, fresh)
-        fresh = (fresh,)
-    return fresh[0][:, None, :]
+        occupied = pair_energy[low : low + chunk.shape[0], None]
+        new = update(low, rows, chunk, ladder, partner, direction[None], occupied, virtual, before)
+        before = (new,)
+    return new[:, None, :]
 
 
 def solution(mesh):

time: 233 us -> 233 us (level)
  the two profiles are of different devices: /device:TPU:1 before, /device:TPU:47 now
where the time goes in v6:
time: 233 us; the launch traced here: 230 us
  waiting for transfers between devices  88.5 us (38%)
  Pallas kernels  52.5 us (23%)
  starting transfers between devices  42.8 us (18%)
  local copies, waits for them, and re-layouts  15.7 us (7%)
  between operations  13.8 us (6%)
  blocking collectives  10 us (4%)
  other arithmetic  6.33 us (3%)
    ppermute x18, waiting for transfers between devices, shifted(): return lax.ppermute(block, 'bra', [(i, (i + by) % 8) for i in range(8)])  69.3 us
    pallas_call x6, Pallas kernels, fold(): pl.pallas_call(functools.partial(fold_body, shifts, classes[0]), in_specs...  28.8 us
    all_to_all x3, starting transfers between devices, exchange(): return lax.all_to_all(slots, 'ket', split_axis=0, concat_axis=0, tiled=True)  21.8 us
    ppermute x18, starting transfers between devices, shifted(): return lax.ppermute(block, 'bra', [(i, (i + by) % 8) for i in range(8)])  20.9 us
    all_to_all x3, waiting for transfers between devices, exchange(): return lax.all_to_all(slots, 'ket', split_axis=0, concat_axis=0, tiled=True)  18.5 us
    pallas_call x2, Pallas kernels, ladder_of(): pl.pallas_call(functools.partial(ladder_body, classes), in_specs=[pl.Bloc...  17.9 us
    all_gather x1, blocking collectives, local(): wanted = lax.all_gather(block_owner[0] * 16 + screen_list[0], 'ket', axis=0)  10 us
    unnamed x44, local copies, waits for them, and re-layouts  8.36 us
  transfers between devices with their start and end apart: 22, of which 13 were waited for; matrix products, arithmetic and copies ran while one was open for 6% of the time, Pallas kernels for 22%

profile of v6, /device:TPU:47, one launch (start us, length us, event | category | flops | bytes accessed | tf_op | source)
XLA Modules:
  0.0 229.6 jit_solution(4762501046758229590)
XLA Ops:
  8.0 1.7 collective-permute-start.3
  9.7 0.8 copy-done.3
  10.6 14.1 %collective-permute-done.refs_0_ = bf16[224,1536]{1,0:T(8,128)(2,1)S(1)} collective-permute-done((bf16[224,1536]{1,0:T(8,128)(2,1)S(1)}, bf16[224,1536]{1,0:T(8,128)(2,1)S(1)}, u32[]{:S(2)}, u32[]{:S(2)}) %collective-permute-start) | collective-permute-done | bytes 688160 | tf_op jit(solution)/shard_map/ppermute | solution.py:301
  24.7 2.8 %collective-permute-start.1 = (bf16[224,1536]{1,0:T(8,128)(2,1)S(1)}, bf16[224,1536]{1,0:T(8,128)(2,1)}, u32[]{:S(2)}, u32[]{:S(2)}) collective-permute-start(bf16[224,1536]{1,0:T(8,128)(2,1)S(1)} %collective-permute-done.refs_0_), channel_id=1, source_target_pairs={{0,224},{32,0},{64,32},{96,64},{128,96},{160,128},{192,160},{224,1... | collective-permute-start | bytes 2064392 | tf_op jit(solution)/shard_map/ppermute | solution.py:301
  28.3 10.0 %all-gather.1 = s32[8,1,32]{2,1,0:T(1,128)S(1)} all-gather(s32[1,1,32]{2,1,0:T(1,128)S(1)} %add_bitcast_fusion), channel_id=1, replica_groups=mesh['bra'=8,'ket'=8,'pair'=4] {'ket'}, dimensions={0}, use_global_device_ids=true | all-gather | bytes 1152 | tf_op jit(solution)/shard_map/all_gather | solution.py:317
  38.3 2.4 %collective-permute-done.1.refs_0_ = bf16[224,1536]{1,0:T(8,128)(2,1)} collective-permute-done((bf16[224,1536]{1,0:T(8,128)(2,1)S(1)}, bf16[224,1536]{1,0:T(8,128)(2,1)}, u32[]{:S(2)}, u32[]{:S(2)}) %collective-permute-start.1) | collective-permute-done | bytes 688160 | tf_op jit(solution)/shard_map/ppermute | solution.py:301
  40.7 3.4 %collective-permute-start.2 = (bf16[224,1536]{1,0:T(8,128)(2,1)}, bf16[224,1536]{1,0:T(8,128)(2,1)S(1)}, u32[]{:S(2)}, u32[]{:S(2)}) collective-permute-start(bf16[224,1536]{1,0:T(8,128)(2,1)} %collective-permute-done.1.refs_0_), channel_id=1, source_target_pairs={{0,224},{32,0},{64,32},{96,64},{128,96},{160,128},{192,160},{224,1... | collective-permute-start | bytes 2064392 | tf_op jit(solution)/shard_map/ppermute | solution.py:301
  44.1 0.8 collective-permute-done.4.refs_1_
  45.4 4.7 %fold.6 = (bf16[8,6,224,128]{3,2,1,0:T(8,128)(2,1)}, s32[1]{0:T(128)}) custom-call(s32[65]{0:T(128)S(1)} %pad_add_fusion.facts, s32[4,1,1536]{2,1,0:T(1,128)S(1)} %dynamic-slice_bitcast_fusion.maps, bf16[224,1536]{1,0:T(8,128)(2,1)} %collective-permute-done.1.refs_0_, bf16[224,1536]{1,0:T(8,128)(2,1)} %collective-permute-done.4.refs_1_), custom_call_target="tpu_custom_call" | custom-call | flops 1056964608 | bytes 2293760 | tf_op jit(solution)/shard_map/fold/pallas_call | solution.py:103
  50.1 7.6 %collective-permute-done.2.first.refs_2_ = bf16[224,1536]{1,0:T(8,128)(2,1)S(1)} collective-permute-done((bf16[224,1536]{1,0:T(8,128)(2,1)}, bf16[224,1536]{1,0:T(8,128)(2,1)S(1)}, u32[]{:S(2)}, u32[]{:S(2)}) %collective-permute-start.2) | collective-permute-done | bytes 688160 | tf_op jit(solution)/shard_map/ppermute | solution.py:301
  57.7 3.2 %collective-permute-done.5.second.refs_1_ = bf16[224,1536]{1,0:T(8,128)(2,1)S(1)} collective-permute-done((bf16[224,1536]{1,0:T(8,128)(2,1)}, bf16[224,1536]{1,0:T(8,128)(2,1)S(1)}, u32[]{:S(2)}, u32[]{:S(2)}) %collective-permute-start.5) | collective-permute-done | bytes 688160 | tf_op jit(solution)/shard_map/ppermute | solution.py:301
  60.9 0.9 halves.2
  61.8 2.5 %collective-permute-start.6 = (bf16[112,1536]{1,0:T(8,128)(2,1)S(1)}, bf16[112,1536]{1,0:T(8,128)(2,1)S(1)}, u32[]{:S(2)}, u32[]{:S(2)}) collective-permute-start(bf16[112,1536]{1,0:T(8,128)(2,1)S(1)} %get-tuple-element.22), channel_id=1, source_target_pairs={{0,224},{32,0},{64,32},{96,64},{128,96},{160,128},{192,160},{224,1... | collective-permute-start | bytes 1032200 | tf_op jit(solution)/shard_map/ppermute | solution.py:301
  64.3 6.0 %fold.11 = (bf16[8,6,224,128]{3,2,1,0:T(8,128)(2,1)}, s32[1]{0:T(128)}) custom-call(s32[65]{0:T(128)S(1)} %pad_add_fusion.facts, s32[4,1,1536]{2,1,0:T(1,128)S(1)} %dynamic-slice_bitcast_fusion.maps, bf16[224,1536]{1,0:T(8,128)(2,1)S(1)} %collective-permute-done.refs_0_, ...), custom_call_target="tpu_custom_call", output_to_operand_aliasing={{0}: (6, {})} | custom-call | flops 2113929216 | bytes 4587520 | tf_op jit(solution)/shard_map/fold/pallas_call | solution.py:103
  71.5 9.1 %all-to-all-start = ((bf16[8,6,224,128]{3,2,1,0:T(8,128)(2,1)}), bf16[8,6,224,128]{3,2,1,0:T(8,128)(2,1)S(1)}, u32[]{:S(2)}, u32[]{:S(2)}) async-start(bf16[8,6,224,128]{3,2,1,0:T(8,128)(2,1)} %joined.5), calls=%async_computation | async-start | bytes 5505024 | tf_op jit(solution)/shard_map/all_to_all | solution.py:348
  80.7 1.9 slice_bitcast_fusion.1.refs_0_
  82.6 1.0 copy-done.8
  83.6 1.2 collective-permute-start.8
  85.0 11.3 %collective-permute-done.8.refs_0_.refs_3_ = bf16[160,1536]{1,0:T(8,128)(2,1)S(1)} collective-permute-done((bf16[160,1536]{1,0:T(8,128)(2,1)}, bf16[160,1536]{1,0:T(8,128)(2,1)S(1)}, u32[]{:S(2)}, u32[]{:S(2)}) %collective-permute-start.8) | collective-permute-done | bytes 491552 | tf_op jit(solution)/shard_map/ppermute | solution.py:301
  96.3 1.2 collective-permute-start.9
  97.8 10.3 %collective-permute-done.9.refs_0_ = bf16[160,1536]{1,0:T(8,128)(2,1)} collective-permute-done((bf16[160,1536]{1,0:T(8,128)(2,1)S(1)}, bf16[160,1536]{1,0:T(8,128)(2,1)}, u32[]{:S(2)}, u32[]{:S(2)}) %collective-permute-start.9) | collective-permute-done | bytes 491552 | tf_op jit(solution)/shard_map/ppermute | solution.py:301
  108.1 1.2 collective-permute-start.10
  109.7 1.1 copy-done.4
  110.8 1.0 copy-done.9
  111.8 3.9 %fold.10 = (bf16[8,2,224,128]{3,2,1,0:T(8,128)(2,1)}, s32[1]{0:T(128)}) custom-call(s32[65]{0:T(128)S(1)} %pad_add_fusion.facts, s32[4,1,1536]{2,1,0:T(1,128)S(1)} %dynamic-slice_bitcast_fusion.maps, bf16[224,1536]{1,0:T(8,128)(2,1)S(1)} %copy-done.4, bf16[112,1536]{1,0:T(8,128)(2,1)S(1)} %collective-permute-done.6.refs_1_, bf16[112,1536]{1,0:T(8,128)(2,1)S(1)} %copy-done.9, ...), custom_call_target="tpu_custom_call" | custom-call | flops 1056964608 | bytes 2293760 | tf_op jit(solution)/shard_map/fold/pallas_call | solution.py:103
  115.7 0.8 copy-done.12
  116.5 0.8 copy-done.14
  117.3 1.5 copy-done.1
  118.8 6.9 %all-to-all-start.1 = ((bf16[8,2,224,128]{3,2,1,0:T(8,128)(2,1)}), bf16[8,2,224,128]{3,2,1,0:T(8,128)(2,1)}, u32[]{:S(2)}, u32[]{:S(2)}) async-start(bf16[8,2,224,128]{3,2,1,0:T(8,128)(2,1)} %joined.6), calls=%async_computation.1 | async-start | bytes 1835008 | tf_op jit(solution)/shard_map/all_to_all | solution.py:348
  125.7 4.3 %fold.7 = (bf16[8,8,160,128]{3,2,1,0:T(8,128)(2,1)}, s32[1]{0:T(128)}) custom-call(s32[65]{0:T(128)S(1)} %pad_add_fusion.facts, s32[4,1,1536]{2,1,0:T(1,128)S(1)} %dynamic-slice_bitcast_fusion.maps, bf16[160,1536]{1,0:T(8,128)(2,1)} %collective-permute-done.9.refs_0_, bf16[160,1536]{1,0:T(8,128)(2,1)} %collective-permute-done.12.refs_1_), custom_call_target="tpu_custom_call" | custom-call | flops 754974720 | bytes 1638400 | tf_op jit(solution)/shard_map/fold/pallas_call | solution.py:103
  130.0 1.6 halves.3
  131.6 2.7 %collective-permute-start.14 = (bf16[80,1536]{1,0:T(8,128)(2,1)S(1)}, bf16[80,1536]{1,0:T(8,128)(2,1)S(1)}, u32[]{:S(2)}, u32[]{:S(2)}) collective-permute-start(bf16[80,1536]{1,0:T(8,128)(2,1)S(1)} %get-tuple-element.25), channel_id=1, source_target_pairs={{0,224},{32,0},{64,32},{96,64},{128,96},{160,128},{192,160},{224,1... | collective-permute-start | bytes 737288 | tf_op jit(solution)/shard_map/ppermute | solution.py:301
  134.3 5.8 %fold.8 = (bf16[8,8,160,128]{3,2,1,0:T(8,128)(2,1)}, s32[1]{0:T(128)}) custom-call(s32[65]{0:T(128)S(1)} %pad_add_fusion.facts, s32[4,1,1536]{2,1,0:T(1,128)S(1)} %dynamic-slice_bitcast_fusion.maps, bf16[160,1536]{1,0:T(8,128)(2,1)S(1)} %copy-done.13, bf16[160,1536]{1,0:T(8,128)(2,1)} %collective-permute-done.13.second.refs_1_, ...), custom_call_target="tpu_custom_call", output_to_operand_aliasing={{0}: (6, {})} | custom-call | flops 1509949440 | bytes 3276800 | tf_op jit(solution)/shard_map/fold/pallas_call | solution.py:103
  140.2 2.8 %collective-permute-done.15.refs_2_ = bf16[80,1536]{1,0:T(8,128)(2,1)S(1)} collective-permute-done((bf16[80,1536]{1,0:T(8,128)(2,1)S(1)}, bf16[80,1536]{1,0:T(8,128)(2,1)S(1)}, u32[]{:S(2)}, u32[]{:S(2)}) %collective-permute-start.15) | collective-permute-done | bytes 245792 | tf_op jit(solution)/shard_map/ppermute | solution.py:301
  143.0 4.1 %fold.9 = (bf16[8,8,160,128]{3,2,1,0:T(8,128)(2,1)}, s32[1]{0:T(128)}) custom-call(s32[65]{0:T(128)S(1)} %pad_add_fusion.facts, s32[4,1,1536]{2,1,0:T(1,128)S(1)} %dynamic-slice_bitcast_fusion.maps, bf16[160,1536]{1,0:T(8,128)(2,1)S(1)} %copy-done.2, bf16[80,1536]{1,0:T(8,128)(2,1)S(1)} %collective-permute-done.14.refs_1_, ...), custom_call_target="tpu_custom_call", output_to_operand_aliasing={{0}: (5, {})} | custom-call | flops 754974720 | bytes 1638400 | tf_op jit(solution)/shard_map/fold/pallas_call | solution.py:103
  147.1 5.8 %all-to-all-start.2 = ((bf16[8,8,160,128]{3,2,1,0:T(8,128)(2,1)}), bf16[8,8,160,128]{3,2,1,0:T(8,128)(2,1)}, u32[]{:S(2)}, u32[]{:S(2)}) async-start(bf16[8,8,160,128]{3,2,1,0:T(8,128)(2,1)} %joined.7), calls=%async_computation.2 | async-start | bytes 5242880 | tf_op jit(solution)/shard_map/all_to_all | solution.py:348
  154.2 9.3 %ladder.3 = (f32[224,1536]{1,0:T(8,128)}, bf16[224,1536]{1,0:T(8,128)(2,1)}) custom-call(s32[33]{0:T(128)} %pad_add_fusion.1.facts, s32[1,1536]{1,0:T(1,128)} %constant_dynamic-slice_fusion.send_map, bf16[4096,1536]{1,0:T(8,128)(2,1)} %bitcast.20, bf16[8,6,224,128]{3,2,1,0:T(8,128)(2,1)} %copy-done.1, bf16[8,2,224,128]{3,2,1,0:T(8,128)(2,1)} %all-to-all-done.1.refs_1_), custom_call_target="tpu_custom_call" | custom-call | flops 2818572288 | bytes 14417920 | tf_op jit(solution)/shard_map/ladder/pallas_call | solution.py:230
  163.6 1.8 collective-permute-start.17
  165.4 18.5 %all-to-all-done.2.refs_0_ = bf16[8,8,160,128]{3,2,1,0:T(8,128)(2,1)} async-done(((bf16[8,8,160,128]{3,2,1,0:T(8,128)(2,1)}), bf16[8,8,160,128]{3,2,1,0:T(8,128)(2,1)}, u32[]{:S(2)}, u32[]{:S(2)}) %all-to-all-start.2) | async-done | bytes 2621472 | tf_op jit(solution)/shard_map/all_to_all | solution.py:348
  183.9 8.6 %ladder.2 = (f32[160,1536]{1,0:T(8,128)}, bf16[160,1536]{1,0:T(8,128)(2,1)}) custom-call(s32[33]{0:T(128)} %pad_add_fusion.1.facts, s32[1,1536]{1,0:T(1,128)} %constant_dynamic-slice_fusion.send_map, bf16[4096,1536]{1,0:T(8,128)(2,1)} %bitcast.21, bf16[8,8,160,128]{3,2,1,0:T(8,128)(2,1)} %all-to-all-done.2.refs_0_), custom_call_target="tpu_custom_call" | custom-call | flops 2013265920 | bytes 13893632 | tf_op jit(solution)/shard_map/ladder/pallas_call | solution.py:230
  192.5 1.8 collective-permute-start.16
  194.3 4.5 %select_reduce_fusion.1 = (f32[1536]{0:T(1024)S(1)}, f32[1536]{0:T(1024)S(1)}) fusion(f32[2048]{0:T(1024)S(1)} %copy-done.19, s32[1536]{0:T(1024)S(1)} %get-tuple-element.37, s32[1536]{0:T(1024)S(1)} %get-tuple-element.38), kind=kLoop, calls=%fused_computation.2 | loop fusion | flops 18871296 | bytes 32768 | tf_op jit(solution)/shard_map/reduce_sum | solution.py:306
  201.3 0.8 copy.23.refs_4_
  202.1 1.4 copy.24.refs_4_
  203.5 0.8 pad_maximum_fusion.refs_5_
  204.3 2.3 %update.2.refs_6_ = bf16[384,1536]{1,0:T(8,128)(2,1)} custom-call(bf16[224,1536]{1,0:T(8,128)(2,1)S(1)} %copy-done.5, f32[224,1536]{1,0:T(8,128)S(1)} %copy-done.6, bf16[224,1536]{1,0:T(8,128)(2,1)} %collective-permute-done.17.refs_2_, f32[1]{0:T(128)} %bitcast.11.refs_3_, f32[224,1]{1,0:T(8,128)S(1)} %copy.23.refs_4_, f32[2,1536]{1,0:T(2,128)S(1)} %pad_maximum_fusion.refs_5_), custom_call_target="tpu_custom_call" | custom-call | flops 2752512 | bytes 3440640 | tf_op jit(solution)/shard_map/update/pallas_call | solution.py:284
  206.6 15.0 %collective-permute-done.16.refs_2_ = bf16[160,1536]{1,0:T(8,128)(2,1)S(1)} collective-permute-done((bf16[160,1536]{1,0:T(8,128)(2,1)}, bf16[160,1536]{1,0:T(8,128)(2,1)S(1)}, u32[]{:S(2)}, u32[]{:S(2)}) %collective-permute-start.16) | collective-permute-done | bytes 491552 | tf_op jit(solution)/shard_map/ppermute | solution.py:301
  221.7 1.0 update.3
  (78 shorter events, 8.6 us)
Async XLA Ops:
  6.5 38.9 %copy-start = (s32[64,1536]{1,0:T(8,128)S(1)}, s32[64,1536]{1,0:T(8,128)}, u32[]{:S(2)}) copy-start(s32[64,1536]{1,0:T(8,128)} %param.12) | copy-start | bytes 1179652
  6.5 1.3 copy-start.16
  6.5 21.7 %copy-start.20 = (s32[1,32]{1,0:T(1,128)S(1)}, s32[1,32]{1,0:T(1,128)}, u32[]{:S(2)}) copy-start(s32[1,32]{1,0:T(1,128)} %param.10) | copy-start | bytes 388
  6.5 21.7 %copy-start.21 = (s32[1,32]{1,0:T(1,128)S(1)}, s32[1,32]{1,0:T(1,128)}, u32[]{:S(2)}) copy-start(s32[1,32]{1,0:T(1,128)} %param.11) | copy-start | bytes 388
  6.5 147.7 %all-gather.4.cloned.1.call-start = ((), (), s32[]{:S(2)}) async-start(), calls=%async_computation.3 | async-start | bytes 15728640 | tf_op jit(solution)/shard_map/all_gather | solution.py:315
  7.9 16.8 %collective-permute-start = (bf16[224,1536]{1,0:T(8,128)(2,1)S(1)}, bf16[224,1536]{1,0:T(8,128)(2,1)S(1)}, u32[]{:S(2)}, u32[]{:S(2)}) collective-permute-start(bf16[224,1536]{1,0:T(8,128)(2,1)S(1)} %slice_bitcast_fusion.refs_0_), channel_id=1, source_target_pairs={{0,224},{32,0},{64,32},{96,64},{128,96},{160,128},{192,160},{224,1... | collective-permute-start | bytes 2064392 | tf_op jit(solution)/shard_map/ppermute | solution.py:301
  8.0 20.2 %collective-permute-start.3 = (bf16[224,1536]{1,0:T(8,128)(2,1)S(1)}, bf16[224,1536]{1,0:T(8,128)(2,1)S(1)}, u32[]{:S(2)}, u32[]{:S(2)}) collective-permute-start(bf16[224,1536]{1,0:T(8,128)(2,1)S(1)} %slice_bitcast_fusion.refs_0_), channel_id=1, source_target_pairs={{0,32},{32,64},{64,96},{96,128},{128,160},{160,192},{192,224},{224... | collective-permute-start | bytes 2064392 | tf_op jit(solution)/shard_map/ppermute | solution.py:301
  9.7 0.8 copy-start.3
  24.7 16.0 %collective-permute-start.1 = (bf16[224,1536]{1,0:T(8,128)(2,1)S(1)}, bf16[224,1536]{1,0:T(8,128)(2,1)}, u32[]{:S(2)}, u32[]{:S(2)}) collective-permute-start(bf16[224,1536]{1,0:T(8,128)(2,1)S(1)} %collective-permute-done.refs_0_), channel_id=1, source_target_pairs={{0,224},{32,0},{64,32},{96,64},{128,96},{160,128},{192,160},{224,1... | collective-permute-start | bytes 2064392 | tf_op jit(solution)/shard_map/ppermute | solution.py:301
  28.2 16.7 %collective-permute-start.4 = (bf16[224,1536]{1,0:T(8,128)(2,1)S(1)}, bf16[224,1536]{1,0:T(8,128)(2,1)}, u32[]{:S(2)}, u32[]{:S(2)}) collective-permute-start(bf16[224,1536]{1,0:T(8,128)(2,1)S(1)} %collective-permute-done.3.refs_3_), channel_id=1, source_target_pairs={{0,32},{32,64},{64,96},{96,128},{128,160},{160,192},{192,224},{224... | collective-permute-start | bytes 2064392 | tf_op jit(solution)/shard_map/ppermute | solution.py:301
  40.7 17.0 %collective-permute-start.2 = (bf16[224,1536]{1,0:T(8,128)(2,1)}, bf16[224,1536]{1,0:T(8,128)(2,1)S(1)}, u32[]{:S(2)}, u32[]{:S(2)}) collective-permute-start(bf16[224,1536]{1,0:T(8,128)(2,1)} %collective-permute-done.1.refs_0_), channel_id=1, source_target_pairs={{0,224},{32,0},{64,32},{96,64},{128,96},{160,128},{192,160},{224,1... | collective-permute-start | bytes 2064392 | tf_op jit(solution)/shard_map/ppermute | solution.py:301
  44.9 16.0 %collective-permute-start.5 = (bf16[224,1536]{1,0:T(8,128)(2,1)}, bf16[224,1536]{1,0:T(8,128)(2,1)S(1)}, u32[]{:S(2)}, u32[]{:S(2)}) collective-permute-start(bf16[224,1536]{1,0:T(8,128)(2,1)} %collective-permute-done.4.refs_1_), channel_id=1, source_target_pairs={{0,32},{32,64},{64,96},{96,128},{128,160},{160,192},{192,224},{224... | collective-permute-start | bytes 2064392 | tf_op jit(solution)/shard_map/ppermute | solution.py:301
  61.8 8.4 %collective-permute-start.6 = (bf16[112,1536]{1,0:T(8,128)(2,1)S(1)}, bf16[112,1536]{1,0:T(8,128)(2,1)S(1)}, u32[]{:S(2)}, u32[]{:S(2)}) collective-permute-start(bf16[112,1536]{1,0:T(8,128)(2,1)S(1)} %get-tuple-element.22), channel_id=1, source_target_pairs={{0,224},{32,0},{64,32},{96,64},{128,96},{160,128},{192,160},{224,1... | collective-permute-start | bytes 1032200 | tf_op jit(solution)/shard_map/ppermute | solution.py:301
  64.3 6.5 %collective-permute-start.7 = (bf16[112,1536]{1,0:T(8,128)(2,1)S(1)}, bf16[112,1536]{1,0:T(8,128)(2,1)S(1)}, u32[]{:S(2)}, u32[]{:S(2)}) collective-permute-start(bf16[112,1536]{1,0:T(8,128)(2,1)S(1)} %get-tuple-element.23), channel_id=1, source_target_pairs={{0,32},{32,64},{64,96},{96,128},{128,160},{160,192},{192,224},{224... | collective-permute-start | bytes 1032200 | tf_op jit(solution)/shard_map/ppermute | solution.py:301
  70.8 0.7 copy-start.7
  71.5 45.7 %all-to-all-start = ((bf16[8,6,224,128]{3,2,1,0:T(8,128)(2,1)}), bf16[8,6,224,128]{3,2,1,0:T(8,128)(2,1)S(1)}, u32[]{:S(2)}, u32[]{:S(2)}) async-start(bf16[8,6,224,128]{3,2,1,0:T(8,128)(2,1)} %joined.5), calls=%async_computation | async-start | bytes 5505024 | tf_op jit(solution)/shard_map/all_to_all | solution.py:348
  82.6 1.0 copy-start.8
  83.6 12.8 %collective-permute-start.8 = (bf16[160,1536]{1,0:T(8,128)(2,1)}, bf16[160,1536]{1,0:T(8,128)(2,1)S(1)}, u32[]{:S(2)}, u32[]{:S(2)}) collective-permute-start(bf16[160,1536]{1,0:T(8,128)(2,1)} %joined.4.refs_0_), channel_id=1, source_target_pairs={{0,224},{32,0},{64,32},{96,64},{128,96},{160,128},{192,160},{224,1... | collective-permute-start | bytes 1474568 | tf_op jit(solution)/shard_map/ppermute | solution.py:301
  84.8 12.8 %collective-permute-start.11 = (bf16[160,1536]{1,0:T(8,128)(2,1)}, bf16[160,1536]{1,0:T(8,128)(2,1)S(1)}, u32[]{:S(2)}, u32[]{:S(2)}) collective-permute-start(bf16[160,1536]{1,0:T(8,128)(2,1)} %joined.4.refs_0_), channel_id=1, source_target_pairs={{0,32},{32,64},{64,96},{96,128},{128,160},{160,192},{192,224},{224... | collective-permute-start | bytes 1474568 | tf_op jit(solution)/shard_map/ppermute | solution.py:301
  96.3 11.7 %collective-permute-start.9 = (bf16[160,1536]{1,0:T(8,128)(2,1)S(1)}, bf16[160,1536]{1,0:T(8,128)(2,1)}, u32[]{:S(2)}, u32[]{:S(2)}) collective-permute-start(bf16[160,1536]{1,0:T(8,128)(2,1)S(1)} %collective-permute-done.8.refs_0_.refs_3_), channel_id=1, source_target_pairs={{0,224},{32,0},{64,32},{96,64},{128,96},{160,128},{192,160},{224,1... | collective-permute-start | bytes 1474568 | tf_op jit(solution)/shard_map/ppermute | solution.py:301
  97.5 12.2 %collective-permute-start.12 = (bf16[160,1536]{1,0:T(8,128)(2,1)S(1)}, bf16[160,1536]{1,0:T(8,128)(2,1)}, u32[]{:S(2)}, u32[]{:S(2)}) collective-permute-start(bf16[160,1536]{1,0:T(8,128)(2,1)S(1)} %collective-permute-done.11.refs_3_.refs_4_), channel_id=1, source_target_pairs={{0,32},{32,64},{64,96},{96,128},{128,160},{160,192},{192,224},{224... | collective-permute-start | bytes 1474568 | tf_op jit(solution)/shard_map/ppermute | solution.py:301
  108.1 21.9 %collective-permute-start.10 = (bf16[160,1536]{1,0:T(8,128)(2,1)}, bf16[160,1536]{1,0:T(8,128)(2,1)}, u32[]{:S(2)}, u32[]{:S(2)}) collective-permute-start(bf16[160,1536]{1,0:T(8,128)(2,1)} %collective-permute-done.9.refs_0_), channel_id=1, source_target_pairs={{0,224},{32,0},{64,32},{96,64},{128,96},{160,128},{192,160},{224,1... | collective-permute-start | bytes 1474568 | tf_op jit(solution)/shard_map/ppermute | solution.py:301
  109.7 20.3 %collective-permute-start.13 = (bf16[160,1536]{1,0:T(8,128)(2,1)}, bf16[160,1536]{1,0:T(8,128)(2,1)}, u32[]{:S(2)}, u32[]{:S(2)}) collective-permute-start(bf16[160,1536]{1,0:T(8,128)(2,1)} %collective-permute-done.12.refs_1_), channel_id=1, source_target_pairs={{0,32},{32,64},{64,96},{96,128},{128,160},{160,192},{192,224},{224... | collective-permute-start | bytes 1474568 | tf_op jit(solution)/shard_map/ppermute | solution.py:301
  109.7 1.1 copy-start.4
  110.8 1.0 copy-start.9
  115.7 0.8 copy-start.12
  116.5 0.8 copy-start.14
  117.3 1.5 copy-start.1
  118.8 28.3 %all-to-all-start.1 = ((bf16[8,2,224,128]{3,2,1,0:T(8,128)(2,1)}), bf16[8,2,224,128]{3,2,1,0:T(8,128)(2,1)}, u32[]{:S(2)}, u32[]{:S(2)}) async-start(bf16[8,2,224,128]{3,2,1,0:T(8,128)(2,1)} %joined.6), calls=%async_computation.1 | async-start | bytes 1835008 | tf_op jit(solution)/shard_map/all_to_all | solution.py:348
  125.7 8.6 %copy-start.13 = (bf16[160,1536]{1,0:T(8,128)(2,1)S(1)}, bf16[160,1536]{1,0:T(8,128)(2,1)}, u32[]{:S(2)}) copy-start(bf16[160,1536]{1,0:T(8,128)(2,1)} %copy-done.12) | copy-start | bytes 1474564
  125.7 8.6 %copy-start.15 = (bf16[160,1536]{1,0:T(8,128)(2,1)S(1)}, bf16[160,1536]{1,0:T(8,128)(2,1)}, u32[]{:S(2)}) copy-start(bf16[160,1536]{1,0:T(8,128)(2,1)} %copy-done.14) | copy-start | bytes 1474564
  131.6 8.5 %collective-permute-start.14 = (bf16[80,1536]{1,0:T(8,128)(2,1)S(1)}, bf16[80,1536]{1,0:T(8,128)(2,1)S(1)}, u32[]{:S(2)}, u32[]{:S(2)}) collective-permute-start(bf16[80,1536]{1,0:T(8,128)(2,1)S(1)} %get-tuple-element.25), channel_id=1, source_target_pairs={{0,224},{32,0},{64,32},{96,64},{128,96},{160,128},{192,160},{224,1... | collective-permute-start | bytes 737288 | tf_op jit(solution)/shard_map/ppermute | solution.py:301
  134.3 8.7 %collective-permute-start.15 = (bf16[80,1536]{1,0:T(8,128)(2,1)S(1)}, bf16[80,1536]{1,0:T(8,128)(2,1)S(1)}, u32[]{:S(2)}, u32[]{:S(2)}) collective-permute-start(bf16[80,1536]{1,0:T(8,128)(2,1)S(1)} %get-tuple-element.26), channel_id=1, source_target_pairs={{0,32},{32,64},{64,96},{96,128},{128,160},{160,192},{192,224},{224... | collective-permute-start | bytes 737288 | tf_op jit(solution)/shard_map/ppermute | solution.py:301
  134.3 8.7 %copy-start.2 = (bf16[160,1536]{1,0:T(8,128)(2,1)S(1)}, bf16[160,1536]{1,0:T(8,128)(2,1)}, u32[]{:S(2)}) copy-start(bf16[160,1536]{1,0:T(8,128)(2,1)} %joined.4.refs_0_) | copy-start | bytes 1474564
  147.1 6.4 %copy-start.17 = (s32[1,2,1536]{2,1,0:T(2,128)S(1)}, s32[1,2,1536]{2,1,0:T(2,128)}, u32[]{:S(2)}) copy-start(s32[1,2,1536]{2,1,0:T(2,128)} %param.13) | copy-start | bytes 36868
  147.1 36.8 %all-to-all-start.2 = ((bf16[8,8,160,128]{3,2,1,0:T(8,128)(2,1)}), bf16[8,8,160,128]{3,2,1,0:T(8,128)(2,1)}, u32[]{:S(2)}, u32[]{:S(2)}) async-start(bf16[8,8,160,128]{3,2,1,0:T(8,128)(2,1)} %joined.7), calls=%async_computation.2 | async-start | bytes 5242880 | tf_op jit(solution)/shard_map/all_to_all | solution.py:348
  163.5 30.7 %copy-start.19 = (f32[2048]{0:T(1024)S(1)}, f32[2048]{0:T(1024)}, u32[]{:S(2)}) copy-start(f32[2048]{0:T(1024)} %param.14) | copy-start | bytes 24580
  163.5 35.3 %copy-start.18 = (f32[384]{0:T(512)S(1)}, f32[384]{0:T(512)}, u32[]{:S(2)}) copy-start(f32[384]{0:T(512)} %param.15) | copy-start | bytes 4612
  163.6 40.7 %copy-start.5 = (bf16[224,1536]{1,0:T(8,128)(2,1)S(1)}, bf16[224,1536]{1,0:T(8,128)(2,1)}, u32[]{:S(2)}) copy-start(bf16[224,1536]{1,0:T(8,128)(2,1)} %copy-done.3) | copy-start | bytes 2064388
  163.6 40.7 %copy-start.6 = (f32[224,1536]{1,0:T(8,128)S(1)}, f32[224,1536]{1,0:T(8,128)}, u32[]{:S(2)}) copy-start(f32[224,1536]{1,0:T(8,128)} %get-tuple-element.35.refs_1_) | copy-start | bytes 4128772
  163.6 40.7 %collective-permute-start.17 = (bf16[224,1536]{1,0:T(8,128)(2,1)}, bf16[224,1536]{1,0:T(8,128)(2,1)}, u32[]{:S(2)}, u32[]{:S(2)}) collective-permute-start(bf16[224,1536]{1,0:T(8,128)(2,1)} %get-tuple-element.36), channel_id=1, source_target_pairs={{0,128},{32,160},{64,192},{96,224},{128,0},{160,32},{192,64},{224,... | collective-permute-start | bytes 2064392 | tf_op jit(solution)/shard_map/ppermute | solution.py:301
  192.5 29.2 %collective-permute-start.16 = (bf16[160,1536]{1,0:T(8,128)(2,1)}, bf16[160,1536]{1,0:T(8,128)(2,1)S(1)}, u32[]{:S(2)}, u32[]{:S(2)}) collective-permute-start(bf16[160,1536]{1,0:T(8,128)(2,1)} %get-tuple-element.34), channel_id=1, source_target_pairs={{0,128},{32,160},{64,192},{96,224},{128,0},{160,32},{192,64},{224,... | collective-permute-start | bytes 1474568 | tf_op jit(solution)/shard_map/ppermute | solution.py:301
  203.5 18.2 %copy-start.10 = (f32[160,1536]{1,0:T(8,128)S(1)}, f32[160,1536]{1,0:T(8,128)}, u32[]{:S(2)}) copy-start(f32[160,1536]{1,0:T(8,128)} %get-tuple-element.33.refs_1_) | copy-start | bytes 2949124
  203.5 18.2 %copy-start.11 = (f32[160,1]{1,0:T(8,128)S(1)}, f32[160,1]{1,0:T(8,128)}, u32[]{:S(2)}) copy-start(f32[160,1]{1,0:T(8,128)} %copy.24.refs_4_) | copy-start | bytes 1924
Sparse Core Ops, SparseCore 0:
  9.2 122.7 all-gather.3

commit v7 on v6

--- a/solution.py
+++ b/solution.py
@@ -8,7 +8,7 @@
 from jax.sharding import PartitionSpec as P
 
 COLS = 256
-FIRST = 224
+FIRST = 256
 VMEM = 40 * 1024 * 1024
 
 
@@ -96,7 +96,7 @@
                     ).wait()
 
 
-def fold(shifts, facts, maps, tiles, classes, before=(), after=()):
+def fold(shifts, facts, maps, tiles, classes, before=(), after=(), weight=1):
     rows, length = tiles[0].shape
     count = len(shifts)
     whole = pltpu.VMEM((count, rows, length), jnp.bfloat16)
@@ -119,7 +119,7 @@
         ],
         compiler_params=pltpu.CompilerParams(vmem_limit_bytes=VMEM),
         cost_estimate=pl.CostEstimate(
-            flops=2 * count * rows * length * length,
+            flops=weight * 2 * count * rows * length * length,
             bytes_accessed=count * rows * (4 * length + 16 * 256),
             transcendentals=0,
         ),
@@ -332,29 +332,30 @@
     cut = FIRST
     everything, later, near = (0, 1, 2, 3), (1, 2, 3), (0,)
 
-    def climb(part, classes):
+    def climb(part, classes, weight):
         one = (shifted(part, -1), shifted(part, 1))
         two = (shifted(one[0], -1), shifted(one[1], 1))
-        slots, done = fold((2,), fold_facts, maps, two, classes)
+        slots, done = fold((2,), fold_facts, maps, two, classes, weight=weight)
         three = (shifted(two[0], -1), shifted(two[1], 1))
         upper, lower = halves(*three, done)
         far = (shifted(upper, -1), shifted(lower, 1))
         odd = (one[0], three[1], three[0], one[1])
-        slots, _ = fold((1, 3), fold_facts, maps, odd, classes, (slots,))
-        return one, far, slots
+        slots, _ = fold((1, 3), fold_facts, maps, odd, classes, (slots,), weight=weight)
+        return one, three, far, slots
 
     def exchange(slots, *others):
-        slots = joined(slots, others, pltpu.HBM)
+        if others:
+            slots = joined(slots, others, pltpu.HBM)
         return lax.all_to_all(slots, "ket", split_axis=0, concat_axis=0, tiled=True)
 
     part = own[:cut]
-    _, far, slots = climb(part, later)
-    first_received = exchange(slots, *far)
-    next_part = joined(own[cut:], far, pltpu.HBM)
-    next_one, next_far, next_slots = climb(next_part, everything)
+    _, three, far, slots = climb(part, later, 1)
+    first_received = exchange(slots)
+    next_part = joined(own[cut:], three, pltpu.HBM)
+    next_one, _, next_far, next_slots = climb(next_part, everything, 8)
     slots, _ = fold((0,), fold_facts, maps, (part, *far), near, (), next_one)
     second_received = exchange(slots, first_received)
-    next_slots, _ = fold((0,), fold_facts, maps, (next_part, *next_far), everything, (next_slots,))
+    next_slots, _ = fold((0,), fold_facts, maps, (next_part, *next_far), everything, (next_slots,), weight=8)
     third_received = exchange(next_slots, second_received)
 
     work = (

time: 233 us -> 239 us (1.026)
  waiting for transfers between devices: 88.5 us -> 96 us
  starting transfers between devices: 42.8 us -> 46.3 us
  local copies, waits for them, and re-layouts: 15.7 us -> 13.1 us
    ppermute x18, waiting for transfers between devices: 69.3 us -> 87.7 us  [shifted(): return lax.ppermute(block, 'bra', [(i, (i + by) % 8) for i in range(8)])]
    all_to_all x3, waiting for transfers between devices: 18.5 us -> 7.66 us  [exchange(): return lax.all_to_all(slots, 'ket', split_axis=0, concat_axis=0, tiled=True)]
    ppermute x18, starting transfers between devices: 20.9 us -> 25.5 us  [shifted(): return lax.ppermute(block, 'bra', [(i, (i + by) % 8) for i in range(8)])]
    unnamed x44 -> x58, local copies, waits for them, and re-layouts: 8.36 us -> 10.2 us
  transfers between devices with their start and end apart: 22 -> 22, of which waited for: 13 -> 14; matrix products, arithmetic and copies ran while one was open for 6% -> 4% of each run, Pallas kernels for 22% -> 21%
where the time goes in v7:
time: 239 us; the launch traced here: 237 us
  waiting for transfers between devices  96 us (40%)
  Pallas kernels  52 us (22%)
  starting transfers between devices  46.3 us (19%)
  between operations  13.8 us (6%)
  local copies, waits for them, and re-layouts  13.1 us (5%)
  blocking collectives  9.94 us (4%)
  other arithmetic  5.58 us (2%)
    ppermute x18, waiting for transfers between devices, shifted(): return lax.ppermute(block, 'bra', [(i, (i + by) % 8) for i in range(8)])  87.7 us
    pallas_call x6, Pallas kernels, fold(): pl.pallas_call(functools.partial(fold_body, shifts, classes[0]), in_specs...  27.1 us
    ppermute x18, starting transfers between devices, shifted(): return lax.ppermute(block, 'bra', [(i, (i + by) % 8) for i in range(8)])  25.5 us
    all_to_all x3, starting transfers between devices, exchange(): return lax.all_to_all(slots, 'ket', split_axis=0, concat_axis=0, tiled=True)  20.7 us
    pallas_call x2, Pallas kernels, ladder_of(): pl.pallas_call(functools.partial(ladder_body, classes), in_specs=[pl.Bloc...  17.9 us
    unnamed x58, local copies, waits for them, and re-layouts  10.2 us
    all_gather x1, blocking collectives, local(): wanted = lax.all_gather(block_owner[0] * 16 + screen_list[0], 'ket', axis=0)  9.94 us
    all_to_all x3, waiting for transfers between devices, exchange(): return lax.all_to_all(slots, 'ket', split_axis=0, concat_axis=0, tiled=True)  7.66 us
  transfers between devices with their start and end apart: 22, of which 14 were waited for; matrix products, arithmetic and copies ran while one was open for 4% of the time, Pallas kernels for 21%

profile of v7, /device:TPU:47, one launch (start us, length us, event | category | flops | bytes accessed | tf_op | source)
XLA Modules:
  0.0 236.7 jit_solution(5889960312959093932)
XLA Ops:
  8.0 1.7 collective-permute-start.3
  9.7 0.9 copy-done.7
  10.6 16.2 %collective-permute-done.refs_0_ = bf16[256,1536]{1,0:T(8,128)(2,1)S(1)} collective-permute-done((bf16[256,1536]{1,0:T(8,128)(2,1)S(1)}, bf16[256,1536]{1,0:T(8,128)(2,1)S(1)}, u32[]{:S(2)}, u32[]{:S(2)}) %collective-permute-start) | collective-permute-done | bytes 786464 | tf_op jit(solution)/shard_map/ppermute | solution.py:301
  26.8 2.8 %collective-permute-start.1 = (bf16[256,1536]{1,0:T(8,128)(2,1)S(1)}, bf16[256,1536]{1,0:T(8,128)(2,1)}, u32[]{:S(2)}, u32[]{:S(2)}) collective-permute-start(bf16[256,1536]{1,0:T(8,128)(2,1)S(1)} %collective-permute-done.refs_0_), channel_id=1, source_target_pairs={{0,224},{32,0},{64,32},{96,64},{128,96},{160,128},{192,160},{224,1... | collective-permute-start | bytes 2359304 | tf_op jit(solution)/shard_map/ppermute | solution.py:301
  30.5 9.9 %all-gather.1 = s32[8,1,32]{2,1,0:T(1,128)S(1)} all-gather(s32[1,1,32]{2,1,0:T(1,128)S(1)} %add_bitcast_fusion), channel_id=1, replica_groups=mesh['bra'=8,'ket'=8,'pair'=4] {'ket'}, dimensions={0}, use_global_device_ids=true | all-gather | bytes 1152 | tf_op jit(solution)/shard_map/all_gather | solution.py:317
  40.4 4.5 %collective-permute-done.1.refs_0_ = bf16[256,1536]{1,0:T(8,128)(2,1)} collective-permute-done((bf16[256,1536]{1,0:T(8,128)(2,1)S(1)}, bf16[256,1536]{1,0:T(8,128)(2,1)}, u32[]{:S(2)}, u32[]{:S(2)}) %collective-permute-start.1) | collective-permute-done | bytes 786464 | tf_op jit(solution)/shard_map/ppermute | solution.py:301
  44.9 3.4 %collective-permute-start.2 = (bf16[256,1536]{1,0:T(8,128)(2,1)}, bf16[256,1536]{1,0:T(8,128)(2,1)S(1)}, u32[]{:S(2)}, u32[]{:S(2)}) collective-permute-start(bf16[256,1536]{1,0:T(8,128)(2,1)} %collective-permute-done.1.refs_0_), channel_id=1, source_target_pairs={{0,224},{32,0},{64,32},{96,64},{128,96},{160,128},{192,160},{224,1... | collective-permute-start | bytes 2359304 | tf_op jit(solution)/shard_map/ppermute | solution.py:301
  48.3 0.8 collective-permute-done.4.refs_1_
  49.6 5.1 %fold.9 = (bf16[8,6,256,128]{3,2,1,0:T(8,128)(2,1)}, s32[1]{0:T(128)}) custom-call(s32[65]{0:T(128)S(1)} %pad_add_fusion.1.facts, s32[4,1,1536]{2,1,0:T(1,128)S(1)} %dynamic-slice_bitcast_fusion.maps, bf16[256,1536]{1,0:T(8,128)(2,1)} %collective-permute-done.1.refs_0_, bf16[256,1536]{1,0:T(8,128)(2,1)} %collective-permute-done.4.refs_1_), custom_call_target="tpu_custom_call" | custom-call | flops 1207959552 | bytes 2621440 | tf_op jit(solution)/shard_map/fold/pallas_call | solution.py:103
  54.8 9.3 %collective-permute-done.2.refs_1_.first.refs_2_ = bf16[256,1536]{1,0:T(8,128)(2,1)S(1)} collective-permute-done((bf16[256,1536]{1,0:T(8,128)(2,1)}, bf16[256,1536]{1,0:T(8,128)(2,1)S(1)}, u32[]{:S(2)}, u32[]{:S(2)}) %collective-permute-start.2) | collective-permute-done | bytes 786464 | tf_op jit(solution)/shard_map/ppermute | solution.py:301
  64.1 3.2 %collective-permute-done.5.refs_2_.second.refs_1_ = bf16[256,1536]{1,0:T(8,128)(2,1)S(1)} collective-permute-done((bf16[256,1536]{1,0:T(8,128)(2,1)}, bf16[256,1536]{1,0:T(8,128)(2,1)S(1)}, u32[]{:S(2)}, u32[]{:S(2)}) %collective-permute-start.5) | collective-permute-done | bytes 786464 | tf_op jit(solution)/shard_map/ppermute | solution.py:301
  67.2 5.6 %fold.11 = (bf16[8,6,256,128]{3,2,1,0:T(8,128)(2,1)}, s32[1]{0:T(128)}) custom-call(s32[65]{0:T(128)S(1)} %pad_add_fusion.1.facts, s32[4,1,1536]{2,1,0:T(1,128)S(1)} %dynamic-slice_bitcast_fusion.maps, bf16[256,1536]{1,0:T(8,128)(2,1)S(1)} %collective-permute-done.refs_0_, ...), custom_call_target="tpu_custom_call", output_to_operand_aliasing={{0}: (6, {})} | custom-call | flops 2415919104 | bytes 5242880 | tf_op jit(solution)/shard_map/fold/pallas_call | solution.py:103
  72.9 7.7 %all-to-all-start = ((bf16[8,6,256,128]{3,2,1,0:T(8,128)(2,1)}), bf16[8,6,256,128]{3,2,1,0:T(8,128)(2,1)S(1)}, u32[]{:S(2)}, u32[]{:S(2)}) async-start(bf16[8,6,256,128]{3,2,1,0:T(8,128)(2,1)} %get-tuple-element.32), calls=%async_computation | async-start | bytes 6291456 | tf_op jit(solution)/shard_map/all_to_all | solution.py:349
  80.6 1.8 slice_bitcast_fusion.1.refs_0_
  82.4 1.1 copy-done.4
  83.6 1.1 copy-done.6
  84.7 2.8 %collective-permute-start.6 = (bf16[128,1536]{1,0:T(8,128)(2,1)}, bf16[128,1536]{1,0:T(8,128)(2,1)S(1)}, u32[]{:S(2)}, u32[]{:S(2)}) collective-permute-start(bf16[128,1536]{1,0:T(8,128)(2,1)} %joined.3.refs_0_), channel_id=1, source_target_pairs={{0,224},{32,0},{64,32},{96,64},{128,96},{160,128},{192,160},{224,1... | collective-permute-start | bytes 1179656 | tf_op jit(solution)/shard_map/ppermute | solution.py:301
  87.5 1.1 halves.3
  88.6 2.9 %collective-permute-start.14 = (bf16[128,1536]{1,0:T(8,128)(2,1)S(1)}, bf16[128,1536]{1,0:T(8,128)(2,1)S(1)}, u32[]{:S(2)}, u32[]{:S(2)}) collective-permute-start(bf16[128,1536]{1,0:T(8,128)(2,1)S(1)} %get-tuple-element.28), channel_id=1, source_target_pairs={{0,224},{32,0},{64,32},{96,64},{128,96},{160,128},{192,160},{224,1... | collective-permute-start | bytes 1179656 | tf_op jit(solution)/shard_map/ppermute | solution.py:301
  91.6 5.5 %collective-permute-done.9.refs_3_.refs_4_ = bf16[128,1536]{1,0:T(8,128)(2,1)S(1)} collective-permute-done((bf16[128,1536]{1,0:T(8,128)(2,1)}, bf16[128,1536]{1,0:T(8,128)(2,1)S(1)}, u32[]{:S(2)}, u32[]{:S(2)}) %collective-permute-start.9) | collective-permute-done | bytes 393248 | tf_op jit(solution)/shard_map/ppermute | solution.py:301
  97.1 2.4 %collective-permute-start.7 = (bf16[128,1536]{1,0:T(8,128)(2,1)S(1)}, bf16[128,1536]{1,0:T(8,128)(2,1)S(1)}, u32[]{:S(2)}, u32[]{:S(2)}) collective-permute-start(bf16[128,1536]{1,0:T(8,128)(2,1)S(1)} %collective-permute-done.6.refs_0_.refs_3_), channel_id=1, source_target_pairs={{0,224},{32,0},{64,32},{96,64},{128,96},{160,128},{192,160},{224,1... | collective-permute-start | bytes 1179656 | tf_op jit(solution)/shard_map/ppermute | solution.py:301
  99.5 4.8 %collective-permute-done.14.refs_1_ = bf16[128,1536]{1,0:T(8,128)(2,1)S(1)} collective-permute-done((bf16[128,1536]{1,0:T(8,128)(2,1)S(1)}, bf16[128,1536]{1,0:T(8,128)(2,1)S(1)}, u32[]{:S(2)}, u32[]{:S(2)}) %collective-permute-start.14) | collective-permute-done | bytes 393248 | tf_op jit(solution)/shard_map/ppermute | solution.py:301
  104.3 1.2 collective-permute-done.15.refs_2_
  105.5 4.1 %fold.10 = (bf16[8,2,256,128]{3,2,1,0:T(8,128)(2,1)}, s32[1]{0:T(128)}) custom-call(s32[65]{0:T(128)S(1)} %pad_add_fusion.1.facts, s32[4,1,1536]{2,1,0:T(1,128)S(1)} %copy-done.17, bf16[256,1536]{1,0:T(8,128)(2,1)S(1)} %copy-done.8, bf16[128,1536]{1,0:T(8,128)(2,1)S(1)} %collective-permute-done.14.refs_1_, ...), custom_call_target="tpu_custom_call" | custom-call | flops 1207959552 | bytes 2621440 | tf_op jit(solution)/shard_map/fold/pallas_call | solution.py:103
  109.6 4.3 %collective-permute-done.10.refs_1_ = bf16[128,1536]{1,0:T(8,128)(2,1)S(1)} collective-permute-done((bf16[128,1536]{1,0:T(8,128)(2,1)S(1)}, bf16[128,1536]{1,0:T(8,128)(2,1)S(1)}, u32[]{:S(2)}, u32[]{:S(2)}) %collective-permute-start.10) | collective-permute-done | bytes 393248 | tf_op jit(solution)/shard_map/ppermute | solution.py:301
  113.9 2.4 collective-permute-start.8
  116.3 3.3 %fold.6 = (bf16[8,8,128,128]{3,2,1,0:T(8,128)(2,1)}, s32[1]{0:T(128)}) custom-call(s32[65]{0:T(128)S(1)} %pad_add_fusion.1.facts, s32[4,1,1536]{2,1,0:T(1,128)S(1)} %copy-done.17, bf16[128,1536]{1,0:T(8,128)(2,1)S(1)} %collective-permute-done.7.refs_0_, bf16[128,1536]{1,0:T(8,128)(2,1)S(1)} %collective-permute-done.10.refs_1_), custom_call_target="tpu_custom_call" | custom-call | flops 4831838208 | bytes 1310720 | tf_op jit(solution)/shard_map/fold/pallas_call | solution.py:103
  119.6 5.1 %collective-permute-done.11.second.refs_1_ = bf16[128,1536]{1,0:T(8,128)(2,1)S(1)} collective-permute-done((bf16[128,1536]{1,0:T(8,128)(2,1)S(1)}, bf16[128,1536]{1,0:T(8,128)(2,1)S(1)}, u32[]{:S(2)}, u32[]{:S(2)}) %collective-permute-start.11) | collective-permute-done | bytes 393248 | tf_op jit(solution)/shard_map/ppermute | solution.py:301
  124.7 1.4 halves.2
  126.2 2.4 %collective-permute-start.12 = (bf16[64,1536]{1,0:T(8,128)(2,1)}, bf16[64,1536]{1,0:T(8,128)(2,1)}, u32[]{:S(2)}, u32[]{:S(2)}) collective-permute-start(bf16[64,1536]{1,0:T(8,128)(2,1)} %get-tuple-element.22), channel_id=1, source_target_pairs={{0,224},{32,0},{64,32},{96,64},{128,96},{160,128},{192,160},{224,1... | collective-permute-start | bytes 589832 | tf_op jit(solution)/shard_map/ppermute | solution.py:301
  128.7 1.6 copy-done.1
  130.3 6.7 %all-to-all-start.1 = ((bf16[8,2,256,128]{3,2,1,0:T(8,128)(2,1)}), bf16[8,2,256,128]{3,2,1,0:T(8,128)(2,1)}, u32[]{:S(2)}, u32[]{:S(2)}) async-start(bf16[8,2,256,128]{3,2,1,0:T(8,128)(2,1)} %joined.4), calls=%async_computation.1 | async-start | bytes 2097152 | tf_op jit(solution)/shard_map/all_to_all | solution.py:349
  137.0 1.0 copy-done.13
  138.0 1.0 copy-done.15
  139.7 1.0 copy-done.20
  140.7 1.0 copy-done.22
  141.7 4.8 %fold.7 = (bf16[8,8,128,128]{3,2,1,0:T(8,128)(2,1)}, s32[1]{0:T(128)}) custom-call(s32[65]{0:T(128)S(1)} %pad_add_fusion.1.facts, s32[4,1,1536]{2,1,0:T(1,128)S(1)} %copy-done.18, bf16[128,1536]{1,0:T(8,128)(2,1)S(1)} %copy-done.22, bf16[128,1536]{1,0:T(8,128)(2,1)S(1)} %copy-done.13, ...), custom_call_target="tpu_custom_call", output_to_operand_aliasing={{0}: (6, {})} | custom-call | flops 9663676416 | bytes 2621440 | tf_op jit(solution)/shard_map/fold/pallas_call | solution.py:103
  146.5 4.1 %fold.8 = (bf16[8,8,128,128]{3,2,1,0:T(8,128)(2,1)}, s32[1]{0:T(128)}) custom-call(s32[65]{0:T(128)S(1)} %pad_add_fusion.1.facts, s32[4,1,1536]{2,1,0:T(1,128)S(1)} %copy-done.18, bf16[128,1536]{1,0:T(8,128)(2,1)S(1)} %copy-done.2, bf16[64,1536]{1,0:T(8,128)(2,1)} %collective-permute-done.12.refs_1_, ...), custom_call_target="tpu_custom_call", output_to_operand_aliasing={{0}: (5, {})} | custom-call | flops 4831838208 | bytes 1310720 | tf_op jit(solution)/shard_map/fold/pallas_call | solution.py:103
  151.1 6.3 %all-to-all-start.2 = ((bf16[8,8,128,128]{3,2,1,0:T(8,128)(2,1)}), bf16[8,8,128,128]{3,2,1,0:T(8,128)(2,1)}, u32[]{:S(2)}, u32[]{:S(2)}) async-start(bf16[8,8,128,128]{3,2,1,0:T(8,128)(2,1)} %joined.5), calls=%async_computation.2 | async-start | bytes 4194304 | tf_op jit(solution)/shard_map/all_to_all | solution.py:349
  158.7 9.8 %ladder.3 = (f32[256,1536]{1,0:T(8,128)}, bf16[256,1536]{1,0:T(8,128)(2,1)}) custom-call(s32[33]{0:T(128)} %pad_add_fusion.facts, s32[1,1536]{1,0:T(1,128)} %constant_dynamic-slice_fusion.send_map, bf16[4096,1536]{1,0:T(8,128)(2,1)} %bitcast.21, bf16[8,6,256,128]{3,2,1,0:T(8,128)(2,1)} %copy-done.1, bf16[8,2,256,128]{3,2,1,0:T(8,128)(2,1)} %all-to-all-done.1.refs_1_), custom_call_target="tpu_custom_call" | custom-call | flops 3221225472 | bytes 14680064 | tf_op jit(solution)/shard_map/ladder/pallas_call | solution.py:230
  168.5 2.3 collective-permute-start.17
  170.8 4.5 %select_reduce_fusion.1 = (f32[1536]{0:T(1024)S(1)}, f32[1536]{0:T(1024)S(1)}) fusion(f32[2048]{0:T(1024)S(1)} %copy-done.26, s32[1536]{0:T(1024)S(1)} %get-tuple-element.37, s32[1536]{0:T(1024)S(1)} %get-tuple-element.38), kind=kLoop, calls=%fused_computation.2 | loop fusion | flops 18871296 | bytes 32768 | tf_op jit(solution)/shard_map/reduce_sum | solution.py:306
  175.5 7.3 %all-to-all-done.2.refs_0_ = bf16[8,8,128,128]{3,2,1,0:T(8,128)(2,1)} async-done(((bf16[8,8,128,128]{3,2,1,0:T(8,128)(2,1)}), bf16[8,8,128,128]{3,2,1,0:T(8,128)(2,1)}, u32[]{:S(2)}, u32[]{:S(2)}) %all-to-all-start.2) | async-done | bytes 2097184 | tf_op jit(solution)/shard_map/all_to_all | solution.py:349
  182.8 8.2 %ladder.2 = (f32[128,1536]{1,0:T(8,128)}, bf16[128,1536]{1,0:T(8,128)(2,1)}) custom-call(s32[33]{0:T(128)} %pad_add_fusion.facts, s32[1,1536]{1,0:T(1,128)} %constant_dynamic-slice_fusion.send_map, bf16[4096,1536]{1,0:T(8,128)(2,1)} %bitcast.22, bf16[8,8,128,128]{3,2,1,0:T(8,128)(2,1)} %all-to-all-done.2.refs_0_), custom_call_target="tpu_custom_call" | custom-call | flops 1610612736 | bytes 13631488 | tf_op jit(solution)/shard_map/ladder/pallas_call | solution.py:230
  190.9 2.3 collective-permute-start.16
  193.4 2.5 %update.2.refs_6_ = bf16[384,1536]{1,0:T(8,128)(2,1)} custom-call(bf16[256,1536]{1,0:T(8,128)(2,1)S(1)} %copy-done.9, f32[256,1536]{1,0:T(8,128)S(1)} %copy-done.10, bf16[256,1536]{1,0:T(8,128)(2,1)} %collective-permute-done.17.refs_2_, f32[1]{0:T(128)} %bitcast.11.refs_3_, f32[256,1]{1,0:T(8,128)S(1)} %copy.23.refs_4_, f32[2,1536]{1,0:T(2,128)S(1)} %pad_maximum_fusion.refs_5_), custom_call_target="tpu_custom_call" | custom-call | flops 3145728 | bytes 3932160 | tf_op jit(solution)/shard_map/update/pallas_call | solution.py:284
  195.9 32.0 %collective-permute-done.16.refs_2_ = bf16[128,1536]{1,0:T(8,128)(2,1)} collective-permute-done((bf16[128,1536]{1,0:T(8,128)(2,1)}, bf16[128,1536]{1,0:T(8,128)(2,1)}, u32[]{:S(2)}, u32[]{:S(2)}) %collective-permute-start.16) | collective-permute-done | bytes 393248 | tf_op jit(solution)/shard_map/ppermute | solution.py:301
  227.9 2.0 update.3
  (92 shorter events, 5.6 us)
Async XLA Ops:
  6.5 43.1 %copy-start = (s32[64,1536]{1,0:T(8,128)S(1)}, s32[64,1536]{1,0:T(8,128)}, u32[]{:S(2)}) copy-start(s32[64,1536]{1,0:T(8,128)} %param.12) | copy-start | bytes 1179652
  6.5 1.3 copy-start.23
  6.5 23.9 %copy-start.27 = (s32[1,32]{1,0:T(1,128)S(1)}, s32[1,32]{1,0:T(1,128)}, u32[]{:S(2)}) copy-start(s32[1,32]{1,0:T(1,128)} %param.10) | copy-start | bytes 388
  6.5 23.9 %copy-start.28 = (s32[1,32]{1,0:T(1,128)S(1)}, s32[1,32]{1,0:T(1,128)}, u32[]{:S(2)}) copy-start(s32[1,32]{1,0:T(1,128)} %param.11) | copy-start | bytes 388
  6.5 152.2 %all-gather.4.cloned.1.call-start = ((), (), s32[]{:S(2)}) async-start(), calls=%async_computation.3 | async-start | bytes 15728640 | tf_op jit(solution)/shard_map/all_gather | solution.py:315
  7.9 18.9 %collective-permute-start = (bf16[256,1536]{1,0:T(8,128)(2,1)S(1)}, bf16[256,1536]{1,0:T(8,128)(2,1)S(1)}, u32[]{:S(2)}, u32[]{:S(2)}) collective-permute-start(bf16[256,1536]{1,0:T(8,128)(2,1)S(1)} %slice_bitcast_fusion.refs_0_), channel_id=1, source_target_pairs={{0,224},{32,0},{64,32},{96,64},{128,96},{160,128},{192,160},{224,1... | collective-permute-start | bytes 2359304 | tf_op jit(solution)/shard_map/ppermute | solution.py:301
  8.0 22.4 %collective-permute-start.3 = (bf16[256,1536]{1,0:T(8,128)(2,1)S(1)}, bf16[256,1536]{1,0:T(8,128)(2,1)S(1)}, u32[]{:S(2)}, u32[]{:S(2)}) collective-permute-start(bf16[256,1536]{1,0:T(8,128)(2,1)S(1)} %slice_bitcast_fusion.refs_0_), channel_id=1, source_target_pairs={{0,32},{32,64},{64,96},{96,128},{128,160},{160,192},{192,224},{224... | collective-permute-start | bytes 2359304 | tf_op jit(solution)/shard_map/ppermute | solution.py:301
  26.8 18.1 %collective-permute-start.1 = (bf16[256,1536]{1,0:T(8,128)(2,1)S(1)}, bf16[256,1536]{1,0:T(8,128)(2,1)}, u32[]{:S(2)}, u32[]{:S(2)}) collective-permute-start(bf16[256,1536]{1,0:T(8,128)(2,1)S(1)} %collective-permute-done.refs_0_), channel_id=1, source_target_pairs={{0,224},{32,0},{64,32},{96,64},{128,96},{160,128},{192,160},{224,1... | collective-permute-start | bytes 2359304 | tf_op jit(solution)/shard_map/ppermute | solution.py:301
  30.4 18.7 %collective-permute-start.4 = (bf16[256,1536]{1,0:T(8,128)(2,1)S(1)}, bf16[256,1536]{1,0:T(8,128)(2,1)}, u32[]{:S(2)}, u32[]{:S(2)}) collective-permute-start(bf16[256,1536]{1,0:T(8,128)(2,1)S(1)} %collective-permute-done.3.refs_3_), channel_id=1, source_target_pairs={{0,32},{32,64},{64,96},{96,128},{128,160},{160,192},{192,224},{224... | collective-permute-start | bytes 2359304 | tf_op jit(solution)/shard_map/ppermute | solution.py:301
  44.9 19.2 %collective-permute-start.2 = (bf16[256,1536]{1,0:T(8,128)(2,1)}, bf16[256,1536]{1,0:T(8,128)(2,1)S(1)}, u32[]{:S(2)}, u32[]{:S(2)}) collective-permute-start(bf16[256,1536]{1,0:T(8,128)(2,1)} %collective-permute-done.1.refs_0_), channel_id=1, source_target_pairs={{0,224},{32,0},{64,32},{96,64},{128,96},{160,128},{192,160},{224,1... | collective-permute-start | bytes 2359304 | tf_op jit(solution)/shard_map/ppermute | solution.py:301
  49.1 18.1 %collective-permute-start.5 = (bf16[256,1536]{1,0:T(8,128)(2,1)}, bf16[256,1536]{1,0:T(8,128)(2,1)S(1)}, u32[]{:S(2)}, u32[]{:S(2)}) collective-permute-start(bf16[256,1536]{1,0:T(8,128)(2,1)} %collective-permute-done.4.refs_1_), channel_id=1, source_target_pairs={{0,32},{32,64},{64,96},{96,128},{128,160},{160,192},{192,224},{224... | collective-permute-start | bytes 2359304 | tf_op jit(solution)/shard_map/ppermute | solution.py:301
  49.6 23.2 %copy-start.16 = (s32[4,1,1536]{2,1,0:T(1,128)}, s32[4,1,1536]{2,1,0:T(1,128)S(1)}, u32[]{:S(2)}) copy-start(s32[4,1,1536]{2,1,0:T(1,128)S(1)} %dynamic-slice_bitcast_fusion.maps) | copy-start | bytes 73732
  64.1 8.8 %copy-start.3 = (bf16[256,1536]{1,0:T(8,128)(2,1)}, bf16[256,1536]{1,0:T(8,128)(2,1)S(1)}, u32[]{:S(2)}) copy-start(bf16[256,1536]{1,0:T(8,128)(2,1)S(1)} %collective-permute-done.2.refs_1_.first.refs_2_) | copy-start | bytes 2359300
  67.2 5.6 %copy-start.5 = (bf16[256,1536]{1,0:T(8,128)(2,1)}, bf16[256,1536]{1,0:T(8,128)(2,1)S(1)}, u32[]{:S(2)}) copy-start(bf16[256,1536]{1,0:T(8,128)(2,1)S(1)} %collective-permute-done.5.refs_2_.second.refs_1_) | copy-start | bytes 2359300
  72.9 55.8 %all-to-all-start = ((bf16[8,6,256,128]{3,2,1,0:T(8,128)(2,1)}), bf16[8,6,256,128]{3,2,1,0:T(8,128)(2,1)S(1)}, u32[]{:S(2)}, u32[]{:S(2)}) async-start(bf16[8,6,256,128]{3,2,1,0:T(8,128)(2,1)} %get-tuple-element.32), calls=%async_computation | async-start | bytes 6291456 | tf_op jit(solution)/shard_map/all_to_all | solution.py:349
  80.6 24.9 %copy-start.8 = (bf16[256,1536]{1,0:T(8,128)(2,1)S(1)}, bf16[256,1536]{1,0:T(8,128)(2,1)}, u32[]{:S(2)}) copy-start(bf16[256,1536]{1,0:T(8,128)(2,1)} %copy-done.7) | copy-start | bytes 2359300
  82.4 1.1 copy-start.4
  83.6 1.1 copy-start.6
  84.7 20.8 %copy-start.17 = (s32[4,1,1536]{2,1,0:T(1,128)S(1)}, s32[4,1,1536]{2,1,0:T(1,128)}, u32[]{:S(2)}) copy-start(s32[4,1,1536]{2,1,0:T(1,128)} %copy-done.16) | copy-start | bytes 73732
  84.7 12.3 %collective-permute-start.9 = (bf16[128,1536]{1,0:T(8,128)(2,1)}, bf16[128,1536]{1,0:T(8,128)(2,1)S(1)}, u32[]{:S(2)}, u32[]{:S(2)}) collective-permute-start(bf16[128,1536]{1,0:T(8,128)(2,1)} %joined.3.refs_0_), channel_id=1, source_target_pairs={{0,32},{32,64},{64,96},{96,128},{128,160},{160,192},{192,224},{224... | collective-permute-start | bytes 1179656 | tf_op jit(solution)/shard_map/ppermute | solution.py:301
  84.7 12.3 %collective-permute-start.6 = (bf16[128,1536]{1,0:T(8,128)(2,1)}, bf16[128,1536]{1,0:T(8,128)(2,1)S(1)}, u32[]{:S(2)}, u32[]{:S(2)}) collective-permute-start(bf16[128,1536]{1,0:T(8,128)(2,1)} %joined.3.refs_0_), channel_id=1, source_target_pairs={{0,224},{32,0},{64,32},{96,64},{128,96},{160,128},{192,160},{224,1... | collective-permute-start | bytes 1179656 | tf_op jit(solution)/shard_map/ppermute | solution.py:301
  88.6 15.7 %collective-permute-start.14 = (bf16[128,1536]{1,0:T(8,128)(2,1)S(1)}, bf16[128,1536]{1,0:T(8,128)(2,1)S(1)}, u32[]{:S(2)}, u32[]{:S(2)}) collective-permute-start(bf16[128,1536]{1,0:T(8,128)(2,1)S(1)} %get-tuple-element.28), channel_id=1, source_target_pairs={{0,224},{32,0},{64,32},{96,64},{128,96},{160,128},{192,160},{224,1... | collective-permute-start | bytes 1179656 | tf_op jit(solution)/shard_map/ppermute | solution.py:301
  91.6 13.9 %collective-permute-start.15 = (bf16[128,1536]{1,0:T(8,128)(2,1)S(1)}, bf16[128,1536]{1,0:T(8,128)(2,1)S(1)}, u32[]{:S(2)}, u32[]{:S(2)}) collective-permute-start(bf16[128,1536]{1,0:T(8,128)(2,1)S(1)} %get-tuple-element.29), channel_id=1, source_target_pairs={{0,32},{32,64},{64,96},{96,128},{128,160},{160,192},{192,224},{224... | collective-permute-start | bytes 1179656 | tf_op jit(solution)/shard_map/ppermute | solution.py:301
  97.0 22.6 %copy-start.19 = (bf16[128,1536]{1,0:T(8,128)(2,1)}, bf16[128,1536]{1,0:T(8,128)(2,1)S(1)}, u32[]{:S(2)}) copy-start(bf16[128,1536]{1,0:T(8,128)(2,1)S(1)} %collective-permute-done.9.refs_3_.refs_4_) | copy-start | bytes 1179652
  97.0 16.9 %collective-permute-start.10 = (bf16[128,1536]{1,0:T(8,128)(2,1)S(1)}, bf16[128,1536]{1,0:T(8,128)(2,1)S(1)}, u32[]{:S(2)}, u32[]{:S(2)}) collective-permute-start(bf16[128,1536]{1,0:T(8,128)(2,1)S(1)} %collective-permute-done.9.refs_3_.refs_4_), channel_id=1, source_target_pairs={{0,32},{32,64},{64,96},{96,128},{128,160},{160,192},{192,224},{224... | collective-permute-start | bytes 1179656 | tf_op jit(solution)/shard_map/ppermute | solution.py:301
  97.1 22.6 %copy-start.21 = (bf16[128,1536]{1,0:T(8,128)(2,1)}, bf16[128,1536]{1,0:T(8,128)(2,1)S(1)}, u32[]{:S(2)}) copy-start(bf16[128,1536]{1,0:T(8,128)(2,1)S(1)} %collective-permute-done.6.refs_0_.refs_3_) | copy-start | bytes 1179652
  97.1 16.8 %collective-permute-start.7 = (bf16[128,1536]{1,0:T(8,128)(2,1)S(1)}, bf16[128,1536]{1,0:T(8,128)(2,1)S(1)}, u32[]{:S(2)}, u32[]{:S(2)}) collective-permute-start(bf16[128,1536]{1,0:T(8,128)(2,1)S(1)} %collective-permute-done.6.refs_0_.refs_3_), channel_id=1, source_target_pairs={{0,224},{32,0},{64,32},{96,64},{128,96},{160,128},{192,160},{224,1... | collective-permute-start | bytes 1179656 | tf_op jit(solution)/shard_map/ppermute | solution.py:301
  113.9 10.8 %collective-permute-start.11 = (bf16[128,1536]{1,0:T(8,128)(2,1)S(1)}, bf16[128,1536]{1,0:T(8,128)(2,1)S(1)}, u32[]{:S(2)}, u32[]{:S(2)}) collective-permute-start(bf16[128,1536]{1,0:T(8,128)(2,1)S(1)} %collective-permute-done.10.refs_1_), channel_id=1, source_target_pairs={{0,32},{32,64},{64,96},{96,128},{128,160},{160,192},{192,224},{224... | collective-permute-start | bytes 1179656 | tf_op jit(solution)/shard_map/ppermute | solution.py:301
  113.9 10.8 %collective-permute-start.8 = (bf16[128,1536]{1,0:T(8,128)(2,1)S(1)}, bf16[128,1536]{1,0:T(8,128)(2,1)S(1)}, u32[]{:S(2)}, u32[]{:S(2)}) collective-permute-start(bf16[128,1536]{1,0:T(8,128)(2,1)S(1)} %collective-permute-done.7.refs_0_), channel_id=1, source_target_pairs={{0,224},{32,0},{64,32},{96,64},{128,96},{160,128},{192,160},{224,1... | collective-permute-start | bytes 1179656 | tf_op jit(solution)/shard_map/ppermute | solution.py:301
  124.7 3.9 %copy-start.12 = (bf16[128,1536]{1,0:T(8,128)(2,1)}, bf16[128,1536]{1,0:T(8,128)(2,1)S(1)}, u32[]{:S(2)}) copy-start(bf16[128,1536]{1,0:T(8,128)(2,1)S(1)} %collective-permute-done.11.second.refs_1_) | copy-start | bytes 1179652
  124.7 3.9 %copy-start.14 = (bf16[128,1536]{1,0:T(8,128)(2,1)}, bf16[128,1536]{1,0:T(8,128)(2,1)S(1)}, u32[]{:S(2)}) copy-start(bf16[128,1536]{1,0:T(8,128)(2,1)S(1)} %collective-permute-done.8.first.refs_2_) | copy-start | bytes 1179652
  126.2 20.3 %collective-permute-start.12 = (bf16[64,1536]{1,0:T(8,128)(2,1)}, bf16[64,1536]{1,0:T(8,128)(2,1)}, u32[]{:S(2)}, u32[]{:S(2)}) collective-permute-start(bf16[64,1536]{1,0:T(8,128)(2,1)} %get-tuple-element.22), channel_id=1, source_target_pairs={{0,224},{32,0},{64,32},{96,64},{128,96},{160,128},{192,160},{224,1... | collective-permute-start | bytes 589832 | tf_op jit(solution)/shard_map/ppermute | solution.py:301
  128.6 17.9 %collective-permute-start.13 = (bf16[64,1536]{1,0:T(8,128)(2,1)}, bf16[64,1536]{1,0:T(8,128)(2,1)}, u32[]{:S(2)}, u32[]{:S(2)}) collective-permute-start(bf16[64,1536]{1,0:T(8,128)(2,1)} %get-tuple-element.23), channel_id=1, source_target_pairs={{0,32},{32,64},{64,96},{96,128},{128,160},{160,192},{192,224},{224... | collective-permute-start | bytes 589832 | tf_op jit(solution)/shard_map/ppermute | solution.py:301
  128.7 1.6 copy-start.1
  130.3 20.8 %all-to-all-start.1 = ((bf16[8,2,256,128]{3,2,1,0:T(8,128)(2,1)}), bf16[8,2,256,128]{3,2,1,0:T(8,128)(2,1)}, u32[]{:S(2)}, u32[]{:S(2)}) async-start(bf16[8,2,256,128]{3,2,1,0:T(8,128)(2,1)} %joined.4), calls=%async_computation.1 | async-start | bytes 2097152 | tf_op jit(solution)/shard_map/all_to_all | solution.py:349
  137.0 1.0 copy-start.13
  138.0 1.0 copy-start.15
  141.7 4.9 %copy-start.2 = (bf16[128,1536]{1,0:T(8,128)(2,1)S(1)}, bf16[128,1536]{1,0:T(8,128)(2,1)}, u32[]{:S(2)}) copy-start(bf16[128,1536]{1,0:T(8,128)(2,1)} %joined.3.refs_0_) | copy-start | bytes 1179652
  151.1 7.0 %copy-start.24 = (s32[1,2,1536]{2,1,0:T(2,128)S(1)}, s32[1,2,1536]{2,1,0:T(2,128)}, u32[]{:S(2)}) copy-start(s32[1,2,1536]{2,1,0:T(2,128)} %param.13) | copy-start | bytes 36868
  151.1 31.7 %all-to-all-start.2 = ((bf16[8,8,128,128]{3,2,1,0:T(8,128)(2,1)}), bf16[8,8,128,128]{3,2,1,0:T(8,128)(2,1)}, u32[]{:S(2)}, u32[]{:S(2)}) async-start(bf16[8,8,128,128]{3,2,1,0:T(8,128)(2,1)} %joined.5), calls=%async_computation.2 | async-start | bytes 4194304 | tf_op jit(solution)/shard_map/all_to_all | solution.py:349
  158.7 12.0 %copy-start.26 = (f32[2048]{0:T(1024)S(1)}, f32[2048]{0:T(1024)}, u32[]{:S(2)}) copy-start(f32[2048]{0:T(1024)} %param.14) | copy-start | bytes 24580
  158.7 16.6 %slice-start = ((f32[384]{0:T(512)}), f32[256]{0:T(256)S(1)}, s32[]{:S(2)}) async-start(f32[384]{0:T(512)} %param.15), calls=%async_computation.4 | async-start | bytes 2048 | tf_op jit(solution)/shard_map/slice | solution.py:369
  168.5 24.9 %collective-permute-start.17 = (bf16[256,1536]{1,0:T(8,128)(2,1)}, bf16[256,1536]{1,0:T(8,128)(2,1)}, u32[]{:S(2)}, u32[]{:S(2)}) collective-permute-start(bf16[256,1536]{1,0:T(8,128)(2,1)} %get-tuple-element.36), channel_id=1, source_target_pairs={{0,128},{32,160},{64,192},{96,224},{128,0},{160,32},{192,64},{224,... | collective-permute-start | bytes 2359304 | tf_op jit(solution)/shard_map/ppermute | solution.py:301
  175.5 17.7 %copy-start.25 = (f32[384]{0:T(512)S(1)}, f32[384]{0:T(512)}, u32[]{:S(2)}) copy-start(f32[384]{0:T(512)} %param.15) | copy-start | bytes 4612
  175.5 17.9 %copy-start.9 = (bf16[256,1536]{1,0:T(8,128)(2,1)S(1)}, bf16[256,1536]{1,0:T(8,128)(2,1)}, u32[]{:S(2)}) copy-start(bf16[256,1536]{1,0:T(8,128)(2,1)} %copy-done.7) | copy-start | bytes 2359300
  175.5 17.9 %copy-start.10 = (f32[256,1536]{1,0:T(8,128)S(1)}, f32[256,1536]{1,0:T(8,128)}, u32[]{:S(2)}) copy-start(f32[256,1536]{1,0:T(8,128)} %get-tuple-element.35.refs_1_) | copy-start | bytes 4718596
  190.9 36.9 %collective-permute-start.16 = (bf16[128,1536]{1,0:T(8,128)(2,1)}, bf16[128,1536]{1,0:T(8,128)(2,1)}, u32[]{:S(2)}, u32[]{:S(2)}) collective-permute-start(bf16[128,1536]{1,0:T(8,128)(2,1)} %get-tuple-element.34), channel_id=1, source_target_pairs={{0,128},{32,160},{64,192},{96,224},{128,0},{160,32},{192,64},{224,... | collective-permute-start | bytes 1179656 | tf_op jit(solution)/shard_map/ppermute | solution.py:301
  193.3 34.5 %copy-start.11 = (f32[128,1536]{1,0:T(8,128)S(1)}, f32[128,1536]{1,0:T(8,128)}, u32[]{:S(2)}) copy-start(f32[128,1536]{1,0:T(8,128)} %get-tuple-element.33.refs_1_) | copy-start | bytes 2359300
  (4 other events, 3.6 us)
Sparse Core Ops, SparseCore 0:
  9.2 122.6 all-gather.3

commit v8 on v5

--- a/solution.py
+++ b/solution.py
@@ -1,5 +1,4 @@
 import functools
-import math
 
 import jax
 import jax.numpy as jnp
@@ -9,6 +8,7 @@
 from jax.sharding import PartitionSpec as P
 
 COLS = 256
+WEIGHT = 1
 VMEM = 40 * 1024 * 1024
 
 
@@ -103,7 +103,7 @@
                         copy.wait()
 
 
-def fold(shifts, facts, maps, tiles, pieces, before):
+def fold(shifts, facts, maps, tiles, pieces, before, weight):
     rows, length = tiles[0].shape
     count = len(shifts)
     whole = pltpu.VMEM((count, rows, length), jnp.bfloat16)
@@ -125,7 +125,7 @@
         ],
         compiler_params=pltpu.CompilerParams(vmem_limit_bytes=VMEM),
         cost_estimate=pl.CostEstimate(
-            flops=2 * count * rows * length * length,
+            flops=weight * 2 * count * rows * length * length,
             bytes_accessed=count * rows * (4 * length + 16 * 256),
             transcendentals=0,
         ),
@@ -178,13 +178,13 @@
     )(first, second, after)
 
 
-def ladder_body(facts, send_map, blocks, received, ladder, sent, operand, rounded, held, sem, held_sem):
+def ladder_body(facts, maps, blocks, received, ladder, sent, operand, rounded, held, sem, held_sem):
     length = rounded.shape[1]
     parts = held_sem.shape[0]
     depth = held.shape[0] // parts
 
     def place(k):
-        tile = facts[1 + k]
+        tile = facts[65 + k]
         z, ket = tile >> 3, tile & 7
         slot = 2 * ((z - facts[0] + 8) & 3) + (z >> 2)
         where = operand.at[:, pl.ds(k * 128, 128)]
@@ -214,12 +214,12 @@
                 rounded[:, columns] = total.astype(jnp.bfloat16)
     for low in range(0, length, COLS):
         columns = slice(low, low + COLS)
-        picks = one_hot(send_map[:, columns], length, COLS)
+        picks = one_hot(maps[4, :, columns], length, COLS)
         moved = jnp.dot(rounded[...], picks, preferred_element_type=jnp.float32)
         sent[:, columns] = moved.astype(jnp.bfloat16)
 
 
-def ladder_of(facts, send_map, blocks, received):
+def ladder_of(facts, maps, blocks, received):
     depth, length = blocks.shape
     rows = received.shape[2]
     vmem = pl.BlockSpec(memory_space=pltpu.VMEM)
@@ -250,44 +250,43 @@
             transcendentals=0,
         ),
         name="ladder",
-    )(facts, send_map, blocks, received)
+    )(facts, maps, blocks, received)
 
 
 def update_body(low, *refs):
-    own, ladder, partner, direction, occupied, virtual, out = refs[:7] if len(refs) == 7 else refs[:6] + refs[7:]
-    residual = ladder[...] + direction[0] * partner[...].astype(jnp.float32)
-    denominator = occupied[...] - virtual[0:1, :] - virtual[1:2, :]
-    out[...] = (own[...].astype(jnp.float32) + residual / denominator).astype(jnp.bfloat16)
-
-
-def update(low, own, ladder, partner, direction, occupied, virtual, before):
+    own, ladder, partner, direction, occupied, virtual = refs[:6]
+    out, fresh, sem = refs[-3:]
+    rows = fresh.shape[0]
+    step = 32
+    copies = []
+    for start in range(0, rows, step):
+        block = slice(start, start + step)
+        residual = ladder[block] + direction[0] * partner[block].astype(jnp.float32)
+        denominator = occupied[block] - virtual[0:1, :] - virtual[1:2, :]
+        new = own[block].astype(jnp.float32) + residual / denominator
+        fresh[block] = new.astype(jnp.bfloat16)
+        copies.append(
+            pltpu.make_async_copy(
+                fresh.at[pl.ds(start, step)], out.at[pl.ds(low + start, step)], sem.at[start // step]
+            )
+        )
+        copies[-1].start()
+    for copy in copies:
+        copy.wait()
+
+
+def update(low, total, own, ladder, partner, direction, occupied, virtual, before):
     rows, length = ladder.shape
-    step = math.gcd(low, rows) if low else rows // 2
-
-    def chunk(width):
-        return pl.BlockSpec((step, width), lambda n: (n, 0))
-
-    def whole(width):
-        return pl.BlockSpec((step, width), lambda n: (n + low // step, 0))
-
+    vmem, held = pl.BlockSpec(memory_space=pltpu.VMEM), pl.BlockSpec(memory_space=pl.ANY)
     return pl.pallas_call(
         functools.partial(update_body, low),
-        grid=(rows // step,),
-        in_specs=[
-            whole(length),
-            chunk(length),
-            chunk(length),
-            pl.BlockSpec(memory_space=pltpu.SMEM),
-            whole(1),
-            pl.BlockSpec((2, length), lambda n: (0, 0)),
-        ]
-        + [pl.BlockSpec(memory_space=pl.ANY)] * len(before),
-        out_specs=whole(length),
-        out_shape=jax.ShapeDtypeStruct(own.shape, jnp.bfloat16),
+        in_specs=[vmem, vmem, vmem, pl.BlockSpec(memory_space=pltpu.SMEM), vmem, vmem]
+        + [held] * len(before),
+        out_specs=held,
+        out_shape=pltpu.HBM((total, length), jnp.bfloat16),
+        scratch_shapes=[pltpu.VMEM((rows, length), jnp.bfloat16), pltpu.SemaphoreType.DMA((rows // 32,))],
         input_output_aliases={6: 0} if before else {},
-        compiler_params=pltpu.CompilerParams(
-            vmem_limit_bytes=VMEM, dimension_semantics=("arbitrary",)
-        ),
+        compiler_params=pltpu.CompilerParams(vmem_limit_bytes=VMEM),
         cost_estimate=pl.CostEstimate(
             flops=8 * rows * length, bytes_accessed=10 * rows * length, transcendentals=0
         ),
@@ -316,12 +315,12 @@
     served = jnp.arange(8, dtype=jnp.int32) * 8 + ket
     match = (wanted >> 4)[:, None, :] == served[None, :, None]
     asked = jnp.max(jnp.where(match, wanted[:, None, :] & 15, -1), axis=2)
-    fold_facts = jnp.concatenate([z.astype(jnp.int32)[None], asked.reshape(-1)])
-    ladder_facts = jnp.concatenate([z.astype(jnp.int32)[None], block_owner[0]])
+    facts = jnp.concatenate([z.astype(jnp.int32)[None], asked.reshape(-1), block_owner[0]])
     grid_maps = mirror_map.reshape(2, 4, 8, length)
     half_maps = lax.dynamic_index_in_dim(grid_maps, z >> 2, 0, keepdims=False)
     maps = lax.dynamic_index_in_dim(half_maps, ket, 1, keepdims=True)
     send_map = lax.dynamic_index_in_dim(mirror_map, ((z + 4) & 7) * 8 + ket, 0, keepdims=True)
+    maps = jnp.concatenate([maps, send_map[None]])
 
     direction = jnp.where(z >= 4, 1.0, -1.0).astype(jnp.float32)
     first = energies(vir_energy, pair_virt[0, 0])
@@ -336,26 +335,31 @@
             part = joined(part, steps[-1][2], pltpu.HBM)
         one = (shifted(part, -1), shifted(part, 1))
         two = (shifted(one[0], -1), shifted(one[1], 1))
-        *slots, done = fold((2,), fold_facts, maps, two, pieces, ())
+        weight = WEIGHT if steps else 1
+        *slots, done = fold((2,), facts, maps, two, pieces, (), weight)
         three = (shifted(two[0], -1), shifted(two[1], 1))
-        upper, lower = halves(*three, done if steps else fold_facts)
+        upper, lower = halves(*three, done if steps else facts)
         far = (shifted(upper, -1), shifted(lower, 1))
         odd = (one[0], three[1], three[0], one[1])
-        *slots, _ = fold((1, 3), fold_facts, maps, odd, pieces, slots)
+        *slots, _ = fold((1, 3), facts, maps, odd, pieces, slots, weight)
         steps.append((part, one, three, far))
         folds.append(slots)
-    fresh, low, last, sents = (), 0, (), ()
+    fresh, low, last = (), 0, ()
     for i, (part, one, three, far) in enumerate(steps):
-        *slots, _ = fold((0,), fold_facts, maps, (part, *far), chunks[i], folds[i])
-        later = steps[i + 1][1] if i + 1 < len(steps) else ()
+        weight = WEIGHT if i else 1
+        *slots, _ = fold((0,), facts, maps, (part, *far), chunks[i], folds[i], weight)
         for piece in slots:
+            later = steps[i + 1][1] if i + 1 < len(steps) else ()
             piece = joined(piece, (*later, *last), pltpu.HBM)
             received = lax.all_to_all(piece, "ket", split_axis=0, concat_axis=0, tiled=True)
-            ladder, sent = ladder_of(ladder_facts, send_map, all_blocks, received)
-            last = (received, *sents)
-            sents = (sent,)
+            ladder, sent = ladder_of(facts, maps, all_blocks, received)
+            last = (received,)
             partner = shifted(sent, 4)
-            new = update(low, own, ladder, partner, direction[None], pair_energy[:, None], virtual, fresh)
+            chunk = own[low : low + piece.shape[2]]
+            occupied = pair_energy[low : low + piece.shape[2], None]
+            new = update(
+                low, rows, chunk, ladder, partner, direction[None], occupied, virtual, fresh
+            )
             fresh = (new,)
             low += piece.shape[2]
     return new[:, None, :]

time: 224 us -> 223 us (level); the launches traced: 224 us -> 219 us
  waiting for transfers between devices: 95.3 us -> 90.6 us
  local copies, waits for them, and re-layouts: 6.24 us -> 9.43 us
  Pallas kernels: 54.6 us -> 51.5 us
    ppermute x18, waiting for transfers between devices: 74.6 us -> 68.4 us  [shifted(): return lax.ppermute(block, 'bra', [(i, (i + by) % 8) for i in range(8)])]
    pallas_call x2, Pallas kernels: 6.18 us -> 3.35 us  [update(): pl.pallas_call(functools.partial(update_body, low), in_specs=[vmem, vmem,...]
    slice x0 -> x3, local copies, waits for them, and re-layouts: none -> 2.28 us  [the longest x2 1.17 us: local(): occupied = pair_energy[low:low + piece.shape[2], None]]
  transfers between devices with their start and end apart: 21 -> 21, of which waited for: 13 -> 14; matrix products, arithmetic and copies ran while one was open for 4% -> 6% of each run, Pallas kernels for 23% -> 23%
where the time goes in v8:
time: 223 us; the launch traced here: 219 us
  waiting for transfers between devices  90.6 us (41%)
  Pallas kernels  51.5 us (23%)
  starting transfers between devices  38.5 us (17%)
  between operations  13.7 us (6%)
  blocking collectives  9.48 us (4%)
  local copies, waits for them, and re-layouts  9.43 us (4%)
  other arithmetic  5.71 us (3%)
    ppermute x18, waiting for transfers between devices, shifted(): return lax.ppermute(block, 'bra', [(i, (i + by) % 8) for i in range(8)])  68.4 us
    pallas_call x6, Pallas kernels, fold(): pl.pallas_call(functools.partial(fold_body, shifts, pieces), in_specs=[pl...  28.6 us
    ppermute x18, starting transfers between devices, shifted(): return lax.ppermute(block, 'bra', [(i, (i + by) % 8) for i in range(8)])  22.8 us
    all_to_all x2, waiting for transfers between devices, local(): lax.all_to_all(piece, 'ket', split_axis=0, concat_axis=0, tiled=True)  21.4 us
    pallas_call x2, Pallas kernels, ladder_of(): pl.pallas_call(ladder_body, in_specs=[pl.BlockSpec(memory_space=pltpu.SME...  18 us
    all_to_all x2, starting transfers between devices, local(): lax.all_to_all(piece, 'ket', split_axis=0, concat_axis=0, tiled=True)  15.7 us
    all_gather x1, blocking collectives, local(): wanted = lax.all_gather(block_owner[0] * 16 + screen_list[0], 'ket', axis=0)  9.48 us
    reduce_sum x1, other arithmetic, energies(): jnp.sum(jnp.where(number == indices[None, :], table[:, None], 0.0), axis=0)  4.53 us
  transfers between devices with their start and end apart: 21, of which 14 were waited for; matrix products, arithmetic and copies ran while one was open for 6% of the time, Pallas kernels for 23%

profile of v8, /device:TPU:47, one launch (start us, length us, event | category | flops | bytes accessed | tf_op | source)
XLA Modules:
  0.0 218.9 jit_solution(7923278181087200146)
XLA Ops:
  6.5 0.7 all-gather.4.cloned.1.call-update
  7.3 1.1 slice_bitcast_fusion.refs_0_
  8.5 1.7 collective-permute-start.3
  10.2 9.5 %all-gather.1 = s32[8,1,32]{2,1,0:T(1,128)S(1)} all-gather(s32[1,1,32]{2,1,0:T(1,128)S(1)} %add_bitcast_fusion), channel_id=1, replica_groups=mesh['bra'=8,'ket'=8,'pair'=4] {'ket'}, dimensions={0}, use_global_device_ids=true | all-gather | bytes 1152 | tf_op jit(solution)/shard_map/all_gather | solution.py:314
  19.7 5.5 %collective-permute-done.refs_0_ = bf16[224,1536]{1,0:T(8,128)(2,1)S(1)} collective-permute-done((bf16[224,1536]{1,0:T(8,128)(2,1)S(1)}, bf16[224,1536]{1,0:T(8,128)(2,1)S(1)}, u32[]{:S(2)}, u32[]{:S(2)}) %collective-permute-start) | collective-permute-done | bytes 688160 | tf_op jit(solution)/shard_map/ppermute | solution.py:298
  25.2 2.8 %collective-permute-start.1 = (bf16[224,1536]{1,0:T(8,128)(2,1)S(1)}, bf16[224,1536]{1,0:T(8,128)(2,1)}, u32[]{:S(2)}, u32[]{:S(2)}) collective-permute-start(bf16[224,1536]{1,0:T(8,128)(2,1)S(1)} %collective-permute-done.refs_0_), channel_id=1, source_target_pairs={{0,224},{32,0},{64,32},{96,64},{128,96},{160,128},{192,160},{224,1... | collective-permute-start | bytes 2064392 | tf_op jit(solution)/shard_map/ppermute | solution.py:298
  28.0 0.7 collective-permute-done.3.refs_3_
  28.7 0.9 copy-done.11
  29.6 1.1 slice_bitcast_fusion.1.refs_0_
  30.7 10.5 %collective-permute-done.1.refs_0_ = bf16[224,1536]{1,0:T(8,128)(2,1)} collective-permute-done((bf16[224,1536]{1,0:T(8,128)(2,1)S(1)}, bf16[224,1536]{1,0:T(8,128)(2,1)}, u32[]{:S(2)}, u32[]{:S(2)}) %collective-permute-start.1) | collective-permute-done | bytes 688160 | tf_op jit(solution)/shard_map/ppermute | solution.py:298
  41.2 3.4 %collective-permute-start.2 = (bf16[224,1536]{1,0:T(8,128)(2,1)}, bf16[224,1536]{1,0:T(8,128)(2,1)S(1)}, u32[]{:S(2)}, u32[]{:S(2)}) collective-permute-start(bf16[224,1536]{1,0:T(8,128)(2,1)} %collective-permute-done.1.refs_0_), channel_id=1, source_target_pairs={{0,224},{32,0},{64,32},{96,64},{128,96},{160,128},{192,160},{224,1... | collective-permute-start | bytes 2064392 | tf_op jit(solution)/shard_map/ppermute | solution.py:298
  44.6 0.8 collective-permute-done.4.refs_1_
  45.8 0.8 copy.25.refs_0_
  46.8 11.5 %collective-permute-done.2.refs_1_.first.refs_2_ = bf16[224,1536]{1,0:T(8,128)(2,1)S(1)} collective-permute-done((bf16[224,1536]{1,0:T(8,128)(2,1)}, bf16[224,1536]{1,0:T(8,128)(2,1)S(1)}, u32[]{:S(2)}, u32[]{:S(2)}) %collective-permute-start.2) | collective-permute-done | bytes 688160 | tf_op jit(solution)/shard_map/ppermute | solution.py:298
  58.2 3.2 %collective-permute-done.5.refs_2_.second.refs_1_ = bf16[224,1536]{1,0:T(8,128)(2,1)S(1)} collective-permute-done((bf16[224,1536]{1,0:T(8,128)(2,1)}, bf16[224,1536]{1,0:T(8,128)(2,1)S(1)}, u32[]{:S(2)}, u32[]{:S(2)}) %collective-permute-start.5) | collective-permute-done | bytes 688160 | tf_op jit(solution)/shard_map/ppermute | solution.py:298
  61.4 2.4 %collective-permute-start.6 = (bf16[160,1536]{1,0:T(8,128)(2,1)}, bf16[160,1536]{1,0:T(8,128)(2,1)S(1)}, u32[]{:S(2)}, u32[]{:S(2)}) collective-permute-start(bf16[160,1536]{1,0:T(8,128)(2,1)} %joined.3.refs_0_), channel_id=1, source_target_pairs={{0,224},{32,0},{64,32},{96,64},{128,96},{160,128},{192,160},{224,1... | collective-permute-start | bytes 1474568 | tf_op jit(solution)/shard_map/ppermute | solution.py:298
  64.1 1.5 collective-permute-start.14
  65.6 4.7 %fold.9 = (bf16[8,8,224,128]{3,2,1,0:T(8,128)(2,1)}, s32[1]{0:T(128)}) custom-call(s32[97]{0:T(128)S(1)} %pad_add_fusion.1.facts._, s32[5,1,1536]{2,1,0:T(1,128)S(1)} %pad_add_fusion.maps, bf16[224,1536]{1,0:T(8,128)(2,1)} %collective-permute-done.1.refs_0_, bf16[224,1536]{1,0:T(8,128)(2,1)} %collective-permute-done.4.refs_1_), custom_call_target="tpu_custom_call" | custom-call | flops 1056964608 | bytes 2293760 | tf_op jit(solution)/shard_map/fold/pallas_call | solution.py:110
  70.4 6.2 %fold.10 = (bf16[8,8,224,128]{3,2,1,0:T(8,128)(2,1)}, s32[1]{0:T(128)}) custom-call(s32[97]{0:T(128)S(1)} %pad_add_fusion.1.facts._, s32[5,1,1536]{2,1,0:T(1,128)S(1)} %pad_add_fusion.maps, bf16[224,1536]{1,0:T(8,128)(2,1)S(1)} %copy-done.10, bf16[224,1536]{1,0:T(8,128)(2,1)S(1)} %collective-permute-done.5.refs_2_.second.refs_1_, ...), custom_call_target="tpu_custom_call", output_to_operand_aliasing={{0}: (6, {})} | custom-call | flops 2113929216 | bytes 4587520 | tf_op jit(solution)/shard_map/fold/pallas_call | solution.py:110
  76.6 2.0 collective-permute-done.14.refs_1_
  78.5 1.8 collective-permute-done.15.refs_2_
  80.4 3.9 %fold.11 = (bf16[8,8,224,128]{3,2,1,0:T(8,128)(2,1)}, s32[1]{0:T(128)}) custom-call(s32[97]{0:T(128)S(1)} %pad_add_fusion.1.facts._, s32[5,1,1536]{2,1,0:T(1,128)S(1)} %pad_add_fusion.maps, bf16[224,1536]{1,0:T(8,128)(2,1)S(1)} %slice_bitcast_fusion.refs_0_, bf16[112,1536]{1,0:T(8,128)(2,1)S(1)} %collective-permute-done.14.refs_1_, ...), custom_call_target="tpu_custom_call", output_to_operand_aliasing={{0}: (5, {})} | custom-call | flops 1056964608 | bytes 2293760 | tf_op jit(solution)/shard_map/fold/pallas_call | solution.py:110
  84.3 0.8 copy-done.5
  85.1 9.3 %all-to-all-start = ((bf16[8,8,224,128]{3,2,1,0:T(8,128)(2,1)}), bf16[8,8,224,128]{3,2,1,0:T(8,128)(2,1)}, u32[]{:S(2)}, u32[]{:S(2)}) async-start(bf16[8,8,224,128]{3,2,1,0:T(8,128)(2,1)} %joined.4), calls=%async_computation | async-start | bytes 7340032 | tf_op jit(solution)/shard_map/all_to_all | solution.py:354
  94.5 1.5 collective-permute-start.7
  96.0 11.4 %collective-permute-done.10.refs_1_ = bf16[160,1536]{1,0:T(8,128)(2,1)S(1)} collective-permute-done((bf16[160,1536]{1,0:T(8,128)(2,1)}, bf16[160,1536]{1,0:T(8,128)(2,1)S(1)}, u32[]{:S(2)}, u32[]{:S(2)}) %collective-permute-start.10) | collective-permute-done | bytes 491552 | tf_op jit(solution)/shard_map/ppermute | solution.py:298
  107.3 2.5 %collective-permute-start.8 = (bf16[160,1536]{1,0:T(8,128)(2,1)S(1)}, bf16[160,1536]{1,0:T(8,128)(2,1)S(1)}, u32[]{:S(2)}, u32[]{:S(2)}) collective-permute-start(bf16[160,1536]{1,0:T(8,128)(2,1)S(1)} %collective-permute-done.7.refs_0_), channel_id=1, source_target_pairs={{0,224},{32,0},{64,32},{96,64},{128,96},{160,128},{192,160},{224,1... | collective-permute-start | bytes 1474568 | tf_op jit(solution)/shard_map/ppermute | solution.py:298
  109.9 3.7 %fold.6 = (bf16[8,8,160,128]{3,2,1,0:T(8,128)(2,1)}, s32[1]{0:T(128)}) custom-call(s32[97]{0:T(128)S(1)} %pad_add_fusion.1.facts._, s32[5,1,1536]{2,1,0:T(1,128)S(1)} %pad_add_fusion.maps, bf16[160,1536]{1,0:T(8,128)(2,1)S(1)} %collective-permute-done.7.refs_0_, bf16[160,1536]{1,0:T(8,128)(2,1)S(1)} %collective-permute-done.10.refs_1_), custom_call_target="tpu_custom_call" | custom-call | flops 754974720 | bytes 1638400 | tf_op jit(solution)/shard_map/fold/pallas_call | solution.py:110
  113.6 6.8 %collective-permute-done.11.second.refs_1_ = bf16[160,1536]{1,0:T(8,128)(2,1)S(1)} collective-permute-done((bf16[160,1536]{1,0:T(8,128)(2,1)S(1)}, bf16[160,1536]{1,0:T(8,128)(2,1)S(1)}, u32[]{:S(2)}, u32[]{:S(2)}) %collective-permute-start.11) | collective-permute-done | bytes 491552 | tf_op jit(solution)/shard_map/ppermute | solution.py:298
  120.4 1.3 halves.2
  121.7 2.4 %collective-permute-start.12 = (bf16[80,1536]{1,0:T(8,128)(2,1)S(1)}, bf16[80,1536]{1,0:T(8,128)(2,1)S(1)}, u32[]{:S(2)}, u32[]{:S(2)}) collective-permute-start(bf16[80,1536]{1,0:T(8,128)(2,1)S(1)} %get-tuple-element.21), channel_id=1, source_target_pairs={{0,224},{32,0},{64,32},{96,64},{128,96},{160,128},{192,160},{224,1... | collective-permute-start | bytes 737288 | tf_op jit(solution)/shard_map/ppermute | solution.py:298
  124.2 6.0 %fold.7 = (bf16[8,8,160,128]{3,2,1,0:T(8,128)(2,1)}, s32[1]{0:T(128)}) custom-call(s32[97]{0:T(128)S(1)} %pad_add_fusion.1.facts._, s32[5,1,1536]{2,1,0:T(1,128)S(1)} %pad_add_fusion.maps, bf16[160,1536]{1,0:T(8,128)(2,1)S(1)} %collective-permute-done.6.refs_0_.refs_1_, ...), custom_call_target="tpu_custom_call", output_to_operand_aliasing={{0}: (6, {})} | custom-call | flops 1509949440 | bytes 3276800 | tf_op jit(solution)/shard_map/fold/pallas_call | solution.py:110
  130.6 4.1 %fold.8 = (bf16[8,8,160,128]{3,2,1,0:T(8,128)(2,1)}, s32[1]{0:T(128)}) custom-call(s32[97]{0:T(128)S(1)} %pad_add_fusion.1.facts._, s32[5,1,1536]{2,1,0:T(1,128)S(1)} %pad_add_fusion.maps, bf16[160,1536]{1,0:T(8,128)(2,1)S(1)} %copy-done.1, bf16[80,1536]{1,0:T(8,128)(2,1)S(1)} %collective-permute-done.12.refs_1_, ...), custom_call_target="tpu_custom_call", output_to_operand_aliasing={{0}: (5, {})} | custom-call | flops 754974720 | bytes 1638400 | tf_op jit(solution)/shard_map/fold/pallas_call | solution.py:110
  134.6 2.0 all-to-all-done.refs_1_.received
  136.6 6.4 %all-to-all-start.1 = ((bf16[8,8,160,128]{3,2,1,0:T(8,128)(2,1)}), bf16[8,8,160,128]{3,2,1,0:T(8,128)(2,1)}, u32[]{:S(2)}, u32[]{:S(2)}) async-start(bf16[8,8,160,128]{3,2,1,0:T(8,128)(2,1)} %joined.5), calls=%async_computation.1 | async-start | bytes 5242880 | tf_op jit(solution)/shard_map/all_to_all | solution.py:354
  143.1 9.4 %ladder.3 = (f32[224,1536]{1,0:T(8,128)}, bf16[224,1536]{1,0:T(8,128)(2,1)}) custom-call(s32[97]{0:T(128)} %copy-done.8, s32[5,1,1536]{2,1,0:T(1,128)} %copy-done.4, bf16[4096,1536]{1,0:T(8,128)(2,1)} %bitcast.22, bf16[8,8,224,128]{3,2,1,0:T(8,128)(2,1)} %all-to-all-done.refs_1_.received), custom_call_target="tpu_custom_call" | custom-call | flops 2818572288 | bytes 14417920 | tf_op jit(solution)/shard_map/ladder/pallas_call | solution.py:226
  152.5 2.0 collective-permute-start.17
  154.5 19.5 %all-to-all-done.1.received = bf16[8,8,160,128]{3,2,1,0:T(8,128)(2,1)} async-done(((bf16[8,8,160,128]{3,2,1,0:T(8,128)(2,1)}), bf16[8,8,160,128]{3,2,1,0:T(8,128)(2,1)}, u32[]{:S(2)}, u32[]{:S(2)}) %all-to-all-start.1) | async-done | bytes 2621472 | tf_op jit(solution)/shard_map/all_to_all | solution.py:354
  174.0 8.6 %ladder.2 = (f32[160,1536]{1,0:T(8,128)}, bf16[160,1536]{1,0:T(8,128)(2,1)}) custom-call(s32[97]{0:T(128)} %copy-done.8, s32[5,1,1536]{2,1,0:T(1,128)} %copy-done.4, bf16[4096,1536]{1,0:T(8,128)(2,1)} %bitcast.23, bf16[8,8,160,128]{3,2,1,0:T(8,128)(2,1)} %all-to-all-done.1.received), custom_call_target="tpu_custom_call" | custom-call | flops 2013265920 | bytes 13893632 | tf_op jit(solution)/shard_map/ladder/pallas_call | solution.py:226
  182.6 2.3 %collective-permute-start.16 = (bf16[160,1536]{1,0:T(8,128)(2,1)}, bf16[160,1536]{1,0:T(8,128)(2,1)S(1)}, u32[]{:S(2)}, u32[]{:S(2)}) collective-permute-start(bf16[160,1536]{1,0:T(8,128)(2,1)} %get-tuple-element.32), channel_id=1, source_target_pairs={{0,128},{32,160},{64,192},{96,224},{128,0},{160,32},{192,64},{224,... | collective-permute-start | bytes 1474568 | tf_op jit(solution)/shard_map/ppermute | solution.py:298
  184.9 4.5 %select_reduce_fusion.1 = (f32[1536]{0:T(1024)S(1)}, f32[1536]{0:T(1024)S(1)}) fusion(f32[2048]{0:T(1024)S(1)} %copy-done.16, s32[1536]{0:T(1024)S(1)} %get-tuple-element.35, s32[1536]{0:T(1024)S(1)} %get-tuple-element.36), kind=kLoop, calls=%fused_computation.2 | loop fusion | flops 18871296 | bytes 32768 | tf_op jit(solution)/shard_map/reduce_sum | solution.py:303
  190.6 0.6 stack.10
  191.8 0.8 copy.23.refs_4_
  192.6 1.4 copy.24.refs_4_
  194.0 0.8 pad_maximum_fusion.refs_5_
  194.8 2.3 %update.2.refs_6_ = bf16[384,1536]{1,0:T(8,128)(2,1)} custom-call(bf16[224,1536]{1,0:T(8,128)(2,1)S(1)} %slice_bitcast_fusion.refs_0_, f32[224,1536]{1,0:T(8,128)S(1)} %copy-done.2, bf16[224,1536]{1,0:T(8,128)(2,1)} %collective-permute-done.17.refs_2_, f32[1]{0:T(128)} %bitcast.12.refs_3_, f32[224,1]{1,0:T(8,128)S(1)} %copy.23.refs_4_, ...), custom_call_target="tpu_custom_call" | custom-call | flops 2752512 | bytes 3440640 | tf_op jit(solution)/shard_map/update/pallas_call | solution.py:281
  197.1 13.9 %collective-permute-done.16.refs_2_ = bf16[160,1536]{1,0:T(8,128)(2,1)S(1)} collective-permute-done((bf16[160,1536]{1,0:T(8,128)(2,1)}, bf16[160,1536]{1,0:T(8,128)(2,1)S(1)}, u32[]{:S(2)}, u32[]{:S(2)}) %collective-permute-start.16) | collective-permute-done | bytes 491552 | tf_op jit(solution)/shard_map/ppermute | solution.py:298
  211.0 1.0 update.3
  (68 shorter events, 3.2 us)
Async XLA Ops:
  6.5 40.2 %copy-start = (s32[64,1536]{1,0:T(8,128)S(1)}, s32[64,1536]{1,0:T(8,128)}, u32[]{:S(2)}) copy-start(s32[64,1536]{1,0:T(8,128)} %param.12) | copy-start | bytes 1179652
  6.5 3.7 %copy-start.17 = (s32[1,32]{1,0:T(1,128)S(1)}, s32[1,32]{1,0:T(1,128)}, u32[]{:S(2)}) copy-start(s32[1,32]{1,0:T(1,128)} %param.10) | copy-start | bytes 388
  6.5 3.7 %copy-start.15 = (s32[1,32]{1,0:T(1,128)S(1)}, s32[1,32]{1,0:T(1,128)}, u32[]{:S(2)}) copy-start(s32[1,32]{1,0:T(1,128)} %param.11) | copy-start | bytes 388
  6.5 136.5 %all-gather.4.cloned.1.call-start = ((), (), s32[]{:S(2)}) async-start(), calls=%async_computation.2 | async-start | bytes 15728640 | tf_op jit(solution)/shard_map/all_gather | solution.py:312
  8.4 16.8 %collective-permute-start = (bf16[224,1536]{1,0:T(8,128)(2,1)S(1)}, bf16[224,1536]{1,0:T(8,128)(2,1)S(1)}, u32[]{:S(2)}, u32[]{:S(2)}) collective-permute-start(bf16[224,1536]{1,0:T(8,128)(2,1)S(1)} %slice_bitcast_fusion.refs_0_), channel_id=1, source_target_pairs={{0,224},{32,0},{64,32},{96,64},{128,96},{160,128},{192,160},{224,1... | collective-permute-start | bytes 2064392 | tf_op jit(solution)/shard_map/ppermute | solution.py:298
  8.5 20.2 %collective-permute-start.3 = (bf16[224,1536]{1,0:T(8,128)(2,1)S(1)}, bf16[224,1536]{1,0:T(8,128)(2,1)S(1)}, u32[]{:S(2)}, u32[]{:S(2)}) collective-permute-start(bf16[224,1536]{1,0:T(8,128)(2,1)S(1)} %slice_bitcast_fusion.refs_0_), channel_id=1, source_target_pairs={{0,32},{32,64},{64,96},{96,128},{128,160},{160,192},{192,224},{224... | collective-permute-start | bytes 2064392 | tf_op jit(solution)/shard_map/ppermute | solution.py:298
  25.2 5.5 %copy-start.9 = (bf16[224,1536]{1,0:T(8,128)(2,1)}, bf16[224,1536]{1,0:T(8,128)(2,1)S(1)}, u32[]{:S(2)}) copy-start(bf16[224,1536]{1,0:T(8,128)(2,1)S(1)} %collective-permute-done.refs_0_) | copy-start | bytes 2064388
  25.2 16.0 %collective-permute-start.1 = (bf16[224,1536]{1,0:T(8,128)(2,1)S(1)}, bf16[224,1536]{1,0:T(8,128)(2,1)}, u32[]{:S(2)}, u32[]{:S(2)}) collective-permute-start(bf16[224,1536]{1,0:T(8,128)(2,1)S(1)} %collective-permute-done.refs_0_), channel_id=1, source_target_pairs={{0,224},{32,0},{64,32},{96,64},{128,96},{160,128},{192,160},{224,1... | collective-permute-start | bytes 2064392 | tf_op jit(solution)/shard_map/ppermute | solution.py:298
  28.7 16.7 %collective-permute-start.4 = (bf16[224,1536]{1,0:T(8,128)(2,1)S(1)}, bf16[224,1536]{1,0:T(8,128)(2,1)}, u32[]{:S(2)}, u32[]{:S(2)}) collective-permute-start(bf16[224,1536]{1,0:T(8,128)(2,1)S(1)} %collective-permute-done.3.refs_3_), channel_id=1, source_target_pairs={{0,32},{32,64},{64,96},{96,128},{128,160},{160,192},{192,224},{224... | collective-permute-start | bytes 2064392 | tf_op jit(solution)/shard_map/ppermute | solution.py:298
  28.7 0.9 copy-start.11
  41.2 17.0 %collective-permute-start.2 = (bf16[224,1536]{1,0:T(8,128)(2,1)}, bf16[224,1536]{1,0:T(8,128)(2,1)S(1)}, u32[]{:S(2)}, u32[]{:S(2)}) collective-permute-start(bf16[224,1536]{1,0:T(8,128)(2,1)} %collective-permute-done.1.refs_0_), channel_id=1, source_target_pairs={{0,224},{32,0},{64,32},{96,64},{128,96},{160,128},{192,160},{224,1... | collective-permute-start | bytes 2064392 | tf_op jit(solution)/shard_map/ppermute | solution.py:298
  45.4 16.0 %collective-permute-start.5 = (bf16[224,1536]{1,0:T(8,128)(2,1)}, bf16[224,1536]{1,0:T(8,128)(2,1)S(1)}, u32[]{:S(2)}, u32[]{:S(2)}) collective-permute-start(bf16[224,1536]{1,0:T(8,128)(2,1)} %collective-permute-done.4.refs_1_), channel_id=1, source_target_pairs={{0,32},{32,64},{64,96},{96,128},{128,160},{160,192},{192,224},{224... | collective-permute-start | bytes 2064392 | tf_op jit(solution)/shard_map/ppermute | solution.py:298
  46.7 83.8 %copy-start.8 = (s32[97]{0:T(128)}, s32[97]{0:T(128)S(1)}, u32[]{:S(2)}) copy-start(s32[97]{0:T(128)S(1)} %pad_add_fusion.1.facts._) | copy-start | bytes 1168
  46.7 23.6 %copy-start.10 = (bf16[224,1536]{1,0:T(8,128)(2,1)S(1)}, bf16[224,1536]{1,0:T(8,128)(2,1)}, u32[]{:S(2)}) copy-start(bf16[224,1536]{1,0:T(8,128)(2,1)} %copy-done.9) | copy-start | bytes 2064388
  46.8 23.6 %copy-start.12 = (bf16[224,1536]{1,0:T(8,128)(2,1)S(1)}, bf16[224,1536]{1,0:T(8,128)(2,1)}, u32[]{:S(2)}) copy-start(bf16[224,1536]{1,0:T(8,128)(2,1)} %copy-done.11) | copy-start | bytes 2064388
  61.4 22.9 %collective-permute-start.6 = (bf16[160,1536]{1,0:T(8,128)(2,1)}, bf16[160,1536]{1,0:T(8,128)(2,1)S(1)}, u32[]{:S(2)}, u32[]{:S(2)}) collective-permute-start(bf16[160,1536]{1,0:T(8,128)(2,1)} %joined.3.refs_0_), channel_id=1, source_target_pairs={{0,224},{32,0},{64,32},{96,64},{128,96},{160,128},{192,160},{224,1... | collective-permute-start | bytes 1474568 | tf_op jit(solution)/shard_map/ppermute | solution.py:298
  63.8 20.5 %collective-permute-start.9 = (bf16[160,1536]{1,0:T(8,128)(2,1)}, bf16[160,1536]{1,0:T(8,128)(2,1)S(1)}, u32[]{:S(2)}, u32[]{:S(2)}) collective-permute-start(bf16[160,1536]{1,0:T(8,128)(2,1)} %joined.3.refs_0_), channel_id=1, source_target_pairs={{0,32},{32,64},{64,96},{96,128},{128,160},{160,192},{192,224},{224... | collective-permute-start | bytes 1474568 | tf_op jit(solution)/shard_map/ppermute | solution.py:298
  64.1 14.4 %collective-permute-start.14 = (bf16[112,1536]{1,0:T(8,128)(2,1)S(1)}, bf16[112,1536]{1,0:T(8,128)(2,1)S(1)}, u32[]{:S(2)}, u32[]{:S(2)}) collective-permute-start(bf16[112,1536]{1,0:T(8,128)(2,1)S(1)} %get-tuple-element.26), channel_id=1, source_target_pairs={{0,224},{32,0},{64,32},{96,64},{128,96},{160,128},{192,160},{224,1... | collective-permute-start | bytes 1032200 | tf_op jit(solution)/shard_map/ppermute | solution.py:298
  65.6 14.7 %collective-permute-start.15 = (bf16[112,1536]{1,0:T(8,128)(2,1)S(1)}, bf16[112,1536]{1,0:T(8,128)(2,1)S(1)}, u32[]{:S(2)}, u32[]{:S(2)}) collective-permute-start(bf16[112,1536]{1,0:T(8,128)(2,1)S(1)} %get-tuple-element.27), channel_id=1, source_target_pairs={{0,32},{32,64},{64,96},{96,128},{128,160},{160,192},{192,224},{224... | collective-permute-start | bytes 1032200 | tf_op jit(solution)/shard_map/ppermute | solution.py:298
  65.6 64.9 %copy-start.4 = (s32[5,1,1536]{2,1,0:T(1,128)}, s32[5,1,1536]{2,1,0:T(1,128)S(1)}, u32[]{:S(2)}) copy-start(s32[5,1,1536]{2,1,0:T(1,128)S(1)} %pad_add_fusion.maps) | copy-start | bytes 92164
  84.3 0.8 copy-start.5
  85.1 51.5 %all-to-all-start = ((bf16[8,8,224,128]{3,2,1,0:T(8,128)(2,1)}), bf16[8,8,224,128]{3,2,1,0:T(8,128)(2,1)}, u32[]{:S(2)}, u32[]{:S(2)}) async-start(bf16[8,8,224,128]{3,2,1,0:T(8,128)(2,1)} %joined.4), calls=%async_computation | async-start | bytes 7340032 | tf_op jit(solution)/shard_map/all_to_all | solution.py:354
  94.4 29.7 %copy-start.6 = (bf16[160,1536]{1,0:T(8,128)(2,1)S(1)}, bf16[160,1536]{1,0:T(8,128)(2,1)}, u32[]{:S(2)}) copy-start(bf16[160,1536]{1,0:T(8,128)(2,1)} %copy-done.5) | copy-start | bytes 1474564
  94.4 12.9 %collective-permute-start.10 = (bf16[160,1536]{1,0:T(8,128)(2,1)}, bf16[160,1536]{1,0:T(8,128)(2,1)S(1)}, u32[]{:S(2)}, u32[]{:S(2)}) collective-permute-start(bf16[160,1536]{1,0:T(8,128)(2,1)} %copy-done.5), channel_id=1, source_target_pairs={{0,32},{32,64},{64,96},{96,128},{128,160},{160,192},{192,224},{224... | collective-permute-start | bytes 1474568 | tf_op jit(solution)/shard_map/ppermute | solution.py:298
  94.5 12.9 %collective-permute-start.7 = (bf16[160,1536]{1,0:T(8,128)(2,1)S(1)}, bf16[160,1536]{1,0:T(8,128)(2,1)S(1)}, u32[]{:S(2)}, u32[]{:S(2)}) collective-permute-start(bf16[160,1536]{1,0:T(8,128)(2,1)S(1)} %collective-permute-done.6.refs_0_.refs_1_), channel_id=1, source_target_pairs={{0,224},{32,0},{64,32},{96,64},{128,96},{160,128},{192,160},{224,1... | collective-permute-start | bytes 1474568 | tf_op jit(solution)/shard_map/ppermute | solution.py:298
  107.3 13.1 %collective-permute-start.11 = (bf16[160,1536]{1,0:T(8,128)(2,1)S(1)}, bf16[160,1536]{1,0:T(8,128)(2,1)S(1)}, u32[]{:S(2)}, u32[]{:S(2)}) collective-permute-start(bf16[160,1536]{1,0:T(8,128)(2,1)S(1)} %collective-permute-done.10.refs_1_), channel_id=1, source_target_pairs={{0,32},{32,64},{64,96},{96,128},{128,160},{160,192},{192,224},{224... | collective-permute-start | bytes 1474568 | tf_op jit(solution)/shard_map/ppermute | solution.py:298
  107.3 13.1 %collective-permute-start.8 = (bf16[160,1536]{1,0:T(8,128)(2,1)S(1)}, bf16[160,1536]{1,0:T(8,128)(2,1)S(1)}, u32[]{:S(2)}, u32[]{:S(2)}) collective-permute-start(bf16[160,1536]{1,0:T(8,128)(2,1)S(1)} %collective-permute-done.7.refs_0_), channel_id=1, source_target_pairs={{0,224},{32,0},{64,32},{96,64},{128,96},{160,128},{192,160},{224,1... | collective-permute-start | bytes 1474568 | tf_op jit(solution)/shard_map/ppermute | solution.py:298
  113.6 16.9 %copy-start.1 = (bf16[160,1536]{1,0:T(8,128)(2,1)S(1)}, bf16[160,1536]{1,0:T(8,128)(2,1)}, u32[]{:S(2)}) copy-start(bf16[160,1536]{1,0:T(8,128)(2,1)} %joined.3.refs_0_) | copy-start | bytes 1474564
  121.7 8.4 %collective-permute-start.12 = (bf16[80,1536]{1,0:T(8,128)(2,1)S(1)}, bf16[80,1536]{1,0:T(8,128)(2,1)S(1)}, u32[]{:S(2)}, u32[]{:S(2)}) collective-permute-start(bf16[80,1536]{1,0:T(8,128)(2,1)S(1)} %get-tuple-element.21), channel_id=1, source_target_pairs={{0,224},{32,0},{64,32},{96,64},{128,96},{160,128},{192,160},{224,1... | collective-permute-start | bytes 737288 | tf_op jit(solution)/shard_map/ppermute | solution.py:298
  124.2 6.4 %collective-permute-start.13 = (bf16[80,1536]{1,0:T(8,128)(2,1)S(1)}, bf16[80,1536]{1,0:T(8,128)(2,1)S(1)}, u32[]{:S(2)}, u32[]{:S(2)}) collective-permute-start(bf16[80,1536]{1,0:T(8,128)(2,1)S(1)} %get-tuple-element.22), channel_id=1, source_target_pairs={{0,32},{32,64},{64,96},{96,128},{128,160},{160,192},{192,224},{224... | collective-permute-start | bytes 737288 | tf_op jit(solution)/shard_map/ppermute | solution.py:298
  136.6 6.4 %copy-start.13 = (s32[1,2,1536]{2,1,0:T(2,128)S(1)}, s32[1,2,1536]{2,1,0:T(2,128)}, u32[]{:S(2)}) copy-start(s32[1,2,1536]{2,1,0:T(2,128)} %param.13) | copy-start | bytes 36868
  136.6 37.4 %all-to-all-start.1 = ((bf16[8,8,160,128]{3,2,1,0:T(8,128)(2,1)}), bf16[8,8,160,128]{3,2,1,0:T(8,128)(2,1)}, u32[]{:S(2)}, u32[]{:S(2)}) async-start(bf16[8,8,160,128]{3,2,1,0:T(8,128)(2,1)} %joined.5), calls=%async_computation.1 | async-start | bytes 5242880 | tf_op jit(solution)/shard_map/all_to_all | solution.py:354
  152.4 32.5 %copy-start.16 = (f32[2048]{0:T(1024)S(1)}, f32[2048]{0:T(1024)}, u32[]{:S(2)}) copy-start(f32[2048]{0:T(1024)} %param.14) | copy-start | bytes 24580
  152.4 37.0 %copy-start.14 = (f32[384]{0:T(512)S(1)}, f32[384]{0:T(512)}, u32[]{:S(2)}) copy-start(f32[384]{0:T(512)} %param.15) | copy-start | bytes 4612
  152.4 42.4 %copy-start.2 = (f32[224,1536]{1,0:T(8,128)S(1)}, f32[224,1536]{1,0:T(8,128)}, u32[]{:S(2)}) copy-start(f32[224,1536]{1,0:T(8,128)} %get-tuple-element.33.refs_1_) | copy-start | bytes 4128772
  152.5 42.4 %collective-permute-start.17 = (bf16[224,1536]{1,0:T(8,128)(2,1)}, bf16[224,1536]{1,0:T(8,128)(2,1)}, u32[]{:S(2)}, u32[]{:S(2)}) collective-permute-start(bf16[224,1536]{1,0:T(8,128)(2,1)} %get-tuple-element.34), channel_id=1, source_target_pairs={{0,128},{32,160},{64,192},{96,224},{128,0},{160,32},{192,64},{224,... | collective-permute-start | bytes 2064392 | tf_op jit(solution)/shard_map/ppermute | solution.py:298
  182.6 28.4 %collective-permute-start.16 = (bf16[160,1536]{1,0:T(8,128)(2,1)}, bf16[160,1536]{1,0:T(8,128)(2,1)S(1)}, u32[]{:S(2)}, u32[]{:S(2)}) collective-permute-start(bf16[160,1536]{1,0:T(8,128)(2,1)} %get-tuple-element.32), channel_id=1, source_target_pairs={{0,128},{32,160},{64,192},{96,224},{128,0},{160,32},{192,64},{224,... | collective-permute-start | bytes 1474568 | tf_op jit(solution)/shard_map/ppermute | solution.py:298
  194.0 17.0 %copy-start.3 = (f32[160,1536]{1,0:T(8,128)S(1)}, f32[160,1536]{1,0:T(8,128)}, u32[]{:S(2)}) copy-start(f32[160,1536]{1,0:T(8,128)} %get-tuple-element.31.refs_1_) | copy-start | bytes 2949124
  194.0 17.0 %copy-start.7 = (f32[160,1]{1,0:T(8,128)S(1)}, f32[160,1]{1,0:T(8,128)}, u32[]{:S(2)}) copy-start(f32[160,1]{1,0:T(8,128)} %copy.24.refs_4_) | copy-start | bytes 1924
Sparse Core Ops, SparseCore 0:
  9.2 122.6 all-gather.3

commit v9 on v8

--- a/solution.py
+++ b/solution.py
@@ -326,19 +326,19 @@
     first = energies(vir_energy, pair_virt[0, 0])
     second = energies(vir_energy, pair_virt[0, 1])
     virtual = jnp.stack([first, second])
-    chunks = ((224,), (160,))
+    chunks = ((256,), (128,))
     steps, folds, low = [], [], 0
     for pieces in chunks:
         part = own[low : low + sum(pieces)]
         low += sum(pieces)
         if steps:
-            part = joined(part, steps[-1][2], pltpu.HBM)
+            part = joined(part, steps[-1][3], pltpu.HBM)
         one = (shifted(part, -1), shifted(part, 1))
         two = (shifted(one[0], -1), shifted(one[1], 1))
         weight = WEIGHT if steps else 1
         *slots, done = fold((2,), facts, maps, two, pieces, (), weight)
         three = (shifted(two[0], -1), shifted(two[1], 1))
-        upper, lower = halves(*three, done if steps else facts)
+        upper, lower = halves(*three, done)
         far = (shifted(upper, -1), shifted(lower, 1))
         odd = (one[0], three[1], three[0], one[1])
         *slots, _ = fold((1, 3), facts, maps, odd, pieces, slots, weight)
@@ -349,8 +349,8 @@
         weight = WEIGHT if i else 1
         *slots, _ = fold((0,), facts, maps, (part, *far), chunks[i], folds[i], weight)
         for piece in slots:
-            later = steps[i + 1][1] if i + 1 < len(steps) else ()
-            piece = joined(piece, (*later, *last), pltpu.HBM)
+            if last:
+                piece = joined(piece, last, pltpu.HBM)
             received = lax.all_to_all(piece, "ket", split_axis=0, concat_axis=0, tiled=True)
             ladder, sent = ladder_of(facts, maps, all_blocks, received)
             last = (received,)

time: 223 us -> 224 us (level); the launches traced: 219 us -> 222 us
  waiting for transfers between devices: 90.6 us -> 101 us
  local copies, waits for them, and re-layouts: 9.43 us -> 4.02 us
    ppermute x18, waiting for transfers between devices: 68.4 us -> 89.7 us  [shifted(): return lax.ppermute(block, 'bra', [(i, (i + by) % 8) for i in range(8)])]
    all_to_all x2, waiting for transfers between devices: 21.4 us -> 10.7 us  [local(): lax.all_to_all(piece, 'ket', split_axis=0, concat_axis=0, tiled=True)]
  transfers between devices with their start and end apart: 21 -> 21, of which waited for: 14 -> 17; matrix products, arithmetic and copies ran while one was open for 6% -> 3% of each run, Pallas kernels for 23% -> 22%
where the time goes in v9:
time: 224 us; the launch traced here: 222 us
  waiting for transfers between devices  101 us (45%)
  Pallas kernels  51 us (23%)
  starting transfers between devices  37.7 us (17%)
  between operations  13.7 us (6%)
  blocking collectives  9.94 us (4%)
  other arithmetic  4.93 us (2%)
  local copies, waits for them, and re-layouts  4.02 us (2%)
    ppermute x18, waiting for transfers between devices, shifted(): return lax.ppermute(block, 'bra', [(i, (i + by) % 8) for i in range(8)])  89.7 us
    pallas_call x6, Pallas kernels, fold(): pl.pallas_call(functools.partial(fold_body, shifts, pieces), in_specs=[pl...  26.4 us
    ppermute x18, starting transfers between devices, shifted(): return lax.ppermute(block, 'bra', [(i, (i + by) % 8) for i in range(8)])  21.2 us
    pallas_call x2, Pallas kernels, ladder_of(): pl.pallas_call(ladder_body, in_specs=[pl.BlockSpec(memory_space=pltpu.SME...  18 us
    all_to_all x2, starting transfers between devices, local(): lax.all_to_all(piece, 'ket', split_axis=0, concat_axis=0, tiled=True)  16.5 us
    all_to_all x2, waiting for transfers between devices, local(): lax.all_to_all(piece, 'ket', split_axis=0, concat_axis=0, tiled=True)  10.7 us
    all_gather x1, blocking collectives, local(): wanted = lax.all_gather(block_owner[0] * 16 + screen_list[0], 'ket', axis=0)  9.94 us
    reduce_sum x1, other arithmetic, energies(): jnp.sum(jnp.where(number == indices[None, :], table[:, None], 0.0), axis=0)  4.54 us
  transfers between devices with their start and end apart: 21, of which 17 were waited for; matrix products, arithmetic and copies ran while one was open for 3% of the time, Pallas kernels for 22%

profile of v9, /device:TPU:47, one launch (start us, length us, event | category | flops | bytes accessed | tf_op | source)
XLA Modules:
  0.0 222.4 jit_solution(6494209044369218001)
XLA Ops:
  6.6 0.7 all-gather.4.cloned.1.call-update
  7.3 0.6 copy-done.8
  8.0 1.7 collective-permute-start.3
  9.7 17.1 %collective-permute-done.refs_0_ = bf16[256,1536]{1,0:T(8,128)(2,1)S(1)} collective-permute-done((bf16[256,1536]{1,0:T(8,128)(2,1)S(1)}, bf16[256,1536]{1,0:T(8,128)(2,1)S(1)}, u32[]{:S(2)}, u32[]{:S(2)}) %collective-permute-start) | collective-permute-done | bytes 786464 | tf_op jit(solution)/shard_map/ppermute | solution.py:298
  26.8 2.8 %collective-permute-start.1 = (bf16[256,1536]{1,0:T(8,128)(2,1)S(1)}, bf16[256,1536]{1,0:T(8,128)(2,1)}, u32[]{:S(2)}, u32[]{:S(2)}) collective-permute-start(bf16[256,1536]{1,0:T(8,128)(2,1)S(1)} %collective-permute-done.refs_0_), channel_id=1, source_target_pairs={{0,224},{32,0},{64,32},{96,64},{128,96},{160,128},{192,160},{224,1... | collective-permute-start | bytes 2359304 | tf_op jit(solution)/shard_map/ppermute | solution.py:298
  29.6 0.8 collective-permute-done.3.refs_3_
  30.5 9.9 %all-gather.1 = s32[8,1,32]{2,1,0:T(1,128)S(1)} all-gather(s32[1,1,32]{2,1,0:T(1,128)S(1)} %add_bitcast_fusion), channel_id=1, replica_groups=mesh['bra'=8,'ket'=8,'pair'=4] {'ket'}, dimensions={0}, use_global_device_ids=true | all-gather | bytes 1152 | tf_op jit(solution)/shard_map/all_gather | solution.py:314
  40.4 0.3 select_reduce_fusion.2
  40.9 4.0 %collective-permute-done.1.refs_0_ = bf16[256,1536]{1,0:T(8,128)(2,1)} collective-permute-done((bf16[256,1536]{1,0:T(8,128)(2,1)S(1)}, bf16[256,1536]{1,0:T(8,128)(2,1)}, u32[]{:S(2)}, u32[]{:S(2)}) %collective-permute-start.1) | collective-permute-done | bytes 786464 | tf_op jit(solution)/shard_map/ppermute | solution.py:298
  44.9 3.4 %collective-permute-start.2 = (bf16[256,1536]{1,0:T(8,128)(2,1)}, bf16[256,1536]{1,0:T(8,128)(2,1)S(1)}, u32[]{:S(2)}, u32[]{:S(2)}) collective-permute-start(bf16[256,1536]{1,0:T(8,128)(2,1)} %collective-permute-done.1.refs_0_), channel_id=1, source_target_pairs={{0,224},{32,0},{64,32},{96,64},{128,96},{160,128},{192,160},{224,1... | collective-permute-start | bytes 2359304 | tf_op jit(solution)/shard_map/ppermute | solution.py:298
  48.3 0.8 collective-permute-done.4.refs_1_
  49.2 5.0 %fold.6 = (bf16[8,8,256,128]{3,2,1,0:T(8,128)(2,1)}, s32[1]{0:T(128)}) custom-call(s32[97]{0:T(128)S(1)} %pad_add_fusion.1.facts, s32[5,1,1536]{2,1,0:T(1,128)S(1)} %pad_add_fusion.maps, bf16[256,1536]{1,0:T(8,128)(2,1)} %collective-permute-done.1.refs_0_, bf16[256,1536]{1,0:T(8,128)(2,1)} %collective-permute-done.4.refs_1_), custom_call_target="tpu_custom_call" | custom-call | flops 1207959552 | bytes 2621440 | tf_op jit(solution)/shard_map/fold/pallas_call | solution.py:110
  54.2 9.9 %collective-permute-done.2.first.refs_2_ = bf16[256,1536]{1,0:T(8,128)(2,1)S(1)} collective-permute-done((bf16[256,1536]{1,0:T(8,128)(2,1)}, bf16[256,1536]{1,0:T(8,128)(2,1)S(1)}, u32[]{:S(2)}, u32[]{:S(2)}) %collective-permute-start.2) | collective-permute-done | bytes 786464 | tf_op jit(solution)/shard_map/ppermute | solution.py:298
  64.1 3.2 %collective-permute-done.5.second.refs_1_ = bf16[256,1536]{1,0:T(8,128)(2,1)S(1)} collective-permute-done((bf16[256,1536]{1,0:T(8,128)(2,1)}, bf16[256,1536]{1,0:T(8,128)(2,1)S(1)}, u32[]{:S(2)}, u32[]{:S(2)}) %collective-permute-start.5) | collective-permute-done | bytes 786464 | tf_op jit(solution)/shard_map/ppermute | solution.py:298
  67.2 1.1 halves.2
  68.3 2.5 %collective-permute-start.6 = (bf16[128,1536]{1,0:T(8,128)(2,1)S(1)}, bf16[128,1536]{1,0:T(8,128)(2,1)S(1)}, u32[]{:S(2)}, u32[]{:S(2)}) collective-permute-start(bf16[128,1536]{1,0:T(8,128)(2,1)S(1)} %get-tuple-element.22), channel_id=1, source_target_pairs={{0,224},{32,0},{64,32},{96,64},{128,96},{160,128},{192,160},{224,1... | collective-permute-start | bytes 1179656 | tf_op jit(solution)/shard_map/ppermute | solution.py:298
  70.8 1.1 copy-done.7
  72.0 5.6 %fold.10 = (bf16[8,8,256,128]{3,2,1,0:T(8,128)(2,1)}, s32[1]{0:T(128)}) custom-call(s32[97]{0:T(128)S(1)} %pad_add_fusion.1.facts, s32[5,1,1536]{2,1,0:T(1,128)S(1)} %pad_add_fusion.maps, bf16[256,1536]{1,0:T(8,128)(2,1)S(1)} %collective-permute-done.refs_0_, ...), custom_call_target="tpu_custom_call", output_to_operand_aliasing={{0}: (6, {})} | custom-call | flops 2415919104 | bytes 5242880 | tf_op jit(solution)/shard_map/fold/pallas_call | solution.py:110
  77.6 0.3 collective-permute-done.7.refs_2_
  77.8 4.2 %fold.11 = (bf16[8,8,256,128]{3,2,1,0:T(8,128)(2,1)}, s32[1]{0:T(128)}) custom-call(s32[97]{0:T(128)S(1)} %pad_add_fusion.1.facts, s32[5,1,1536]{2,1,0:T(1,128)S(1)} %pad_add_fusion.maps, bf16[256,1536]{1,0:T(8,128)(2,1)S(1)} %slice_bitcast_fusion.refs_0_, bf16[128,1536]{1,0:T(8,128)(2,1)S(1)} %collective-permute-done.6.refs_1_, ...), custom_call_target="tpu_custom_call", output_to_operand_aliasing={{0}: (5, {})} | custom-call | flops 1207959552 | bytes 2621440 | tf_op jit(solution)/shard_map/fold/pallas_call | solution.py:110
  82.0 9.2 %all-to-all-start = ((bf16[8,8,256,128]{3,2,1,0:T(8,128)(2,1)}), bf16[8,8,256,128]{3,2,1,0:T(8,128)(2,1)}, u32[]{:S(2)}, u32[]{:S(2)}) async-start(bf16[8,8,256,128]{3,2,1,0:T(8,128)(2,1)} %get-tuple-element.32), calls=%async_computation | async-start | bytes 8388608 | tf_op jit(solution)/shard_map/all_to_all | solution.py:354
  91.3 1.0 slice_bitcast_fusion.1.refs_0_
  92.3 0.7 copy.25.refs_0_
  93.0 1.4 collective-permute-start.8
  94.5 9.2 %collective-permute-done.8.refs_0_ = bf16[128,1536]{1,0:T(8,128)(2,1)S(1)} collective-permute-done((bf16[128,1536]{1,0:T(8,128)(2,1)}, bf16[128,1536]{1,0:T(8,128)(2,1)S(1)}, u32[]{:S(2)}, u32[]{:S(2)}) %collective-permute-start.8) | collective-permute-done | bytes 393248 | tf_op jit(solution)/shard_map/ppermute | solution.py:298
  103.7 1.4 collective-permute-start.9
  105.2 8.2 %collective-permute-done.9.refs_0_ = bf16[128,1536]{1,0:T(8,128)(2,1)S(1)} collective-permute-done((bf16[128,1536]{1,0:T(8,128)(2,1)S(1)}, bf16[128,1536]{1,0:T(8,128)(2,1)S(1)}, u32[]{:S(2)}, u32[]{:S(2)}) %collective-permute-start.9) | collective-permute-done | bytes 393248 | tf_op jit(solution)/shard_map/ppermute | solution.py:298
  113.3 1.4 collective-permute-start.10
  114.7 0.4 collective-permute-done.12.refs_1_
  115.0 3.3 %fold.7 = (bf16[8,8,128,128]{3,2,1,0:T(8,128)(2,1)}, s32[1]{0:T(128)}) custom-call(s32[97]{0:T(128)S(1)} %pad_add_fusion.1.facts, s32[5,1,1536]{2,1,0:T(1,128)S(1)} %pad_add_fusion.maps, bf16[128,1536]{1,0:T(8,128)(2,1)S(1)} %collective-permute-done.9.refs_0_, bf16[128,1536]{1,0:T(8,128)(2,1)S(1)} %collective-permute-done.12.refs_1_), custom_call_target="tpu_custom_call" | custom-call | flops 603979776 | bytes 1310720 | tf_op jit(solution)/shard_map/fold/pallas_call | solution.py:110
  118.3 3.8 %collective-permute-done.10.first.refs_2_ = bf16[128,1536]{1,0:T(8,128)(2,1)S(1)} collective-permute-done((bf16[128,1536]{1,0:T(8,128)(2,1)S(1)}, bf16[128,1536]{1,0:T(8,128)(2,1)S(1)}, u32[]{:S(2)}, u32[]{:S(2)}) %collective-permute-start.10) | collective-permute-done | bytes 393248 | tf_op jit(solution)/shard_map/ppermute | solution.py:298
  122.1 2.9 %collective-permute-done.13.second.refs_1_ = bf16[128,1536]{1,0:T(8,128)(2,1)S(1)} collective-permute-done((bf16[128,1536]{1,0:T(8,128)(2,1)S(1)}, bf16[128,1536]{1,0:T(8,128)(2,1)S(1)}, u32[]{:S(2)}, u32[]{:S(2)}) %collective-permute-start.13) | collective-permute-done | bytes 393248 | tf_op jit(solution)/shard_map/ppermute | solution.py:298
  125.1 1.1 halves.3
  126.2 2.5 %collective-permute-start.14 = (bf16[64,1536]{1,0:T(8,128)(2,1)S(1)}, bf16[64,1536]{1,0:T(8,128)(2,1)S(1)}, u32[]{:S(2)}, u32[]{:S(2)}) collective-permute-start(bf16[64,1536]{1,0:T(8,128)(2,1)S(1)} %get-tuple-element.25), channel_id=1, source_target_pairs={{0,224},{32,0},{64,32},{96,64},{128,96},{160,128},{192,160},{224,1... | collective-permute-start | bytes 589832 | tf_op jit(solution)/shard_map/ppermute | solution.py:298
  128.7 4.8 %fold.8 = (bf16[8,8,128,128]{3,2,1,0:T(8,128)(2,1)}, s32[1]{0:T(128)}) custom-call(s32[97]{0:T(128)S(1)} %pad_add_fusion.1.facts, s32[5,1,1536]{2,1,0:T(1,128)S(1)} %pad_add_fusion.maps, bf16[128,1536]{1,0:T(8,128)(2,1)S(1)} %collective-permute-done.8.refs_0_, ...), custom_call_target="tpu_custom_call", output_to_operand_aliasing={{0}: (6, {})} | custom-call | flops 1207959552 | bytes 2621440 | tf_op jit(solution)/shard_map/fold/pallas_call | solution.py:110
  133.6 3.6 %fold.9 = (bf16[8,8,128,128]{3,2,1,0:T(8,128)(2,1)}, s32[1]{0:T(128)}) custom-call(s32[97]{0:T(128)S(1)} %pad_add_fusion.1.facts, s32[5,1,1536]{2,1,0:T(1,128)S(1)} %pad_add_fusion.maps, bf16[128,1536]{1,0:T(8,128)(2,1)S(1)} %copy-done.1, bf16[64,1536]{1,0:T(8,128)(2,1)S(1)} %collective-permute-done.14.refs_1_, ...), custom_call_target="tpu_custom_call", output_to_operand_aliasing={{0}: (5, {})} | custom-call | flops 603979776 | bytes 1310720 | tf_op jit(solution)/shard_map/fold/pallas_call | solution.py:110
  137.2 1.9 all-to-all-done.refs_1_.received
  139.1 7.3 %all-to-all-start.1 = ((bf16[8,8,128,128]{3,2,1,0:T(8,128)(2,1)}), bf16[8,8,128,128]{3,2,1,0:T(8,128)(2,1)}, u32[]{:S(2)}, u32[]{:S(2)}) async-start(bf16[8,8,128,128]{3,2,1,0:T(8,128)(2,1)} %joined.3), calls=%async_computation.1 | async-start | bytes 4194304 | tf_op jit(solution)/shard_map/all_to_all | solution.py:354
  146.4 9.7 %ladder.3 = (f32[256,1536]{1,0:T(8,128)}, bf16[256,1536]{1,0:T(8,128)(2,1)}) custom-call(s32[97]{0:T(128)} %copy-done.5, s32[5,1,1536]{2,1,0:T(1,128)} %copy-done.4, bf16[4096,1536]{1,0:T(8,128)(2,1)} %bitcast.23, bf16[8,8,256,128]{3,2,1,0:T(8,128)(2,1)} %all-to-all-done.refs_1_.received), custom_call_target="tpu_custom_call" | custom-call | flops 3221225472 | bytes 14680064 | tf_op jit(solution)/shard_map/ladder/pallas_call | solution.py:226
  156.2 2.0 collective-permute-start.17
  158.2 4.5 %select_reduce_fusion.1 = (f32[1536]{0:T(1024)S(1)}, f32[1536]{0:T(1024)S(1)}) fusion(f32[2048]{0:T(1024)S(1)} %copy-done.12, s32[1536]{0:T(1024)S(1)} %get-tuple-element.37, s32[1536]{0:T(1024)S(1)} %get-tuple-element.38), kind=kLoop, calls=%fused_computation.2 | loop fusion | flops 18871296 | bytes 32768 | tf_op jit(solution)/shard_map/reduce_sum | solution.py:303
  162.9 8.8 %all-to-all-done.1.received = bf16[8,8,128,128]{3,2,1,0:T(8,128)(2,1)} async-done(((bf16[8,8,128,128]{3,2,1,0:T(8,128)(2,1)}), bf16[8,8,128,128]{3,2,1,0:T(8,128)(2,1)}, u32[]{:S(2)}, u32[]{:S(2)}) %all-to-all-start.1) | async-done | bytes 2097184 | tf_op jit(solution)/shard_map/all_to_all | solution.py:354
  171.7 8.2 %ladder.2 = (f32[128,1536]{1,0:T(8,128)}, bf16[128,1536]{1,0:T(8,128)(2,1)}) custom-call(s32[97]{0:T(128)} %copy-done.5, s32[5,1,1536]{2,1,0:T(1,128)} %copy-done.4, bf16[4096,1536]{1,0:T(8,128)(2,1)} %bitcast.24, bf16[8,8,128,128]{3,2,1,0:T(8,128)(2,1)} %all-to-all-done.1.received), custom_call_target="tpu_custom_call" | custom-call | flops 1610612736 | bytes 13631488 | tf_op jit(solution)/shard_map/ladder/pallas_call | solution.py:226
  180.0 2.0 collective-permute-start.16
  182.1 23.1 %collective-permute-done.17.refs_2_ = bf16[256,1536]{1,0:T(8,128)(2,1)} collective-permute-done((bf16[256,1536]{1,0:T(8,128)(2,1)}, bf16[256,1536]{1,0:T(8,128)(2,1)}, u32[]{:S(2)}, u32[]{:S(2)}) %collective-permute-start.17) | collective-permute-done | bytes 786464 | tf_op jit(solution)/shard_map/ppermute | solution.py:298
  205.2 2.4 %update.2.refs_6_ = bf16[384,1536]{1,0:T(8,128)(2,1)} custom-call(bf16[256,1536]{1,0:T(8,128)(2,1)S(1)} %slice_bitcast_fusion.refs_0_, f32[256,1536]{1,0:T(8,128)S(1)} %copy-done.2, bf16[256,1536]{1,0:T(8,128)(2,1)} %collective-permute-done.17.refs_2_, f32[1]{0:T(128)} %bitcast.12.refs_3_, f32[256,1]{1,0:T(8,128)S(1)} %copy.23.refs_4_, ...), custom_call_target="tpu_custom_call" | custom-call | flops 3145728 | bytes 3932160 | tf_op jit(solution)/shard_map/update/pallas_call | solution.py:281
  207.6 6.0 %collective-permute-done.16.refs_2_ = bf16[128,1536]{1,0:T(8,128)(2,1)} collective-permute-done((bf16[128,1536]{1,0:T(8,128)(2,1)}, bf16[128,1536]{1,0:T(8,128)(2,1)}, u32[]{:S(2)}, u32[]{:S(2)}) %collective-permute-start.16) | collective-permute-done | bytes 393248 | tf_op jit(solution)/shard_map/ppermute | solution.py:298
  213.6 2.0 update.3
  (60 shorter events, 1.1 us)
Async XLA Ops:
  6.5 42.6 %copy-start = (s32[64,1536]{1,0:T(8,128)S(1)}, s32[64,1536]{1,0:T(8,128)}, u32[]{:S(2)}) copy-start(s32[64,1536]{1,0:T(8,128)} %param.12) | copy-start | bytes 1179652
  6.5 1.3 copy-start.8
  6.5 23.9 %copy-start.13 = (s32[1,32]{1,0:T(1,128)S(1)}, s32[1,32]{1,0:T(1,128)}, u32[]{:S(2)}) copy-start(s32[1,32]{1,0:T(1,128)} %param.10) | copy-start | bytes 388
  6.5 23.9 %copy-start.11 = (s32[1,32]{1,0:T(1,128)S(1)}, s32[1,32]{1,0:T(1,128)}, u32[]{:S(2)}) copy-start(s32[1,32]{1,0:T(1,128)} %param.11) | copy-start | bytes 388
  6.5 139.9 %all-gather.4.cloned.1.call-start = ((), (), s32[]{:S(2)}) async-start(), calls=%async_computation.2 | async-start | bytes 15728640 | tf_op jit(solution)/shard_map/all_gather | solution.py:312
  7.9 18.9 %collective-permute-start = (bf16[256,1536]{1,0:T(8,128)(2,1)S(1)}, bf16[256,1536]{1,0:T(8,128)(2,1)S(1)}, u32[]{:S(2)}, u32[]{:S(2)}) collective-permute-start(bf16[256,1536]{1,0:T(8,128)(2,1)S(1)} %slice_bitcast_fusion.refs_0_), channel_id=1, source_target_pairs={{0,224},{32,0},{64,32},{96,64},{128,96},{160,128},{192,160},{224,1... | collective-permute-start | bytes 2359304 | tf_op jit(solution)/shard_map/ppermute | solution.py:298
  8.0 22.4 %collective-permute-start.3 = (bf16[256,1536]{1,0:T(8,128)(2,1)S(1)}, bf16[256,1536]{1,0:T(8,128)(2,1)S(1)}, u32[]{:S(2)}, u32[]{:S(2)}) collective-permute-start(bf16[256,1536]{1,0:T(8,128)(2,1)S(1)} %slice_bitcast_fusion.refs_0_), channel_id=1, source_target_pairs={{0,32},{32,64},{64,96},{96,128},{128,160},{160,192},{192,224},{224... | collective-permute-start | bytes 2359304 | tf_op jit(solution)/shard_map/ppermute | solution.py:298
  26.8 18.1 %collective-permute-start.1 = (bf16[256,1536]{1,0:T(8,128)(2,1)S(1)}, bf16[256,1536]{1,0:T(8,128)(2,1)}, u32[]{:S(2)}, u32[]{:S(2)}) collective-permute-start(bf16[256,1536]{1,0:T(8,128)(2,1)S(1)} %collective-permute-done.refs_0_), channel_id=1, source_target_pairs={{0,224},{32,0},{64,32},{96,64},{128,96},{160,128},{192,160},{224,1... | collective-permute-start | bytes 2359304 | tf_op jit(solution)/shard_map/ppermute | solution.py:298
  30.4 37.9 %copy-start.6 = (bf16[256,1536]{1,0:T(8,128)(2,1)}, bf16[256,1536]{1,0:T(8,128)(2,1)S(1)}, u32[]{:S(2)}) copy-start(bf16[256,1536]{1,0:T(8,128)(2,1)S(1)} %collective-permute-done.3.refs_3_) | copy-start | bytes 2359300
  30.4 18.7 %collective-permute-start.4 = (bf16[256,1536]{1,0:T(8,128)(2,1)S(1)}, bf16[256,1536]{1,0:T(8,128)(2,1)}, u32[]{:S(2)}, u32[]{:S(2)}) collective-permute-start(bf16[256,1536]{1,0:T(8,128)(2,1)S(1)} %collective-permute-done.3.refs_3_), channel_id=1, source_target_pairs={{0,32},{32,64},{64,96},{96,128},{128,160},{160,192},{192,224},{224... | collective-permute-start | bytes 2359304 | tf_op jit(solution)/shard_map/ppermute | solution.py:298
  40.9 92.7 %copy-start.5 = (s32[97]{0:T(128)}, s32[97]{0:T(128)S(1)}, u32[]{:S(2)}) copy-start(s32[97]{0:T(128)S(1)} %pad_add_fusion.1.facts) | copy-start | bytes 1168
  44.9 19.2 %collective-permute-start.2 = (bf16[256,1536]{1,0:T(8,128)(2,1)}, bf16[256,1536]{1,0:T(8,128)(2,1)S(1)}, u32[]{:S(2)}, u32[]{:S(2)}) collective-permute-start(bf16[256,1536]{1,0:T(8,128)(2,1)} %collective-permute-done.1.refs_0_), channel_id=1, source_target_pairs={{0,224},{32,0},{64,32},{96,64},{128,96},{160,128},{192,160},{224,1... | collective-permute-start | bytes 2359304 | tf_op jit(solution)/shard_map/ppermute | solution.py:298
  49.2 18.1 %collective-permute-start.5 = (bf16[256,1536]{1,0:T(8,128)(2,1)}, bf16[256,1536]{1,0:T(8,128)(2,1)S(1)}, u32[]{:S(2)}, u32[]{:S(2)}) collective-permute-start(bf16[256,1536]{1,0:T(8,128)(2,1)} %collective-permute-done.4.refs_1_), channel_id=1, source_target_pairs={{0,32},{32,64},{64,96},{96,128},{128,160},{160,192},{192,224},{224... | collective-permute-start | bytes 2359304 | tf_op jit(solution)/shard_map/ppermute | solution.py:298
  49.2 84.4 %copy-start.4 = (s32[5,1,1536]{2,1,0:T(1,128)}, s32[5,1,1536]{2,1,0:T(1,128)S(1)}, u32[]{:S(2)}) copy-start(s32[5,1,1536]{2,1,0:T(1,128)S(1)} %pad_add_fusion.maps) | copy-start | bytes 92164
  68.3 9.2 %collective-permute-start.6 = (bf16[128,1536]{1,0:T(8,128)(2,1)S(1)}, bf16[128,1536]{1,0:T(8,128)(2,1)S(1)}, u32[]{:S(2)}, u32[]{:S(2)}) collective-permute-start(bf16[128,1536]{1,0:T(8,128)(2,1)S(1)} %get-tuple-element.22), channel_id=1, source_target_pairs={{0,224},{32,0},{64,32},{96,64},{128,96},{160,128},{192,160},{224,1... | collective-permute-start | bytes 1179656 | tf_op jit(solution)/shard_map/ppermute | solution.py:298
  70.8 7.0 %collective-permute-start.7 = (bf16[128,1536]{1,0:T(8,128)(2,1)S(1)}, bf16[128,1536]{1,0:T(8,128)(2,1)S(1)}, u32[]{:S(2)}, u32[]{:S(2)}) collective-permute-start(bf16[128,1536]{1,0:T(8,128)(2,1)S(1)} %get-tuple-element.23), channel_id=1, source_target_pairs={{0,32},{32,64},{64,96},{96,128},{128,160},{160,192},{192,224},{224... | collective-permute-start | bytes 1179656 | tf_op jit(solution)/shard_map/ppermute | solution.py:298
  70.8 1.1 copy-start.7
  82.0 57.0 %all-to-all-start = ((bf16[8,8,256,128]{3,2,1,0:T(8,128)(2,1)}), bf16[8,8,256,128]{3,2,1,0:T(8,128)(2,1)}, u32[]{:S(2)}, u32[]{:S(2)}) async-start(bf16[8,8,256,128]{3,2,1,0:T(8,128)(2,1)} %get-tuple-element.32), calls=%async_computation | async-start | bytes 8388608 | tf_op jit(solution)/shard_map/all_to_all | solution.py:354
  93.0 10.7 %collective-permute-start.8 = (bf16[128,1536]{1,0:T(8,128)(2,1)}, bf16[128,1536]{1,0:T(8,128)(2,1)S(1)}, u32[]{:S(2)}, u32[]{:S(2)}) collective-permute-start(bf16[128,1536]{1,0:T(8,128)(2,1)} %joined.2.refs_0_), channel_id=1, source_target_pairs={{0,224},{32,0},{64,32},{96,64},{128,96},{160,128},{192,160},{224,1... | collective-permute-start | bytes 1179656 | tf_op jit(solution)/shard_map/ppermute | solution.py:298
  94.4 10.7 %collective-permute-start.11 = (bf16[128,1536]{1,0:T(8,128)(2,1)}, bf16[128,1536]{1,0:T(8,128)(2,1)S(1)}, u32[]{:S(2)}, u32[]{:S(2)}) collective-permute-start(bf16[128,1536]{1,0:T(8,128)(2,1)} %joined.2.refs_0_), channel_id=1, source_target_pairs={{0,32},{32,64},{64,96},{96,128},{128,160},{160,192},{192,224},{224... | collective-permute-start | bytes 1179656 | tf_op jit(solution)/shard_map/ppermute | solution.py:298
  103.7 9.6 %collective-permute-start.9 = (bf16[128,1536]{1,0:T(8,128)(2,1)S(1)}, bf16[128,1536]{1,0:T(8,128)(2,1)S(1)}, u32[]{:S(2)}, u32[]{:S(2)}) collective-permute-start(bf16[128,1536]{1,0:T(8,128)(2,1)S(1)} %collective-permute-done.8.refs_0_), channel_id=1, source_target_pairs={{0,224},{32,0},{64,32},{96,64},{128,96},{160,128},{192,160},{224,1... | collective-permute-start | bytes 1179656 | tf_op jit(solution)/shard_map/ppermute | solution.py:298
  105.1 10.0 %collective-permute-start.12 = (bf16[128,1536]{1,0:T(8,128)(2,1)S(1)}, bf16[128,1536]{1,0:T(8,128)(2,1)S(1)}, u32[]{:S(2)}, u32[]{:S(2)}) collective-permute-start(bf16[128,1536]{1,0:T(8,128)(2,1)S(1)} %collective-permute-done.11.refs_3_), channel_id=1, source_target_pairs={{0,32},{32,64},{64,96},{96,128},{128,160},{160,192},{192,224},{224... | collective-permute-start | bytes 1179656 | tf_op jit(solution)/shard_map/ppermute | solution.py:298
  113.3 8.8 %collective-permute-start.10 = (bf16[128,1536]{1,0:T(8,128)(2,1)S(1)}, bf16[128,1536]{1,0:T(8,128)(2,1)S(1)}, u32[]{:S(2)}, u32[]{:S(2)}) collective-permute-start(bf16[128,1536]{1,0:T(8,128)(2,1)S(1)} %collective-permute-done.9.refs_0_), channel_id=1, source_target_pairs={{0,224},{32,0},{64,32},{96,64},{128,96},{160,128},{192,160},{224,1... | collective-permute-start | bytes 1179656 | tf_op jit(solution)/shard_map/ppermute | solution.py:298
  115.0 10.0 %collective-permute-start.13 = (bf16[128,1536]{1,0:T(8,128)(2,1)S(1)}, bf16[128,1536]{1,0:T(8,128)(2,1)S(1)}, u32[]{:S(2)}, u32[]{:S(2)}) collective-permute-start(bf16[128,1536]{1,0:T(8,128)(2,1)S(1)} %collective-permute-done.12.refs_1_), channel_id=1, source_target_pairs={{0,32},{32,64},{64,96},{96,128},{128,160},{160,192},{192,224},{224... | collective-permute-start | bytes 1179656 | tf_op jit(solution)/shard_map/ppermute | solution.py:298
  118.3 15.3 %copy-start.1 = (bf16[128,1536]{1,0:T(8,128)(2,1)S(1)}, bf16[128,1536]{1,0:T(8,128)(2,1)}, u32[]{:S(2)}) copy-start(bf16[128,1536]{1,0:T(8,128)(2,1)} %joined.2.refs_0_) | copy-start | bytes 1179652
  126.2 7.3 %collective-permute-start.14 = (bf16[64,1536]{1,0:T(8,128)(2,1)S(1)}, bf16[64,1536]{1,0:T(8,128)(2,1)S(1)}, u32[]{:S(2)}, u32[]{:S(2)}) collective-permute-start(bf16[64,1536]{1,0:T(8,128)(2,1)S(1)} %get-tuple-element.25), channel_id=1, source_target_pairs={{0,224},{32,0},{64,32},{96,64},{128,96},{160,128},{192,160},{224,1... | collective-permute-start | bytes 589832 | tf_op jit(solution)/shard_map/ppermute | solution.py:298
  128.7 4.9 %collective-permute-start.15 = (bf16[64,1536]{1,0:T(8,128)(2,1)S(1)}, bf16[64,1536]{1,0:T(8,128)(2,1)S(1)}, u32[]{:S(2)}, u32[]{:S(2)}) collective-permute-start(bf16[64,1536]{1,0:T(8,128)(2,1)S(1)} %get-tuple-element.26), channel_id=1, source_target_pairs={{0,32},{32,64},{64,96},{96,128},{128,160},{160,192},{192,224},{224... | collective-permute-start | bytes 589832 | tf_op jit(solution)/shard_map/ppermute | solution.py:298
  139.1 7.3 %copy-start.9 = (s32[1,2,1536]{2,1,0:T(2,128)S(1)}, s32[1,2,1536]{2,1,0:T(2,128)}, u32[]{:S(2)}) copy-start(s32[1,2,1536]{2,1,0:T(2,128)} %param.13) | copy-start | bytes 36868
  139.1 32.6 %all-to-all-start.1 = ((bf16[8,8,128,128]{3,2,1,0:T(8,128)(2,1)}), bf16[8,8,128,128]{3,2,1,0:T(8,128)(2,1)}, u32[]{:S(2)}, u32[]{:S(2)}) async-start(bf16[8,8,128,128]{3,2,1,0:T(8,128)(2,1)} %joined.3), calls=%async_computation.1 | async-start | bytes 4194304 | tf_op jit(solution)/shard_map/all_to_all | solution.py:354
  146.4 11.8 %copy-start.12 = (f32[2048]{0:T(1024)S(1)}, f32[2048]{0:T(1024)}, u32[]{:S(2)}) copy-start(f32[2048]{0:T(1024)} %param.14) | copy-start | bytes 24580
  146.4 16.3 %slice-start = ((f32[384]{0:T(512)}), f32[256]{0:T(256)S(1)}, s32[]{:S(2)}) async-start(f32[384]{0:T(512)} %param.15), calls=%async_computation.3 | async-start | bytes 2048 | tf_op jit(solution)/shard_map/slice | solution.py:359
  156.2 49.0 %collective-permute-start.17 = (bf16[256,1536]{1,0:T(8,128)(2,1)}, bf16[256,1536]{1,0:T(8,128)(2,1)}, u32[]{:S(2)}, u32[]{:S(2)}) collective-permute-start(bf16[256,1536]{1,0:T(8,128)(2,1)} %get-tuple-element.36), channel_id=1, source_target_pairs={{0,128},{32,160},{64,192},{96,224},{128,0},{160,32},{192,64},{224,... | collective-permute-start | bytes 2359304 | tf_op jit(solution)/shard_map/ppermute | solution.py:298
  162.9 19.0 %copy-start.10 = (f32[384]{0:T(512)S(1)}, f32[384]{0:T(512)}, u32[]{:S(2)}) copy-start(f32[384]{0:T(512)} %param.15) | copy-start | bytes 4612
  162.9 42.3 %copy-start.2 = (f32[256,1536]{1,0:T(8,128)S(1)}, f32[256,1536]{1,0:T(8,128)}, u32[]{:S(2)}) copy-start(f32[256,1536]{1,0:T(8,128)} %get-tuple-element.35.refs_1_) | copy-start | bytes 4718596
  180.0 33.7 %collective-permute-start.16 = (bf16[128,1536]{1,0:T(8,128)(2,1)}, bf16[128,1536]{1,0:T(8,128)(2,1)}, u32[]{:S(2)}, u32[]{:S(2)}) collective-permute-start(bf16[128,1536]{1,0:T(8,128)(2,1)} %get-tuple-element.34), channel_id=1, source_target_pairs={{0,128},{32,160},{64,192},{96,224},{128,0},{160,32},{192,64},{224,... | collective-permute-start | bytes 1179656 | tf_op jit(solution)/shard_map/ppermute | solution.py:298
  182.1 31.5 %copy-start.3 = (f32[128,1536]{1,0:T(8,128)S(1)}, f32[128,1536]{1,0:T(8,128)}, u32[]{:S(2)}) copy-start(f32[128,1536]{1,0:T(8,128)} %get-tuple-element.33.refs_1_) | copy-start | bytes 2359300
Sparse Core Ops, SparseCore 0:
  9.2 122.6 all-gather.3

commit v10 on v9

--- a/solution.py
+++ b/solution.py
@@ -326,7 +326,7 @@
     first = energies(vir_energy, pair_virt[0, 0])
     second = energies(vir_energy, pair_virt[0, 1])
     virtual = jnp.stack([first, second])
-    chunks = ((256,), (128,))
+    chunks = ((224,), (160,))
     steps, folds, low = [], [], 0
     for pieces in chunks:
         part = own[low : low + sum(pieces)]

time: 224 us -> 228 us (1.018); the launches traced: 222 us -> 223 us
  waiting for transfers between devices: 101 us -> 94.1 us
  local copies, waits for them, and re-layouts: 4.02 us -> 9.33 us
    ppermute x18, waiting for transfers between devices: 89.7 us -> 73.6 us  [shifted(): return lax.ppermute(block, 'bra', [(i, (i + by) % 8) for i in range(8)])]
    all_to_all x2, waiting for transfers between devices: 10.7 us -> 19.8 us  [local(): lax.all_to_all(piece, 'ket', split_axis=0, concat_axis=0, tiled=True)]
  transfers between devices with their start and end apart: 21 -> 21, of which waited for: 17 -> 12; matrix products, arithmetic and copies ran while one was open for 3% -> 6% of each run, Pallas kernels for 22% -> 23%
where the time goes in v10:
time: 228 us; the launch traced here: 223 us
  waiting for transfers between devices  94.1 us (41%)
  Pallas kernels  52.1 us (23%)
  starting transfers between devices  37.8 us (17%)
  between operations  13.8 us (6%)
  blocking collectives  10.3 us (5%)
  local copies, waits for them, and re-layouts  9.33 us (4%)
  other arithmetic  5.72 us (3%)
    ppermute x18, waiting for transfers between devices, shifted(): return lax.ppermute(block, 'bra', [(i, (i + by) % 8) for i in range(8)])  73.6 us
    pallas_call x6, Pallas kernels, fold(): pl.pallas_call(functools.partial(fold_body, shifts, pieces), in_specs=[pl...  28.6 us
    ppermute x18, starting transfers between devices, shifted(): return lax.ppermute(block, 'bra', [(i, (i + by) % 8) for i in range(8)])  20.5 us
    all_to_all x2, waiting for transfers between devices, local(): lax.all_to_all(piece, 'ket', split_axis=0, concat_axis=0, tiled=True)  19.8 us
    pallas_call x2, Pallas kernels, ladder_of(): pl.pallas_call(ladder_body, in_specs=[pl.BlockSpec(memory_space=pltpu.SME...  18 us
    all_to_all x2, starting transfers between devices, local(): lax.all_to_all(piece, 'ket', split_axis=0, concat_axis=0, tiled=True)  17.3 us
    all_gather x1, blocking collectives, local(): wanted = lax.all_gather(block_owner[0] * 16 + screen_list[0], 'ket', axis=0)  10.3 us
  transfers between devices with their start and end apart: 21, of which 12 were waited for; matrix products, arithmetic and copies ran while one was open for 6% of the time, Pallas kernels for 23%

profile of v10, /device:TPU:47, one launch (start us, length us, event | category | flops | bytes accessed | tf_op | source)
XLA Modules:
  0.0 223.1 jit_solution(8760222587152283269)
XLA Ops:
  6.6 0.7 all-gather.4.cloned.1.call-update
  8.0 1.7 collective-permute-start.3
  9.7 15.1 %collective-permute-done.refs_0_ = bf16[224,1536]{1,0:T(8,128)(2,1)S(1)} collective-permute-done((bf16[224,1536]{1,0:T(8,128)(2,1)S(1)}, bf16[224,1536]{1,0:T(8,128)(2,1)S(1)}, u32[]{:S(2)}, u32[]{:S(2)}) %collective-permute-start) | collective-permute-done | bytes 688160 | tf_op jit(solution)/shard_map/ppermute | solution.py:298
  24.8 2.7 %collective-permute-start.1 = (bf16[224,1536]{1,0:T(8,128)(2,1)S(1)}, bf16[224,1536]{1,0:T(8,128)(2,1)}, u32[]{:S(2)}, u32[]{:S(2)}) collective-permute-start(bf16[224,1536]{1,0:T(8,128)(2,1)S(1)} %collective-permute-done.refs_0_), channel_id=1, source_target_pairs={{0,224},{32,0},{64,32},{96,64},{128,96},{160,128},{192,160},{224,1... | collective-permute-start | bytes 2064392 | tf_op jit(solution)/shard_map/ppermute | solution.py:298
  27.5 0.8 copy-done.9
  28.4 10.3 %all-gather.1 = s32[8,1,32]{2,1,0:T(1,128)S(1)} all-gather(s32[1,1,32]{2,1,0:T(1,128)S(1)} %add_bitcast_fusion), channel_id=1, replica_groups=mesh['bra'=8,'ket'=8,'pair'=4] {'ket'}, dimensions={0}, use_global_device_ids=true | all-gather | bytes 1152 | tf_op jit(solution)/shard_map/all_gather | solution.py:314
  38.7 2.2 collective-permute-done.1.refs_0_
  40.9 3.2 %collective-permute-start.2 = (bf16[224,1536]{1,0:T(8,128)(2,1)}, bf16[224,1536]{1,0:T(8,128)(2,1)S(1)}, u32[]{:S(2)}, u32[]{:S(2)}) collective-permute-start(bf16[224,1536]{1,0:T(8,128)(2,1)} %collective-permute-done.1.refs_0_), channel_id=1, source_target_pairs={{0,224},{32,0},{64,32},{96,64},{128,96},{160,128},{192,160},{224,1... | collective-permute-start | bytes 2064392 | tf_op jit(solution)/shard_map/ppermute | solution.py:298
  44.1 1.9 collective-permute-done.4.refs_1_
  46.5 4.8 %fold.6 = (bf16[8,8,224,128]{3,2,1,0:T(8,128)(2,1)}, s32[1]{0:T(128)}) custom-call(s32[97]{0:T(128)S(1)} %pad_add_fusion.1.facts, s32[5,1,1536]{2,1,0:T(1,128)S(1)} %pad_add_fusion.maps, bf16[224,1536]{1,0:T(8,128)(2,1)} %collective-permute-done.1.refs_0_, bf16[224,1536]{1,0:T(8,128)(2,1)} %collective-permute-done.4.refs_1_), custom_call_target="tpu_custom_call" | custom-call | flops 1056964608 | bytes 2293760 | tf_op jit(solution)/shard_map/fold/pallas_call | solution.py:110
  51.3 6.5 %collective-permute-done.2.first.refs_2_ = bf16[224,1536]{1,0:T(8,128)(2,1)S(1)} collective-permute-done((bf16[224,1536]{1,0:T(8,128)(2,1)}, bf16[224,1536]{1,0:T(8,128)(2,1)S(1)}, u32[]{:S(2)}, u32[]{:S(2)}) %collective-permute-start.2) | collective-permute-done | bytes 688160 | tf_op jit(solution)/shard_map/ppermute | solution.py:298
  57.7 4.0 %collective-permute-done.5.second.refs_1_ = bf16[224,1536]{1,0:T(8,128)(2,1)S(1)} collective-permute-done((bf16[224,1536]{1,0:T(8,128)(2,1)}, bf16[224,1536]{1,0:T(8,128)(2,1)S(1)}, u32[]{:S(2)}, u32[]{:S(2)}) %collective-permute-start.5) | collective-permute-done | bytes 688160 | tf_op jit(solution)/shard_map/ppermute | solution.py:298
  61.7 1.0 halves.2
  62.7 2.5 %collective-permute-start.6 = (bf16[112,1536]{1,0:T(8,128)(2,1)S(1)}, bf16[112,1536]{1,0:T(8,128)(2,1)S(1)}, u32[]{:S(2)}, u32[]{:S(2)}) collective-permute-start(bf16[112,1536]{1,0:T(8,128)(2,1)S(1)} %get-tuple-element.22), channel_id=1, source_target_pairs={{0,224},{32,0},{64,32},{96,64},{128,96},{160,128},{192,160},{224,1... | collective-permute-start | bytes 1032200 | tf_op jit(solution)/shard_map/ppermute | solution.py:298
  65.2 1.1 copy-done.6
  66.3 5.7 %fold.10 = (bf16[8,8,224,128]{3,2,1,0:T(8,128)(2,1)}, s32[1]{0:T(128)}) custom-call(s32[97]{0:T(128)S(1)} %pad_add_fusion.1.facts, s32[5,1,1536]{2,1,0:T(1,128)S(1)} %pad_add_fusion.maps, bf16[224,1536]{1,0:T(8,128)(2,1)S(1)} %copy-done.10, bf16[224,1536]{1,0:T(8,128)(2,1)S(1)} %copy-done.6, ...), custom_call_target="tpu_custom_call", output_to_operand_aliasing={{0}: (6, {})} | custom-call | flops 2113929216 | bytes 4587520 | tf_op jit(solution)/shard_map/fold/pallas_call | solution.py:110
  72.0 4.2 %fold.11 = (bf16[8,8,224,128]{3,2,1,0:T(8,128)(2,1)}, s32[1]{0:T(128)}) custom-call(s32[97]{0:T(128)S(1)} %pad_add_fusion.1.facts, s32[5,1,1536]{2,1,0:T(1,128)S(1)} %pad_add_fusion.maps, bf16[224,1536]{1,0:T(8,128)(2,1)S(1)} %slice_bitcast_fusion.refs_0_, bf16[112,1536]{1,0:T(8,128)(2,1)S(1)} %collective-permute-done.6.refs_1_, ...), custom_call_target="tpu_custom_call", output_to_operand_aliasing={{0}: (5, {})} | custom-call | flops 1056964608 | bytes 2293760 | tf_op jit(solution)/shard_map/fold/pallas_call | solution.py:110
  76.2 8.8 %all-to-all-start = ((bf16[8,8,224,128]{3,2,1,0:T(8,128)(2,1)}), bf16[8,8,224,128]{3,2,1,0:T(8,128)(2,1)}, u32[]{:S(2)}, u32[]{:S(2)}) async-start(bf16[8,8,224,128]{3,2,1,0:T(8,128)(2,1)} %get-tuple-element.32), calls=%async_computation | async-start | bytes 7340032 | tf_op jit(solution)/shard_map/all_to_all | solution.py:354
  85.0 1.1 slice_bitcast_fusion.1.refs_0_
  86.1 0.8 copy.24.refs_0_
  86.9 1.5 collective-permute-start.8
  88.4 11.3 %collective-permute-done.8.refs_0_ = bf16[160,1536]{1,0:T(8,128)(2,1)S(1)} collective-permute-done((bf16[160,1536]{1,0:T(8,128)(2,1)}, bf16[160,1536]{1,0:T(8,128)(2,1)S(1)}, u32[]{:S(2)}, u32[]{:S(2)}) %collective-permute-start.8) | collective-permute-done | bytes 491552 | tf_op jit(solution)/shard_map/ppermute | solution.py:298
  99.6 1.5 collective-permute-start.9
  101.1 10.3 %collective-permute-done.9.refs_0_ = bf16[160,1536]{1,0:T(8,128)(2,1)S(1)} collective-permute-done((bf16[160,1536]{1,0:T(8,128)(2,1)S(1)}, bf16[160,1536]{1,0:T(8,128)(2,1)S(1)}, u32[]{:S(2)}, u32[]{:S(2)}) %collective-permute-start.9) | collective-permute-done | bytes 491552 | tf_op jit(solution)/shard_map/ppermute | solution.py:298
  111.4 1.5 collective-permute-start.10
  112.8 0.8 collective-permute-done.12.refs_1_
  113.7 3.8 %fold.7 = (bf16[8,8,160,128]{3,2,1,0:T(8,128)(2,1)}, s32[1]{0:T(128)}) custom-call(s32[97]{0:T(128)S(1)} %pad_add_fusion.1.facts, s32[5,1,1536]{2,1,0:T(1,128)S(1)} %pad_add_fusion.maps, bf16[160,1536]{1,0:T(8,128)(2,1)S(1)} %collective-permute-done.9.refs_0_, bf16[160,1536]{1,0:T(8,128)(2,1)S(1)} %collective-permute-done.12.refs_1_), custom_call_target="tpu_custom_call" | custom-call | flops 754974720 | bytes 1638400 | tf_op jit(solution)/shard_map/fold/pallas_call | solution.py:110
  117.5 4.8 %collective-permute-done.10.first.refs_2_ = bf16[160,1536]{1,0:T(8,128)(2,1)S(1)} collective-permute-done((bf16[160,1536]{1,0:T(8,128)(2,1)S(1)}, bf16[160,1536]{1,0:T(8,128)(2,1)S(1)}, u32[]{:S(2)}, u32[]{:S(2)}) %collective-permute-start.10) | collective-permute-done | bytes 491552 | tf_op jit(solution)/shard_map/ppermute | solution.py:298
  122.3 3.5 %collective-permute-done.13.second.refs_1_ = bf16[160,1536]{1,0:T(8,128)(2,1)S(1)} collective-permute-done((bf16[160,1536]{1,0:T(8,128)(2,1)S(1)}, bf16[160,1536]{1,0:T(8,128)(2,1)S(1)}, u32[]{:S(2)}, u32[]{:S(2)}) %collective-permute-start.13) | collective-permute-done | bytes 491552 | tf_op jit(solution)/shard_map/ppermute | solution.py:298
  125.8 1.3 halves.3
  127.1 2.5 %collective-permute-start.14 = (bf16[80,1536]{1,0:T(8,128)(2,1)S(1)}, bf16[80,1536]{1,0:T(8,128)(2,1)S(1)}, u32[]{:S(2)}, u32[]{:S(2)}) collective-permute-start(bf16[80,1536]{1,0:T(8,128)(2,1)S(1)} %get-tuple-element.25), channel_id=1, source_target_pairs={{0,224},{32,0},{64,32},{96,64},{128,96},{160,128},{192,160},{224,1... | collective-permute-start | bytes 737288 | tf_op jit(solution)/shard_map/ppermute | solution.py:298
  129.5 5.7 %fold.8 = (bf16[8,8,160,128]{3,2,1,0:T(8,128)(2,1)}, s32[1]{0:T(128)}) custom-call(s32[97]{0:T(128)S(1)} %pad_add_fusion.1.facts, s32[5,1,1536]{2,1,0:T(1,128)S(1)} %pad_add_fusion.maps, bf16[160,1536]{1,0:T(8,128)(2,1)S(1)} %collective-permute-done.8.refs_0_, ...), custom_call_target="tpu_custom_call", output_to_operand_aliasing={{0}: (6, {})} | custom-call | flops 1509949440 | bytes 3276800 | tf_op jit(solution)/shard_map/fold/pallas_call | solution.py:110
  135.3 4.4 %fold.9 = (bf16[8,8,160,128]{3,2,1,0:T(8,128)(2,1)}, s32[1]{0:T(128)}) custom-call(s32[97]{0:T(128)S(1)} %pad_add_fusion.1.facts, s32[5,1,1536]{2,1,0:T(1,128)S(1)} %pad_add_fusion.maps, bf16[160,1536]{1,0:T(8,128)(2,1)S(1)} %copy-done.1, bf16[80,1536]{1,0:T(8,128)(2,1)S(1)} %collective-permute-done.14.refs_1_, ...), custom_call_target="tpu_custom_call", output_to_operand_aliasing={{0}: (5, {})} | custom-call | flops 754974720 | bytes 1638400 | tf_op jit(solution)/shard_map/fold/pallas_call | solution.py:110
  139.8 8.4 %all-to-all-start.1 = ((bf16[8,8,160,128]{3,2,1,0:T(8,128)(2,1)}), bf16[8,8,160,128]{3,2,1,0:T(8,128)(2,1)}, u32[]{:S(2)}, u32[]{:S(2)}) async-start(bf16[8,8,160,128]{3,2,1,0:T(8,128)(2,1)} %joined.3), calls=%async_computation.1 | async-start | bytes 5242880 | tf_op jit(solution)/shard_map/all_to_all | solution.py:354
  148.3 9.3 %ladder.3 = (f32[224,1536]{1,0:T(8,128)}, bf16[224,1536]{1,0:T(8,128)(2,1)}) custom-call(s32[97]{0:T(128)} %copy-done.8, s32[5,1,1536]{2,1,0:T(1,128)} %copy-done.4, bf16[4096,1536]{1,0:T(8,128)(2,1)} %bitcast.22, bf16[8,8,224,128]{3,2,1,0:T(8,128)(2,1)} %all-to-all-done.refs_1_.received), custom_call_target="tpu_custom_call" | custom-call | flops 2818572288 | bytes 14417920 | tf_op jit(solution)/shard_map/ladder/pallas_call | solution.py:226
  157.7 1.7 collective-permute-start.17
  159.4 19.8 %all-to-all-done.1.received = bf16[8,8,160,128]{3,2,1,0:T(8,128)(2,1)} async-done(((bf16[8,8,160,128]{3,2,1,0:T(8,128)(2,1)}), bf16[8,8,160,128]{3,2,1,0:T(8,128)(2,1)}, u32[]{:S(2)}, u32[]{:S(2)}) %all-to-all-start.1) | async-done | bytes 2621472 | tf_op jit(solution)/shard_map/all_to_all | solution.py:354
  179.2 8.6 %ladder.2 = (f32[160,1536]{1,0:T(8,128)}, bf16[160,1536]{1,0:T(8,128)(2,1)}) custom-call(s32[97]{0:T(128)} %copy-done.8, s32[5,1,1536]{2,1,0:T(1,128)} %copy-done.4, bf16[4096,1536]{1,0:T(8,128)(2,1)} %bitcast.23, bf16[8,8,160,128]{3,2,1,0:T(8,128)(2,1)} %all-to-all-done.1.received), custom_call_target="tpu_custom_call" | custom-call | flops 2013265920 | bytes 13893632 | tf_op jit(solution)/shard_map/ladder/pallas_call | solution.py:226
  187.8 1.7 collective-permute-start.16
  189.5 4.5 %select_reduce_fusion.1 = (f32[1536]{0:T(1024)S(1)}, f32[1536]{0:T(1024)S(1)}) fusion(f32[2048]{0:T(1024)S(1)} %copy-done.15, s32[1536]{0:T(1024)S(1)} %get-tuple-element.37, s32[1536]{0:T(1024)S(1)} %get-tuple-element.38), kind=kLoop, calls=%fused_computation.2 | loop fusion | flops 18871296 | bytes 32768 | tf_op jit(solution)/shard_map/reduce_sum | solution.py:303
  194.7 0.7 slice.30
  195.9 0.6 stack.9
  196.5 0.8 copy.22.refs_4_
  197.4 1.4 copy.23.refs_4_
  198.8 0.8 pad_maximum_fusion.refs_5_
  199.6 2.3 %update.2.refs_6_ = bf16[384,1536]{1,0:T(8,128)(2,1)} custom-call(bf16[224,1536]{1,0:T(8,128)(2,1)S(1)} %slice_bitcast_fusion.refs_0_, f32[224,1536]{1,0:T(8,128)S(1)} %copy-done.2, bf16[224,1536]{1,0:T(8,128)(2,1)} %collective-permute-done.17.refs_2_, f32[1]{0:T(128)} %bitcast.12.refs_3_, f32[224,1]{1,0:T(8,128)S(1)} %copy.22.refs_4_, ...), custom_call_target="tpu_custom_call" | custom-call | flops 2752512 | bytes 3440640 | tf_op jit(solution)/shard_map/update/pallas_call | solution.py:281
  201.9 13.3 %collective-permute-done.16.refs_2_ = bf16[160,1536]{1,0:T(8,128)(2,1)S(1)} collective-permute-done((bf16[160,1536]{1,0:T(8,128)(2,1)}, bf16[160,1536]{1,0:T(8,128)(2,1)S(1)}, u32[]{:S(2)}, u32[]{:S(2)}) %collective-permute-start.16) | collective-permute-done | bytes 491552 | tf_op jit(solution)/shard_map/ppermute | solution.py:298
  215.2 1.0 update.3
  (65 shorter events, 2.6 us)
Async XLA Ops:
  6.5 32.2 %copy-start = (s32[64,1536]{1,0:T(8,128)S(1)}, s32[64,1536]{1,0:T(8,128)}, u32[]{:S(2)}) copy-start(s32[64,1536]{1,0:T(8,128)} %param.12) | copy-start | bytes 1179652
  6.5 1.3 copy-start.11
  6.5 21.8 %copy-start.16 = (s32[1,32]{1,0:T(1,128)S(1)}, s32[1,32]{1,0:T(1,128)}, u32[]{:S(2)}) copy-start(s32[1,32]{1,0:T(1,128)} %param.10) | copy-start | bytes 388
  6.5 21.8 %copy-start.14 = (s32[1,32]{1,0:T(1,128)S(1)}, s32[1,32]{1,0:T(1,128)}, u32[]{:S(2)}) copy-start(s32[1,32]{1,0:T(1,128)} %param.11) | copy-start | bytes 388
  6.5 141.7 %all-gather.4.cloned.1.call-start = ((), (), s32[]{:S(2)}) async-start(), calls=%async_computation.2 | async-start | bytes 15728640 | tf_op jit(solution)/shard_map/all_gather | solution.py:312
  7.9 16.9 %collective-permute-start = (bf16[224,1536]{1,0:T(8,128)(2,1)S(1)}, bf16[224,1536]{1,0:T(8,128)(2,1)S(1)}, u32[]{:S(2)}, u32[]{:S(2)}) collective-permute-start(bf16[224,1536]{1,0:T(8,128)(2,1)S(1)} %slice_bitcast_fusion.refs_0_), channel_id=1, source_target_pairs={{0,224},{32,0},{64,32},{96,64},{128,96},{160,128},{192,160},{224,1... | collective-permute-start | bytes 2064392 | tf_op jit(solution)/shard_map/ppermute | solution.py:298
  8.0 20.3 %collective-permute-start.3 = (bf16[224,1536]{1,0:T(8,128)(2,1)S(1)}, bf16[224,1536]{1,0:T(8,128)(2,1)}, u32[]{:S(2)}, u32[]{:S(2)}) collective-permute-start(bf16[224,1536]{1,0:T(8,128)(2,1)S(1)} %slice_bitcast_fusion.refs_0_), channel_id=1, source_target_pairs={{0,32},{32,64},{64,96},{96,128},{128,160},{160,192},{192,224},{224... | collective-permute-start | bytes 2064392 | tf_op jit(solution)/shard_map/ppermute | solution.py:298
  24.8 16.1 %collective-permute-start.1 = (bf16[224,1536]{1,0:T(8,128)(2,1)S(1)}, bf16[224,1536]{1,0:T(8,128)(2,1)}, u32[]{:S(2)}, u32[]{:S(2)}) collective-permute-start(bf16[224,1536]{1,0:T(8,128)(2,1)S(1)} %collective-permute-done.refs_0_), channel_id=1, source_target_pairs={{0,224},{32,0},{64,32},{96,64},{128,96},{160,128},{192,160},{224,1... | collective-permute-start | bytes 2064392 | tf_op jit(solution)/shard_map/ppermute | solution.py:298
  27.5 0.8 copy-start.9
  28.3 17.6 %collective-permute-start.4 = (bf16[224,1536]{1,0:T(8,128)(2,1)}, bf16[224,1536]{1,0:T(8,128)(2,1)}, u32[]{:S(2)}, u32[]{:S(2)}) collective-permute-start(bf16[224,1536]{1,0:T(8,128)(2,1)} %collective-permute-done.3.refs_3_), channel_id=1, source_target_pairs={{0,32},{32,64},{64,96},{96,128},{128,160},{160,192},{192,224},{224... | collective-permute-start | bytes 2064392 | tf_op jit(solution)/shard_map/ppermute | solution.py:298
  40.9 16.8 %collective-permute-start.2 = (bf16[224,1536]{1,0:T(8,128)(2,1)}, bf16[224,1536]{1,0:T(8,128)(2,1)S(1)}, u32[]{:S(2)}, u32[]{:S(2)}) collective-permute-start(bf16[224,1536]{1,0:T(8,128)(2,1)} %collective-permute-done.1.refs_0_), channel_id=1, source_target_pairs={{0,224},{32,0},{64,32},{96,64},{128,96},{160,128},{192,160},{224,1... | collective-permute-start | bytes 2064392 | tf_op jit(solution)/shard_map/ppermute | solution.py:298
  46.0 15.7 %collective-permute-start.5 = (bf16[224,1536]{1,0:T(8,128)(2,1)}, bf16[224,1536]{1,0:T(8,128)(2,1)S(1)}, u32[]{:S(2)}, u32[]{:S(2)}) collective-permute-start(bf16[224,1536]{1,0:T(8,128)(2,1)} %collective-permute-done.4.refs_1_), channel_id=1, source_target_pairs={{0,32},{32,64},{64,96},{96,128},{128,160},{160,192},{192,224},{224... | collective-permute-start | bytes 2064392 | tf_op jit(solution)/shard_map/ppermute | solution.py:298
  46.4 18.8 %copy-start.10 = (bf16[224,1536]{1,0:T(8,128)(2,1)S(1)}, bf16[224,1536]{1,0:T(8,128)(2,1)}, u32[]{:S(2)}) copy-start(bf16[224,1536]{1,0:T(8,128)(2,1)} %copy-done.9) | copy-start | bytes 2064388
  46.4 88.9 %copy-start.8 = (s32[97]{0:T(128)}, s32[97]{0:T(128)S(1)}, u32[]{:S(2)}) copy-start(s32[97]{0:T(128)S(1)} %pad_add_fusion.1.facts) | copy-start | bytes 1168
  46.5 88.8 %copy-start.4 = (s32[5,1,1536]{2,1,0:T(1,128)}, s32[5,1,1536]{2,1,0:T(1,128)S(1)}, u32[]{:S(2)}) copy-start(s32[5,1,1536]{2,1,0:T(1,128)S(1)} %pad_add_fusion.maps) | copy-start | bytes 92164
  61.7 1.0 copy-start.5
  62.7 9.3 %collective-permute-start.6 = (bf16[112,1536]{1,0:T(8,128)(2,1)S(1)}, bf16[112,1536]{1,0:T(8,128)(2,1)S(1)}, u32[]{:S(2)}, u32[]{:S(2)}) collective-permute-start(bf16[112,1536]{1,0:T(8,128)(2,1)S(1)} %get-tuple-element.22), channel_id=1, source_target_pairs={{0,224},{32,0},{64,32},{96,64},{128,96},{160,128},{192,160},{224,1... | collective-permute-start | bytes 1032200 | tf_op jit(solution)/shard_map/ppermute | solution.py:298
  65.1 6.8 %collective-permute-start.7 = (bf16[112,1536]{1,0:T(8,128)(2,1)S(1)}, bf16[112,1536]{1,0:T(8,128)(2,1)S(1)}, u32[]{:S(2)}, u32[]{:S(2)}) collective-permute-start(bf16[112,1536]{1,0:T(8,128)(2,1)S(1)} %get-tuple-element.23), channel_id=1, source_target_pairs={{0,32},{32,64},{64,96},{96,128},{128,160},{160,192},{192,224},{224... | collective-permute-start | bytes 1032200 | tf_op jit(solution)/shard_map/ppermute | solution.py:298
  65.2 1.1 copy-start.6
  76.2 63.5 %all-to-all-start = ((bf16[8,8,224,128]{3,2,1,0:T(8,128)(2,1)}), bf16[8,8,224,128]{3,2,1,0:T(8,128)(2,1)}, u32[]{:S(2)}, u32[]{:S(2)}) async-start(bf16[8,8,224,128]{3,2,1,0:T(8,128)(2,1)} %get-tuple-element.32), calls=%async_computation | async-start | bytes 7340032 | tf_op jit(solution)/shard_map/all_to_all | solution.py:354
  86.9 12.8 %collective-permute-start.8 = (bf16[160,1536]{1,0:T(8,128)(2,1)}, bf16[160,1536]{1,0:T(8,128)(2,1)S(1)}, u32[]{:S(2)}, u32[]{:S(2)}) collective-permute-start(bf16[160,1536]{1,0:T(8,128)(2,1)} %joined.2.refs_0_), channel_id=1, source_target_pairs={{0,224},{32,0},{64,32},{96,64},{128,96},{160,128},{192,160},{224,1... | collective-permute-start | bytes 1474568 | tf_op jit(solution)/shard_map/ppermute | solution.py:298
  88.3 12.8 %collective-permute-start.11 = (bf16[160,1536]{1,0:T(8,128)(2,1)}, bf16[160,1536]{1,0:T(8,128)(2,1)S(1)}, u32[]{:S(2)}, u32[]{:S(2)}) collective-permute-start(bf16[160,1536]{1,0:T(8,128)(2,1)} %joined.2.refs_0_), channel_id=1, source_target_pairs={{0,32},{32,64},{64,96},{96,128},{128,160},{160,192},{192,224},{224... | collective-permute-start | bytes 1474568 | tf_op jit(solution)/shard_map/ppermute | solution.py:298
  99.6 11.7 %collective-permute-start.9 = (bf16[160,1536]{1,0:T(8,128)(2,1)S(1)}, bf16[160,1536]{1,0:T(8,128)(2,1)S(1)}, u32[]{:S(2)}, u32[]{:S(2)}) collective-permute-start(bf16[160,1536]{1,0:T(8,128)(2,1)S(1)} %collective-permute-done.8.refs_0_), channel_id=1, source_target_pairs={{0,224},{32,0},{64,32},{96,64},{128,96},{160,128},{192,160},{224,1... | collective-permute-start | bytes 1474568 | tf_op jit(solution)/shard_map/ppermute | solution.py:298
  101.1 12.6 %collective-permute-start.12 = (bf16[160,1536]{1,0:T(8,128)(2,1)S(1)}, bf16[160,1536]{1,0:T(8,128)(2,1)S(1)}, u32[]{:S(2)}, u32[]{:S(2)}) collective-permute-start(bf16[160,1536]{1,0:T(8,128)(2,1)S(1)} %collective-permute-done.11.refs_3_), channel_id=1, source_target_pairs={{0,32},{32,64},{64,96},{96,128},{128,160},{160,192},{192,224},{224... | collective-permute-start | bytes 1474568 | tf_op jit(solution)/shard_map/ppermute | solution.py:298
  111.4 10.9 %collective-permute-start.10 = (bf16[160,1536]{1,0:T(8,128)(2,1)S(1)}, bf16[160,1536]{1,0:T(8,128)(2,1)S(1)}, u32[]{:S(2)}, u32[]{:S(2)}) collective-permute-start(bf16[160,1536]{1,0:T(8,128)(2,1)S(1)} %collective-permute-done.9.refs_0_), channel_id=1, source_target_pairs={{0,224},{32,0},{64,32},{96,64},{128,96},{160,128},{192,160},{224,1... | collective-permute-start | bytes 1474568 | tf_op jit(solution)/shard_map/ppermute | solution.py:298
  113.7 12.1 %collective-permute-start.13 = (bf16[160,1536]{1,0:T(8,128)(2,1)S(1)}, bf16[160,1536]{1,0:T(8,128)(2,1)S(1)}, u32[]{:S(2)}, u32[]{:S(2)}) collective-permute-start(bf16[160,1536]{1,0:T(8,128)(2,1)S(1)} %collective-permute-done.12.refs_1_), channel_id=1, source_target_pairs={{0,32},{32,64},{64,96},{96,128},{128,160},{160,192},{192,224},{224... | collective-permute-start | bytes 1474568 | tf_op jit(solution)/shard_map/ppermute | solution.py:298
  125.8 9.5 %copy-start.1 = (bf16[160,1536]{1,0:T(8,128)(2,1)S(1)}, bf16[160,1536]{1,0:T(8,128)(2,1)}, u32[]{:S(2)}) copy-start(bf16[160,1536]{1,0:T(8,128)(2,1)} %joined.2.refs_0_) | copy-start | bytes 1474564
  127.1 8.2 %collective-permute-start.14 = (bf16[80,1536]{1,0:T(8,128)(2,1)S(1)}, bf16[80,1536]{1,0:T(8,128)(2,1)S(1)}, u32[]{:S(2)}, u32[]{:S(2)}) collective-permute-start(bf16[80,1536]{1,0:T(8,128)(2,1)S(1)} %get-tuple-element.25), channel_id=1, source_target_pairs={{0,224},{32,0},{64,32},{96,64},{128,96},{160,128},{192,160},{224,1... | collective-permute-start | bytes 737288 | tf_op jit(solution)/shard_map/ppermute | solution.py:298
  129.5 5.8 %collective-permute-start.15 = (bf16[80,1536]{1,0:T(8,128)(2,1)S(1)}, bf16[80,1536]{1,0:T(8,128)(2,1)S(1)}, u32[]{:S(2)}, u32[]{:S(2)}) collective-permute-start(bf16[80,1536]{1,0:T(8,128)(2,1)S(1)} %get-tuple-element.26), channel_id=1, source_target_pairs={{0,32},{32,64},{64,96},{96,128},{128,160},{160,192},{192,224},{224... | collective-permute-start | bytes 737288 | tf_op jit(solution)/shard_map/ppermute | solution.py:298
  139.7 8.5 %copy-start.12 = (s32[1,2,1536]{2,1,0:T(2,128)S(1)}, s32[1,2,1536]{2,1,0:T(2,128)}, u32[]{:S(2)}) copy-start(s32[1,2,1536]{2,1,0:T(2,128)} %param.13) | copy-start | bytes 36868
  139.8 39.4 %all-to-all-start.1 = ((bf16[8,8,160,128]{3,2,1,0:T(8,128)(2,1)}), bf16[8,8,160,128]{3,2,1,0:T(8,128)(2,1)}, u32[]{:S(2)}, u32[]{:S(2)}) async-start(bf16[8,8,160,128]{3,2,1,0:T(8,128)(2,1)} %joined.3), calls=%async_computation.1 | async-start | bytes 5242880 | tf_op jit(solution)/shard_map/all_to_all | solution.py:354
  157.6 31.9 %copy-start.15 = (f32[2048]{0:T(1024)S(1)}, f32[2048]{0:T(1024)}, u32[]{:S(2)}) copy-start(f32[2048]{0:T(1024)} %param.14) | copy-start | bytes 24580
  157.6 36.5 %copy-start.13 = (f32[384]{0:T(512)S(1)}, f32[384]{0:T(512)}, u32[]{:S(2)}) copy-start(f32[384]{0:T(512)} %param.15) | copy-start | bytes 4612
  157.6 42.0 %copy-start.2 = (f32[224,1536]{1,0:T(8,128)S(1)}, f32[224,1536]{1,0:T(8,128)}, u32[]{:S(2)}) copy-start(f32[224,1536]{1,0:T(8,128)} %get-tuple-element.35.refs_1_) | copy-start | bytes 4128772
  157.7 42.0 %collective-permute-start.17 = (bf16[224,1536]{1,0:T(8,128)(2,1)}, bf16[224,1536]{1,0:T(8,128)(2,1)}, u32[]{:S(2)}, u32[]{:S(2)}) collective-permute-start(bf16[224,1536]{1,0:T(8,128)(2,1)} %get-tuple-element.36), channel_id=1, source_target_pairs={{0,128},{32,160},{64,192},{96,224},{128,0},{160,32},{192,64},{224,... | collective-permute-start | bytes 2064392 | tf_op jit(solution)/shard_map/ppermute | solution.py:298
  187.8 27.4 %collective-permute-start.16 = (bf16[160,1536]{1,0:T(8,128)(2,1)}, bf16[160,1536]{1,0:T(8,128)(2,1)S(1)}, u32[]{:S(2)}, u32[]{:S(2)}) collective-permute-start(bf16[160,1536]{1,0:T(8,128)(2,1)} %get-tuple-element.34), channel_id=1, source_target_pairs={{0,128},{32,160},{64,192},{96,224},{128,0},{160,32},{192,64},{224,... | collective-permute-start | bytes 1474568 | tf_op jit(solution)/shard_map/ppermute | solution.py:298
  198.8 16.4 %copy-start.3 = (f32[160,1536]{1,0:T(8,128)S(1)}, f32[160,1536]{1,0:T(8,128)}, u32[]{:S(2)}) copy-start(f32[160,1536]{1,0:T(8,128)} %get-tuple-element.33.refs_1_) | copy-start | bytes 2949124
  198.8 16.4 %copy-start.7 = (f32[160,1]{1,0:T(8,128)S(1)}, f32[160,1]{1,0:T(8,128)}, u32[]{:S(2)}) copy-start(f32[160,1]{1,0:T(8,128)} %copy.23.refs_4_) | copy-start | bytes 1924
Sparse Core Ops, SparseCore 0:
  9.2 122.6 all-gather.3
